TPU v7x, 32 devices: a whole 2x2x4 slice. The times are simulated.
32 devices in a mesh: dp: 8 (over z, x), ctx: 4 (over y, core).
Axes of the slice: x: 2, y: 2, z: 4, core: 2. Of those that a mesh axis runs over, the one named last changes fastest.
Arguments:
- tokens: bfloat16 [8, 2048, 1152], P('dp', 'ctx'), may hold values from -6 to 6
- cotangent: bfloat16 [8, 2048, 1152], P('dp', 'ctx'), may hold values from -6 to 6
- lengths: int32 [8, 2], P('dp'), may hold values from 512 to 1536, as said below
- w_qkv: float32 [1152, 1536], P(('dp', 'ctx')), may hold values from -0.1875 to 0.1875
- w_out: float32 [1024, 1152], P(('dp', 'ctx')), may hold values from -0.1875 to 0.1875
- w_gate_up: float32 [1152, 13824], P(('dp', 'ctx')), may hold values from -0.1875 to 0.1875
- w_down: float32 [6912, 1152], P(('dp', 'ctx')), may hold values from -0.078125 to 0.078125
- gains: float32 [4, 1152], P(None, ('dp', 'ctx')), may hold values from 0.4 to 5
- head_gains: float32 [2, 256], P(None, ('dp', 'ctx')), may hold values from 0.5 to 1.5
- first_qkv: float32 [1152, 1536], P(('dp', 'ctx')), may hold values from -0.00012207031 to 0.00012207031
- first_out: float32 [1024, 1152], P(('dp', 'ctx')), may hold values from -0.00012207031 to 0.00012207031
- first_gate_up: float32 [1152, 13824], P(('dp', 'ctx')), may hold values from -0.00012207031 to 0.00012207031
- first_down: float32 [6912, 1152], P(('dp', 'ctx')), may hold values from -0.00012207031 to 0.00012207031
- first_gains: float32 [4, 1152], P(None, ('dp', 'ctx')), may hold values from -0.00048828125 to 0.00048828125
- first_head: float32 [2, 256], P(None, ('dp', 'ctx')), may hold values from -0.00048828125 to 0.00048828125
- second_qkv: float32 [1152, 1536], P(('dp', 'ctx')), may hold values from 1.9745092e-09 to 7.823528e-09
- second_out: float32 [1024, 1152], P(('dp', 'ctx')), may hold values from 1.9745092e-09 to 7.823528e-09
- second_gate_up: float32 [1152, 13824], P(('dp', 'ctx')), may hold values from 1.9745092e-09 to 7.823528e-09
- second_down: float32 [6912, 1152], P(('dp', 'ctx')), may hold values from 1.9745092e-09 to 7.823528e-09
- second_gains: float32 [4, 1152], P(None, ('dp', 'ctx')), may hold values from 3.129411e-08 to 1.2666663e-07
- second_head: float32 [2, 256], P(None, ('dp', 'ctx')), may hold values from 3.129411e-08 to 1.2666663e-07
Outputs:
- output: bfloat16 [8, 2048, 1152], P('dp', 'ctx')
- input_grad: float32 [8, 2048, 1152], P('dp', 'ctx')
- new_qkv: float32 [1152, 1536], P(('dp', 'ctx'))
- new_out: float32 [1024, 1152], P(('dp', 'ctx'))
- new_gate_up: float32 [1152, 13824], P(('dp', 'ctx'))
- new_down: float32 [6912, 1152], P(('dp', 'ctx'))
- new_gains: float32 [4, 1152], P(None, ('dp', 'ctx'))
- new_head_gains: float32 [2, 256], P(None, ('dp', 'ctx'))
- new_first_qkv: float32 [1152, 1536], P(('dp', 'ctx'))
- new_first_out: float32 [1024, 1152], P(('dp', 'ctx'))
- new_first_gate_up: float32 [1152, 13824], P(('dp', 'ctx'))
- new_first_down: float32 [6912, 1152], P(('dp', 'ctx'))
- new_first_gains: float32 [4, 1152], P(None, ('dp', 'ctx'))
- new_first_head: float32 [2, 256], P(None, ('dp', 'ctx'))
- new_second_qkv: float32 [1152, 1536], P(('dp', 'ctx'))
- new_second_out: float32 [1024, 1152], P(('dp', 'ctx'))
- new_second_gate_up: float32 [1152, 13824], P(('dp', 'ctx'))
- new_second_down: float32 [6912, 1152], P(('dp', 'ctx'))
- new_second_gains: float32 [4, 1152], P(None, ('dp', 'ctx'))
- new_second_head: float32 [2, 256], P(None, ('dp', 'ctx'))
- grad_norm: float32 [], replicated
Inputs may be any that keep to these rules, and one draw needn't show every extreme that they name: `lengths`: each row holds 1536 and 512 in either order, so it sums to 2048.
All inputs are finite; a program needn't handle non-finite values.
Results may differ from a plain program's by a relative error of at most 0.019.
The roundings to bfloat16 on the way count: a program that leaves them out, or rounds other values in their place, can miss the bound.
Values may be sent and summed in bfloat16 or wider, within the bound.
No kernel may reach another device: no remote copies, remote signals or barrier semaphores. Data moves between devices by JAX's collectives and lax.ppermute only.
A program may use at most 384 MiB of HBM per device.

v0:
```python
from functools import partial

import jax
import jax.numpy as jnp
from jax import lax
from jax.sharding import PartitionSpec as P

D = 1152
H = 4
HD = 256
FF = 6912
STEP = 10


EPSILON = 1e-06
ROPE_BASE = 1000000.0
BETA_ONE = 0.9
BETA_TWO = 0.95
ADAM_EPSILON = 1e-08
WEIGHT_DECAY = 0.1
GAIN_RATE = 1.0


def stored_positions(stored, count, per_device):
    half = per_device // 2
    device = stored // per_device
    within = stored % per_device
    block = jnp.where(within < half, device, 2 * count - 1 - device)
    return block * half + within % half


def document_of(positions, doc_lengths):
    ends = jnp.cumsum(doc_lengths)
    starts = ends - doc_lengths
    inside = (positions[:, None] >= starts[None, :]) & (positions[:, None] < ends[None, :])
    numbers = jnp.arange(doc_lengths.shape[0], dtype=jnp.int32)
    doc_ids = jnp.sum(jnp.where(inside, numbers[None, :], 0), axis=1)
    doc_starts = jnp.sum(jnp.where(inside, starts[None, :], 0), axis=1)
    return (doc_ids, doc_starts)


def rope_tables(offsets, width):
    half = width // 2
    freq = jnp.exp(-jnp.log(ROPE_BASE) * jnp.arange(half, dtype=jnp.float32) * (2.0 / width))
    angle = offsets.astype(jnp.float32)[:, None] * freq[None, :]
    return (jnp.cos(angle), jnp.sin(angle))


def rotate(field, cos_t, sin_t):
    half = field.shape[-1] // 2
    first_half = field[..., :half]
    second_half = field[..., half:]
    return jnp.concatenate(
        [first_half * cos_t - second_half * sin_t, second_half * cos_t + first_half * sin_t],
        axis=-1,
    )


def rotate_back(grad, cos_t, sin_t):
    half = grad.shape[-1] // 2
    first_half = grad[..., :half]
    second_half = grad[..., half:]
    return jnp.concatenate(
        [first_half * cos_t + second_half * sin_t, second_half * cos_t - first_half * sin_t],
        axis=-1,
    )


def norm_forward(field, gain):
    scale = lax.rsqrt(jnp.mean(field * field, axis=-1, keepdims=True) + EPSILON)
    return (field * scale * gain, scale)


def norm_backward(field, scale, gain, grad):
    weighted = grad * gain
    field_grad = scale * weighted - field * (scale * scale * scale) * jnp.mean(
        weighted * field, axis=-1, keepdims=True
    )
    gain_grad = jnp.sum((grad * field * scale).reshape(-1, field.shape[-1]), axis=0)
    return (field_grad, gain_grad)


def adam_update(weight, first, second, grad, rate, decay):
    first_new = BETA_ONE * first + (1.0 - BETA_ONE) * grad
    second_new = BETA_TWO * second + (1.0 - BETA_TWO) * grad * grad
    first_hat = first_new / (1.0 - BETA_ONE**STEP)
    second_hat = second_new / (1.0 - BETA_TWO**STEP)
    updated = weight - rate * (first_hat / (jnp.sqrt(second_hat) + ADAM_EPSILON) + decay * weight)
    return (updated, first_new, second_new)


def local(
    tokens,
    cotangent,
    lengths,
    w_qkv,
    w_out,
    w_gate_up,
    w_down,
    gains,
    head_gains,
    first_qkv,
    first_out,
    first_gate_up,
    first_down,
    first_gains,
    first_head,
    second_qkv,
    second_out,
    second_gate_up,
    second_down,
    second_gains,
    second_head,
):
    row_count = tokens.shape[1]
    inputs = tokens[0].astype(jnp.float32)
    grad_result = cotangent[0].astype(jnp.float32)
    doc_lengths = lengths[0]
    ctx_count = lax.axis_size("ctx")
    ctx_place = lax.axis_index("ctx")
    score_scale = HD ** (-0.5)
    shards = (
        w_qkv.astype(jnp.bfloat16),
        w_out.astype(jnp.bfloat16),
        w_gate_up.astype(jnp.bfloat16),
        w_down.astype(jnp.bfloat16),
        gains.astype(jnp.bfloat16),
        head_gains.astype(jnp.bfloat16),
    )
    full_qkv, full_out, full_gate_up, full_down, gain_low, head_low = (
        lax.all_gather(shards[0], ("dp", "ctx"), axis=0, tiled=True),
        lax.all_gather(shards[1], ("dp", "ctx"), axis=0, tiled=True),
        lax.all_gather(shards[2], ("dp", "ctx"), axis=0, tiled=True),
        lax.all_gather(shards[3], ("dp", "ctx"), axis=0, tiled=True),
        lax.all_gather(shards[4], ("dp", "ctx"), axis=1, tiled=True),
        lax.all_gather(shards[5], ("dp", "ctx"), axis=1, tiled=True),
    )
    gain_rows = gain_low.astype(jnp.float32)
    head_rows = head_low.astype(jnp.float32)
    local_rows = ctx_place * row_count + jnp.arange(row_count, dtype=jnp.int32)
    query_pos = stored_positions(local_rows, ctx_count, row_count)
    key_pos = stored_positions(
        jnp.arange(ctx_count * row_count, dtype=jnp.int32), ctx_count, row_count
    )
    query_doc, query_start = document_of(query_pos, doc_lengths)
    key_doc, key_start = document_of(key_pos, doc_lengths)
    allowed = (query_doc[:, None] == key_doc[None, :]) & (key_pos[None, :] <= query_pos[:, None])
    cos_t, sin_t = rope_tables(query_pos - query_start, HD)
    normed, scale_in = norm_forward(inputs, gain_rows[0])
    normed_low = normed.astype(jnp.bfloat16)
    qkv = jnp.dot(normed_low, full_qkv, preferred_element_type=jnp.float32)
    query = qkv[:, : H * HD].reshape(row_count, H, HD)
    key_part = qkv[:, H * HD : (H + 1) * HD]
    value_part = qkv[:, (H + 1) * HD :]
    query_normed, query_scale = norm_forward(query, head_rows[0])
    key_normed, key_scale = norm_forward(key_part, head_rows[1])
    query_low = rotate(query_normed, cos_t[:, None, :], sin_t[:, None, :]).astype(jnp.bfloat16)
    key_low = rotate(key_normed, cos_t, sin_t).astype(jnp.bfloat16)
    value_low = value_part.astype(jnp.bfloat16)
    keys_all, values_all = (
        lax.all_gather(key_low, "ctx", axis=0, tiled=True),
        lax.all_gather(value_low, "ctx", axis=0, tiled=True),
    )
    scores = (
        jnp.einsum("qhd,kd->hqk", query_low, keys_all, preferred_element_type=jnp.float32)
        * score_scale
    )
    masked = jnp.where(allowed[None], scores, -1e30)
    row_peak = jnp.max(masked, axis=-1, keepdims=True)
    log_total = row_peak + jnp.log(jnp.sum(jnp.exp(masked - row_peak), axis=-1, keepdims=True))
    probs = jnp.exp(masked - log_total)
    mixed = jnp.einsum(
        "hqk,kd->qhd", probs.astype(jnp.bfloat16), values_all, preferred_element_type=jnp.float32
    )
    mixed_low = mixed.reshape(row_count, H * HD).astype(jnp.bfloat16)
    proj = jnp.dot(mixed_low, full_out, preferred_element_type=jnp.float32)
    branch_attn, scale_attn = norm_forward(proj, gain_rows[1])
    resid = inputs + branch_attn
    pre_ff, scale_pre = norm_forward(resid, gain_rows[2])
    pre_low = pre_ff.astype(jnp.bfloat16)
    gate_up = jnp.dot(pre_low, full_gate_up, preferred_element_type=jnp.float32)
    gate = gate_up[:, :FF]
    upper = gate_up[:, FF:]
    activ = jax.nn.gelu(gate, approximate=True)
    hidden_low = (activ * upper).astype(jnp.bfloat16)
    ffn = jnp.dot(hidden_low, full_down, preferred_element_type=jnp.float32)
    branch_ffn, scale_ffn = norm_forward(ffn, gain_rows[3])
    result = resid + branch_ffn
    full_qkv, full_out, full_gate_up, full_down, gain_low, head_low = (
        lax.all_gather(shards[0], ("dp", "ctx"), axis=0, tiled=True),
        lax.all_gather(shards[1], ("dp", "ctx"), axis=0, tiled=True),
        lax.all_gather(shards[2], ("dp", "ctx"), axis=0, tiled=True),
        lax.all_gather(shards[3], ("dp", "ctx"), axis=0, tiled=True),
        lax.all_gather(shards[4], ("dp", "ctx"), axis=1, tiled=True),
        lax.all_gather(shards[5], ("dp", "ctx"), axis=1, tiled=True),
    )
    keys_all, values_all = (
        lax.all_gather(key_low, "ctx", axis=0, tiled=True),
        lax.all_gather(value_low, "ctx", axis=0, tiled=True),
    )
    ffn_grad, gain_grad_d = norm_backward(ffn, scale_ffn, gain_rows[3], grad_result)
    ffn_low = ffn_grad.astype(jnp.bfloat16)
    grad_down = jnp.dot(hidden_low.T, ffn_low, preferred_element_type=jnp.float32)
    hidden_grad = jnp.dot(ffn_low, full_down.T, preferred_element_type=jnp.float32)
    gelu_value, gelu_pull = jax.vjp(partial(jax.nn.gelu, approximate=True), gate)
    gate_grad = gelu_pull(hidden_grad * upper)[0]
    upper_grad = hidden_grad * activ
    gate_up_low = jnp.concatenate([gate_grad, upper_grad], axis=1).astype(jnp.bfloat16)
    grad_gate_up = jnp.dot(pre_low.T, gate_up_low, preferred_element_type=jnp.float32)
    pre_grad = jnp.dot(gate_up_low, full_gate_up.T, preferred_element_type=jnp.float32)
    resid_part, gain_grad_c = norm_backward(resid, scale_pre, gain_rows[2], pre_grad)
    resid_grad = grad_result + resid_part
    proj_grad, gain_grad_b = norm_backward(proj, scale_attn, gain_rows[1], resid_grad)
    proj_low = proj_grad.astype(jnp.bfloat16)
    grad_out = jnp.dot(mixed_low.T, proj_low, preferred_element_type=jnp.float32)
    mixed_grad = jnp.dot(proj_low, full_out.T, preferred_element_type=jnp.float32)
    mixed_grad = mixed_grad.reshape(row_count, H, HD).astype(jnp.bfloat16)
    rescored = (
        jnp.einsum("qhd,kd->hqk", query_low, keys_all, preferred_element_type=jnp.float32)
        * score_scale
    )
    again_probs = jnp.exp(jnp.where(allowed[None], rescored, -1e30) - log_total)
    prob_grad = jnp.einsum(
        "qhd,kd->hqk", mixed_grad, values_all, preferred_element_type=jnp.float32
    )
    inner = jnp.sum(again_probs * prob_grad, axis=-1, keepdims=True)
    score_grad = (again_probs * (prob_grad - inner)).astype(jnp.bfloat16)
    query_grad = (
        jnp.einsum("hqk,kd->qhd", score_grad, keys_all, preferred_element_type=jnp.float32)
        * score_scale
    )
    key_terms = (
        jnp.einsum("hqk,qhd->kd", score_grad, query_low, preferred_element_type=jnp.float32)
        * score_scale
    )
    value_terms = jnp.einsum(
        "hqk,qhd->kd",
        again_probs.astype(jnp.bfloat16),
        mixed_grad,
        preferred_element_type=jnp.float32,
    )
    key_grad, value_grad = (
        lax.psum_scatter(
            key_terms.astype(jnp.bfloat16), "ctx", scatter_dimension=0, tiled=True
        ).astype(jnp.float32),
        lax.psum_scatter(
            value_terms.astype(jnp.bfloat16), "ctx", scatter_dimension=0, tiled=True
        ).astype(jnp.float32),
    )
    query_turned = rotate_back(query_grad, cos_t[:, None, :], sin_t[:, None, :])
    key_turned = rotate_back(key_grad, cos_t, sin_t)
    query_raw, head_grad_q = norm_backward(query, query_scale, head_rows[0], query_turned)
    key_raw, head_grad_k = norm_backward(key_part, key_scale, head_rows[1], key_turned)
    qkv_low = jnp.concatenate(
        [query_raw.reshape(row_count, H * HD), key_raw, value_grad], axis=1
    ).astype(jnp.bfloat16)
    grad_qkv = jnp.dot(normed_low.T, qkv_low, preferred_element_type=jnp.float32)
    normed_grad = jnp.dot(qkv_low, full_qkv.T, preferred_element_type=jnp.float32)
    input_part, gain_grad_a = norm_backward(inputs, scale_in, gain_rows[0], normed_grad)
    input_grad = resid_grad + input_part
    gain_grads = jnp.stack([gain_grad_a, gain_grad_b, gain_grad_c, gain_grad_d], axis=0)
    head_grads = jnp.stack([head_grad_q, head_grad_k], axis=0)
    reduced = (
        lax.psum_scatter(grad_qkv, ("dp", "ctx"), scatter_dimension=0, tiled=True),
        lax.psum_scatter(grad_out, ("dp", "ctx"), scatter_dimension=0, tiled=True),
        lax.psum_scatter(grad_gate_up, ("dp", "ctx"), scatter_dimension=0, tiled=True),
        lax.psum_scatter(grad_down, ("dp", "ctx"), scatter_dimension=0, tiled=True),
        lax.psum_scatter(gain_grads, ("dp", "ctx"), scatter_dimension=1, tiled=True),
        lax.psum_scatter(head_grads, ("dp", "ctx"), scatter_dimension=1, tiled=True),
    )
    local_squares = jnp.float32(0.0)
    for piece in reduced:
        local_squares = local_squares + jnp.sum(piece * piece)
    total_squares = lax.psum(local_squares, ("dp", "ctx"))
    grad_norm = jnp.sqrt(total_squares)
    factor = 1.0 / jnp.maximum(grad_norm, 1.0)
    weights = (w_qkv, w_out, w_gate_up, w_down, gains, head_gains)
    firsts = (first_qkv, first_out, first_gate_up, first_down, first_gains, first_head)
    seconds = (second_qkv, second_out, second_gate_up, second_down, second_gains, second_head)
    rates = (D ** (-0.5), (H * HD) ** (-0.5), D ** (-0.5), FF ** (-0.5), GAIN_RATE, GAIN_RATE)
    decays = (WEIGHT_DECAY, WEIGHT_DECAY, WEIGHT_DECAY, WEIGHT_DECAY, 0.0, 0.0)
    updates = [
        adam_update(
            weights[index],
            firsts[index],
            seconds[index],
            reduced[index] * factor,
            rates[index],
            decays[index],
        )
        for index in range(6)
    ]
    return (
        result.astype(jnp.bfloat16)[None],
        input_grad[None],
        updates[0][0],
        updates[1][0],
        updates[2][0],
        updates[3][0],
        updates[4][0],
        updates[5][0],
        updates[0][1],
        updates[1][1],
        updates[2][1],
        updates[3][1],
        updates[4][1],
        updates[5][1],
        updates[0][2],
        updates[1][2],
        updates[2][2],
        updates[3][2],
        updates[4][2],
        updates[5][2],
        grad_norm,
    )


def solution(mesh):
    in_specs = (
        P("dp", "ctx", None),
        P("dp", "ctx", None),
        P("dp", None),
        P(("dp", "ctx"), None),
        P(("dp", "ctx"), None),
        P(("dp", "ctx"), None),
        P(("dp", "ctx"), None),
        P(None, ("dp", "ctx")),
        P(None, ("dp", "ctx")),
        P(("dp", "ctx"), None),
        P(("dp", "ctx"), None),
        P(("dp", "ctx"), None),
        P(("dp", "ctx"), None),
        P(None, ("dp", "ctx")),
        P(None, ("dp", "ctx")),
        P(("dp", "ctx"), None),
        P(("dp", "ctx"), None),
        P(("dp", "ctx"), None),
        P(("dp", "ctx"), None),
        P(None, ("dp", "ctx")),
        P(None, ("dp", "ctx")),
    )
    out_specs = (
        P("dp", "ctx", None),
        P("dp", "ctx", None),
        P(("dp", "ctx"), None),
        P(("dp", "ctx"), None),
        P(("dp", "ctx"), None),
        P(("dp", "ctx"), None),
        P(None, ("dp", "ctx")),
        P(None, ("dp", "ctx")),
        P(("dp", "ctx"), None),
        P(("dp", "ctx"), None),
        P(("dp", "ctx"), None),
        P(("dp", "ctx"), None),
        P(None, ("dp", "ctx")),
        P(None, ("dp", "ctx")),
        P(("dp", "ctx"), None),
        P(("dp", "ctx"), None),
        P(("dp", "ctx"), None),
        P(("dp", "ctx"), None),
        P(None, ("dp", "ctx")),
        P(None, ("dp", "ctx")),
        P(),
    )
    return jax.shard_map(local, mesh=mesh, in_specs=in_specs, out_specs=out_specs, check_vma=False)
```

profile of v0, /device:TPU:0, one launch (start us, length us, event | category | flops | bytes accessed | tf_op | source)
XLA Modules:
  0.0 2495.3 jit_solution(9955711178328993131)
XLA Ops:
  9.6 43.3 %all-gather = bf16[32,36,4]{1,2,0:T(4,128)(2,1)S(1)} all-gather(bf16[1,36,4]{1,2,0:T(4,128)(2,1)S(1)} %convert_bitcast_fusion.2), channel_id=1, replica_groups=mesh['dp'=8,'ctx'=4] {'dp','ctx'}, dimensions={0}, use_global_device_ids=true | all-gather | bytes 9504 | tf_op jit(solution)/shard_map/all_gather | solution.py:135
  53.7 36.6 %all-gather.2 = bf16[32,8,2]{1,2,0:T(2,128)(2,1)S(1)} all-gather(bf16[1,8,2]{1,2,0:T(2,128)(2,1)S(1)} %convert_bitcast_fusion.3), channel_id=1, replica_groups=mesh['dp'=8,'ctx'=4] {'dp','ctx'}, dimensions={0}, use_global_device_ids=true | all-gather | bytes 1056 | tf_op jit(solution)/shard_map/all_gather | solution.py:136
  97.3 5.6 reshape.442
  103.0 4.6 fusion.65
  129.5 4.5 fusion.15
  134.1 4.1 exponential_reduce_fusion
  139.9 5.0 all-gather.11.cloned.1.call-done
  145.0 11.0 convolution_convert_fusion.1
  155.9 49.7 %all-gather.15.cloned.1.call-done = bf16[1024,1152]{1,0:T(8,128)(2,1)} async-done(((bf16[32,1152]{1,0:T(8,128)(2,1)}), bf16[1024,1152]{1,0:T(8,128)(2,1)}) %all-gather.15.cloned.1.call-update) | async-done | bytes 2359312 | tf_op jit(solution)/shard_map/all_gather | solution.py:132
  205.6 3.4 multiply_reduce_fusion.6
  211.1 200.5 %all-gather.21.cloned.1.call-done = bf16[32,36,13824]{2,1,0:T(8,128)(2,1)} async-done(((bf16[1,36,13824]{2,1,0:T(8,128)(2,1)}), bf16[32,36,13824]{2,1,0:T(8,128)(2,1)}) %all-gather.21.cloned.1.call-update) | async-done | bytes 31850512 | tf_op jit(solution)/shard_map/all_gather | solution.py:133
  411.5 29.1 %reshape.446 = bf16[1152,13824]{1,0:T(8,128)(2,1)} reshape(bf16[32,36,13824]{2,1,0:T(8,128)(2,1)} %all-gather.21.cloned.1.call-done) | data formatting | bytes 63700992
  440.7 28.4 %fusion.101 = f32[512,13824]{1,0:T(8,128)} fusion(bf16[1152,13824]{1,0:T(8,128)(2,1)} %reshape.446, f32[512,1152]{1,0:T(8,128)S(1)} %get-tuple-element.59, f32[1152]{0:T(1024)S(1)} %get-tuple-element.32, f32[512]{0:T(512)S(1)} %get-tuple-element.86), kind=kOutput, calls=%fused_computation.237 | convolution fusion | flops 16309223424 | bytes 62528000 | tf_op jit(solution)/shard_map/dot_general | solution.py:181
  469.0 14.9 multiply_convert_fusion.1
  483.9 40.1 %all-gather.17.cloned.1.call-done = bf16[6912,1152]{1,0:T(8,128)(2,1)} async-done(((bf16[216,1152]{1,0:T(8,128)(2,1)}), bf16[6912,1152]{1,0:T(8,128)(2,1)}) %all-gather.17.cloned.1.call-update) | async-done | bytes 15925264 | tf_op jit(solution)/shard_map/all_gather | solution.py:134
  524.0 14.4 multiply_reduce_fusion.4
  542.2 28.4 %fusion.11 = (bf16[512,6912]{1,0:T(8,128)(2,1)}, bf16[512,6912]{1,0:T(8,128)(2,1)}) fusion(f32[512,13824]{1,0:T(8,128)} %fusion.101, bf16[6912,1152]{1,0:T(8,128)(2,1)} %all-gather.17.cloned.1.call-done, f32[512,1152]{1,0:T(8,128)} %copy-done.34, bf16[1,512,1152]{2,1,0:T(8,128)(2,1)S(1)} %copy-done.22, f32[512]{0:T(512)} %broadcast_multiply_fusion.5, ...), kind=kOutput, calls=%fused_computation.16 | convolution fusion | flops 8242790400 | bytes 61942272 | tf_op jit(solution)/shard_map/dot_general | solution.py:204
  570.6 28.0 %multiply_reduce_fusion = (f32[1152]{0:T(1024)}, f32[512]{0:T(512)}, f32[512,1152]{1,0:T(8,128)}) fusion(f32[512,1152]{1,0:T(8,128)S(1)} %get-tuple-element.59, f32[512]{0:T(512)S(1)} %get-tuple-element.86, f32[1152]{0:T(1024)S(1)} %get-tuple-element.32, bf16[1152,13824]{1,0:T(8,128)(2,1)} %reshape.446, bf16[512,6912]{1,0:T(8,128)(2,1)} %get-tuple-element.61, ...), kind=kOutput, calls=%fused_computation.58 | convolution fusion | flops 16339302400 | bytes 50738176 | tf_op jit(solution)/shard_map/dot_general | solution.py:210
  599.3 4.1 multiply_reduce_fusion.1
  608.0 11.7 fusion.2
  619.7 12.9 fusion.4
  632.6 3.2 copy-done.16
  635.8 3.4 fusion.19
  639.3 11.5 fusion.20
  650.9 5.2 fusion.115
  663.0 19.3 fusion.104
  682.3 33.2 %fusion.13 = f32[1152,13824]{1,0:T(8,128)} fusion(bf16[512,6912]{1,0:T(8,128)(2,1)} %get-tuple-element.61, bf16[512,6912]{1,0:T(8,128)(2,1)} %get-tuple-element.60, f32[512,1152]{1,0:T(8,128)S(1)} %get-tuple-element.59, f32[1152]{0:T(1024)S(1)} %get-tuple-element.32, f32[512]{0:T(512)S(1)} %get-tuple-element.86), kind=kOutput, calls=%fused_computation.22 | convolution fusion | flops 16337534976 | bytes 80222720 | tf_op jit(solution)/shard_map/dot_general | solution.py:209
  715.5 995.4 %fusion.1 = f32[48,13824]{1,0:T(8,128)} fusion(f32[1152,13824]{1,0:T(8,128)} %fusion.13), kind=kCustom, calls=%all-reduce-scatter.1 | all-reduce-scatter fusion | flops 21233664 | bytes 66355200
  1714.1 19.5 collective-permute-start.10
  1733.6 4.2 collective-permute-start.4
  1737.9 6.8 multiply_bitcast_fusion
  1762.8 6.4 fusion.54
  1769.2 167.3 %fusion = f32[40,1536]{1,0:T(8,128)} fusion(f32[1152,1536]{1,0:T(8,128)} %fusion.54), kind=kCustom, calls=%all-reduce-scatter | all-reduce-scatter fusion | flops 1966081 | bytes 7323648
  1937.3 7.2 collective-permute-start.3
  1944.4 6.1 collective-permute-start
  1950.5 4.6 collective-permute-start.1
  1955.1 6.4 collective-permute-start.2
  1961.6 3.7 collective-permute-start.5
  1968.0 4.7 collective-permute-start.7
  1972.7 3.3 collective-permute-start.8
  1976.0 7.0 collective-permute-start.9
  1990.4 3.9 fusion.35
  1994.3 320.4 %all-reduce.7 = (f32[4,1152]{1,0:T(4,128)S(1)}, f32[2,256]{1,0:T(2,128)S(1)}) all-reduce(f32[4,1152]{1,0:T(4,128)S(1)} %pad_maximum_fusion.12, f32[2,256]{1,0:T(2,128)S(1)} %pad_maximum_fusion.13), channel_id=8, replica_groups=mesh['dp'=8,'ctx'=4] {'dp','ctx'}, use_global_device_ids=true, to_apply=%region_33.34.clone | all-reduce | flops 5120 | bytes 40960
  2316.6 4.1 concatenate.41
  2321.7 96.3 %concatenate.42 = f32[420,13824]{1,0:T(8,128)} concatenate(f32[36,13824]{1,0:T(8,128)} %collective-permute-done.11, f32[48,13824]{1,0:T(8,128)} %collective-permute-done.10, f32[48,13824]{1,0:T(8,128)} %collective-permute-done.9, f32[48,13824]{1,0:T(8,128)} %collective-permute-done.8, f32[48,13824]{1,0:T(8,128)} %collective-permute-done.7, f32[48,13824]{1,0:T(8,128)} %collective-permute-done.6, ...), dimensions={0} | concatenate | bytes 46448640
  2428.7 3.7 fusion.32
  2432.3 38.0 %psum.7 = f32[]{:T(128)} all-reduce(f32[]{:T(128)S(6)} %add.375), channel_id=1, replica_groups=mesh['dp'=8,'ctx'=4] {'dp','ctx'}, use_global_device_ids=true, to_apply=%region_39.40 | all-reduce | flops 1 | bytes 8 | tf_op jit(solution)/shard_map/psum | solution.py:274
  2473.9 7.9 multiply_subtract_fusion
  (341 shorter events, 100.9 us)
Async XLA Ops:
  7.2 90.1 %all-gather.19.cloned.1.call-start = ((), (), s32[]{:S(2)}) async-start(), calls=%async_computation.11 | async-start | bytes 4055040 | tf_op jit(solution)/shard_map/all_gather | solution.py:131
  8.9 120.6 %all-gather.13.cloned.1.call-start = ((), (), s32[]{:S(2)}) async-start(), calls=%async_computation.5 | async-start | bytes 1310720 | tf_op jit(solution)/shard_map/all_gather | solution.py:161
  92.6 10.3 copy-start.96
  93.9 9.0 copy-start.67
  93.9 115.7 %copy-start.59 = (f32[1152]{0:T(1024)}, f32[1152]{0:T(1024)S(1)}, u32[]{:S(2)}) copy-start(f32[1152]{0:T(1024)S(1)} %get-tuple-element.33) | copy-start | bytes 13828
  96.1 12.4 copy-start.79
  111.1 18.1 copy-start.30
  111.9 33.1 %all-gather.11.cloned.1.call-start = ((), (), s32[]{:S(2)}) async-start(), calls=%async_computation.4 | async-start | bytes 1310720 | tf_op jit(solution)/shard_map/all_gather | solution.py:162
  112.7 92.9 %all-gather.15.cloned.1.call-start = ((), (), s32[]{:S(2)}) async-start(), calls=%async_computation.6 | async-start | bytes 2433024 | tf_op jit(solution)/shard_map/all_gather | solution.py:132
  114.3 297.2 %all-gather.21.cloned.1.call-start = ((), (), s32[]{:S(2)}) async-start(), calls=%async_computation.12 | async-start | bytes 36495360 | tf_op jit(solution)/shard_map/all_gather | solution.py:133
  117.3 406.7 %all-gather.17.cloned.1.call-start = ((), (), s32[]{:S(2)}) async-start(), calls=%async_computation.7 | async-start | bytes 16422912 | tf_op jit(solution)/shard_map/all_gather | solution.py:134
  118.2 1637.8 %reduce-scatter.13.cloned.1.call-start = ((), (), s32[]{:S(2)}) async-start(), calls=%async_computation.8 | async-start | bytes 1310720 | tf_op jit(solution)/shard_map/reduce_scatter | solution.py:243
  120.0 24.9 copy-start.5
  139.9 16.0 copy-start.52
  155.9 53.1 %copy-start.21 = (bf16[256,4,512]{2,0,1:T(8,128)(2,1)}, bf16[256,4,512]{2,0,1:T(8,128)(2,1)S(1)}, u32[]{:S(2)}) copy-start(bf16[256,4,512]{2,0,1:T(8,128)(2,1)S(1)} %convolution_convert_fusion.1) | copy-start | bytes 3145732
  483.9 55.1 %copy-start.22 = (bf16[1,512,1152]{2,1,0:T(8,128)(2,1)S(1)}, bf16[1,512,1152]{2,1,0:T(8,128)(2,1)}, u32[]{:S(2)}) copy-start(bf16[1,512,1152]{2,1,0:T(8,128)(2,1)} %param.22) | copy-start | bytes 3538948
  524.0 15.0 copy-start.69
  570.6 28.7 %copy-start.64 = (f32[512]{0:T(512)S(1)}, f32[512]{0:T(512)}, u32[]{:S(2)}) copy-start(f32[512]{0:T(512)} %copy-done.63) | copy-start | bytes 6148
  607.6 12.1 copy-start.29
  619.7 16.1 copy-start.49
  619.7 16.1 copy-start.51
  639.3 1123.5 %reduce-scatter.15.cloned.1.call-start = ((), (), s32[]{:S(2)}) async-start(), calls=%async_computation.9 | async-start | bytes 1310720 | tf_op jit(solution)/shard_map/reduce_scatter | solution.py:246
  650.8 1770.3 %reduce-scatter.17.cloned.1.call-start = ((), (), s32[]{:S(2)}) async-start(), calls=%async_computation.10 | async-start | bytes 4866048 | tf_op jit(solution)/shard_map/reduce_scatter | solution.py:265
  656.1 1768.5 %reduce-scatter.19.cloned.1.call-start = ((), (), s32[]{:S(2)}) async-start(), calls=%async_computation.13 | async-start | bytes 32845824
  1710.9 27.0 %copy-start.102 = (bf16[2048,256]{1,0:T(8,128)(2,1)S(1)}, bf16[2048,256]{1,0:T(8,128)(2,1)}, u32[]{:S(2)}) copy-start(bf16[2048,256]{1,0:T(8,128)(2,1)} %all-gather.13.cloned.1.call-done) | copy-start | bytes 3145732
  1714.1 30.5 %copy-start.31 = (f32[512,128]{1,0:T(8,128)S(1)}, f32[512,128]{1,0:T(8,128)}, u32[]{:S(2)}) copy-start(f32[512,128]{1,0:T(8,128)} %copy-done.30) | copy-start | bytes 786436
  1714.1 30.5 %copy-start.33 = (f32[512,128]{1,0:T(8,128)S(1)}, f32[512,128]{1,0:T(8,128)}, u32[]{:S(2)}) copy-start(f32[512,128]{1,0:T(8,128)} %get-tuple-element.76) | copy-start | bytes 786436
  1714.1 258.6 %collective-permute-start.10 = (f32[48,13824]{1,0:T(8,128)}, f32[48,13824]{1,0:T(8,128)}, u32[]{:S(2)}, u32[]{:S(2)}) collective-permute-start(f32[48,13824]{1,0:T(8,128)} %fusion.1), channel_id=1, source_target_pairs={{0,7},{1,8},{2,9},{3,10},{4,11},{5,12},{6,13},{7,14},{8,15},{9,16}... | collective-permute-start | bytes 7962632
  1733.6 242.4 %collective-permute-start.4 = (f32[48,13824]{1,0:T(8,128)}, f32[48,13824]{1,0:T(8,128)}, u32[]{:S(2)}, u32[]{:S(2)}) collective-permute-start(f32[48,13824]{1,0:T(8,128)} %fusion.1), channel_id=1, source_target_pairs={{0,1},{1,2},{2,3},{3,4},{4,5},{5,6},{6,7},{7,8},{8,9},{9,10},{10,1... | collective-permute-start | bytes 7962632
  1750.7 199.8 %collective-permute-start.11 = (f32[36,13824]{1,0:T(8,128)}, f32[36,13824]{1,0:T(8,128)}, u32[]{:S(2)}, u32[]{:S(2)}) collective-permute-start(f32[36,13824]{1,0:T(8,128)} %slice.103), channel_id=1, source_target_pairs={{0,8},{1,9},{2,10},{3,11},{4,12},{5,13},{6,14},{7,15},{8,16},{9,17... | collective-permute-start | bytes 5971976
  1769.2 213.9 %copy-start.37 = (f32[512,4]{1,0:T(8,128)S(1)}, f32[512,4]{1,0:T(8,128)}, u32[]{:S(2)}) copy-start(f32[512,4]{1,0:T(8,128)} %copy-done.36) | copy-start | bytes 24580
  1937.3 17.9 collective-permute-start.3
  1944.4 17.2 collective-permute-start
  1950.5 14.7 collective-permute-start.1
  1955.1 12.9 collective-permute-start.2
  1961.6 359.9 %collective-permute-start.5 = (f32[48,13824]{1,0:T(8,128)}, f32[48,13824]{1,0:T(8,128)}, u32[]{:S(2)}, u32[]{:S(2)}) collective-permute-start(f32[48,13824]{1,0:T(8,128)} %fusion.1), channel_id=1, source_target_pairs={{0,2},{1,3},{2,4},{3,5},{4,6},{5,7},{6,8},{7,9},{8,10},{9,11},{10,... | collective-permute-start | bytes 7962632
  1965.2 356.3 %collective-permute-start.6 = (f32[48,13824]{1,0:T(8,128)}, f32[48,13824]{1,0:T(8,128)}, u32[]{:S(2)}, u32[]{:S(2)}) collective-permute-start(f32[48,13824]{1,0:T(8,128)} %fusion.1), channel_id=1, source_target_pairs={{0,3},{1,4},{2,5},{3,6},{4,7},{5,8},{6,9},{7,10},{8,11},{9,12},{10... | collective-permute-start | bytes 7962632
  1968.0 353.5 %collective-permute-start.7 = (f32[48,13824]{1,0:T(8,128)}, f32[48,13824]{1,0:T(8,128)}, u32[]{:S(2)}, u32[]{:S(2)}) collective-permute-start(f32[48,13824]{1,0:T(8,128)} %fusion.1), channel_id=1, source_target_pairs={{0,4},{1,5},{2,6},{3,7},{4,8},{5,9},{6,10},{7,11},{8,12},{9,13},{1... | collective-permute-start | bytes 7962632
  1972.7 348.8 %collective-permute-start.8 = (f32[48,13824]{1,0:T(8,128)}, f32[48,13824]{1,0:T(8,128)}, u32[]{:S(2)}, u32[]{:S(2)}) collective-permute-start(f32[48,13824]{1,0:T(8,128)} %fusion.1), channel_id=1, source_target_pairs={{0,5},{1,6},{2,7},{3,8},{4,9},{5,10},{6,11},{7,12},{8,13},{9,14},{... | collective-permute-start | bytes 7962632
  1976.0 345.5 %collective-permute-start.9 = (f32[48,13824]{1,0:T(8,128)}, f32[48,13824]{1,0:T(8,128)}, u32[]{:S(2)}, u32[]{:S(2)}) collective-permute-start(f32[48,13824]{1,0:T(8,128)} %fusion.1), channel_id=1, source_target_pairs={{0,6},{1,7},{2,8},{3,9},{4,10},{5,11},{6,12},{7,13},{8,14},{9,15},... | collective-permute-start | bytes 7962632
  1990.4 326.2 %copy-start.40 = (f32[40,1536]{1,0:T(8,128)S(1)}, f32[40,1536]{1,0:T(8,128)}, u32[]{:S(2)}) copy-start(f32[40,1536]{1,0:T(8,128)} %fusion) | copy-start | bytes 737284
  2418.0 10.6 copy-start.8
  2418.0 10.6 copy-start.83
  2473.9 7.9 copy-start.55
  2473.9 7.9 copy-start.56
  2473.9 10.0 copy-start.27
  2473.9 10.0 copy-start.43
  2473.9 10.0 copy-start.44
  (78 other events, 232.8 us)
Sparse Core Ops, SparseCore 0:
  11.5 63.9 all-gather.18
  112.0 13.9 all-gather.12
  128.2 16.7 all-gather.10
  148.3 57.2 all-gather.14
  208.9 202.5 all-gather.20
  414.8 109.1 all-gather.16
  639.4 23.0 reduce-scatter.12
  665.2 24.8 reduce-scatter.14
  695.6 137.7 reduce-scatter.16
  840.8 442.5 reduce-scatter.18
where the time goes:
time: 2510 us; the launch traced here: 2500 us
  blocking collectives  1600 us (64%)
  waiting for transfers between devices  295 us (12%)
  matrix products  226 us (9%)
  local copies, waits for them, and re-layouts  173 us (7%)
  other arithmetic  106 us (4%)
  starting transfers between devices  72.9 us (3%)
    unnamed x3, blocking collectives  1480 us
    all_gather x1, waiting for transfers between devices, local(): lax.all_gather(shards[2], ('dp', 'ctx'), axis=0, tiled=True)  200 us
    unnamed x220, local copies, waits for them, and re-layouts  158 us
    unnamed x13, starting transfers between devices  72.5 us
  transfers between devices with their start and end apart: 22, of which 4 were waited for; matrix products, arithmetic and copies ran while one was open for 60% of the time, Pallas kernels for 0%

commit v1 on v0

v1 whole, which is shorter than its diff:
```python
from functools import partial

import jax
import jax.numpy as jnp
from jax import lax
from jax.experimental import pallas as pl
from jax.experimental.pallas import tpu as pltpu
from jax.sharding import PartitionSpec as P

D = 1152
H = 4
HD = 256
FF = 6912
STEP = 10

EPSILON = 1e-06
ROPE_BASE = 1000000.0
BETA_ONE = 0.9
BETA_TWO = 0.95
ADAM_EPSILON = 1e-08
WEIGHT_DECAY = 0.1
GAIN_RATE = 1.0


def rope_tables(offsets, width):
    half = width // 2
    freq = jnp.exp(-jnp.log(ROPE_BASE) * jnp.arange(half, dtype=jnp.float32) * (2.0 / width))
    angle = offsets.astype(jnp.float32)[:, None] * freq[None, :]
    return (jnp.cos(angle), jnp.sin(angle))


def adam_update(weight, first, second, grad, rate, decay):
    first_new = BETA_ONE * first + (1.0 - BETA_ONE) * grad
    second_new = BETA_TWO * second + (1.0 - BETA_TWO) * grad * grad
    first_hat = first_new / (1.0 - BETA_ONE**STEP)
    second_hat = second_new / (1.0 - BETA_TWO**STEP)
    updated = weight - rate * (first_hat / (jnp.sqrt(second_hat) + ADAM_EPSILON) + decay * weight)
    return (updated, first_new, second_new)


def exchange(parts, axis):
    return lax.all_to_all(parts, axis, split_axis=0, concat_axis=0, tiled=True)


def swap(value, bit):
    count = lax.axis_size("ctx")
    return lax.ppermute(value, "ctx", [(i, i ^ bit) for i in range(count)])


def swap_dp(value, bit):
    count = lax.axis_size("dp")
    return lax.ppermute(value, "dp", [(i, i ^ bit) for i in range(count)])


def gather_ctx(block):
    far = swap(block, 2)
    return [block, swap(block, 1), far, swap(far, 1)]


def add_low(a, b):
    return a + b


def reduce_ctx(blocks):
    near, far = jnp.concatenate([blocks[1], blocks[3]]), None
    near = swap(near, 1)
    size = blocks[0].shape[0]
    far = swap(add_low(blocks[2], near[size:]), 2)
    mine = blocks[0].astype(jnp.float32) + near[:size].astype(jnp.float32)
    return mine + far.astype(jnp.float32)


def reorder(value, bit, rows):
    parts = [value[j * rows : (j + 1) * rows] for j in range(value.shape[0] // rows)]
    return jnp.concatenate([parts[j ^ bit] for j in range(len(parts))])


def sum_all(value):
    bit = 1
    while bit < lax.axis_size("ctx"):
        value = value + swap(value, bit)
        bit *= 2
    bit = 1
    while bit < lax.axis_size("dp"):
        value = value + swap_dp(value, bit)
        bit *= 2
    return value


def tie(value, *tokens):
    return lax.optimization_barrier((value, *tokens))[0]


class Ring:
    def __init__(self):
        count = self.count = lax.axis_size("dp")
        self.ctx = lax.axis_size("ctx")
        self.order = list(range(0, count, 2)) + list(range(count - 1, 0, -2))
        self.hops = (count // 2, count - 1 - count // 2)
        table = [
            [self.order[(self.order.index(i) + sense * step) % count] for step in range(count)]
            for sense in (1, -1)
            for i in range(count)
        ]
        row = (lax.axis_index("ctx") % 2) * count + lax.axis_index("dp")
        self.places = lax.dynamic_slice(
            jnp.array(table, jnp.int32), (row, 0), (1, count), allow_negative_indices=False
        )[0]

    def send(self, value, way):
        pairs = []
        for place, source in enumerate(self.order):
            for c in range(self.ctx):
                target = self.order[(place + (way if c % 2 == 0 else -way)) % self.count]
                pairs.append((source * self.ctx + c, target * self.ctx + c))
        return lax.ppermute(value, ("dp", "ctx"), pairs)

    def ways(self, hop):
        return [way for way, last in zip((1, -1), self.hops) if hop <= last]


class Gather:
    def __init__(self, ring, block):
        self.ring, self.hop = ring, 0
        self.held = {1: block, -1: block}
        self.parts, self.steps = [block], [0]

    def advance(self, *tokens):
        self.hop += 1
        for way in self.ring.ways(self.hop):
            self.held[way] = self.ring.send(tie(self.held[way], *tokens), way)
            self.parts.append(self.held[way])
            self.steps.append(-way * self.hop % self.ring.count)
        return list(self.held.values())

    def finish(self):
        while self.hop < self.ring.hops[0]:
            self.advance()
        return self

    def whole(self):
        block = self.parts[0]
        rows = block.shape[0]
        found = jnp.zeros((rows * self.ring.count, block.shape[1]), block.dtype)
        starts = self.ring.places * rows
        for step, part in zip(self.steps, self.parts):
            found = lax.dynamic_update_slice(
                found, part, (starts[step], 0), allow_negative_indices=False
            )
        return found


class Reduce:
    def __init__(self, ring, whole):
        self.ring, self.source, self.hop = ring, whole, ring.hops[0]
        self.rows = whole.shape[0] // ring.count
        self.starts = ring.places * self.rows
        self.held = {way: self.piece(way * last) for way, last in zip((1, -1), ring.hops)}
        self.total = None

    def piece(self, step):
        return lax.dynamic_slice(
            self.source,
            (self.starts[step % self.ring.count], 0),
            (self.rows, self.source.shape[1]),
            allow_negative_indices=False,
        )

    def tokens(self):
        return list(self.held.values())

    def send(self, *tokens):
        self.came = {
            way: self.ring.send(tie(self.held[way], *tokens), way) for way in self.ring.ways(self.hop)
        }
        return self

    def absorb(self, *tokens):
        for way, came in self.came.items():
            came = tie(came, *tokens) if tokens else came
            if self.hop > 1:
                self.held[way] = add_low(came, self.piece(way * (self.hop - 1)))
            else:
                mine = self.piece(0) if self.total is None else self.total
                self.total = mine.astype(jnp.float32) + came.astype(jnp.float32)
        self.hop -= 1
        return self.tokens() if self.total is None else [self.total]

    def finish(self):
        while self.hop > 0:
            self.send().absorb()
        return self.total


LOW = jnp.bfloat16
F32 = jnp.float32
TILE = 256
LONG = 6
SHORT = 2
GELU_A = 0.7978845608028654
GELU_B = 0.044715
VMEM = 56 * 2**20


def mm(a, b):
    return jnp.dot(a, b, preferred_element_type=F32)


def mm_nt(a, b):
    return lax.dot_general(a, b, (((1,), (1,)), ((), ())), preferred_element_type=F32)


def mm_tn(a, b):
    return lax.dot_general(a, b, (((0,), (0,)), ((), ())), preferred_element_type=F32)


def call(body, out_shape, in_specs, out_specs, args, grid=(1,), flops=0, scratch=(), into=(), prefetch=()):
    given = len(prefetch)
    used = len(in_specs)

    def kernel(*refs):
        body(*refs[: given + used], *refs[given + used + len(into) :])

    nbytes = sum(a.size * a.dtype.itemsize for a in args)
    nbytes += sum(o.size * o.dtype.itemsize for o in jax.tree.leaves(out_shape))
    return pl.pallas_call(
        kernel,
        out_shape=out_shape,
        grid_spec=pltpu.PrefetchScalarGridSpec(
            num_scalar_prefetch=given,
            grid=grid,
            in_specs=list(in_specs) + [pl.BlockSpec(memory_space=pl.ANY)] * len(into),
            out_specs=out_specs,
            scratch_shapes=list(scratch),
        ),
        compiler_params=pltpu.CompilerParams(vmem_limit_bytes=VMEM),
        cost_estimate=pl.CostEstimate(flops=flops // 16, bytes_accessed=nbytes // 16, transcendentals=0),
        input_output_aliases={given + used + i: i for i in range(len(into))},
    )(*prefetch, *args, *into)


def held(shape):
    return pl.BlockSpec(shape, lambda *_: (0,) * len(shape), pipeline_mode=pl.Buffered(1))


def like(shape, dtype):
    return jax.ShapeDtypeStruct(shape, dtype)


def scale_of(v):
    return lax.rsqrt(jnp.mean(v * v, axis=-1, keepdims=True) + EPSILON)


def norm_pull(v, s, g, dy):
    w = dy * g
    return s * w - v * (s * s * s) * jnp.mean(w * v, axis=-1, keepdims=True)


def turn(v, cos_t, sin_t, sign):
    half = v.shape[-1] // 2
    a, b = v[:, :half], v[:, half:]
    return jnp.concatenate([a * cos_t - sign * (b * sin_t), b * cos_t + sign * (a * sin_t)], axis=-1)


def stored_block(p):
    return jnp.where(p < 4, 2 * p, 2 * (7 - p) + 1)


def hidden_room(rows, dp):
    unit = max(16, 256 // dp)
    return -(-rows // unit) * unit


def pack_columns(w_gate_up, dp, ctx):
    rows, wide = w_gate_up.shape
    ff = wide // 2
    step = ff // (dp * ctx)
    room = hidden_room(step, dp)
    part = dp * room

    def body(w, out):
        zeros = [jnp.zeros((rows, room - step), F32)] if room > step else []
        for c in range(ctx):
            for side in range(2):
                cut = []
                for d in range(dp):
                    at = side * ff + (d * ctx + c) * step
                    cut += [w[:, at : at + step]] + zeros
                out[c, :, side * part : (side + 1) * part] = jnp.concatenate(cut, axis=1).astype(LOW)

    return call(
        body,
        like((ctx, rows, 2 * part), LOW),
        [held((rows, wide))],
        held((ctx, rows, 2 * part)),
        (w_gate_up,),
    )


def unpack_columns(parts, dp, ctx, step):
    rows, wide = parts.shape[1], parts.shape[2]
    part = wide // 2
    room = part // dp
    ff = dp * ctx * step

    def body(p, out):
        for c in range(ctx):
            own = p[c].astype(F32)
            for side in range(2):
                for d in range(dp):
                    at = side * ff + (d * ctx + c) * step
                    start = side * part + d * room
                    out[:, at : at + step] = own[:, start : start + step]

    return call(
        body,
        like((rows, 2 * ff), F32),
        [held(parts.shape)],
        held((rows, 2 * ff)),
        (parts,),
    )


class Blocks:
    def __init__(self, gathered, rows=None):
        block, self.cols = gathered.parts[0].shape
        self.rows = rows = rows or block
        count = gathered.ring.count
        self.height = rows * count
        if rows % 16:
            whole = gathered.whole().reshape(count, block, self.cols)[:, :rows]
            self.parts, self.steps = [whole.reshape(self.height, self.cols)], [0]
            self.rows = self.height
        else:
            self.parts, self.steps = gathered.parts, gathered.steps

    def specs(self):
        return [pl.BlockSpec(memory_space=pl.ANY)] * len(self.parts)

    def scratch(self):
        return [
            pltpu.VMEM((self.height, self.cols), LOW),
            pltpu.SemaphoreType.DMA((len(self.parts),)),
        ]

    def load(self, places, refs, room, sems):
        @pl.when(pl.program_id(0) == 0)
        def _():
            copies = []
            for i, (step, ref) in enumerate(zip(self.steps, refs)):
                at = pl.multiple_of(places[step] * self.rows, 16) if len(refs) > 1 else 0
                copies.append(
                    pltpu.make_async_copy(
                        ref.at[pl.ds(0, self.rows), :], room.at[pl.ds(at, self.rows), :], sems.at[i]
                    )
                )
            for copy in copies:
                copy.start()
            for copy in copies:
                copy.wait()


def unpack_small(gathered, first, dp, ctx, out_rows, gain_cols, head_cols):
    block, wide = gathered.parts[0].shape
    rows = block - first
    direct = first % 16 == 0 and rows % 16 == 0
    if direct:
        parts, steps = gathered.parts, gathered.steps
    else:
        parts, steps = [gathered.whole().reshape(dp, block, wide)[:, first:]], [0]
    half = out_rows // 2
    count = len(parts)

    def body(places, *refs):
        gain, head, out, room, sems = refs[count:]
        copies = []
        for i, ref in enumerate(refs[:count]):
            if direct:
                source, target = ref.at[pl.ds(first, rows), :], room.at[places[steps[i]]]
            else:
                source, target = ref, room
            copies.append(pltpu.make_async_copy(source, target, sems.at[i]))
        for copy in copies:
            copy.start()
        for copy in copies:
            copy.wait()
        lines = []
        for d in range(dp):
            extra = room[d, : 4 * ctx, :].astype(F32)
            lines += [extra[4 * c : 4 * c + 1] for c in range(ctx)]
            at, own = d * out_rows, room[d, 4 * ctx :, :]
            out[at : at + out_rows, :wide] = own[:out_rows]
            out[at : at + half, wide:] = own[out_rows:, : D - wide]
            out[at + half : at + out_rows, wide:] = own[out_rows:, D - wide :]
        for g in range(4):
            cut = [line[:, g * gain_cols : (g + 1) * gain_cols] for line in lines]
            gain[g : g + 1, :] = jnp.concatenate(cut, axis=1)
        for g in range(2):
            at = 4 * gain_cols + g * head_cols
            cut = [line[:, at : at + head_cols] for line in lines]
            head[g : g + 1, :] = jnp.concatenate(cut, axis=1)

    return call(
        body,
        [like((4, D), F32), like((2, HD), F32), like((HD, D), LOW)],
        [pl.BlockSpec(memory_space=pl.ANY)] * count,
        [held((4, D)), held((2, HD)), held((HD, D))],
        tuple(parts),
        scratch=[pltpu.VMEM((dp, rows, wide), LOW), pltpu.SemaphoreType.DMA((count,))],
        prefetch=(gathered.ring.places,),
    )


def input_stage(x, w_in, gain, head_rows, cos_t, sin_t, row_map, places):
    seq = x.shape[0]
    count = len(w_in.parts)

    def body(_, pl_ref, x0, x1, g, hg, cos, sin, *refs):
        q, k, v, raw, n_ref, w, sems = refs[count:]
        w_in.load(pl_ref, refs[:count], w, sems)
        for i, x_ref in enumerate((x0, x1)):
            at = slice(i * TILE, (i + 1) * TILE)
            xf = x_ref[...].astype(F32)
            n = (xf * scale_of(xf) * g[...]).astype(LOW)
            n_ref[at, :] = n
            y = mm(n, w[...])
            qy, ky = y[:, :HD], y[:, HD : 2 * HD]
            raw[at, :] = y[:, : 2 * HD]
            c, s = cos[at, :], sin[at, :]
            q[at, :] = turn(qy * scale_of(qy) * hg[0:1], c, s, 1.0).astype(LOW)
            k[at, :] = turn(ky * scale_of(ky) * hg[1:2], c, s, 1.0).astype(LOW)
            v[at, :] = y[:, 2 * HD :].astype(LOW)

    def block(cols):
        return pl.BlockSpec((2 * TILE, cols), lambda p, m, s: (p, 0))

    return call(
        body,
        [like((seq, HD), LOW)] * 3 + [like((seq, 2 * HD), F32), like((seq, D), LOW)],
        [
            pl.BlockSpec((TILE, D), lambda p, m, s: (m[2 * p], 0)),
            pl.BlockSpec((TILE, D), lambda p, m, s: (m[2 * p + 1], 0)),
            held((1, D)),
            held((2, HD)),
            block(HD // 2),
            block(HD // 2),
        ]
        + w_in.specs(),
        [block(HD)] * 3 + [block(2 * HD), block(D)],
        (x, x, gain, head_rows, cos_t, sin_t, *w_in.parts),
        grid=(seq // TILE // 2,),
        flops=2 * seq * D * 3 * HD,
        scratch=w_in.scratch(),
        prefetch=(row_map, places),
    )


def scores_of(q, k, doc_step):
    s = mm_nt(q, k) * HD ** (-0.5)
    row = lax.broadcasted_iota(jnp.int32, s.shape, 0) + doc_step * TILE
    col = lax.broadcasted_iota(jnp.int32, s.shape, 1)
    return jnp.where(col <= row, s, -1e30)


def attention(q, k, v, base):
    seq = q.shape[0]

    def body(b, q_ref, k_ref, v_ref, mixed, lse):
        for doc, count in enumerate((LONG, SHORT)):
            first = b[doc]
            for i in range(count):
                p = first + i
                at = pl.ds(pl.multiple_of(p * TILE, TILE), TILE)
                keys = pl.ds(pl.multiple_of(first * TILE, TILE), (i + 1) * TILE)
                s = scores_of(q_ref[at, :], k_ref[keys, :], i)
                peak = jnp.max(s, axis=-1, keepdims=True)
                e = jnp.exp(s - peak)
                total = jnp.sum(e, axis=-1, keepdims=True)
                lse[at, :] = peak + jnp.log(total)
                probs = (e * (1.0 / total)).astype(LOW)
                to = pl.ds(pl.multiple_of(stored_block(p) * TILE, TILE), TILE)
                mixed[to, :] = mm(probs, v_ref[keys, :]).astype(LOW)

    return call(
        body,
        [like((seq, HD), LOW), like((seq, 1), F32)],
        [held((seq, HD))] * 3,
        [held((seq, HD)), held((seq, 1))],
        (q, k, v),
        flops=4 * 24 * TILE * TILE * HD,
        prefetch=(base,),
    )


def attention_back(q, k, v, raw, lse, grads, head_rows, cos_t, sin_t, base):
    seq = q.shape[0]
    chip = seq // 2

    def pull_head(v_raw, g, dy, cos, sin):
        dy = turn(dy, cos, sin, -1.0)
        s = scale_of(v_raw)
        return norm_pull(v_raw, s, g, dy), jnp.sum(dy * v_raw * s, axis=0, keepdims=True)

    def body(b, q_ref, k_ref, v_ref, raw_ref, l_ref, *refs):
        hg, cos, sin, out, head_out, dk, dv, mixed_grad = refs[6:]
        for i in range(2):
            mine, near, far = refs[3 * i : 3 * i + 3]
            rows = pl.ds(pl.multiple_of((b[2] if i == 0 else 1 - b[2]) * chip, chip), chip)
            mixed_grad[rows, :] = (
                mine[0].astype(F32) + near[0].astype(F32) + far[...].astype(F32)
            ).astype(LOW)
        dk[...] = jnp.zeros_like(dk)
        dv[...] = jnp.zeros_like(dv)
        head_q = jnp.zeros((1, HD), F32)
        for doc, count in enumerate((LONG, SHORT)):
            first = b[doc]
            for i in range(count):
                p = first + i
                at = pl.ds(pl.multiple_of(p * TILE, TILE), TILE)
                keys = pl.ds(pl.multiple_of(first * TILE, TILE), (i + 1) * TILE)
                src = pl.ds(pl.multiple_of(stored_block(p) * TILE, TILE), TILE)
                do = mixed_grad[src, :]
                qs = q_ref[at, :]
                probs = jnp.exp(scores_of(qs, k_ref[keys, :], i) - l_ref[at, :])
                dp = mm_nt(do, v_ref[keys, :])
                inner = jnp.sum(probs * dp, axis=-1, keepdims=True)
                ds = (probs * (dp - inner)).astype(LOW)
                dq = mm(ds, k_ref[keys, :]) * HD ** (-0.5)
                dk[keys, :] += mm_tn(ds, qs)
                dv[keys, :] += mm_tn(probs.astype(LOW), do)
                dq, part = pull_head(raw_ref[at, :HD], hg[0:1], dq, cos[at, :], sin[at, :])
                head_q += part
                out[at, :HD] = dq.astype(LOW)
        head_k = jnp.zeros((1, HD), F32)
        for p in range(seq // TILE):
            at = slice(p * TILE, (p + 1) * TILE)
            dkp, part = pull_head(
                raw_ref[at, HD:], hg[1:2], dk[at, :] * HD ** (-0.5), cos[at, :], sin[at, :]
            )
            head_k += part
            out[at, HD : 2 * HD] = dkp.astype(LOW)
            out[at, 2 * HD :] = dv[at, :].astype(LOW)
        head_out[0:1, :] = head_q
        head_out[1:2, :] = head_k

    pair = pl.BlockSpec((1, chip, HD), lambda *_: (0, 0, 0), pipeline_mode=pl.Buffered(1))
    return call(
        body,
        [like((seq, 3 * HD), LOW), like((2, HD), F32)],
        [held((seq, HD))] * 3
        + [held((seq, 2 * HD)), held((seq, 1))]
        + [pair, pair, held((chip, HD))] * 2
        + [held((2, HD))]
        + [held((seq, HD // 2))] * 2,
        [held((seq, 3 * HD)), held((2, HD))],
        (q, k, v, raw, lse, *grads, head_rows, cos_t, sin_t),
        flops=10 * 24 * TILE * TILE * HD,
        scratch=[pltpu.VMEM((seq, HD), F32)] * 2 + [pltpu.VMEM((seq, HD), LOW)],
        prefetch=(base,),
    )


def project(mixed, outs, x, gains, stored_map):
    seq = x.shape[0]

    def body(_, m0, m1, m2, m3, w0, w1, w2, w3, x_ref, g, proj, pre):
        for i in range(2):
            at = slice(i * TILE, (i + 1) * TILE)
            y = mm(m0[at, :], w0[...]) + mm(m1[at, :], w1[...])
            y = y + mm(m2[at, :], w2[...]) + mm(m3[at, :], w3[...])
            proj[at, :] = y
            r = x_ref[at, :].astype(F32) + y * scale_of(y) * g[1:2]
            pre[at, :] = (r * scale_of(r) * g[2:3]).astype(LOW)

    def block(cols):
        return pl.BlockSpec((2 * TILE, cols), lambda r, m: (r, 0))

    return call(
        body,
        [like((seq, D), F32), like((seq, D), LOW)],
        [pl.BlockSpec((2 * TILE, HD), lambda r, m: (m[2 * r] // 2, 0))] * 4
        + [held((HD, D))] * 4
        + [block(D), held((4, D))],
        [block(D), block(D)],
        (*mixed, *outs, x, gains),
        grid=(seq // TILE // 2,),
        flops=2 * seq * D * H * HD,
        prefetch=(stored_map,),
    )


def gate_stage(pre, w, places, half, into=()):
    seq, part = pre.shape[0], w.cols // 2
    rows = 512
    first = half * (seq // 2 // rows)
    count = len(w.parts)

    def pieces(g, u):
        t = jnp.tanh(GELU_A * (g + GELU_B * (g * g * g)))
        a = 0.5 * g * (1.0 + t)
        slope = 0.5 * (1.0 + t) + (0.5 * g) * (1.0 - t * t) * (GELU_A * (1.0 + 3.0 * GELU_B * (g * g)))
        return a * u, u * slope, a

    def body(pl_ref, p_ref, *refs):
        hidden, ab, room, sems = refs[count:]
        w.load(pl_ref, refs[:count], room, sems)
        @pl.loop(0, part // 256)
        def _(i):
            at = pl.multiple_of(i * 256, 256)
            gate, up = pl.ds(at, 256), pl.ds(pl.multiple_of(part + at, 256), 256)
            h, b, a = pieces(mm(p_ref[...], room[:, gate]), mm(p_ref[...], room[:, up]))
            hidden[:, gate] = h.astype(LOW)
            ab[:, gate] = b.astype(LOW)
            ab[:, up] = a.astype(LOW)

    def block(cols):
        return pl.BlockSpec((rows, cols), lambda r, m: (first + r, 0))

    return call(
        body,
        [like((seq, part), LOW), like((seq, 2 * part), LOW)],
        [block(D)] + w.specs(),
        [block(part), block(2 * part)],
        (pre, *w.parts),
        grid=(seq // 2 // rows,),
        flops=2 * seq * D * part,
        scratch=w.scratch(),
        into=into,
        prefetch=(places,),
    )


def down_stage(hidden, w, places, half):
    seq, part = hidden.shape
    rows = seq // 4
    count = len(w.parts)

    def body(pl_ref, h, *refs):
        even, odd, room, sems = refs[count:]
        w.load(pl_ref, refs[:count], room, sems)
        odd[...] = mm(h[rows:, :], room[...]).astype(LOW)
        even[...] = mm(h[:rows, :], room[...]).astype(LOW)

    return call(
        body,
        [like((rows, D), LOW)] * 2,
        [
            pl.BlockSpec(
                (2 * rows, part), lambda r, m: (half, 0), pipeline_mode=pl.Buffered(1)
            )
        ]
        + w.specs(),
        [held((rows, D))] * 2,
        (hidden, *w.parts),
        flops=4 * rows * D * part,
        scratch=w.scratch(),
        prefetch=(places,),
    )


def ffn_stage(parts, near, far, proj, x, cot, gains):
    rows = cot.shape[0]

    def body(p, n, f, proj_ref, x_ref, c_ref, g, out, grad, gain):
        y = p[...].astype(F32) + n[...].astype(F32) + f[...].astype(F32)
        pr = proj_ref[...]
        s = scale_of(y)
        r = x_ref[...].astype(F32) + pr * scale_of(pr) * g[1:2]
        out[...] = (r + y * s * g[3:4]).astype(LOW)
        dy = c_ref[...].astype(F32)
        grad[...] = norm_pull(y, s, g[3:4], dy).astype(LOW)
        part = jnp.sum(dy * y * s, axis=0, keepdims=True)

        @pl.when(pl.program_id(0) == 0)
        def _():
            gain[...] = part

        @pl.when(pl.program_id(0) > 0)
        def _():
            gain[...] += part

    block = pl.BlockSpec((TILE, D), lambda r: (r, 0))
    return call(
        body,
        [like((rows, D), LOW), like((rows, D), LOW), like((1, D), F32)],
        [block] * 6 + [held((4, D))],
        [block, block, held((1, D))],
        (parts, near, far, proj, x, cot, gains),
        grid=(rows // TILE,),
    )


def hidden_back(grad, w, ab, places, half, into=()):
    seq, part = ab.shape[0], ab.shape[1] // 2
    rows = 512
    first = half * (seq // 2 // rows)
    count = len(w.parts)

    def body(pl_ref, g_ref, ab_ref, *refs):
        out, room, sems = refs[count:]
        w.load(pl_ref, refs[:count], room, sems)
        @pl.loop(0, part // 256)
        def _(i):
            at = pl.multiple_of(i * 256, 256)
            hg = mm_nt(g_ref[...], room[pl.ds(at, 256), :])
            for side in (pl.ds(at, 256), pl.ds(pl.multiple_of(part + at, 256), 256)):
                out[:, side] = (hg * ab_ref[:, side].astype(F32)).astype(LOW)

    def block(cols):
        return pl.BlockSpec((rows, cols), lambda r, m: (first + r, 0))

    return call(
        body,
        [like((seq, 2 * part), LOW)],
        [pl.BlockSpec((rows, D), lambda r, m: (r, 0)), block(2 * part)] + w.specs(),
        [block(2 * part)],
        (grad, ab, *w.parts),
        grid=(seq // 2 // rows,),
        flops=seq * D * part,
        scratch=w.scratch(),
        into=into,
        prefetch=(places,),
    )[0]


def residual_back(gu, w, outs, proj, x, cot, gains, stored_map, places, half, into=()):
    seq, wide = gu.shape
    own = cot.shape[0] // TILE
    steps = seq // 2 // TILE
    first = half * steps
    count = len(w.parts)

    def body(_, pl_ref, gu_ref, w0, w1, w2, w3, proj_ref, x_ref, c_ref, g, *refs):
        rg, pg, even, odd, gain, room, sems, *made = refs[count:]
        w.load(pl_ref, refs[:count], room, sems)
        step = pl.program_id(0)

        def multiply(turn):
            made[turn][...] = mm_nt(gu_ref[...], room[...])

        def finish(turn):
            dy = made[turn][...]
            pr = proj_ref[...]
            sp = scale_of(pr)
            r = x_ref[...].astype(F32) + pr * sp * g[1:2]
            s = scale_of(r)
            dr = norm_pull(r, s, g[2:3], dy)
            if half == 0:
                dr = dr + jnp.where(step <= own, 1.0, 0.0) * c_ref[...].astype(F32)
            rg[...] = dr.astype(LOW)
            low = norm_pull(pr, sp, g[1:2], dr).astype(LOW)
            pg[...] = low
            even[0] = mm_nt(low, w0[...]).astype(LOW)
            odd[0] = mm_nt(low, w1[...]).astype(LOW)
            even[1] = mm_nt(low, w2[...]).astype(LOW)
            odd[1] = mm_nt(low, w3[...]).astype(LOW)
            before = jnp.where(step == 1, 0.0, gain[...])
            gain[0:1, :] = before[0:1] + jnp.sum(dr * pr * sp, axis=0, keepdims=True)
            gain[1:2, :] = before[1:2] + jnp.sum(dy * r * s, axis=0, keepdims=True)

        @pl.when(step == 0)
        def _():
            multiply(0)

        for turn in range(2):

            @pl.when((step > 0) & (step < steps) & (step % 2 == turn))
            def _():
                multiply(turn)
                finish(1 - turn)

        @pl.when(step == steps)
        def _():
            finish((steps - 1) % 2)

    def last(i):
        return jnp.maximum(i - 1, 0)

    def block(cols):
        return pl.BlockSpec((TILE, cols), lambda i, m, p: (first + last(i), 0))

    heads = pl.BlockSpec((2, TILE, HD), lambda i, m, p: (0, m[first + last(i)] % steps, 0))
    return call(
        body,
        [like((seq, D), LOW), like((seq, D), LOW)]
        + [like((2, seq // 2, HD), LOW)] * 2
        + [like((2, D), F32)],
        [pl.BlockSpec((TILE, wide), lambda i, m, p: (first + jnp.minimum(i, steps - 1), 0))]
        + [held((HD, D))] * 4
        + [block(D), block(D)]
        + [pl.BlockSpec((TILE, D), lambda i, m, p: (jnp.minimum(last(i), own - 1), 0)), held((4, D))]
        + w.specs(),
        [
            block(D),
            pl.BlockSpec((TILE, D), lambda i, m, p: (m[first + last(i)], 0)),
            heads,
            heads,
            held((2, D)),
        ],
        (gu, *outs, proj, x, cot, gains, *w.parts),
        grid=(steps + 1,),
        flops=seq * D * (wide + H * HD),
        scratch=w.scratch() + [pltpu.VMEM((TILE, D), F32)] * 2,
        into=into,
        prefetch=(stored_map, places),
    )


def input_back(qkv, w_in, x, rg, gain, pos_map, places):
    seq = x.shape[0]
    rows = 2 * TILE
    count = len(w_in.parts)

    def body(_, pl_ref, q0, q1, x_ref, rg_ref, g, *refs):
        even, odd, gain_out, w, sems = refs[count:]
        w_in.load(pl_ref, refs[:count], w, sems)
        step = pl.program_id(0)
        total = jnp.zeros((1, D), F32)
        made = []
        for i, q_ref in enumerate((q0, q1)):
            at = slice(i * TILE, (i + 1) * TILE)
            dy = mm_nt(q_ref[...], w[...])
            xf = x_ref[at, :].astype(F32)
            s = scale_of(xf)
            made.append((rg_ref[at, :].astype(F32) + norm_pull(xf, s, g[...], dy)).astype(LOW))
            total += jnp.sum(dy * xf * s, axis=0, keepdims=True)
        gain_out[...] = jnp.where(step == 0, 0.0, gain_out[...]) + total

        @pl.when(step % 2 == 0)
        def _():
            even[:TILE, :], even[TILE:, :] = made

        @pl.when(step % 2 == 1)
        def _():
            odd[:TILE, :], odd[TILE:, :] = made

    block = pl.BlockSpec((rows, D), lambda i, m, s: (i, 0))
    out = pl.BlockSpec((rows, D), lambda i, m, s: (i // 2, 0))
    return call(
        body,
        [like((seq // 2, D), LOW)] * 2 + [like((1, D), F32)],
        [
            pl.BlockSpec((TILE, 3 * HD), lambda i, m, s: (m[2 * i], 0)),
            pl.BlockSpec((TILE, 3 * HD), lambda i, m, s: (m[2 * i + 1], 0)),
            block,
            block,
            held((1, D)),
        ]
        + w_in.specs(),
        [out, out, held((1, D))],
        (qkv, qkv, x, rg, gain, *w_in.parts),
        grid=(seq // rows,),
        flops=2 * seq * D * 3 * HD,
        scratch=w_in.scratch(),
        prefetch=(pos_map, places),
    )


def local(
    tokens,
    cotangent,
    lengths,
    w_qkv,
    w_out,
    w_gate_up,
    w_down,
    gains,
    head_gains,
    first_qkv,
    first_out,
    first_gate_up,
    first_down,
    first_gains,
    first_head,
    second_qkv,
    second_out,
    second_gate_up,
    second_down,
    second_gains,
    second_head,
):
    low = jnp.bfloat16
    f32 = jnp.float32
    rows = tokens.shape[1]
    dp = lax.axis_size("dp")
    ctx = lax.axis_size("ctx")
    place = lax.axis_index("ctx")
    seq = rows * ctx
    in_rows = w_qkv.shape[0]
    out_rows = w_out.shape[0]
    ff_rows = w_down.shape[0]
    gain_cols = gains.shape[1]
    head_cols = head_gains.shape[1]
    qkv_cols = 3 * HD
    ring = Ring()

    q_cols = w_qkv[:, : H * HD].astype(low).reshape(in_rows, ctx, HD).transpose(1, 0, 2)
    kv_cols = jnp.broadcast_to(w_qkv[:, H * HD :].astype(low)[None], (ctx, in_rows, 2 * HD))
    extra = jnp.concatenate(
        [gains.astype(low).reshape(-1), head_gains.astype(low).reshape(-1)]
    )
    extra = jnp.pad(extra, (0, 4 * qkv_cols - extra.shape[0])).reshape(4, qkv_cols)
    small_sent = jnp.concatenate(
        [
            jnp.concatenate([q_cols, kv_cols], axis=2),
            jnp.broadcast_to(extra[None], (ctx, 4, qkv_cols)),
        ],
        axis=1,
    )
    to_user = [((dp * c + d), d * ctx + c) for d in range(dp) for c in range(ctx)]
    to_owner = [(b, a) for a, b in to_user]
    out_mine = lax.ppermute(w_out.astype(low), ("dp", "ctx"), to_user)
    half = out_rows // 2
    small = exchange(small_sent, "ctx")
    packed = pack_columns(tie(w_gate_up, small_sent), dp, ctx)
    own_rows = ctx * in_rows
    small_ring = Gather(
        ring,
        jnp.concatenate(
            [
                small[:, :in_rows].reshape(own_rows, qkv_cols),
                small[:, in_rows:].reshape(4 * ctx, qkv_cols),
                out_mine[:, :qkv_cols],
                jnp.concatenate([out_mine[:half, qkv_cols:], out_mine[half:, qkv_cols:]], axis=1),
            ]
        ),
    )
    down_block = jnp.pad(w_down.astype(low), ((0, hidden_room(ff_rows, dp) - ff_rows), (0, 0)))
    down_ring = Gather(ring, down_block)
    down_first = down_ring.advance()
    tokens_far = swap(tie(tokens[0], small), 2)
    tokens_near = swap(tie(tokens[0], small), 1)
    gate_up_cols = exchange(packed, "ctx").reshape(own_rows, -1)
    first_len = lengths[0, 0]
    pos = tie(jnp.arange(seq, dtype=jnp.int32), packed)
    cos_t, sin_t = rope_tables(pos - jnp.where(pos < first_len, 0, first_len), HD)
    small_ring.advance(*down_first)
    small_ring.advance(cos_t, sin_t)
    small_ring.advance(gate_up_cols, tokens_near)
    tokens_last = swap(tie(tokens_far, *small_ring.held.values()), 1)
    tokens_all = jnp.concatenate([tokens[0], tokens_near, tokens_far, tokens_last])
    while small_ring.hop < ring.hops[0]:
        small_ring.advance()
    small_seen = list(small_ring.held.values())
    gate_ring = Gather(ring, gate_up_cols)
    gate_seen = gate_ring.advance(*small_seen, tokens_last)
    w_in = Blocks(small_ring, own_rows)
    places = ring.places
    gain_rows, head_rows, out_mine = unpack_small(
        small_ring, own_rows, dp, ctx, out_rows, gain_cols, head_cols
    )
    out_far, out_near = swap(out_mine, 2), swap(out_mine, 1)

    blocks = seq // TILE
    split = first_len // TILE
    base = jnp.where(split == LONG, jnp.array([0, LONG, 0]), jnp.array([SHORT, 0, 0]))
    base = (base + jnp.array([0, 0, 1]) * (place // 2)).astype(jnp.int32)
    tiles = jnp.arange(blocks, dtype=jnp.int32)
    stored_map = 2 * (place ^ (tiles // 2)) + tiles % 2
    owner = jnp.where(tiles < ctx, tiles, 2 * ctx - 1 - tiles)
    row_map = 2 * (place ^ owner) + (tiles >= ctx)
    pos_map = jnp.where(tiles % 2 == 0, stored_map // 2, 2 * ctx - 1 - stored_map // 2)

    q, k, v, raw, normed = input_stage(
        tokens_all, w_in, gain_rows[0:1], head_rows, cos_t, sin_t, row_map, places
    )
    gate_ring.advance(q)
    mixed, lse = attention(tie(q, *gate_seen, out_far, out_near), k, v, base)
    mixed_far, mixed_near = swap(mixed, 2), swap(mixed, 1)
    out_parts = [out_mine, out_near, out_far, swap(tie(out_far, mixed), 1)]
    down_ring.advance(mixed)
    gate_ring.advance(mixed)
    mixed_parts = [mixed, mixed_near, mixed_far, swap(mixed_far, 1)]
    proj, pre_low = project(mixed_parts, out_parts, tokens_all, gain_rows, stored_map)
    while gate_ring.hop < ring.hops[0]:
        gate_ring.advance(pre_low)
        if down_ring.hop < ring.hops[0]:
            down_ring.advance(pre_low)
    down_ring.finish()
    full_gate_up = Blocks(gate_ring)
    full_down = Blocks(down_ring)
    buffers = gate_stage(pre_low, full_gate_up, places, 1)
    even, odd = down_stage(buffers[0], full_down, places, 1)
    summed = add_low(even, swap(odd, 1))
    far = swap(summed, 2)
    hidden_low, slopes = gate_stage(tie(pre_low, summed), full_gate_up, places, 0, buffers)
    even, odd = down_stage(tie(hidden_low, far), full_down, places, 0)
    near = swap(odd, 1)
    result, ffn_grad, gain_grad_d = ffn_stage(
        even, near, far, proj, tokens[0], cotangent[0], gain_rows
    )

    far = swap(ffn_grad, 2)
    ffn_here = jnp.concatenate([ffn_grad, swap(ffn_grad, 1)])
    residual = partial(
        residual_back,
        w=full_gate_up,
        outs=out_parts,
        proj=proj,
        x=tokens_all,
        cot=cotangent[0],
        gains=gain_rows,
        stored_map=stored_map,
        places=places,
    )
    gate_up_low = hidden_back(ffn_here, full_down, slopes, places, 0)
    resid_grad, proj_low, even, odd, gain_grad_here = residual(gate_up_low, half=0)
    far = tie(far, resid_grad)
    ffn_there = jnp.concatenate([far, swap(far, 1)])
    near = swap(odd, 1)
    parts_here = (even, near)
    far_there = swap(tie(add_low(even[1], near[1]), ffn_there), 2)
    ffn_low = jnp.concatenate([ffn_here, ffn_there])
    grad_down = mm_tn(hidden_low, ffn_low).astype(low)
    down_sum = Reduce(ring, grad_down).send()
    gate_up_low = hidden_back(
        tie(ffn_there, *down_sum.tokens()), full_down, slopes, places, 1, (gate_up_low,)
    )
    held_down = down_sum.absorb(gate_up_low)
    grad_gate_up = mm_tn(tie(pre_low, *held_down), gate_up_low).astype(low)
    gate_sum = Reduce(ring, grad_gate_up)
    held_down = down_sum.send().absorb(grad_gate_up)
    resid_grad, proj_low, even, odd, gain_grad_there = residual(
        tie(gate_up_low, *held_down, *gate_sum.tokens()), half=1, into=(resid_grad, proj_low)
    )
    held_gate = gate_sum.send().absorb(odd)
    held_down = down_sum.send().absorb(odd)
    near = swap(tie(odd, *held_gate, *held_down), 1)
    summed = add_low(even[1], near[1])
    far_here = swap(summed, 2)
    gate_sum.send(summed)
    down_sum.send(summed)
    proj_low = tie(proj_low, summed)
    grad_out = [mm_tn(m, proj_low).astype(low) for m in mixed_parts]
    far_here = tie(far_here, *grad_out)
    grad_out = reduce_ctx(grad_out).astype(low)
    qkv_low, head_grads = attention_back(
        q,
        k,
        v,
        raw,
        lse,
        parts_here + (far_here,) + (even, near, far_there),
        head_rows,
        cos_t,
        sin_t,
        base,
    )
    held_gate = gate_sum.absorb(qkv_low)
    down_sum.absorb(qkv_low)
    down_own = down_sum.finish()
    gate_sum.send()
    grad_in = mm_tn(tie(normed, down_own, *held_gate), qkv_low).astype(low)
    down_own = down_own[:ff_rows]
    grad_out = grad_out.reshape(dp, out_rows, D)
    in_blocks = jnp.concatenate(
        [
            grad_in.reshape(dp, own_rows, qkv_cols),
            grad_out[:, :, :qkv_cols],
            jnp.concatenate(
                [grad_out[:, :half, qkv_cols:], grad_out[:, half:, qkv_cols:]], axis=2
            ),
        ],
        axis=1,
    )
    in_sum = Reduce(ring, in_blocks.reshape(-1, qkv_cols)).send()
    input_even, input_odd, gain_grad_a = input_back(
        tie(qkv_low, *in_sum.tokens(), *held_gate),
        w_in,
        tokens_all,
        resid_grad,
        gain_rows[0:1],
        pos_map,
        places,
    )
    in_sum.absorb(input_odd)
    held_gate = gate_sum.absorb(input_odd)
    in_sum.send(*held_gate)
    gate_up_own = gate_sum.finish().astype(low)
    gate_up_own = exchange(gate_up_own.reshape(ctx, in_rows, -1), "ctx")
    near = swap(input_odd, 1)
    gain_grad_bc = gain_grad_here + gain_grad_there
    in_sum.absorb()

    in_own = in_sum.finish().astype(low)
    gate_up_own = unpack_columns(gate_up_own, dp, ctx, ff_rows)
    out_own = in_own[own_rows:]
    out_own = jnp.concatenate(
        [
            out_own[:out_rows],
            jnp.concatenate(
                [out_own[out_rows:, : D - qkv_cols], out_own[out_rows:, D - qkv_cols :]], axis=0
            ),
        ],
        axis=1,
    )
    out_own = lax.ppermute(out_own, ("dp", "ctx"), to_owner).astype(f32)
    in_own = exchange(in_own[:own_rows].reshape(ctx, in_rows, qkv_cols), "ctx").astype(f32)
    summed = tie(add_low(input_even[rows:], near[rows:]), gate_up_own, in_own)
    far = swap(summed, 2)
    input_grad = (
        input_even[:rows].astype(f32) + near[:rows].astype(f32) + far.astype(f32)
    )
    qkv_own = jnp.concatenate(
        [
            in_own[:, :, :HD].transpose(1, 0, 2).reshape(in_rows, H * HD),
            jnp.sum(in_own[:, :, HD:], axis=0),
        ],
        axis=1,
    )
    gain_grads = jnp.concatenate([gain_grad_a, gain_grad_bc, gain_grad_d], axis=0)
    local_squares = jnp.float32(0.0)
    for piece in (qkv_own, out_own, gate_up_own, down_own):
        local_squares = local_squares + jnp.sum(piece * piece)
    lines = jnp.concatenate([gain_grads.reshape(-1, 128), head_grads.reshape(-1, 128)])
    squares = jnp.pad(local_squares.reshape(1, 1), ((0, 7), (0, 127)))
    sums = sum_all(tie(jnp.concatenate([lines, squares]), summed))
    small_grads = sums[: lines.shape[0]]
    index = lax.axis_index("dp") * ctx + place
    gains_own = lax.dynamic_slice_in_dim(
        small_grads[: 4 * D // 128].reshape(4, D), index * gain_cols, gain_cols, axis=1
    )
    head_own = lax.dynamic_slice_in_dim(
        small_grads[4 * D // 128 :].reshape(2, HD), index * head_cols, head_cols, axis=1
    )
    reduced = (qkv_own, out_own, gate_up_own, down_own, gains_own, head_own)
    total_squares = sums[lines.shape[0], 0] + jnp.sum(small_grads * small_grads)
    total_squares = tie(total_squares, far)
    grad_norm = jnp.sqrt(total_squares)
    factor = 1.0 / jnp.maximum(grad_norm, 1.0)
    weights = (w_qkv, w_out, w_gate_up, w_down, gains, head_gains)
    firsts = (first_qkv, first_out, first_gate_up, first_down, first_gains, first_head)
    seconds = (second_qkv, second_out, second_gate_up, second_down, second_gains, second_head)
    rates = (D ** (-0.5), (H * HD) ** (-0.5), D ** (-0.5), FF ** (-0.5), GAIN_RATE, GAIN_RATE)
    decays = (WEIGHT_DECAY, WEIGHT_DECAY, WEIGHT_DECAY, WEIGHT_DECAY, 0.0, 0.0)
    updates = [
        adam_update(
            weights[index],
            firsts[index],
            seconds[index],
            reduced[index] * factor,
            rates[index],
            decays[index],
        )
        for index in range(6)
    ]
    return (
        result[None],
        input_grad[None],
        updates[0][0],
        updates[1][0],
        updates[2][0],
        updates[3][0],
        updates[4][0],
        updates[5][0],
        updates[0][1],
        updates[1][1],
        updates[2][1],
        updates[3][1],
        updates[4][1],
        updates[5][1],
        updates[0][2],
        updates[1][2],
        updates[2][2],
        updates[3][2],
        updates[4][2],
        updates[5][2],
        grad_norm,
    )


def solution(mesh):
    in_specs = (
        P("dp", "ctx", None),
        P("dp", "ctx", None),
        P("dp", None),
        P(("dp", "ctx"), None),
        P(("dp", "ctx"), None),
        P(("dp", "ctx"), None),
        P(("dp", "ctx"), None),
        P(None, ("dp", "ctx")),
        P(None, ("dp", "ctx")),
        P(("dp", "ctx"), None),
        P(("dp", "ctx"), None),
        P(("dp", "ctx"), None),
        P(("dp", "ctx"), None),
        P(None, ("dp", "ctx")),
        P(None, ("dp", "ctx")),
        P(("dp", "ctx"), None),
        P(("dp", "ctx"), None),
        P(("dp", "ctx"), None),
        P(("dp", "ctx"), None),
        P(None, ("dp", "ctx")),
        P(None, ("dp", "ctx")),
    )
    out_specs = (
        P("dp", "ctx", None),
        P("dp", "ctx", None),
        P(("dp", "ctx"), None),
        P(("dp", "ctx"), None),
        P(("dp", "ctx"), None),
        P(("dp", "ctx"), None),
        P(None, ("dp", "ctx")),
        P(None, ("dp", "ctx")),
        P(("dp", "ctx"), None),
        P(("dp", "ctx"), None),
        P(("dp", "ctx"), None),
        P(("dp", "ctx"), None),
        P(None, ("dp", "ctx")),
        P(None, ("dp", "ctx")),
        P(("dp", "ctx"), None),
        P(("dp", "ctx"), None),
        P(("dp", "ctx"), None),
        P(("dp", "ctx"), None),
        P(None, ("dp", "ctx")),
        P(None, ("dp", "ctx")),
        P(),
    )
    return jax.shard_map(local, mesh=mesh, in_specs=in_specs, out_specs=out_specs, check_vma=False)
```

time: 2510 us -> 701 us (0.28)
  blocking collectives: 1600 us -> 0 us
  Pallas kernels: 0 us -> 245 us
  matrix products: 226 us -> 50.5 us
  local copies, waits for them, and re-layouts: 173 us -> 30.4 us
  waiting for transfers between devices: 295 us -> 203 us
  other arithmetic: 106 us -> 76.3 us
    unnamed x3 -> x0, blocking collectives: 1480 us -> none
    all_gather x6 -> x0, waiting for transfers between devices: 295 us -> none  [the longest x1 200 us: local(): lax.all_gather(shards[2], ('dp', 'ctx'), axis=0, tiled=True)]
    pallas_call x0 -> x17, Pallas kernels: none -> 245 us  [call(): pl.pallas_call(kernel, out_shape=out_shape, grid_spec=pltpu.PrefetchScala...]
    ppermute x0 -> x72, waiting for transfers between devices: none -> 186 us  [the longest x42 89.8 us: send(): return lax.ppermute(value, ('dp', 'ctx'), pairs)]
    dot_general x18 -> x7, matrix products: 226 us -> 50.5 us  [mm_tn(): lax.dot_general(a, b, (((0,), (0,)), ((), ())), preferred_element_type=F32)]
    unnamed x220 -> x187, local copies, waits for them, and re-layouts: 158 us -> 12.8 us
    all_gather x2 -> x0, blocking collectives: 79.9 us -> none  [the longest x1 43.3 us: local(): lax.all_gather(shards[4], ('dp', 'ctx'), axis=1, tiled=True)]
    unnamed x13 -> x0, starting transfers between devices: 72.5 us -> none
  transfers between devices with their start and end apart: 22 -> 76, of which waited for: 4 -> 33; matrix products, arithmetic and copies ran while one was open for 60% -> 14% of each run, Pallas kernels for 0% -> 30%
where the time goes in v1:
time: 701 us; the launch traced here: 696 us
  Pallas kernels  245 us (35%)
  waiting for transfers between devices  203 us (29%)
  starting transfers between devices  83.8 us (12%)
  other arithmetic  76.3 us (11%)
  matrix products  50.5 us (7%)
  local copies, waits for them, and re-layouts  30.4 us (4%)
  between operations  7.67 us (1%)
    pallas_call x17, Pallas kernels, call(): pl.pallas_call(kernel, out_shape=out_shape, grid_spec=pltpu.PrefetchScala...  245 us
    ppermute x42, waiting for transfers between devices, send(): return lax.ppermute(value, ('dp', 'ctx'), pairs)  89.8 us
    ppermute x25, waiting for transfers between devices, swap(): return lax.ppermute(value, 'ctx', [(i, i ^ bit) for i in range(count)])  87.5 us
    dot_general x7, matrix products, mm_tn(): lax.dot_general(a, b, (((0,), (0,)), ((), ())), preferred_element_type=F32)  50.5 us
    ppermute x42, starting transfers between devices, send(): return lax.ppermute(value, ('dp', 'ctx'), pairs)  46.2 us
    add x13, other arithmetic, add_low(): return a + b  29.1 us
    ppermute x25, starting transfers between devices, swap(): return lax.ppermute(value, 'ctx', [(i, i ^ bit) for i in range(count)])  17.1 us
    all_to_all x4, waiting for transfers between devices, exchange(): return lax.all_to_all(parts, axis, split_axis=0, concat_axis=0, tiled=True)  16.4 us
  transfers between devices with their start and end apart: 76, of which 33 were waited for; matrix products, arithmetic and copies ran while one was open for 14% of the time, Pallas kernels for 30%

profile of v1, /device:TPU:0, one launch (start us, length us, event | category | flops | bytes accessed | tf_op | source)
XLA Modules:
  0.0 696.5 jit_solution(1171690232215410380)
XLA Ops:
  6.4 3.4 all-to-all-start
  15.6 4.8 all-to-all-start.1
  28.5 5.6 multiply_sine_fusion
  39.7 7.0 %collective-permute-done.6.refs_4_.refs_11_.refs_10_ = bf16[208,768]{1,0:T(8,128)(2,1)} collective-permute-done((bf16[208,768]{1,0:T(8,128)(2,1)S(1)}, bf16[208,768]{1,0:T(8,128)(2,1)}, u32[]{:S(2)}, u32[]{:S(2)}) %collective-permute-start.6) | collective-permute-done | bytes 319520 | tf_op jit(solution)/shard_map/ppermute | solution.py:116
  48.8 13.0 %collective-permute-done.1 = bf16[512,1152]{1,0:T(8,128)(2,1)} collective-permute-done((bf16[512,1152]{1,0:T(8,128)(2,1)S(1)}, bf16[512,1152]{1,0:T(8,128)(2,1)}, u32[]{:S(2)}, u32[]{:S(2)}) %collective-permute-start.1) | collective-permute-done | bytes 1179680 | tf_op jit(solution)/shard_map/ppermute | solution.py:47
  63.7 6.6 collective-permute-done.12.refs_8_.refs_15_.refs_14_
  79.5 5.0 pad_maximum_fusion.refs_2_.refs_3_.refs_9_.refs_8_.refs_4_
  84.5 12.1 %shard_map.402 = (bf16[2048,256]{1,0:T(8,128)(2,1)}, bf16[2048,256]{1,0:T(8,128)(2,1)}, bf16[2048,256]{1,0:T(8,128)(2,1)}, f32[2048,512]{1,0:T(8,128)}, bf16[2048,1152]{1,0:T(8,128)(2,1)}) custom-call(s32[8]{0:T(128)} %fusion.28.refs_0_, s32[8]{0:T(128)} %fusion.31.refs_0_.refs_1_, ...), custom_call_target="tpu_custom_call" | custom-call | flops 226492416 | bytes 1634720 | tf_op jit(solution)/shard_map/pallas_call | solution.py:226
  96.7 9.1 %shard_map.403 = (bf16[2048,256]{1,0:T(8,128)(2,1)}, f32[2048,1]{1,0:T(8,128)}) custom-call(s32[3]{0:T(128)} %fusion.24.refs_0_, bf16[2048,256]{1,0:T(8,128)(2,1)} %get-tuple-element.128.refs_1_, bf16[2048,256]{1,0:T(8,128)(2,1)} %get-tuple-element.129.refs_2_, bf16[2048,256]{1,0:T(8,128)(2,1)} %get-tuple-element.130.refs_3_), custom_call_target="tpu_custom_call" | custom-call | flops 100663296 | bytes 262656 | tf_op jit(solution)/shard_map/pallas_call | solution.py:226
  109.8 22.0 %collective-permute-done.18.refs_3_ = bf16[2048,256]{1,0:T(8,128)(2,1)S(1)} collective-permute-done((bf16[2048,256]{1,0:T(8,128)(2,1)}, bf16[2048,256]{1,0:T(8,128)(2,1)S(1)}, u32[]{:S(2)}, u32[]{:S(2)}) %collective-permute-start.18) | collective-permute-done | bytes 1048608 | tf_op jit(solution)/shard_map/ppermute | solution.py:47
  139.4 13.1 %shard_map.404 = (f32[2048,1152]{1,0:T(8,128)}, bf16[2048,1152]{1,0:T(8,128)(2,1)}) custom-call(s32[8]{0:T(128)} %fusion.27.refs_0_, bf16[2048,256]{1,0:T(8,128)(2,1)} %get-tuple-element.131.refs_1_, bf16[2048,256]{1,0:T(8,128)(2,1)} %copy-done.48, bf16[2048,256]{1,0:T(8,128)(2,1)} %copy-done.45, bf16[2048,256]{1,0:T(8,128)(2,1)} %collective-permute-done.19.refs_4_, ...), custom_call_target="tpu_custom_call" | custom-call | flops 301989888 | bytes 1590400 | tf_op jit(solution)/shard_map/pallas_call | solution.py:226
  157.8 8.7 %collective-permute-done.26.refs_5_.refs_6_ = bf16[224,1152]{1,0:T(8,128)(2,1)S(1)} collective-permute-done((bf16[224,1152]{1,0:T(8,128)(2,1)S(1)}, bf16[224,1152]{1,0:T(8,128)(2,1)S(1)}, u32[]{:S(2)}, u32[]{:S(2)}) %collective-permute-start.26) | collective-permute-done | bytes 516128 | tf_op jit(solution)/shard_map/ppermute | solution.py:116
  166.5 7.0 %collective-permute-done.27.refs_6_.refs_7_ = bf16[224,1152]{1,0:T(8,128)(2,1)S(1)} collective-permute-done((bf16[224,1152]{1,0:T(8,128)(2,1)S(1)}, bf16[224,1152]{1,0:T(8,128)(2,1)S(1)}, u32[]{:S(2)}, u32[]{:S(2)}) %collective-permute-start.27) | collective-permute-done | bytes 516128 | tf_op jit(solution)/shard_map/ppermute | solution.py:116
  175.2 16.7 %collective-permute-done.28.refs_7_.refs_8_ = bf16[224,1152]{1,0:T(8,128)(2,1)S(1)} collective-permute-done((bf16[224,1152]{1,0:T(8,128)(2,1)S(1)}, bf16[224,1152]{1,0:T(8,128)(2,1)S(1)}, u32[]{:S(2)}, u32[]{:S(2)}) %collective-permute-start.28) | collective-permute-done | bytes 516128 | tf_op jit(solution)/shard_map/ppermute | solution.py:116
  193.9 23.6 %shard_map.405 = (bf16[2048,1792]{1,0:T(8,128)(2,1)}, bf16[2048,3584]{1,0:T(8,128)(2,1)}) custom-call(s32[8]{0:T(128)} %fusion.31.refs_0_.refs_1_, bf16[2048,1152]{1,0:T(8,128)(2,1)} %get-tuple-element.164.refs_1_, bf16[144,3584]{1,0:T(8,128)(2,1)} %copy-done, bf16[144,3584]{1,0:T(8,128)(2,1)} %copy-done.2, bf16[144,3584]{1,0:T(8,128)(2,1)} %copy-done.3, ...), custom_call_target="tpu_custom_call" | custom-call | flops 528482304 | bytes 2187264 | tf_op jit(solution)/shard_map/pallas_call | solution.py:226
  218.5 10.8 %shard_map.406 = (bf16[512,1152]{1,0:T(8,128)(2,1)}, bf16[512,1152]{1,0:T(8,128)(2,1)}) custom-call(s32[8]{0:T(128)} %fusion.31.refs_0_.refs_1_, bf16[2048,1792]{1,0:T(8,128)(2,1)} %get-tuple-element.139.refs_1_.refs_10_, bf16[224,1152]{1,0:T(8,128)(2,1)} %copy-done.9, bf16[224,1152]{1,0:T(8,128)(2,1)} %copy-done.12, bf16[224,1152]{1,0:T(8,128)(2,1)} %copy-done.14, ...), custom_call_target="tpu_custom_call" | custom-call | flops 264241152 | bytes 864256 | tf_op jit(solution)/shard_map/pallas_call | solution.py:226
  235.6 23.5 %shard_map.407 = (bf16[2048,1792]{1,0:T(8,128)(2,1)}, bf16[2048,3584]{1,0:T(8,128)(2,1)}) custom-call(s32[8]{0:T(128)} %fusion.31.refs_0_.refs_1_, bf16[2048,1152]{1,0:T(8,128)(2,1)} %get-tuple-element.164.refs_1_, bf16[144,3584]{1,0:T(8,128)(2,1)} %copy-done, bf16[144,3584]{1,0:T(8,128)(2,1)} %copy-done.2, ...), custom_call_target="tpu_custom_call", output_to_operand_aliasing={{0}: (10, {}), {1}: (11, {})} | custom-call | flops 528482304 | bytes 2187264 | tf_op jit(solution)/shard_map/pallas_call | solution.py:226
  262.1 10.8 %shard_map.408 = (bf16[512,1152]{1,0:T(8,128)(2,1)}, bf16[512,1152]{1,0:T(8,128)(2,1)}) custom-call(s32[8]{0:T(128)} %fusion.31.refs_0_.refs_1_, bf16[2048,1792]{1,0:T(8,128)(2,1)} %get-tuple-element.149.refs_1_, bf16[224,1152]{1,0:T(8,128)(2,1)} %copy-done.9, bf16[224,1152]{1,0:T(8,128)(2,1)} %copy-done.12, bf16[224,1152]{1,0:T(8,128)(2,1)} %copy-done.14, ...), custom_call_target="tpu_custom_call" | custom-call | flops 264241152 | bytes 864256 | tf_op jit(solution)/shard_map/pallas_call | solution.py:226
  277.0 5.9 shard_map.409
  289.3 16.2 %shard_map.410.refs_2_.refs_11_ = bf16[2048,3584]{1,0:T(8,128)(2,1)} custom-call(s32[8]{0:T(128)} %fusion.31.refs_0_.refs_1_, bf16[1024,1152]{1,0:T(8,128)(2,1)} %pad_maximum_fusion.1.refs_1_, bf16[2048,3584]{1,0:T(8,128)(2,1)} %get-tuple-element.157.refs_2_, bf16[224,1152]{1,0:T(8,128)(2,1)} %copy-done.9, bf16[224,1152]{1,0:T(8,128)(2,1)} %copy-done.12, ...), custom_call_target="tpu_custom_call" | custom-call | flops 264241152 | bytes 2240512 | tf_op jit(solution)/shard_map/pallas_call | solution.py:226
  305.6 38.4 %shard_map.411 = (bf16[2048,1152]{1,0:T(8,128)(2,1)}, bf16[2048,1152]{1,0:T(8,128)(2,1)}, bf16[2,1024,256]{2,1,0:T(8,128)(2,1)}, bf16[2,1024,256]{2,1,0:T(8,128)(2,1)}, f32[2,1152]{1,0:T(2,128)}) custom-call(s32[8]{0:T(128)} %fusion.27.refs_0_, s32[8]{0:T(128)} %fusion.31.refs_0_.refs_1_, bf16[2048,3584]{1,0:T(8,128)(2,1)} %shard_map.410.refs_2_.refs_11_, ...), custom_call_target="tpu_custom_call" | custom-call | flops 679477248 | bytes 3262144 | tf_op jit(solution)/shard_map/pallas_call | solution.py:226
  347.1 12.1 %convolution_convert_fusion.1 = bf16[1792,1152]{1,0:T(8,128)(2,1)S(1)} fusion(bf16[2048,1792]{1,0:T(8,128)(2,1)S(1)} %bitcast.71, bf16[512,1152]{1,0:T(8,128)(2,1)S(1)} %collective-permute-done.37, bf16[512,1152]{1,0:T(8,128)(2,1)} %collective-permute-done.36, bf16[512,1152]{1,0:T(8,128)(2,1)} %copy-done.44, bf16[512,1152]{1,0:T(8,128)(2,1)} %get-tuple-element.156), kind=kOutput, calls=%fused_computation.1 | convolution fusion | flops 8476655616 | bytes 16187392 | tf_op jit(solution)/shard_map/dot_general | solution.py:214
  366.2 16.1 %shard_map.412.refs_2_ = bf16[2048,3584]{1,0:T(8,128)(2,1)} custom-call(s32[8]{0:T(128)} %fusion.31.refs_0_.refs_1_, bf16[1024,1152]{1,0:T(8,128)(2,1)} %copy-done.21, bf16[2048,3584]{1,0:T(8,128)(2,1)} %get-tuple-element.157.refs_2_, bf16[224,1152]{1,0:T(8,128)(2,1)} %copy-done.9, bf16[224,1152]{1,0:T(8,128)(2,1)} %copy-done.12, ...), custom_call_target="tpu_custom_call", output_to_operand_aliasing={{}: (11, {})} | custom-call | flops 264241152 | bytes 2240512 | tf_op jit(solution)/shard_map/pallas_call | solution.py:226
  384.2 22.8 %convolution_convert_fusion = bf16[1152,3584]{1,0:T(8,128)(2,1)} fusion(bf16[2048,1152]{1,0:T(8,128)(2,1)S(1)} %bitcast.73, bf16[2048,3584]{1,0:T(8,128)(2,1)} %shard_map.412.refs_2_), kind=kOutput, calls=%fused_computation | convolution fusion | flops 16915562496 | bytes 27656192 | tf_op jit(solution)/shard_map/dot_general | solution.py:214
  408.7 3.3 constant_dynamic-slice_fusion.4
  416.1 3.7 dynamic-slice_add_fusion.7
  421.8 26.2 %shard_map.413 = (bf16[2048,1152]{1,0:T(8,128)(2,1)}, bf16[2048,1152]{1,0:T(8,128)(2,1)}, bf16[2,1024,256]{2,1,0:T(8,128)(2,1)}, bf16[2,1024,256]{2,1,0:T(8,128)(2,1)}, f32[2,1152]{1,0:T(2,128)}) custom-call(s32[8]{0:T(128)} %fusion.27.refs_0_, s32[8]{0:T(128)} %fusion.31.refs_0_.refs_1_, ...), custom_call_target="tpu_custom_call", output_to_operand_aliasing={{0}: (19, {}), {1}: (20, {})} | custom-call | flops 679477248 | bytes 3262144 | tf_op jit(solution)/shard_map/pallas_call | solution.py:226
  450.8 3.9 dynamic-slice_add_fusion.5
  469.3 8.2 %collective-permute-done.45.refs_8_ = bf16[1024,256]{1,0:T(8,128)(2,1)S(1)} collective-permute-done((bf16[1024,256]{1,0:T(8,128)(2,1)S(1)}, bf16[1024,256]{1,0:T(8,128)(2,1)S(1)}, u32[]{:S(2)}, u32[]{:S(2)}) %collective-permute-start.45) | collective-permute-done | bytes 524320 | tf_op jit(solution)/shard_map/ppermute | solution.py:47
  482.3 5.9 collective-permute-done.46.refs_11_
  489.0 16.4 %shard_map.414 = (bf16[2048,768]{1,0:T(8,128)(2,1)}, f32[2,256]{1,0:T(2,128)}) custom-call(s32[3]{0:T(128)} %fusion.24.refs_0_, bf16[2048,256]{1,0:T(8,128)(2,1)} %get-tuple-element.128.refs_1_, bf16[2048,256]{1,0:T(8,128)(2,1)} %get-tuple-element.129.refs_2_, bf16[2048,256]{1,0:T(8,128)(2,1)} %get-tuple-element.130.refs_3_, ...), custom_call_target="tpu_custom_call" | custom-call | flops 251658240 | bytes 1114880 | tf_op jit(solution)/shard_map/pallas_call | solution.py:226
  506.4 4.1 dynamic-slice_add_fusion.2
  515.5 6.2 convolution_convert_fusion.2
  521.8 5.5 collective-permute-done.52
  531.4 13.7 %shard_map.415 = (bf16[1024,1152]{1,0:T(8,128)(2,1)}, bf16[1024,1152]{1,0:T(8,128)(2,1)}, f32[1,1152]{1,0:T(1,128)}) custom-call(s32[8]{0:T(128)} %compare_select_fusion.1.refs_0_, s32[8]{0:T(128)} %fusion.31.refs_0_.refs_1_, bf16[2048,768]{1,0:T(8,128)(2,1)} %get-tuple-element.190.refs_2_.refs_3_, bf16[2048,768]{1,0:T(8,128)(2,1)} %get-tuple-element.190.refs_2_.refs_3_, ...), custom_call_target="tpu_custom_call" | custom-call | flops 226492416 | bytes 1438272 | tf_op jit(solution)/shard_map/pallas_call | solution.py:226
  545.9 5.0 dynamic-slice_add_fusion.1
  552.9 5.4 collective-permute-done.62
  563.9 5.8 collective-permute-done.60
  575.0 22.6 %collective-permute-done.61 = bf16[192,768]{1,0:T(8,128)(2,1)S(1)} collective-permute-done((bf16[192,768]{1,0:T(8,128)(2,1)S(1)}, bf16[192,768]{1,0:T(8,128)(2,1)S(1)}, u32[]{:S(2)}, u32[]{:S(2)}) %collective-permute-start.61) | collective-permute-done | bytes 294944 | tf_op jit(solution)/shard_map/ppermute | solution.py:116
  599.2 3.4 all-to-all-start.3
  608.4 3.5 all-to-all-start.2
  614.6 12.9 %all-to-all-done.2.refs_0_ = bf16[4,36,3584]{2,1,0:T(8,128)(2,1)S(1)} async-done(((bf16[4,36,3584]{2,1,0:T(8,128)(2,1)}), bf16[4,36,3584]{2,1,0:T(8,128)(2,1)S(1)}, u32[]{:S(2)}, u32[]{:S(2)}) %all-to-all-start.2) | async-done | bytes 1032224 | tf_op jit(solution)/shard_map/all_to_all | solution.py:42
  644.6 18.2 %collective-permute-done.68 = f32[48,128]{1,0:T(8,128)S(1)} collective-permute-done((f32[48,128]{1,0:T(8,128)S(1)}, f32[48,128]{1,0:T(8,128)S(1)}, u32[]{:S(2)}, u32[]{:S(2)}) %collective-permute-start.68) | collective-permute-done | bytes 24608 | tf_op jit(solution)/shard_map/ppermute | solution.py:47
  666.8 3.6 collective-permute-done.70
  672.2 3.4 collective-permute-done.71
  679.5 4.0 multiply_subtract_fusion.1
  684.5 3.9 multiply_subtract_fusion
  690.8 3.5 add_bitcast_fusion
  (418 shorter events, 182.1 us)
Async XLA Ops:
  2.1 23.6 %collective-permute-start.3 = (bf16[224,1152]{1,0:T(8,128)(2,1)S(1)}, bf16[224,1152]{1,0:T(8,128)(2,1)S(1)}, u32[]{:S(2)}, u32[]{:S(2)}) collective-permute-start(bf16[224,1152]{1,0:T(8,128)(2,1)S(1)} %pad.13.refs_2_.refs_3_), channel_id=1, source_target_pairs={{0,8},{1,5},{2,10},{3,7},{8,16},{9,1},{10,18},{11,3},{16,24},{17,9... | collective-permute-start | bytes 1548296 | tf_op jit(solution)/shard_map/ppermute | solution.py:116
  5.2 20.6 %collective-permute-start.4 = (bf16[224,1152]{1,0:T(8,128)(2,1)S(1)}, bf16[224,1152]{1,0:T(8,128)(2,1)S(1)}, u32[]{:S(2)}, u32[]{:S(2)}) collective-permute-start(bf16[224,1152]{1,0:T(8,128)(2,1)S(1)} %pad.13.refs_2_.refs_3_), channel_id=1, source_target_pairs={{0,4},{1,9},{2,6},{3,11},{8,0},{9,17},{10,2},{11,19},{16,8},{17,25... | collective-permute-start | bytes 1548296 | tf_op jit(solution)/shard_map/ppermute | solution.py:116
  15.6 22.8 %all-to-all-start.1 = ((bf16[4,36,3584]{2,1,0:T(8,128)(2,1)}), bf16[4,36,3584]{2,1,0:T(8,128)(2,1)}, u32[]{:S(2)}, u32[]{:S(2)}) async-start(bf16[4,36,3584]{2,1,0:T(8,128)(2,1)} %shard_map.400), calls=%async_computation.1 | async-start | bytes 2293760 | tf_op jit(solution)/shard_map/all_to_all | solution.py:42
  20.4 26.4 %collective-permute-start = (bf16[512,1152]{1,0:T(8,128)(2,1)S(1)}, bf16[512,1152]{1,0:T(8,128)(2,1)}, u32[]{:S(2)}, u32[]{:S(2)}) collective-permute-start(bf16[512,1152]{1,0:T(8,128)(2,1)S(1)} %bitcast.83), channel_id=1, source_target_pairs={{0,1},{1,0},{2,3},{3,2},{4,5},{5,4},{6,7},{7,6},{8,9},{9,8},{10,11... | collective-permute-start | bytes 3538952 | tf_op jit(solution)/shard_map/ppermute | solution.py:47
  21.4 40.4 %collective-permute-start.1 = (bf16[512,1152]{1,0:T(8,128)(2,1)S(1)}, bf16[512,1152]{1,0:T(8,128)(2,1)}, u32[]{:S(2)}, u32[]{:S(2)}) collective-permute-start(bf16[512,1152]{1,0:T(8,128)(2,1)S(1)} %bitcast.84), channel_id=1, source_target_pairs={{0,2},{1,3},{2,0},{3,1},{4,6},{5,7},{6,4},{7,5},{8,10},{9,11},{10,... | collective-permute-start | bytes 3538952 | tf_op jit(solution)/shard_map/ppermute | solution.py:47
  46.8 15.0 %collective-permute-start.7 = (bf16[208,768]{1,0:T(8,128)(2,1)}, bf16[208,768]{1,0:T(8,128)(2,1)}, u32[]{:S(2)}, u32[]{:S(2)}) collective-permute-start(bf16[208,768]{1,0:T(8,128)(2,1)} %collective-permute-done.6.refs_4_.refs_11_.refs_10_), channel_id=1, source_target_pairs={{0,8},{1,5},{2,10},{3,7},{8,16},{9,1},{10,18},{11,3},{16,24},{17,9... | collective-permute-start | bytes 958472 | tf_op jit(solution)/shard_map/ppermute | solution.py:116
  46.8 15.0 %collective-permute-start.10 = (bf16[208,768]{1,0:T(8,128)(2,1)}, bf16[208,768]{1,0:T(8,128)(2,1)}, u32[]{:S(2)}, u32[]{:S(2)}) collective-permute-start(bf16[208,768]{1,0:T(8,128)(2,1)} %collective-permute-done.9.refs_5_.refs_12_.refs_11_), channel_id=1, source_target_pairs={{0,4},{1,9},{2,6},{3,11},{8,0},{9,17},{10,2},{11,19},{16,8},{17,25... | collective-permute-start | bytes 958472 | tf_op jit(solution)/shard_map/ppermute | solution.py:116
  71.0 25.7 %collective-permute-start.13 = (bf16[144,3584]{1,0:T(8,128)(2,1)S(1)}, bf16[144,3584]{1,0:T(8,128)(2,1)S(1)}, u32[]{:S(2)}, u32[]{:S(2)}) collective-permute-start(bf16[144,3584]{1,0:T(8,128)(2,1)S(1)} %reshape.108.refs_2_.refs_11_), channel_id=1, source_target_pairs={{0,8},{1,5},{2,10},{3,7},{8,16},{9,1},{10,18},{11,3},{16,24},{17,9... | collective-permute-start | bytes 3096584 | tf_op jit(solution)/shard_map/ppermute | solution.py:116
  71.1 25.6 %collective-permute-start.14 = (bf16[144,3584]{1,0:T(8,128)(2,1)S(1)}, bf16[144,3584]{1,0:T(8,128)(2,1)S(1)}, u32[]{:S(2)}, u32[]{:S(2)}) collective-permute-start(bf16[144,3584]{1,0:T(8,128)(2,1)S(1)} %reshape.108.refs_2_.refs_11_), channel_id=1, source_target_pairs={{0,4},{1,9},{2,6},{3,11},{8,0},{9,17},{10,2},{11,19},{16,8},{17,25... | collective-permute-start | bytes 3096584 | tf_op jit(solution)/shard_map/ppermute | solution.py:116
  78.0 18.6 %collective-permute-start.15 = (bf16[256,1152]{1,0:T(8,128)(2,1)}, bf16[256,1152]{1,0:T(8,128)(2,1)S(1)}, u32[]{:S(2)}, u32[]{:S(2)}) collective-permute-start(bf16[256,1152]{1,0:T(8,128)(2,1)} %get-tuple-element.127.refs_5_.refs_3_), channel_id=1, source_target_pairs={{0,2},{1,3},{2,0},{3,1},{4,6},{5,7},{6,4},{7,5},{8,10},{9,11},{10,... | collective-permute-start | bytes 1769480 | tf_op jit(solution)/shard_map/ppermute | solution.py:47
  78.1 18.6 %collective-permute-start.16 = (bf16[256,1152]{1,0:T(8,128)(2,1)}, bf16[256,1152]{1,0:T(8,128)(2,1)S(1)}, u32[]{:S(2)}, u32[]{:S(2)}) collective-permute-start(bf16[256,1152]{1,0:T(8,128)(2,1)} %get-tuple-element.127.refs_5_.refs_3_), channel_id=1, source_target_pairs={{0,1},{1,0},{2,3},{3,2},{4,5},{5,4},{6,7},{7,6},{8,9},{9,8},{10,11... | collective-permute-start | bytes 1769480 | tf_op jit(solution)/shard_map/ppermute | solution.py:47
  105.9 26.0 %collective-permute-start.18 = (bf16[2048,256]{1,0:T(8,128)(2,1)}, bf16[2048,256]{1,0:T(8,128)(2,1)S(1)}, u32[]{:S(2)}, u32[]{:S(2)}) collective-permute-start(bf16[2048,256]{1,0:T(8,128)(2,1)} %get-tuple-element.131.refs_1_), channel_id=1, source_target_pairs={{0,2},{1,3},{2,0},{3,1},{4,6},{5,7},{6,4},{7,5},{8,10},{9,11},{10,... | collective-permute-start | bytes 3145736 | tf_op jit(solution)/shard_map/ppermute | solution.py:47
  107.8 24.7 %collective-permute-start.21 = (bf16[144,3584]{1,0:T(8,128)(2,1)S(1)}, bf16[144,3584]{1,0:T(8,128)(2,1)S(1)}, u32[]{:S(2)}, u32[]{:S(2)}) collective-permute-start(bf16[144,3584]{1,0:T(8,128)(2,1)S(1)} %collective-permute-done.13.refs_3_.refs_12_), channel_id=1, source_target_pairs={{0,8},{1,5},{2,10},{3,7},{8,16},{9,1},{10,18},{11,3},{16,24},{17,9... | collective-permute-start | bytes 3096584 | tf_op jit(solution)/shard_map/ppermute | solution.py:116
  107.8 26.2 %collective-permute-start.22 = (bf16[144,3584]{1,0:T(8,128)(2,1)S(1)}, bf16[144,3584]{1,0:T(8,128)(2,1)S(1)}, u32[]{:S(2)}, u32[]{:S(2)}) collective-permute-start(bf16[144,3584]{1,0:T(8,128)(2,1)S(1)} %collective-permute-done.14.refs_4_.refs_13_), channel_id=1, source_target_pairs={{0,4},{1,9},{2,6},{3,11},{8,0},{9,17},{10,2},{11,19},{16,8},{17,25... | collective-permute-start | bytes 3096584 | tf_op jit(solution)/shard_map/ppermute | solution.py:116
  109.8 28.6 %collective-permute-start.17 = (bf16[2048,256]{1,0:T(8,128)(2,1)}, bf16[2048,256]{1,0:T(8,128)(2,1)S(1)}, u32[]{:S(2)}, u32[]{:S(2)}) collective-permute-start(bf16[2048,256]{1,0:T(8,128)(2,1)} %get-tuple-element.131.refs_1_), channel_id=1, source_target_pairs={{0,1},{1,0},{2,3},{3,2},{4,5},{5,4},{6,7},{7,6},{8,9},{9,8},{10,11... | collective-permute-start | bytes 3145736 | tf_op jit(solution)/shard_map/ppermute | solution.py:47
  132.5 22.9 %collective-permute-start.23 = (bf16[144,3584]{1,0:T(8,128)(2,1)S(1)}, bf16[144,3584]{1,0:T(8,128)(2,1)S(1)}, u32[]{:S(2)}, u32[]{:S(2)}) collective-permute-start(bf16[144,3584]{1,0:T(8,128)(2,1)S(1)} %collective-permute-done.21.refs_5_.refs_14_), channel_id=1, source_target_pairs={{0,8},{1,5},{2,10},{3,7},{8,16},{9,1},{10,18},{11,3},{16,24},{17,9... | collective-permute-start | bytes 3096584 | tf_op jit(solution)/shard_map/ppermute | solution.py:116
  134.0 32.4 %collective-permute-start.26 = (bf16[224,1152]{1,0:T(8,128)(2,1)S(1)}, bf16[224,1152]{1,0:T(8,128)(2,1)S(1)}, u32[]{:S(2)}, u32[]{:S(2)}) collective-permute-start(bf16[224,1152]{1,0:T(8,128)(2,1)S(1)} %copy-done.13), channel_id=1, source_target_pairs={{0,8},{1,5},{2,10},{3,7},{8,16},{9,1},{10,18},{11,3},{16,24},{17,9... | collective-permute-start | bytes 1548296 | tf_op jit(solution)/shard_map/ppermute | solution.py:116
  136.5 55.4 %collective-permute-start.24 = (bf16[144,3584]{1,0:T(8,128)(2,1)S(1)}, bf16[144,3584]{1,0:T(8,128)(2,1)S(1)}, u32[]{:S(2)}, u32[]{:S(2)}) collective-permute-start(bf16[144,3584]{1,0:T(8,128)(2,1)S(1)} %collective-permute-done.22.refs_6_.refs_15_), channel_id=1, source_target_pairs={{0,4},{1,9},{2,6},{3,11},{8,0},{9,17},{10,2},{11,19},{16,8},{17,25... | collective-permute-start | bytes 3096584 | tf_op jit(solution)/shard_map/ppermute | solution.py:116
  155.4 36.5 %collective-permute-start.25 = (bf16[144,3584]{1,0:T(8,128)(2,1)S(1)}, bf16[144,3584]{1,0:T(8,128)(2,1)S(1)}, u32[]{:S(2)}, u32[]{:S(2)}) collective-permute-start(bf16[144,3584]{1,0:T(8,128)(2,1)S(1)} %collective-permute-done.23.refs_7_.refs_16_), channel_id=1, source_target_pairs={{0,8},{1,5},{2,10},{3,7},{8,16},{9,1},{10,18},{11,3},{16,24},{17,9... | collective-permute-start | bytes 3096584 | tf_op jit(solution)/shard_map/ppermute | solution.py:116
  155.4 18.1 %collective-permute-start.27 = (bf16[224,1152]{1,0:T(8,128)(2,1)S(1)}, bf16[224,1152]{1,0:T(8,128)(2,1)S(1)}, u32[]{:S(2)}, u32[]{:S(2)}) collective-permute-start(bf16[224,1152]{1,0:T(8,128)(2,1)S(1)} %copy-done.15), channel_id=1, source_target_pairs={{0,4},{1,9},{2,6},{3,11},{8,0},{9,17},{10,2},{11,19},{16,8},{17,25... | collective-permute-start | bytes 1548296 | tf_op jit(solution)/shard_map/ppermute | solution.py:116
  166.5 25.4 %collective-permute-start.28 = (bf16[224,1152]{1,0:T(8,128)(2,1)S(1)}, bf16[224,1152]{1,0:T(8,128)(2,1)S(1)}, u32[]{:S(2)}, u32[]{:S(2)}) collective-permute-start(bf16[224,1152]{1,0:T(8,128)(2,1)S(1)} %collective-permute-done.26.refs_5_.refs_6_), channel_id=1, source_target_pairs={{0,8},{1,5},{2,10},{3,7},{8,16},{9,1},{10,18},{11,3},{16,24},{17,9... | collective-permute-start | bytes 1548296 | tf_op jit(solution)/shard_map/ppermute | solution.py:116
  173.5 44.0 %collective-permute-start.29 = (bf16[224,1152]{1,0:T(8,128)(2,1)S(1)}, bf16[224,1152]{1,0:T(8,128)(2,1)S(1)}, u32[]{:S(2)}, u32[]{:S(2)}) collective-permute-start(bf16[224,1152]{1,0:T(8,128)(2,1)S(1)} %collective-permute-done.27.refs_6_.refs_7_), channel_id=1, source_target_pairs={{0,4},{1,9},{2,6},{3,11},{8,0},{9,17},{10,2},{11,19},{16,8},{17,25... | collective-permute-start | bytes 1548296 | tf_op jit(solution)/shard_map/ppermute | solution.py:116
  191.9 25.7 %collective-permute-start.30 = (bf16[224,1152]{1,0:T(8,128)(2,1)S(1)}, bf16[224,1152]{1,0:T(8,128)(2,1)S(1)}, u32[]{:S(2)}, u32[]{:S(2)}) collective-permute-start(bf16[224,1152]{1,0:T(8,128)(2,1)S(1)} %collective-permute-done.28.refs_7_.refs_8_), channel_id=1, source_target_pairs={{0,8},{1,5},{2,10},{3,7},{8,16},{9,1},{10,18},{11,3},{16,24},{17,9... | collective-permute-start | bytes 1548296 | tf_op jit(solution)/shard_map/ppermute | solution.py:116
  234.0 28.1 %collective-permute-start.32 = (bf16[512,1152]{1,0:T(8,128)(2,1)S(1)}, bf16[512,1152]{1,0:T(8,128)(2,1)S(1)}, u32[]{:S(2)}, u32[]{:S(2)}) collective-permute-start(bf16[512,1152]{1,0:T(8,128)(2,1)S(1)} %add.264), channel_id=1, source_target_pairs={{0,2},{1,3},{2,0},{3,1},{4,6},{5,7},{6,4},{7,5},{8,10},{9,11},{10,... | collective-permute-start | bytes 3538952 | tf_op jit(solution)/shard_map/ppermute | solution.py:47
  283.1 60.8 %collective-permute-start.36 = (bf16[512,1152]{1,0:T(8,128)(2,1)}, bf16[512,1152]{1,0:T(8,128)(2,1)}, u32[]{:S(2)}, u32[]{:S(2)}) collective-permute-start(bf16[512,1152]{1,0:T(8,128)(2,1)} %get-tuple-element.156), channel_id=1, source_target_pairs={{0,2},{1,3},{2,0},{3,1},{4,6},{5,7},{6,4},{7,5},{8,10},{9,11},{10,... | collective-permute-start | bytes 3538952 | tf_op jit(solution)/shard_map/ppermute | solution.py:47
  361.5 20.8 %collective-permute-start.38 = (bf16[224,1152]{1,0:T(8,128)(2,1)S(1)}, bf16[224,1152]{1,0:T(8,128)(2,1)S(1)}, u32[]{:S(2)}, u32[]{:S(2)}) collective-permute-start(bf16[224,1152]{1,0:T(8,128)(2,1)S(1)} %get-tuple-element.236), channel_id=1, source_target_pairs={{0,8},{1,5},{2,10},{3,7},{8,16},{9,1},{10,18},{11,3},{16,24},{17,9... | collective-permute-start | bytes 1548296 | tf_op jit(solution)/shard_map/ppermute | solution.py:116
  364.8 48.9 %collective-permute-start.40 = (bf16[224,1152]{1,0:T(8,128)(2,1)}, bf16[224,1152]{1,0:T(8,128)(2,1)}, u32[]{:S(2)}, u32[]{:S(2)}) collective-permute-start(bf16[224,1152]{1,0:T(8,128)(2,1)} %get-tuple-element.235), channel_id=1, source_target_pairs={{0,4},{1,9},{2,6},{3,11},{8,0},{9,17},{10,2},{11,19},{16,8},{17,25... | collective-permute-start | bytes 1548296 | tf_op jit(solution)/shard_map/ppermute | solution.py:116
  412.0 36.0 %collective-permute-start.41 = (bf16[144,3584]{1,0:T(8,128)(2,1)S(1)}, bf16[144,3584]{1,0:T(8,128)(2,1)S(1)}, u32[]{:S(2)}, u32[]{:S(2)}) collective-permute-start(bf16[144,3584]{1,0:T(8,128)(2,1)S(1)} %get-tuple-element.230), channel_id=1, source_target_pairs={{0,8},{1,5},{2,10},{3,7},{8,16},{9,1},{10,18},{11,3},{16,24},{17,9... | collective-permute-start | bytes 3096584 | tf_op jit(solution)/shard_map/ppermute | solution.py:116
  419.8 31.0 %collective-permute-start.42 = (bf16[224,1152]{1,0:T(8,128)(2,1)}, bf16[224,1152]{1,0:T(8,128)(2,1)}, u32[]{:S(2)}, u32[]{:S(2)}) collective-permute-start(bf16[224,1152]{1,0:T(8,128)(2,1)} %get-tuple-element.234), channel_id=1, source_target_pairs={{0,8},{1,5},{2,10},{3,7},{8,16},{9,1},{10,18},{11,3},{16,24},{17,9... | collective-permute-start | bytes 1548296 | tf_op jit(solution)/shard_map/ppermute | solution.py:116
  421.5 29.3 %collective-permute-start.43 = (bf16[224,1152]{1,0:T(8,128)(2,1)}, bf16[224,1152]{1,0:T(8,128)(2,1)}, u32[]{:S(2)}, u32[]{:S(2)}) collective-permute-start(bf16[224,1152]{1,0:T(8,128)(2,1)} %get-tuple-element.233), channel_id=1, source_target_pairs={{0,4},{1,9},{2,6},{3,11},{8,0},{9,17},{10,2},{11,19},{16,8},{17,25... | collective-permute-start | bytes 1548296 | tf_op jit(solution)/shard_map/ppermute | solution.py:116
  462.5 16.6 %collective-permute-start.51 = (bf16[512,1152]{1,0:T(8,128)(2,1)S(1)}, bf16[512,1152]{1,0:T(8,128)(2,1)S(1)}, u32[]{:S(2)}, u32[]{:S(2)}) collective-permute-start(bf16[512,1152]{1,0:T(8,128)(2,1)S(1)} %pad_maximum_fusion.2), channel_id=1, source_target_pairs={{0,1},{1,0},{2,3},{3,2},{4,5},{5,4},{6,7},{7,6},{8,9},{9,8},{10,11... | collective-permute-start | bytes 3538952 | tf_op jit(solution)/shard_map/ppermute | solution.py:47
  463.6 41.8 %collective-permute-start.49 = (bf16[144,3584]{1,0:T(8,128)(2,1)S(1)}, bf16[144,3584]{1,0:T(8,128)(2,1)S(1)}, u32[]{:S(2)}, u32[]{:S(2)}) collective-permute-start(bf16[144,3584]{1,0:T(8,128)(2,1)S(1)} %dynamic-slice_add_fusion.4), channel_id=1, source_target_pairs={{0,8},{1,5},{2,10},{3,7},{8,16},{9,1},{10,18},{11,3},{16,24},{17,9... | collective-permute-start | bytes 3096584 | tf_op jit(solution)/shard_map/ppermute | solution.py:116
  464.9 40.5 %collective-permute-start.50 = (bf16[144,3584]{1,0:T(8,128)(2,1)S(1)}, bf16[144,3584]{1,0:T(8,128)(2,1)S(1)}, u32[]{:S(2)}, u32[]{:S(2)}) collective-permute-start(bf16[144,3584]{1,0:T(8,128)(2,1)S(1)} %get-tuple-element.187), channel_id=1, source_target_pairs={{0,4},{1,9},{2,6},{3,11},{8,0},{9,17},{10,2},{11,19},{16,8},{17,25... | collective-permute-start | bytes 3096584 | tf_op jit(solution)/shard_map/ppermute | solution.py:116
  465.7 22.5 %collective-permute-start.46 = (bf16[1024,256]{1,0:T(8,128)(2,1)S(1)}, bf16[1024,256]{1,0:T(8,128)(2,1)S(1)}, u32[]{:S(2)}, u32[]{:S(2)}) collective-permute-start(bf16[1024,256]{1,0:T(8,128)(2,1)S(1)} %fusion.9), channel_id=1, source_target_pairs={{0,2},{1,3},{2,0},{3,1},{4,6},{5,7},{6,4},{7,5},{8,10},{9,11},{10,... | collective-permute-start | bytes 1572872 | tf_op jit(solution)/shard_map/ppermute | solution.py:47
  477.5 28.0 %collective-permute-start.47 = (bf16[224,1152]{1,0:T(8,128)(2,1)}, bf16[224,1152]{1,0:T(8,128)(2,1)S(1)}, u32[]{:S(2)}, u32[]{:S(2)}) collective-permute-start(bf16[224,1152]{1,0:T(8,128)(2,1)} %get-tuple-element.181), channel_id=1, source_target_pairs={{0,8},{1,5},{2,10},{3,7},{8,16},{9,1},{10,18},{11,3},{16,24},{17,9... | collective-permute-start | bytes 1548296 | tf_op jit(solution)/shard_map/ppermute | solution.py:116
  479.1 26.3 %collective-permute-start.48 = (bf16[224,1152]{1,0:T(8,128)(2,1)}, bf16[224,1152]{1,0:T(8,128)(2,1)S(1)}, u32[]{:S(2)}, u32[]{:S(2)}) collective-permute-start(bf16[224,1152]{1,0:T(8,128)(2,1)} %get-tuple-element.183), channel_id=1, source_target_pairs={{0,4},{1,9},{2,6},{3,11},{8,0},{9,17},{10,2},{11,19},{16,8},{17,25... | collective-permute-start | bytes 1548296 | tf_op jit(solution)/shard_map/ppermute | solution.py:116
  513.4 32.5 %collective-permute-start.56 = (bf16[144,3584]{1,0:T(8,128)(2,1)S(1)}, bf16[144,3584]{1,0:T(8,128)(2,1)}, u32[]{:S(2)}, u32[]{:S(2)}) collective-permute-start(bf16[144,3584]{1,0:T(8,128)(2,1)S(1)} %get-tuple-element.227), channel_id=1, source_target_pairs={{0,4},{1,9},{2,6},{3,11},{8,0},{9,17},{10,2},{11,19},{16,8},{17,25... | collective-permute-start | bytes 3096584 | tf_op jit(solution)/shard_map/ppermute | solution.py:116
  514.6 31.3 %collective-permute-start.54 = (bf16[144,3584]{1,0:T(8,128)(2,1)S(1)}, bf16[144,3584]{1,0:T(8,128)(2,1)}, u32[]{:S(2)}, u32[]{:S(2)}) collective-permute-start(bf16[144,3584]{1,0:T(8,128)(2,1)S(1)} %get-tuple-element.228), channel_id=1, source_target_pairs={{0,8},{1,5},{2,10},{3,7},{8,16},{9,1},{10,18},{11,3},{16,24},{17,9... | collective-permute-start | bytes 3096584 | tf_op jit(solution)/shard_map/ppermute | solution.py:116
  529.1 15.9 %collective-permute-start.58 = (bf16[192,768]{1,0:T(8,128)(2,1)S(1)}, bf16[192,768]{1,0:T(8,128)(2,1)S(1)}, u32[]{:S(2)}, u32[]{:S(2)}) collective-permute-start(bf16[192,768]{1,0:T(8,128)(2,1)S(1)} %get-tuple-element.242), channel_id=1, source_target_pairs={{0,8},{1,5},{2,10},{3,7},{8,16},{9,1},{10,18},{11,3},{16,24},{17,9... | collective-permute-start | bytes 884744 | tf_op jit(solution)/shard_map/ppermute | solution.py:116
  561.9 40.7 %collective-permute-start.55 = (bf16[144,3584]{1,0:T(8,128)(2,1)}, bf16[144,3584]{1,0:T(8,128)(2,1)}, u32[]{:S(2)}, u32[]{:S(2)}) collective-permute-start(bf16[144,3584]{1,0:T(8,128)(2,1)} %get-tuple-element.225), channel_id=1, source_target_pairs={{0,8},{1,5},{2,10},{3,7},{8,16},{9,1},{10,18},{11,3},{16,24},{17,9... | collective-permute-start | bytes 3096584 | tf_op jit(solution)/shard_map/ppermute | solution.py:116
  563.5 39.0 %collective-permute-start.57 = (bf16[144,3584]{1,0:T(8,128)(2,1)S(1)}, bf16[144,3584]{1,0:T(8,128)(2,1)}, u32[]{:S(2)}, u32[]{:S(2)}) collective-permute-start(bf16[144,3584]{1,0:T(8,128)(2,1)S(1)} %get-tuple-element.226), channel_id=1, source_target_pairs={{0,4},{1,9},{2,6},{3,11},{8,0},{9,17},{10,2},{11,19},{16,8},{17,25... | collective-permute-start | bytes 3096584 | tf_op jit(solution)/shard_map/ppermute | solution.py:116
  563.9 67.6 %collective-permute-start.53 = (bf16[1024,1152]{1,0:T(8,128)(2,1)}, bf16[1024,1152]{1,0:T(8,128)(2,1)}, u32[]{:S(2)}, u32[]{:S(2)}) collective-permute-start(bf16[1024,1152]{1,0:T(8,128)(2,1)} %get-tuple-element.193), channel_id=1, source_target_pairs={{0,1},{1,0},{2,3},{3,2},{4,5},{5,4},{6,7},{7,6},{8,9},{9,8},{10,11... | collective-permute-start | bytes 7077896 | tf_op jit(solution)/shard_map/ppermute | solution.py:47
  572.9 24.7 %collective-permute-start.61 = (bf16[192,768]{1,0:T(8,128)(2,1)S(1)}, bf16[192,768]{1,0:T(8,128)(2,1)S(1)}, u32[]{:S(2)}, u32[]{:S(2)}) collective-permute-start(bf16[192,768]{1,0:T(8,128)(2,1)S(1)} %get-tuple-element.237), channel_id=1, source_target_pairs={{0,8},{1,5},{2,10},{3,7},{8,16},{9,1},{10,18},{11,3},{16,24},{17,9... | collective-permute-start | bytes 884744 | tf_op jit(solution)/shard_map/ppermute | solution.py:116
  574.5 23.1 %collective-permute-start.64 = (bf16[192,768]{1,0:T(8,128)(2,1)S(1)}, bf16[192,768]{1,0:T(8,128)(2,1)S(1)}, u32[]{:S(2)}, u32[]{:S(2)}) collective-permute-start(bf16[192,768]{1,0:T(8,128)(2,1)S(1)} %get-tuple-element.238), channel_id=1, source_target_pairs={{0,4},{1,9},{2,6},{3,11},{8,0},{9,17},{10,2},{11,19},{16,8},{17,25... | collective-permute-start | bytes 884744 | tf_op jit(solution)/shard_map/ppermute | solution.py:116
  608.4 19.0 %all-to-all-start.2 = ((bf16[4,36,3584]{2,1,0:T(8,128)(2,1)}), bf16[4,36,3584]{2,1,0:T(8,128)(2,1)S(1)}, u32[]{:S(2)}, u32[]{:S(2)}) async-start(bf16[4,36,3584]{2,1,0:T(8,128)(2,1)} %reshape.112), calls=%async_computation.2 | async-start | bytes 2293760 | tf_op jit(solution)/shard_map/all_to_all | solution.py:42
  612.9 23.2 %collective-permute-start.66 = (bf16[32,1152]{1,0:T(8,128)(2,1)S(1)}, bf16[32,1152]{1,0:T(8,128)(2,1)S(1)}, u32[]{:S(2)}, u32[]{:S(2)}) collective-permute-start(bf16[32,1152]{1,0:T(8,128)(2,1)S(1)} %maximum_maximum_fusion.2), channel_id=1, source_target_pairs={{0,0},{1,8},{2,16},{3,24},{4,1},{5,9},{6,17},{7,25},{8,2},{9,10},{... | collective-permute-start | bytes 221192 | tf_op jit(solution)/shard_map/ppermute | solution.py:1097
  634.1 45.2 %collective-permute-start.65 = (bf16[512,1152]{1,0:T(8,128)(2,1)}, bf16[512,1152]{1,0:T(8,128)(2,1)}, u32[]{:S(2)}, u32[]{:S(2)}) collective-permute-start(bf16[512,1152]{1,0:T(8,128)(2,1)} %slice_add_fusion), channel_id=1, source_target_pairs={{0,2},{1,3},{2,0},{3,1},{4,6},{5,7},{6,4},{7,5},{8,10},{9,11},{10,... | collective-permute-start | bytes 3538952 | tf_op jit(solution)/shard_map/ppermute | solution.py:47
  644.5 18.3 %collective-permute-start.68 = (f32[48,128]{1,0:T(8,128)S(1)}, f32[48,128]{1,0:T(8,128)S(1)}, u32[]{:S(2)}, u32[]{:S(2)}) collective-permute-start(f32[48,128]{1,0:T(8,128)S(1)} %add.300), channel_id=1, source_target_pairs={{0,2},{1,3},{2,0},{3,1},{4,6},{5,7},{6,4},{7,5},{8,10},{9,11},{10,... | collective-permute-start | bytes 73736 | tf_op jit(solution)/shard_map/ppermute | solution.py:47
  (120 other events, 1437.9 us)

commit v2 on v1

--- a/solution.py
+++ b/solution.py
@@ -75,11 +75,8 @@
     return jnp.concatenate([parts[j ^ bit] for j in range(len(parts))])
 
 
-def sum_all(value):
-    bit = 1
-    while bit < lax.axis_size("ctx"):
-        value = value + swap(value, bit)
-        bit *= 2
+def sum_rest(value):
+    value = value + swap(value, 1)
     bit = 1
     while bit < lax.axis_size("dp"):
         value = value + swap_dp(value, bit)
@@ -266,16 +263,15 @@
     return jnp.where(p < 4, 2 * p, 2 * (7 - p) + 1)
 
 
-def hidden_room(rows, dp):
-    unit = max(16, 256 // dp)
-    return -(-rows // unit) * unit
+def padded(rows):
+    return -(-rows // 16) * 16
 
 
 def pack_columns(w_gate_up, dp, ctx):
     rows, wide = w_gate_up.shape
     ff = wide // 2
     step = ff // (dp * ctx)
-    room = hidden_room(step, dp)
+    room = padded(step)
     part = dp * room
 
     def body(w, out):
@@ -589,6 +585,10 @@
     )
 
 
+def column_cuts(main, width):
+    return [(at, min(width, main - at)) for at in range(0, main, width)]
+
+
 def gate_stage(pre, w, places, half, into=()):
     seq, part = pre.shape[0], w.cols // 2
     rows = 512
@@ -604,14 +604,24 @@
     def body(pl_ref, p_ref, *refs):
         hidden, ab, room, sems = refs[count:]
         w.load(pl_ref, refs[:count], room, sems)
-        @pl.loop(0, part // 256)
-        def _(i):
-            at = pl.multiple_of(i * 256, 256)
-            gate, up = pl.ds(at, 256), pl.ds(pl.multiple_of(part + at, 256), 256)
-            h, b, a = pieces(mm(p_ref[...], room[:, gate]), mm(p_ref[...], room[:, up]))
-            hidden[:, gate] = h.astype(LOW)
-            ab[:, gate] = b.astype(LOW)
-            ab[:, up] = a.astype(LOW)
+        p = p_ref[...]
+
+        def multiply(at, wide):
+            return mm(p, room[:, at : at + wide]), mm(p, room[:, part + at : part + at + wide])
+
+        def finish(at, wide, made):
+            h, b, a = pieces(*made)
+            hidden[:, at : at + wide] = h.astype(LOW)
+            ab[:, at : at + wide] = b.astype(LOW)
+            ab[:, part + at : part + at + wide] = a.astype(LOW)
+
+        last = None
+        for cut in column_cuts(part, 256):
+            made = multiply(*cut)
+            if last is not None:
+                finish(*last)
+            last = (*cut, made)
+        finish(*last)
 
     def block(cols):
         return pl.BlockSpec((rows, cols), lambda r, m: (first + r, 0))
@@ -699,12 +709,11 @@
     def body(pl_ref, g_ref, ab_ref, *refs):
         out, room, sems = refs[count:]
         w.load(pl_ref, refs[:count], room, sems)
-        @pl.loop(0, part // 256)
-        def _(i):
-            at = pl.multiple_of(i * 256, 256)
-            hg = mm_nt(g_ref[...], room[pl.ds(at, 256), :])
-            for side in (pl.ds(at, 256), pl.ds(pl.multiple_of(part + at, 256), 256)):
-                out[:, side] = (hg * ab_ref[:, side].astype(F32)).astype(LOW)
+        g = g_ref[...]
+        for at, wide in column_cuts(part, 256):
+            hg = mm_nt(g, room[at : at + wide, :])
+            for side in (at, part + at):
+                out[:, side : side + wide] = (hg * ab_ref[:, side : side + wide].astype(F32)).astype(LOW)
 
     def block(cols):
         return pl.BlockSpec((rows, cols), lambda r, m: (first + r, 0))
@@ -925,18 +934,17 @@
             ]
         ),
     )
-    down_block = jnp.pad(w_down.astype(low), ((0, hidden_room(ff_rows, dp) - ff_rows), (0, 0)))
+    down_block = jnp.pad(w_down.astype(low), ((0, padded(ff_rows) - ff_rows), (0, 0)))
     down_ring = Gather(ring, down_block)
     down_first = down_ring.advance()
     tokens_far = swap(tie(tokens[0], small), 2)
     tokens_near = swap(tie(tokens[0], small), 1)
-    gate_up_cols = exchange(packed, "ctx").reshape(own_rows, -1)
+    gate_up_cols = exchange(tie(packed, tokens_far), "ctx").reshape(own_rows, -1)
     first_len = lengths[0, 0]
     pos = tie(jnp.arange(seq, dtype=jnp.int32), packed)
     cos_t, sin_t = rope_tables(pos - jnp.where(pos < first_len, 0, first_len), HD)
     small_ring.advance(*down_first)
     small_ring.advance(cos_t, sin_t)
-    small_ring.advance(gate_up_cols, tokens_near)
     tokens_last = swap(tie(tokens_far, *small_ring.held.values()), 1)
     tokens_all = jnp.concatenate([tokens[0], tokens_near, tokens_far, tokens_last])
     while small_ring.hop < ring.hops[0]:
@@ -964,8 +972,10 @@
     q, k, v, raw, normed = input_stage(
         tokens_all, w_in, gain_rows[0:1], head_rows, cos_t, sin_t, row_map, places
     )
+    down_second = down_ring.advance(q, *gate_seen)
     gate_ring.advance(q)
     mixed, lse = attention(tie(q, *gate_seen, out_far, out_near), k, v, base)
+    mixed = tie(mixed, *down_second)
     mixed_far, mixed_near = swap(mixed, 2), swap(mixed, 1)
     out_parts = [out_mine, out_near, out_far, swap(tie(out_far, mixed), 1)]
     down_ring.advance(mixed)
@@ -1004,27 +1014,28 @@
         places=places,
     )
     gate_up_low = hidden_back(ffn_here, full_down, slopes, places, 0)
-    resid_grad, proj_low, even, odd, gain_grad_here = residual(gate_up_low, half=0)
-    far = tie(far, resid_grad)
+    far = tie(far, gate_up_low)
     ffn_there = jnp.concatenate([far, swap(far, 1)])
-    near = swap(odd, 1)
+    gate_up_low = hidden_back(ffn_there, full_down, slopes, places, 1, (gate_up_low,))
+    grad_gate_up = mm_tn(pre_low, gate_up_low).astype(low)
+    gate_sum = Reduce(ring, grad_gate_up).send()
+    resid_grad, proj_low, even, odd, gain_grad_here = residual(
+        tie(gate_up_low, *gate_sum.tokens()), half=0
+    )
+    held_gate = gate_sum.absorb(resid_grad)
+    near = swap(tie(odd, *held_gate), 1)
     parts_here = (even, near)
-    far_there = swap(tie(add_low(even[1], near[1]), ffn_there), 2)
+    summed = add_low(even[1], near[1])
+    far_there = swap(summed, 2)
+    gate_sum.send()
     ffn_low = jnp.concatenate([ffn_here, ffn_there])
-    grad_down = mm_tn(hidden_low, ffn_low).astype(low)
+    grad_down = mm_tn(hidden_low, tie(ffn_low, summed, *held_gate)).astype(low)
     down_sum = Reduce(ring, grad_down).send()
-    gate_up_low = hidden_back(
-        tie(ffn_there, *down_sum.tokens()), full_down, slopes, places, 1, (gate_up_low,)
-    )
-    held_down = down_sum.absorb(gate_up_low)
-    grad_gate_up = mm_tn(tie(pre_low, *held_down), gate_up_low).astype(low)
-    gate_sum = Reduce(ring, grad_gate_up)
-    held_down = down_sum.send().absorb(grad_gate_up)
     resid_grad, proj_low, even, odd, gain_grad_there = residual(
-        tie(gate_up_low, *held_down, *gate_sum.tokens()), half=1, into=(resid_grad, proj_low)
-    )
-    held_gate = gate_sum.send().absorb(odd)
-    held_down = down_sum.send().absorb(odd)
+        tie(gate_up_low, far_there, *down_sum.tokens()), half=1, into=(resid_grad, proj_low)
+    )
+    held_gate = gate_sum.absorb(odd)
+    held_down = down_sum.absorb(odd)
     near = swap(tie(odd, *held_gate, *held_down), 1)
     summed = add_low(even[1], near[1])
     far_here = swap(summed, 2)
@@ -1047,11 +1058,10 @@
         base,
     )
     held_gate = gate_sum.absorb(qkv_low)
-    down_sum.absorb(qkv_low)
-    down_own = down_sum.finish()
+    held_down = down_sum.absorb(qkv_low)
     gate_sum.send()
-    grad_in = mm_tn(tie(normed, down_own, *held_gate), qkv_low).astype(low)
-    down_own = down_own[:ff_rows]
+    down_sum.send()
+    grad_in = mm_tn(tie(normed, *held_gate, *held_down), qkv_low).astype(low)
     grad_out = grad_out.reshape(dp, out_rows, D)
     in_blocks = jnp.concatenate(
         [
@@ -1065,7 +1075,7 @@
     )
     in_sum = Reduce(ring, in_blocks.reshape(-1, qkv_cols)).send()
     input_even, input_odd, gain_grad_a = input_back(
-        tie(qkv_low, *in_sum.tokens(), *held_gate),
+        tie(qkv_low, *in_sum.tokens()),
         w_in,
         tokens_all,
         resid_grad,
@@ -1073,12 +1083,15 @@
         pos_map,
         places,
     )
+    gate_sum.absorb(input_odd)
+    down_sum.absorb(input_odd)
     in_sum.absorb(input_odd)
-    held_gate = gate_sum.absorb(input_odd)
-    in_sum.send(*held_gate)
     gate_up_own = gate_sum.finish().astype(low)
+    in_sum.send(gate_up_own)
+    down_own = down_sum.finish()[:ff_rows]
     gate_up_own = exchange(gate_up_own.reshape(ctx, in_rows, -1), "ctx")
     near = swap(input_odd, 1)
+    summed = add_low(input_even[rows:], near[rows:])
     gain_grad_bc = gain_grad_here + gain_grad_there
     in_sum.absorb()
 
@@ -1096,11 +1109,6 @@
     )
     out_own = lax.ppermute(out_own, ("dp", "ctx"), to_owner).astype(f32)
     in_own = exchange(in_own[:own_rows].reshape(ctx, in_rows, qkv_cols), "ctx").astype(f32)
-    summed = tie(add_low(input_even[rows:], near[rows:]), gate_up_own, in_own)
-    far = swap(summed, 2)
-    input_grad = (
-        input_even[:rows].astype(f32) + near[:rows].astype(f32) + far.astype(f32)
-    )
     qkv_own = jnp.concatenate(
         [
             in_own[:, :, :HD].transpose(1, 0, 2).reshape(in_rows, H * HD),
@@ -1114,7 +1122,13 @@
         local_squares = local_squares + jnp.sum(piece * piece)
     lines = jnp.concatenate([gain_grads.reshape(-1, 128), head_grads.reshape(-1, 128)])
     squares = jnp.pad(local_squares.reshape(1, 1), ((0, 7), (0, 127)))
-    sums = sum_all(tie(jnp.concatenate([lines, squares]), summed))
+    sums = tie(jnp.concatenate([lines, squares]), summed)
+    sums = sums + swap(sums, 2)
+    far = swap(tie(summed, sums), 2)
+    input_grad = (
+        input_even[:rows].astype(f32) + near[:rows].astype(f32) + far.astype(f32)
+    )
+    sums = sum_rest(sums)
     small_grads = sums[: lines.shape[0]]
     index = lax.axis_index("dp") * ctx + place
     gains_own = lax.dynamic_slice_in_dim(
@@ -1125,7 +1139,6 @@
     )
     reduced = (qkv_own, out_own, gate_up_own, down_own, gains_own, head_own)
     total_squares = sums[lines.shape[0], 0] + jnp.sum(small_grads * small_grads)
-    total_squares = tie(total_squares, far)
     grad_norm = jnp.sqrt(total_squares)
     factor = 1.0 / jnp.maximum(grad_norm, 1.0)
     weights = (w_qkv, w_out, w_gate_up, w_down, gains, head_gains)
@@ -1133,6 +1146,7 @@
     seconds = (second_qkv, second_out, second_gate_up, second_down, second_gains, second_head)
     rates = (D ** (-0.5), (H * HD) ** (-0.5), D ** (-0.5), FF ** (-0.5), GAIN_RATE, GAIN_RATE)
     decays = (WEIGHT_DECAY, WEIGHT_DECAY, WEIGHT_DECAY, WEIGHT_DECAY, 0.0, 0.0)
+    reduced = reduced[:2] + (tie(gate_up_own, far, grad_norm),) + reduced[3:]
     updates = [
         adam_update(
             weights[index],

time: 701 us -> 672 us (0.959)
  waiting for transfers between devices: 203 us -> 179 us
  Pallas kernels: 245 us -> 223 us
  other arithmetic: 76.3 us -> 92.5 us
    pallas_call x17, Pallas kernels: 245 us -> 223 us  [call(): pl.pallas_call(kernel, out_shape=out_shape, grid_spec=pltpu.PrefetchScala...]
    ppermute x42, waiting for transfers between devices: 89.8 us -> 80.4 us  [send(): return lax.ppermute(value, ('dp', 'ctx'), pairs)]
    ppermute x25, waiting for transfers between devices: 87.5 us -> 78.4 us  [swap(): return lax.ppermute(value, 'ctx', [(i, i ^ bit) for i in range(count)])]
    add x13, other arithmetic: 29.1 us -> 37.4 us  [add_low(): return a + b]
    unnamed x187 -> x154, local copies, waits for them, and re-layouts: 12.8 us -> 16 us
  transfers between devices with their start and end apart: 76 -> 76, of which waited for: 33 -> 34; matrix products, arithmetic and copies ran while one was open for 14% -> 14% of each run, Pallas kernels for 30% -> 27%
where the time goes in v2:
time: 672 us; the launch traced here: 662 us
  Pallas kernels  223 us (33%)
  waiting for transfers between devices  179 us (27%)
  other arithmetic  92.5 us (14%)
  starting transfers between devices  82.1 us (12%)
  matrix products  46.8 us (7%)
  local copies, waits for them, and re-layouts  32.1 us (5%)
  between operations  7.35 us (1%)
    pallas_call x17, Pallas kernels, call(): pl.pallas_call(kernel, out_shape=out_shape, grid_spec=pltpu.PrefetchScala...  223 us
    ppermute x42, waiting for transfers between devices, send(): return lax.ppermute(value, ('dp', 'ctx'), pairs)  80.4 us
    ppermute x25, waiting for transfers between devices, swap(): return lax.ppermute(value, 'ctx', [(i, i ^ bit) for i in range(count)])  78.4 us
    ppermute x42, starting transfers between devices, send(): return lax.ppermute(value, ('dp', 'ctx'), pairs)  48.4 us
    dot_general x7, matrix products, mm_tn(): lax.dot_general(a, b, (((0,), (0,)), ((), ())), preferred_element_type=F32)  46.8 us
    add x13, other arithmetic, add_low(): return a + b  37.4 us
    all_to_all x4, starting transfers between devices, exchange(): return lax.all_to_all(parts, axis, split_axis=0, concat_axis=0, tiled=True)  16.9 us
    unnamed x154, local copies, waits for them, and re-layouts  16 us
  transfers between devices with their start and end apart: 76, of which 34 were waited for; matrix products, arithmetic and copies ran while one was open for 14% of the time, Pallas kernels for 27%

profile of v2, /device:TPU:0, one launch (start us, length us, event | category | flops | bytes accessed | tf_op | source)
XLA Modules:
  0.0 662.1 jit_solution(15475698503980890221)
XLA Ops:
  6.4 3.4 all-to-all-start
  22.2 5.6 multiply_sine_fusion
  32.5 6.2 collective-permute-done.6.refs_4_.refs_11_.refs_10_
  40.8 4.4 collective-permute-done.1
  45.8 3.7 all-to-all-start.1
  52.6 7.2 %collective-permute-done.10.refs_6_.refs_13_.refs_12_ = bf16[208,768]{1,0:T(8,128)(2,1)} collective-permute-done((bf16[208,768]{1,0:T(8,128)(2,1)S(1)}, bf16[208,768]{1,0:T(8,128)(2,1)}, u32[]{:S(2)}, u32[]{:S(2)}) %collective-permute-start.10) | collective-permute-done | bytes 319520 | tf_op jit(solution)/shard_map/ppermute | solution.py:113
  60.2 5.0 all-to-all-done.1
  78.1 5.5 pad_maximum_fusion.refs_2_.refs_3_.refs_9_.refs_8_.refs_4_
  83.5 12.1 %shard_map.402 = (bf16[2048,256]{1,0:T(8,128)(2,1)}, bf16[2048,256]{1,0:T(8,128)(2,1)}, bf16[2048,256]{1,0:T(8,128)(2,1)}, f32[2048,512]{1,0:T(8,128)}, bf16[2048,1152]{1,0:T(8,128)(2,1)}) custom-call(s32[8]{0:T(128)} %fusion.21.refs_0_, s32[8]{0:T(128)} %fusion.24.refs_0_.refs_1_, ...), custom_call_target="tpu_custom_call" | custom-call | flops 226492416 | bytes 1634720 | tf_op jit(solution)/shard_map/pallas_call | solution.py:223
  98.5 8.6 %shard_map.403 = (bf16[2048,256]{1,0:T(8,128)(2,1)}, f32[2048,1]{1,0:T(8,128)}) custom-call(s32[3]{0:T(128)} %fusion.17.refs_0_, bf16[2048,256]{1,0:T(8,128)(2,1)} %get-tuple-element.128.refs_1_, bf16[2048,256]{1,0:T(8,128)(2,1)} %get-tuple-element.129.refs_2_, bf16[2048,256]{1,0:T(8,128)(2,1)} %get-tuple-element.130.refs_3_), custom_call_target="tpu_custom_call" | custom-call | flops 100663296 | bytes 262656 | tf_op jit(solution)/shard_map/pallas_call | solution.py:223
  107.1 3.4 collective-permute-done.18.refs_6_.refs_7_
  111.8 24.1 %collective-permute-done.20.refs_3_ = bf16[2048,256]{1,0:T(8,128)(2,1)S(1)} collective-permute-done((bf16[2048,256]{1,0:T(8,128)(2,1)}, bf16[2048,256]{1,0:T(8,128)(2,1)S(1)}, u32[]{:S(2)}, u32[]{:S(2)}) %collective-permute-start.20) | collective-permute-done | bytes 1048608 | tf_op jit(solution)/shard_map/ppermute | solution.py:47
  138.5 22.9 %collective-permute-done.24.refs_6_.refs_15_ = bf16[144,3584]{1,0:T(8,128)(2,1)S(1)} collective-permute-done((bf16[144,3584]{1,0:T(8,128)(2,1)S(1)}, bf16[144,3584]{1,0:T(8,128)(2,1)S(1)}, u32[]{:S(2)}, u32[]{:S(2)}) %collective-permute-start.24) | collective-permute-done | bytes 1032224 | tf_op jit(solution)/shard_map/ppermute | solution.py:113
  164.3 13.0 %shard_map.404 = (f32[2048,1152]{1,0:T(8,128)}, bf16[2048,1152]{1,0:T(8,128)(2,1)}) custom-call(s32[8]{0:T(128)} %fusion.20.refs_0_, bf16[2048,256]{1,0:T(8,128)(2,1)} %get-tuple-element.134.refs_1_, bf16[2048,256]{1,0:T(8,128)(2,1)} %copy-done.46, bf16[2048,256]{1,0:T(8,128)(2,1)} %copy-done.43, bf16[2048,256]{1,0:T(8,128)(2,1)} %collective-permute-done.21.refs_4_, ...), custom_call_target="tpu_custom_call" | custom-call | flops 301989888 | bytes 1590400 | tf_op jit(solution)/shard_map/pallas_call | solution.py:223
  179.9 21.5 %collective-permute-done.28.refs_7_.refs_8_ = bf16[224,1152]{1,0:T(8,128)(2,1)S(1)} collective-permute-done((bf16[224,1152]{1,0:T(8,128)(2,1)S(1)}, bf16[224,1152]{1,0:T(8,128)(2,1)S(1)}, u32[]{:S(2)}, u32[]{:S(2)}) %collective-permute-start.28) | collective-permute-done | bytes 516128 | tf_op jit(solution)/shard_map/ppermute | solution.py:113
  204.1 20.6 %shard_map.405 = (bf16[2048,1792]{1,0:T(8,128)(2,1)}, bf16[2048,3584]{1,0:T(8,128)(2,1)}) custom-call(s32[8]{0:T(128)} %fusion.24.refs_0_.refs_1_, bf16[2048,1152]{1,0:T(8,128)(2,1)} %get-tuple-element.148.refs_1_, bf16[144,3584]{1,0:T(8,128)(2,1)} %copy-done, bf16[144,3584]{1,0:T(8,128)(2,1)} %copy-done.2, bf16[144,3584]{1,0:T(8,128)(2,1)} %copy-done.3, ...), custom_call_target="tpu_custom_call" | custom-call | flops 528482304 | bytes 2187264 | tf_op jit(solution)/shard_map/pallas_call | solution.py:223
  225.8 10.8 %shard_map.406 = (bf16[512,1152]{1,0:T(8,128)(2,1)}, bf16[512,1152]{1,0:T(8,128)(2,1)}) custom-call(s32[8]{0:T(128)} %fusion.24.refs_0_.refs_1_, bf16[2048,1792]{1,0:T(8,128)(2,1)} %get-tuple-element.142.refs_1_.refs_10_, bf16[224,1152]{1,0:T(8,128)(2,1)} %copy-done.9, bf16[224,1152]{1,0:T(8,128)(2,1)} %collective-permute-done.3.refs_3_.refs_4_, ...), custom_call_target="tpu_custom_call" | custom-call | flops 264241152 | bytes 864256 | tf_op jit(solution)/shard_map/pallas_call | solution.py:223
  241.7 21.0 %shard_map.407 = (bf16[2048,1792]{1,0:T(8,128)(2,1)}, bf16[2048,3584]{1,0:T(8,128)(2,1)}) custom-call(s32[8]{0:T(128)} %fusion.24.refs_0_.refs_1_, bf16[2048,1152]{1,0:T(8,128)(2,1)} %get-tuple-element.148.refs_1_, bf16[144,3584]{1,0:T(8,128)(2,1)} %copy-done, bf16[144,3584]{1,0:T(8,128)(2,1)} %copy-done.2, ...), custom_call_target="tpu_custom_call", output_to_operand_aliasing={{0}: (10, {}), {1}: (11, {})} | custom-call | flops 528482304 | bytes 2187264 | tf_op jit(solution)/shard_map/pallas_call | solution.py:223
  262.7 6.7 %collective-permute-done.32.refs_2_ = bf16[512,1152]{1,0:T(8,128)(2,1)S(1)} collective-permute-done((bf16[512,1152]{1,0:T(8,128)(2,1)S(1)}, bf16[512,1152]{1,0:T(8,128)(2,1)S(1)}, u32[]{:S(2)}, u32[]{:S(2)}) %collective-permute-start.32) | collective-permute-done | bytes 1179680 | tf_op jit(solution)/shard_map/ppermute | solution.py:47
  269.3 10.8 %shard_map.408 = (bf16[512,1152]{1,0:T(8,128)(2,1)}, bf16[512,1152]{1,0:T(8,128)(2,1)}) custom-call(s32[8]{0:T(128)} %fusion.24.refs_0_.refs_1_, bf16[2048,1792]{1,0:T(8,128)(2,1)} %get-tuple-element.151.refs_1_, bf16[224,1152]{1,0:T(8,128)(2,1)} %copy-done.9, bf16[224,1152]{1,0:T(8,128)(2,1)} %collective-permute-done.3.refs_3_.refs_4_, ...), custom_call_target="tpu_custom_call" | custom-call | flops 264241152 | bytes 864256 | tf_op jit(solution)/shard_map/pallas_call | solution.py:223
  284.3 5.9 shard_map.409
  296.6 13.2 %shard_map.410.refs_11_ = bf16[2048,3584]{1,0:T(8,128)(2,1)} custom-call(s32[8]{0:T(128)} %fusion.24.refs_0_.refs_1_, bf16[1024,1152]{1,0:T(8,128)(2,1)} %pad_maximum_fusion.2.refs_1_, bf16[2048,3584]{1,0:T(8,128)(2,1)} %get-tuple-element.159.refs_2_, bf16[224,1152]{1,0:T(8,128)(2,1)} %copy-done.9, bf16[224,1152]{1,0:T(8,128)(2,1)} %collective-permute-done.3.refs_3_.refs_4_, ...), custom_call_target="tpu_custom_call" | custom-call | flops 264241152 | bytes 2240512 | tf_op jit(solution)/shard_map/pallas_call | solution.py:223
  309.8 9.0 %collective-permute-done.34 = bf16[512,1152]{1,0:T(8,128)(2,1)S(1)} collective-permute-done((bf16[512,1152]{1,0:T(8,128)(2,1)}, bf16[512,1152]{1,0:T(8,128)(2,1)S(1)}, u32[]{:S(2)}, u32[]{:S(2)}) %collective-permute-start.34) | collective-permute-done | bytes 1179680 | tf_op jit(solution)/shard_map/ppermute | solution.py:47
  324.3 13.4 %shard_map.411.refs_2_ = bf16[2048,3584]{1,0:T(8,128)(2,1)} custom-call(s32[8]{0:T(128)} %fusion.24.refs_0_.refs_1_, bf16[1024,1152]{1,0:T(8,128)(2,1)} %pad_maximum_fusion.3.refs_1_, bf16[2048,3584]{1,0:T(8,128)(2,1)} %get-tuple-element.159.refs_2_, bf16[224,1152]{1,0:T(8,128)(2,1)} %copy-done.9, ...), custom_call_target="tpu_custom_call", output_to_operand_aliasing={{}: (11, {})} | custom-call | flops 264241152 | bytes 2240512 | tf_op jit(solution)/shard_map/pallas_call | solution.py:223
  337.8 20.8 %convolution_convert_fusion = bf16[1152,3584]{1,0:T(8,128)(2,1)S(1)} fusion(bf16[2048,1152]{1,0:T(8,128)(2,1)S(1)} %bitcast.74, bf16[2048,3584]{1,0:T(8,128)(2,1)} %shard_map.411.refs_2_), kind=kOutput, calls=%fused_computation | convolution fusion | flops 16915562496 | bytes 27656192 | tf_op jit(solution)/shard_map/dot_general | solution.py:211
  366.4 27.8 %shard_map.412 = (bf16[2048,1152]{1,0:T(8,128)(2,1)}, bf16[2048,1152]{1,0:T(8,128)(2,1)}, bf16[2,1024,256]{2,1,0:T(8,128)(2,1)}, bf16[2,1024,256]{2,1,0:T(8,128)(2,1)}, f32[2,1152]{1,0:T(2,128)}) custom-call(s32[8]{0:T(128)} %fusion.20.refs_0_, s32[8]{0:T(128)} %fusion.24.refs_0_.refs_1_, bf16[2048,3584]{1,0:T(8,128)(2,1)} %shard_map.411.refs_2_, ...), custom_call_target="tpu_custom_call" | custom-call | flops 679477248 | bytes 3262144 | tf_op jit(solution)/shard_map/pallas_call | solution.py:223
  394.2 3.8 dynamic-slice_add_fusion.4
  405.5 10.5 %convolution_convert_fusion.1 = bf16[1792,1152]{1,0:T(8,128)(2,1)S(1)} fusion(bf16[2048,1792]{1,0:T(8,128)(2,1)S(1)} %bitcast.72, bf16[2048,1152]{1,0:T(8,128)(2,1)S(1)} %pad_maximum_fusion.1), kind=kOutput, calls=%fused_computation.1 | convolution fusion | flops 8457781248 | bytes 16187392 | tf_op jit(solution)/shard_map/dot_general | solution.py:211
  422.1 26.4 %shard_map.413 = (bf16[2048,1152]{1,0:T(8,128)(2,1)}, bf16[2048,1152]{1,0:T(8,128)(2,1)}, bf16[2,1024,256]{2,1,0:T(8,128)(2,1)}, bf16[2,1024,256]{2,1,0:T(8,128)(2,1)}, f32[2,1152]{1,0:T(2,128)}) custom-call(s32[8]{0:T(128)} %fusion.20.refs_0_, s32[8]{0:T(128)} %fusion.24.refs_0_.refs_1_, ...), custom_call_target="tpu_custom_call", output_to_operand_aliasing={{0}: (19, {}), {1}: (20, {})} | custom-call | flops 679477248 | bytes 3262144 | tf_op jit(solution)/shard_map/pallas_call | solution.py:223
  451.7 5.2 dynamic-slice_add_fusion.2
  475.9 5.1 collective-permute-done.44.refs_8_
  481.8 16.5 %shard_map.414 = (bf16[2048,768]{1,0:T(8,128)(2,1)}, f32[2,256]{1,0:T(2,128)}) custom-call(s32[3]{0:T(128)} %fusion.17.refs_0_, bf16[2048,256]{1,0:T(8,128)(2,1)} %get-tuple-element.128.refs_1_, bf16[2048,256]{1,0:T(8,128)(2,1)} %get-tuple-element.129.refs_2_, bf16[2048,256]{1,0:T(8,128)(2,1)} %get-tuple-element.130.refs_3_, ...), custom_call_target="tpu_custom_call" | custom-call | flops 251658240 | bytes 1114880 | tf_op jit(solution)/shard_map/pallas_call | solution.py:223
  498.3 3.5 collective-permute-done.47
  501.8 5.1 dynamic-slice_add_fusion
  514.3 6.3 convolution_convert_fusion.2
  520.6 4.6 collective-permute-done.50
  532.4 13.7 %shard_map.415 = (bf16[1024,1152]{1,0:T(8,128)(2,1)}, bf16[1024,1152]{1,0:T(8,128)(2,1)}, f32[1,1152]{1,0:T(1,128)}) custom-call(s32[8]{0:T(128)} %compare_select_fusion.1.refs_0_, s32[8]{0:T(128)} %fusion.24.refs_0_.refs_1_, bf16[2048,768]{1,0:T(8,128)(2,1)} %get-tuple-element.190.refs_2_.refs_3_, bf16[2048,768]{1,0:T(8,128)(2,1)} %get-tuple-element.190.refs_2_.refs_3_, ...), custom_call_target="tpu_custom_call" | custom-call | flops 226492416 | bytes 1438272 | tf_op jit(solution)/shard_map/pallas_call | solution.py:223
  554.0 3.5 all-to-all-start.3
  563.1 4.2 dynamic-slice_add_fusion.6
  577.4 4.9 collective-permute-done.63
  594.1 6.3 all-to-all-start.2
  602.2 4.3 all-to-all-done.2
  612.9 3.8 collective-permute-done.66
  618.3 3.4 collective-permute-done.69
  641.9 4.8 multiply_subtract_fusion.1
  646.7 6.7 %collective-permute-done.67 = bf16[512,1152]{1,0:T(8,128)(2,1)} collective-permute-done((bf16[512,1152]{1,0:T(8,128)(2,1)}, bf16[512,1152]{1,0:T(8,128)(2,1)}, u32[]{:S(2)}, u32[]{:S(2)}) %collective-permute-start.67) | collective-permute-done | bytes 1179680 | tf_op jit(solution)/shard_map/ppermute | solution.py:47
  653.4 3.9 multiply_subtract_fusion
  657.3 3.4 add_bitcast_fusion
  (386 shorter events, 198.3 us)
Async XLA Ops:
  2.1 16.5 %collective-permute-start.3 = (bf16[224,1152]{1,0:T(8,128)(2,1)S(1)}, bf16[224,1152]{1,0:T(8,128)(2,1)}, u32[]{:S(2)}, u32[]{:S(2)}) collective-permute-start(bf16[224,1152]{1,0:T(8,128)(2,1)S(1)} %pad.13.refs_2_.refs_3_), channel_id=1, source_target_pairs={{0,8},{1,5},{2,10},{3,7},{8,16},{9,1},{10,18},{11,3},{16,24},{17,9... | collective-permute-start | bytes 1548296 | tf_op jit(solution)/shard_map/ppermute | solution.py:113
  15.6 29.7 %collective-permute-start.1 = (bf16[512,1152]{1,0:T(8,128)(2,1)}, bf16[512,1152]{1,0:T(8,128)(2,1)}, u32[]{:S(2)}, u32[]{:S(2)}) collective-permute-start(bf16[512,1152]{1,0:T(8,128)(2,1)} %bitcast.2.refs_4_), channel_id=1, source_target_pairs={{0,2},{1,3},{2,0},{3,1},{4,6},{5,7},{6,4},{7,5},{8,10},{9,11},{10,... | collective-permute-start | bytes 3538952 | tf_op jit(solution)/shard_map/ppermute | solution.py:47
  45.2 22.9 %collective-permute-start.9 = (bf16[512,1152]{1,0:T(8,128)(2,1)}, bf16[512,1152]{1,0:T(8,128)(2,1)}, u32[]{:S(2)}, u32[]{:S(2)}) collective-permute-start(bf16[512,1152]{1,0:T(8,128)(2,1)} %collective-permute-done.1), channel_id=1, source_target_pairs={{0,1},{1,0},{2,3},{3,2},{4,5},{5,4},{6,7},{7,6},{8,9},{9,8},{10,11... | collective-permute-start | bytes 3538952 | tf_op jit(solution)/shard_map/ppermute | solution.py:47
  45.4 32.7 %collective-permute-start = (bf16[512,1152]{1,0:T(8,128)(2,1)}, bf16[512,1152]{1,0:T(8,128)(2,1)}, u32[]{:S(2)}, u32[]{:S(2)}) collective-permute-start(bf16[512,1152]{1,0:T(8,128)(2,1)} %bitcast.2.refs_4_), channel_id=1, source_target_pairs={{0,1},{1,0},{2,3},{3,2},{4,5},{5,4},{6,7},{7,6},{8,9},{9,8},{10,11... | collective-permute-start | bytes 3538952 | tf_op jit(solution)/shard_map/ppermute | solution.py:47
  45.8 19.4 %all-to-all-start.1 = ((bf16[4,36,3584]{2,1,0:T(8,128)(2,1)}), bf16[4,36,3584]{2,1,0:T(8,128)(2,1)S(1)}, u32[]{:S(2)}, u32[]{:S(2)}) async-start(bf16[4,36,3584]{2,1,0:T(8,128)(2,1)} %shard_map.400), calls=%async_computation.1 | async-start | bytes 2293760 | tf_op jit(solution)/shard_map/all_to_all | solution.py:42
  50.8 14.6 %collective-permute-start.11 = (bf16[208,768]{1,0:T(8,128)(2,1)S(1)}, bf16[208,768]{1,0:T(8,128)(2,1)}, u32[]{:S(2)}, u32[]{:S(2)}) collective-permute-start(bf16[208,768]{1,0:T(8,128)(2,1)S(1)} %collective-permute-done.8.refs_5_.refs_12_.refs_11_), channel_id=1, source_target_pairs={{0,4},{1,9},{2,6},{3,11},{8,0},{9,17},{10,2},{11,19},{16,8},{17,25... | collective-permute-start | bytes 958472 | tf_op jit(solution)/shard_map/ppermute | solution.py:113
  68.2 27.5 %collective-permute-start.13 = (bf16[144,3584]{1,0:T(8,128)(2,1)S(1)}, bf16[144,3584]{1,0:T(8,128)(2,1)S(1)}, u32[]{:S(2)}, u32[]{:S(2)}) collective-permute-start(bf16[144,3584]{1,0:T(8,128)(2,1)S(1)} %reshape.108.refs_2_.refs_11_), channel_id=1, source_target_pairs={{0,8},{1,5},{2,10},{3,7},{8,16},{9,1},{10,18},{11,3},{16,24},{17,9... | collective-permute-start | bytes 3096584 | tf_op jit(solution)/shard_map/ppermute | solution.py:113
  68.2 27.5 %collective-permute-start.14 = (bf16[144,3584]{1,0:T(8,128)(2,1)S(1)}, bf16[144,3584]{1,0:T(8,128)(2,1)S(1)}, u32[]{:S(2)}, u32[]{:S(2)}) collective-permute-start(bf16[144,3584]{1,0:T(8,128)(2,1)S(1)} %reshape.108.refs_2_.refs_11_), channel_id=1, source_target_pairs={{0,4},{1,9},{2,6},{3,11},{8,0},{9,17},{10,2},{11,19},{16,8},{17,25... | collective-permute-start | bytes 3096584 | tf_op jit(solution)/shard_map/ppermute | solution.py:113
  75.0 23.5 %collective-permute-start.15 = (bf16[256,1152]{1,0:T(8,128)(2,1)}, bf16[256,1152]{1,0:T(8,128)(2,1)}, u32[]{:S(2)}, u32[]{:S(2)}) collective-permute-start(bf16[256,1152]{1,0:T(8,128)(2,1)} %get-tuple-element.127.refs_5_.refs_3_), channel_id=1, source_target_pairs={{0,2},{1,3},{2,0},{3,1},{4,6},{5,7},{6,4},{7,5},{8,10},{9,11},{10,... | collective-permute-start | bytes 1769480 | tf_op jit(solution)/shard_map/ppermute | solution.py:47
  76.7 21.8 %collective-permute-start.16 = (bf16[256,1152]{1,0:T(8,128)(2,1)}, bf16[256,1152]{1,0:T(8,128)(2,1)}, u32[]{:S(2)}, u32[]{:S(2)}) collective-permute-start(bf16[256,1152]{1,0:T(8,128)(2,1)} %get-tuple-element.127.refs_5_.refs_3_), channel_id=1, source_target_pairs={{0,1},{1,0},{2,3},{3,2},{4,5},{5,4},{6,7},{7,6},{8,9},{9,8},{10,11... | collective-permute-start | bytes 1769480 | tf_op jit(solution)/shard_map/ppermute | solution.py:47
  95.7 14.8 %collective-permute-start.18 = (bf16[224,1152]{1,0:T(8,128)(2,1)}, bf16[224,1152]{1,0:T(8,128)(2,1)S(1)}, u32[]{:S(2)}, u32[]{:S(2)}) collective-permute-start(bf16[224,1152]{1,0:T(8,128)(2,1)} %collective-permute-done.4.refs_4_.refs_5_), channel_id=1, source_target_pairs={{0,4},{1,9},{2,6},{3,11},{8,0},{9,17},{10,2},{11,19},{16,8},{17,25... | collective-permute-start | bytes 1548296 | tf_op jit(solution)/shard_map/ppermute | solution.py:113
  110.6 25.3 %collective-permute-start.20 = (bf16[2048,256]{1,0:T(8,128)(2,1)}, bf16[2048,256]{1,0:T(8,128)(2,1)S(1)}, u32[]{:S(2)}, u32[]{:S(2)}) collective-permute-start(bf16[2048,256]{1,0:T(8,128)(2,1)} %get-tuple-element.134.refs_1_), channel_id=1, source_target_pairs={{0,2},{1,3},{2,0},{3,1},{4,6},{5,7},{6,4},{7,5},{8,10},{9,11},{10,... | collective-permute-start | bytes 3145736 | tf_op jit(solution)/shard_map/ppermute | solution.py:47
  111.0 26.3 %collective-permute-start.23 = (bf16[144,3584]{1,0:T(8,128)(2,1)S(1)}, bf16[144,3584]{1,0:T(8,128)(2,1)S(1)}, u32[]{:S(2)}, u32[]{:S(2)}) collective-permute-start(bf16[144,3584]{1,0:T(8,128)(2,1)S(1)} %collective-permute-done.13.refs_3_.refs_12_), channel_id=1, source_target_pairs={{0,8},{1,5},{2,10},{3,7},{8,16},{9,1},{10,18},{11,3},{16,24},{17,9... | collective-permute-start | bytes 3096584 | tf_op jit(solution)/shard_map/ppermute | solution.py:113
  111.0 52.1 %collective-permute-start.19 = (bf16[2048,256]{1,0:T(8,128)(2,1)}, bf16[2048,256]{1,0:T(8,128)(2,1)S(1)}, u32[]{:S(2)}, u32[]{:S(2)}) collective-permute-start(bf16[2048,256]{1,0:T(8,128)(2,1)} %get-tuple-element.134.refs_1_), channel_id=1, source_target_pairs={{0,1},{1,0},{2,3},{3,2},{4,5},{5,4},{6,7},{7,6},{8,9},{9,8},{10,11... | collective-permute-start | bytes 3145736 | tf_op jit(solution)/shard_map/ppermute | solution.py:47
  135.9 28.4 %collective-permute-start.21 = (bf16[2048,256]{1,0:T(8,128)(2,1)S(1)}, bf16[2048,256]{1,0:T(8,128)(2,1)}, u32[]{:S(2)}, u32[]{:S(2)}) collective-permute-start(bf16[2048,256]{1,0:T(8,128)(2,1)S(1)} %collective-permute-done.20.refs_3_), channel_id=1, source_target_pairs={{0,1},{1,0},{2,3},{3,2},{4,5},{5,4},{6,7},{7,6},{8,9},{9,8},{10,11... | collective-permute-start | bytes 3145736 | tf_op jit(solution)/shard_map/ppermute | solution.py:47
  135.9 25.5 %collective-permute-start.24 = (bf16[144,3584]{1,0:T(8,128)(2,1)S(1)}, bf16[144,3584]{1,0:T(8,128)(2,1)S(1)}, u32[]{:S(2)}, u32[]{:S(2)}) collective-permute-start(bf16[144,3584]{1,0:T(8,128)(2,1)S(1)} %collective-permute-done.14.refs_4_.refs_13_), channel_id=1, source_target_pairs={{0,4},{1,9},{2,6},{3,11},{8,0},{9,17},{10,2},{11,19},{16,8},{17,25... | collective-permute-start | bytes 3096584 | tf_op jit(solution)/shard_map/ppermute | solution.py:113
  137.3 40.1 %collective-permute-start.25 = (bf16[144,3584]{1,0:T(8,128)(2,1)S(1)}, bf16[144,3584]{1,0:T(8,128)(2,1)S(1)}, u32[]{:S(2)}, u32[]{:S(2)}) collective-permute-start(bf16[144,3584]{1,0:T(8,128)(2,1)S(1)} %collective-permute-done.23.refs_5_.refs_14_), channel_id=1, source_target_pairs={{0,8},{1,5},{2,10},{3,7},{8,16},{9,1},{10,18},{11,3},{16,24},{17,9... | collective-permute-start | bytes 3096584 | tf_op jit(solution)/shard_map/ppermute | solution.py:113
  137.9 25.1 %collective-permute-start.22 = (bf16[256,1152]{1,0:T(8,128)(2,1)}, bf16[256,1152]{1,0:T(8,128)(2,1)S(1)}, u32[]{:S(2)}, u32[]{:S(2)}) collective-permute-start(bf16[256,1152]{1,0:T(8,128)(2,1)} %collective-permute-done.15.refs_7_.refs_5_), channel_id=1, source_target_pairs={{0,1},{1,0},{2,3},{3,2},{4,5},{5,4},{6,7},{7,6},{8,9},{9,8},{10,11... | collective-permute-start | bytes 1769480 | tf_op jit(solution)/shard_map/ppermute | solution.py:47
  161.4 40.8 %collective-permute-start.26 = (bf16[144,3584]{1,0:T(8,128)(2,1)S(1)}, bf16[144,3584]{1,0:T(8,128)(2,1)S(1)}, u32[]{:S(2)}, u32[]{:S(2)}) collective-permute-start(bf16[144,3584]{1,0:T(8,128)(2,1)S(1)} %collective-permute-done.24.refs_6_.refs_15_), channel_id=1, source_target_pairs={{0,4},{1,9},{2,6},{3,11},{8,0},{9,17},{10,2},{11,19},{16,8},{17,25... | collective-permute-start | bytes 3096584 | tf_op jit(solution)/shard_map/ppermute | solution.py:113
  177.3 24.8 %collective-permute-start.27 = (bf16[144,3584]{1,0:T(8,128)(2,1)S(1)}, bf16[144,3584]{1,0:T(8,128)(2,1)S(1)}, u32[]{:S(2)}, u32[]{:S(2)}) collective-permute-start(bf16[144,3584]{1,0:T(8,128)(2,1)S(1)} %collective-permute-done.25.refs_7_.refs_16_), channel_id=1, source_target_pairs={{0,8},{1,5},{2,10},{3,7},{8,16},{9,1},{10,18},{11,3},{16,24},{17,9... | collective-permute-start | bytes 3096584 | tf_op jit(solution)/shard_map/ppermute | solution.py:113
  177.9 23.5 %collective-permute-start.28 = (bf16[224,1152]{1,0:T(8,128)(2,1)S(1)}, bf16[224,1152]{1,0:T(8,128)(2,1)S(1)}, u32[]{:S(2)}, u32[]{:S(2)}) collective-permute-start(bf16[224,1152]{1,0:T(8,128)(2,1)S(1)} %collective-permute-done.17.refs_5_.refs_6_), channel_id=1, source_target_pairs={{0,8},{1,5},{2,10},{3,7},{8,16},{9,1},{10,18},{11,3},{16,24},{17,9... | collective-permute-start | bytes 1548296 | tf_op jit(solution)/shard_map/ppermute | solution.py:113
  178.0 46.8 %collective-permute-start.29 = (bf16[224,1152]{1,0:T(8,128)(2,1)S(1)}, bf16[224,1152]{1,0:T(8,128)(2,1)S(1)}, u32[]{:S(2)}, u32[]{:S(2)}) collective-permute-start(bf16[224,1152]{1,0:T(8,128)(2,1)S(1)} %collective-permute-done.18.refs_6_.refs_7_), channel_id=1, source_target_pairs={{0,4},{1,9},{2,6},{3,11},{8,0},{9,17},{10,2},{11,19},{16,8},{17,25... | collective-permute-start | bytes 1548296 | tf_op jit(solution)/shard_map/ppermute | solution.py:113
  201.4 23.3 %collective-permute-start.30 = (bf16[224,1152]{1,0:T(8,128)(2,1)S(1)}, bf16[224,1152]{1,0:T(8,128)(2,1)S(1)}, u32[]{:S(2)}, u32[]{:S(2)}) collective-permute-start(bf16[224,1152]{1,0:T(8,128)(2,1)S(1)} %collective-permute-done.28.refs_7_.refs_8_), channel_id=1, source_target_pairs={{0,8},{1,5},{2,10},{3,7},{8,16},{9,1},{10,18},{11,3},{16,24},{17,9... | collective-permute-start | bytes 1548296 | tf_op jit(solution)/shard_map/ppermute | solution.py:113
  241.3 28.1 %collective-permute-start.32 = (bf16[512,1152]{1,0:T(8,128)(2,1)S(1)}, bf16[512,1152]{1,0:T(8,128)(2,1)S(1)}, u32[]{:S(2)}, u32[]{:S(2)}) collective-permute-start(bf16[512,1152]{1,0:T(8,128)(2,1)S(1)} %add.264), channel_id=1, source_target_pairs={{0,2},{1,3},{2,0},{3,1},{4,6},{5,7},{6,4},{7,5},{8,10},{9,11},{10,... | collective-permute-start | bytes 3538952 | tf_op jit(solution)/shard_map/ppermute | solution.py:47
  290.4 28.5 %collective-permute-start.34 = (bf16[512,1152]{1,0:T(8,128)(2,1)}, bf16[512,1152]{1,0:T(8,128)(2,1)S(1)}, u32[]{:S(2)}, u32[]{:S(2)}) collective-permute-start(bf16[512,1152]{1,0:T(8,128)(2,1)} %get-tuple-element.158), channel_id=1, source_target_pairs={{0,2},{1,3},{2,0},{3,1},{4,6},{5,7},{6,4},{7,5},{8,10},{9,11},{10,... | collective-permute-start | bytes 3538952 | tf_op jit(solution)/shard_map/ppermute | solution.py:47
  365.0 29.3 %collective-permute-start.37 = (bf16[144,3584]{1,0:T(8,128)(2,1)}, bf16[144,3584]{1,0:T(8,128)(2,1)}, u32[]{:S(2)}, u32[]{:S(2)}) collective-permute-start(bf16[144,3584]{1,0:T(8,128)(2,1)} %get-tuple-element.232), channel_id=1, source_target_pairs={{0,8},{1,5},{2,10},{3,7},{8,16},{9,1},{10,18},{11,3},{16,24},{17,9... | collective-permute-start | bytes 3096584 | tf_op jit(solution)/shard_map/ppermute | solution.py:113
  398.8 49.8 %collective-permute-start.41 = (bf16[144,3584]{1,0:T(8,128)(2,1)}, bf16[144,3584]{1,0:T(8,128)(2,1)}, u32[]{:S(2)}, u32[]{:S(2)}) collective-permute-start(bf16[144,3584]{1,0:T(8,128)(2,1)} %get-tuple-element.231), channel_id=1, source_target_pairs={{0,4},{1,9},{2,6},{3,11},{8,0},{9,17},{10,2},{11,19},{16,8},{17,25... | collective-permute-start | bytes 3096584 | tf_op jit(solution)/shard_map/ppermute | solution.py:113
  402.7 45.8 %collective-permute-start.40 = (bf16[144,3584]{1,0:T(8,128)(2,1)}, bf16[144,3584]{1,0:T(8,128)(2,1)}, u32[]{:S(2)}, u32[]{:S(2)}) collective-permute-start(bf16[144,3584]{1,0:T(8,128)(2,1)} %dynamic-slice_add_fusion.4), channel_id=1, source_target_pairs={{0,8},{1,5},{2,10},{3,7},{8,16},{9,1},{10,18},{11,3},{16,24},{17,9... | collective-permute-start | bytes 3096584 | tf_op jit(solution)/shard_map/ppermute | solution.py:113
  405.2 16.9 %collective-permute-start.39 = (bf16[1024,256]{1,0:T(8,128)(2,1)S(1)}, bf16[1024,256]{1,0:T(8,128)(2,1)}, u32[]{:S(2)}, u32[]{:S(2)}) collective-permute-start(bf16[1024,256]{1,0:T(8,128)(2,1)S(1)} %fusion.3), channel_id=1, source_target_pairs={{0,2},{1,3},{2,0},{3,1},{4,6},{5,7},{6,4},{7,5},{8,10},{9,11},{10,... | collective-permute-start | bytes 1572872 | tf_op jit(solution)/shard_map/ppermute | solution.py:47
  420.3 28.2 %collective-permute-start.42 = (bf16[224,1152]{1,0:T(8,128)(2,1)}, bf16[224,1152]{1,0:T(8,128)(2,1)}, u32[]{:S(2)}, u32[]{:S(2)}) collective-permute-start(bf16[224,1152]{1,0:T(8,128)(2,1)} %get-tuple-element.238), channel_id=1, source_target_pairs={{0,8},{1,5},{2,10},{3,7},{8,16},{9,1},{10,18},{11,3},{16,24},{17,9... | collective-permute-start | bytes 1548296 | tf_op jit(solution)/shard_map/ppermute | solution.py:113
  465.4 36.5 %collective-permute-start.45 = (bf16[144,3584]{1,0:T(8,128)(2,1)}, bf16[144,3584]{1,0:T(8,128)(2,1)}, u32[]{:S(2)}, u32[]{:S(2)}) collective-permute-start(bf16[144,3584]{1,0:T(8,128)(2,1)} %get-tuple-element.181), channel_id=1, source_target_pairs={{0,8},{1,5},{2,10},{3,7},{8,16},{9,1},{10,18},{11,3},{16,24},{17,9... | collective-permute-start | bytes 3096584 | tf_op jit(solution)/shard_map/ppermute | solution.py:113
  466.9 34.9 %collective-permute-start.46 = (bf16[144,3584]{1,0:T(8,128)(2,1)}, bf16[144,3584]{1,0:T(8,128)(2,1)}, u32[]{:S(2)}, u32[]{:S(2)}) collective-permute-start(bf16[144,3584]{1,0:T(8,128)(2,1)} %get-tuple-element.183), channel_id=1, source_target_pairs={{0,4},{1,9},{2,6},{3,11},{8,0},{9,17},{10,2},{11,19},{16,8},{17,25... | collective-permute-start | bytes 3096584 | tf_op jit(solution)/shard_map/ppermute | solution.py:113
  467.4 13.6 %collective-permute-start.44 = (bf16[1024,256]{1,0:T(8,128)(2,1)S(1)}, bf16[1024,256]{1,0:T(8,128)(2,1)S(1)}, u32[]{:S(2)}, u32[]{:S(2)}) collective-permute-start(bf16[1024,256]{1,0:T(8,128)(2,1)S(1)} %fusion.2), channel_id=1, source_target_pairs={{0,2},{1,3},{2,0},{3,1},{4,6},{5,7},{6,4},{7,5},{8,10},{9,11},{10,... | collective-permute-start | bytes 1572872 | tf_op jit(solution)/shard_map/ppermute | solution.py:47
  471.5 30.3 %collective-permute-start.47 = (bf16[224,1152]{1,0:T(8,128)(2,1)}, bf16[224,1152]{1,0:T(8,128)(2,1)}, u32[]{:S(2)}, u32[]{:S(2)}) collective-permute-start(bf16[224,1152]{1,0:T(8,128)(2,1)} %dynamic-slice_add_fusion.9), channel_id=1, source_target_pairs={{0,8},{1,5},{2,10},{3,7},{8,16},{9,1},{10,18},{11,3},{16,24},{17,9... | collective-permute-start | bytes 1548296 | tf_op jit(solution)/shard_map/ppermute | solution.py:113
  473.0 28.8 %collective-permute-start.48 = (bf16[224,1152]{1,0:T(8,128)(2,1)}, bf16[224,1152]{1,0:T(8,128)(2,1)}, u32[]{:S(2)}, u32[]{:S(2)}) collective-permute-start(bf16[224,1152]{1,0:T(8,128)(2,1)} %get-tuple-element.187), channel_id=1, source_target_pairs={{0,4},{1,9},{2,6},{3,11},{8,0},{9,17},{10,2},{11,19},{16,8},{17,25... | collective-permute-start | bytes 1548296 | tf_op jit(solution)/shard_map/ppermute | solution.py:113
  510.3 14.9 %collective-permute-start.50 = (bf16[256,1152]{1,0:T(8,128)(2,1)S(1)}, bf16[256,1152]{1,0:T(8,128)(2,1)S(1)}, u32[]{:S(2)}, u32[]{:S(2)}) collective-permute-start(bf16[256,1152]{1,0:T(8,128)(2,1)S(1)} %copy-done.69), channel_id=1, source_target_pairs={{0,2},{1,3},{2,0},{3,1},{4,6},{5,7},{6,4},{7,5},{8,10},{9,11},{10,... | collective-permute-start | bytes 1769480 | tf_op jit(solution)/shard_map/ppermute | solution.py:47
  512.1 35.5 %collective-permute-start.53 = (bf16[144,3584]{1,0:T(8,128)(2,1)}, bf16[144,3584]{1,0:T(8,128)(2,1)S(1)}, u32[]{:S(2)}, u32[]{:S(2)}) collective-permute-start(bf16[144,3584]{1,0:T(8,128)(2,1)} %get-tuple-element.228), channel_id=1, source_target_pairs={{0,8},{1,5},{2,10},{3,7},{8,16},{9,1},{10,18},{11,3},{16,24},{17,9... | collective-permute-start | bytes 3096584 | tf_op jit(solution)/shard_map/ppermute | solution.py:113
  514.0 33.6 %collective-permute-start.54 = (bf16[144,3584]{1,0:T(8,128)(2,1)}, bf16[144,3584]{1,0:T(8,128)(2,1)S(1)}, u32[]{:S(2)}, u32[]{:S(2)}) collective-permute-start(bf16[144,3584]{1,0:T(8,128)(2,1)} %get-tuple-element.227), channel_id=1, source_target_pairs={{0,4},{1,9},{2,6},{3,11},{8,0},{9,17},{10,2},{11,19},{16,8},{17,25... | collective-permute-start | bytes 3096584 | tf_op jit(solution)/shard_map/ppermute | solution.py:113
  527.9 18.3 %collective-permute-start.52 = (bf16[192,768]{1,0:T(8,128)(2,1)S(1)}, bf16[192,768]{1,0:T(8,128)(2,1)S(1)}, u32[]{:S(2)}, u32[]{:S(2)}) collective-permute-start(bf16[192,768]{1,0:T(8,128)(2,1)S(1)} %get-tuple-element.244), channel_id=1, source_target_pairs={{0,8},{1,5},{2,10},{3,7},{8,16},{9,1},{10,18},{11,3},{16,24},{17,9... | collective-permute-start | bytes 884744 | tf_op jit(solution)/shard_map/ppermute | solution.py:113
  530.4 21.7 %collective-permute-start.64 = (bf16[224,1152]{1,0:T(8,128)(2,1)S(1)}, bf16[224,1152]{1,0:T(8,128)(2,1)S(1)}, u32[]{:S(2)}, u32[]{:S(2)}) collective-permute-start(bf16[224,1152]{1,0:T(8,128)(2,1)S(1)} %get-tuple-element.235), channel_id=1, source_target_pairs={{0,4},{1,9},{2,6},{3,11},{8,0},{9,17},{10,2},{11,19},{16,8},{17,25... | collective-permute-start | bytes 1548296 | tf_op jit(solution)/shard_map/ppermute | solution.py:113
  530.4 22.4 %collective-permute-start.62 = (bf16[224,1152]{1,0:T(8,128)(2,1)S(1)}, bf16[224,1152]{1,0:T(8,128)(2,1)}, u32[]{:S(2)}, u32[]{:S(2)}) collective-permute-start(bf16[224,1152]{1,0:T(8,128)(2,1)S(1)} %get-tuple-element.236), channel_id=1, source_target_pairs={{0,8},{1,5},{2,10},{3,7},{8,16},{9,1},{10,18},{11,3},{16,24},{17,9... | collective-permute-start | bytes 1548296 | tf_op jit(solution)/shard_map/ppermute | solution.py:113
  552.1 58.0 %collective-permute-start.51 = (bf16[1024,1152]{1,0:T(8,128)(2,1)}, bf16[1024,1152]{1,0:T(8,128)(2,1)}, u32[]{:S(2)}, u32[]{:S(2)}) collective-permute-start(bf16[1024,1152]{1,0:T(8,128)(2,1)} %get-tuple-element.193), channel_id=1, source_target_pairs={{0,1},{1,0},{2,3},{3,2},{4,5},{5,4},{6,7},{7,6},{8,9},{9,8},{10,11... | collective-permute-start | bytes 7077896 | tf_op jit(solution)/shard_map/ppermute | solution.py:47
  554.0 32.6 %all-to-all-start.3 = ((bf16[4,36,3584]{2,1,0:T(8,128)(2,1)}), bf16[4,36,3584]{2,1,0:T(8,128)(2,1)S(1)}, u32[]{:S(2)}, u32[]{:S(2)}) async-start(bf16[4,36,3584]{2,1,0:T(8,128)(2,1)} %reshape.116), calls=%async_computation.3 | async-start | bytes 2293760 | tf_op jit(solution)/shard_map/all_to_all | solution.py:42
  567.3 15.0 %collective-permute-start.63 = (bf16[224,1152]{1,0:T(8,128)(2,1)}, bf16[224,1152]{1,0:T(8,128)(2,1)}, u32[]{:S(2)}, u32[]{:S(2)}) collective-permute-start(bf16[224,1152]{1,0:T(8,128)(2,1)} %get-tuple-element.233), channel_id=1, source_target_pairs={{0,8},{1,5},{2,10},{3,7},{8,16},{9,1},{10,18},{11,3},{16,24},{17,9... | collective-permute-start | bytes 1548296 | tf_op jit(solution)/shard_map/ppermute | solution.py:113
  568.8 15.0 %collective-permute-start.65 = (bf16[224,1152]{1,0:T(8,128)(2,1)}, bf16[224,1152]{1,0:T(8,128)(2,1)}, u32[]{:S(2)}, u32[]{:S(2)}) collective-permute-start(bf16[224,1152]{1,0:T(8,128)(2,1)} %get-tuple-element.234), channel_id=1, source_target_pairs={{0,4},{1,9},{2,6},{3,11},{8,0},{9,17},{10,2},{11,19},{16,8},{17,25... | collective-permute-start | bytes 1548296 | tf_op jit(solution)/shard_map/ppermute | solution.py:113
  574.6 15.9 %collective-permute-start.57 = (bf16[192,768]{1,0:T(8,128)(2,1)}, bf16[192,768]{1,0:T(8,128)(2,1)}, u32[]{:S(2)}, u32[]{:S(2)}) collective-permute-start(bf16[192,768]{1,0:T(8,128)(2,1)} %get-tuple-element.239), channel_id=1, source_target_pairs={{0,8},{1,5},{2,10},{3,7},{8,16},{9,1},{10,18},{11,3},{16,24},{17,9... | collective-permute-start | bytes 884744 | tf_op jit(solution)/shard_map/ppermute | solution.py:113
  576.1 14.5 %collective-permute-start.60 = (bf16[192,768]{1,0:T(8,128)(2,1)}, bf16[192,768]{1,0:T(8,128)(2,1)}, u32[]{:S(2)}, u32[]{:S(2)}) collective-permute-start(bf16[192,768]{1,0:T(8,128)(2,1)} %get-tuple-element.240), channel_id=1, source_target_pairs={{0,4},{1,9},{2,6},{3,11},{8,0},{9,17},{10,2},{11,19},{16,8},{17,25... | collective-permute-start | bytes 884744 | tf_op jit(solution)/shard_map/ppermute | solution.py:113
  627.4 26.1 %collective-permute-start.67 = (bf16[512,1152]{1,0:T(8,128)(2,1)}, bf16[512,1152]{1,0:T(8,128)(2,1)}, u32[]{:S(2)}, u32[]{:S(2)}) collective-permute-start(bf16[512,1152]{1,0:T(8,128)(2,1)} %slice_add_fusion), channel_id=1, source_target_pairs={{0,2},{1,3},{2,0},{3,1},{4,6},{5,7},{6,4},{7,5},{8,10},{9,11},{10,... | collective-permute-start | bytes 3538952 | tf_op jit(solution)/shard_map/ppermute | solution.py:47
  (104 other events, 1296.6 us)

commit v3 on v2

--- a/solution.py
+++ b/solution.py
@@ -196,7 +196,7 @@
 SHORT = 2
 GELU_A = 0.7978845608028654
 GELU_B = 0.044715
-VMEM = 56 * 2**20
+VMEM = 36 * 2**20
 
 
 def mm(a, b):
@@ -973,14 +973,14 @@
         tokens_all, w_in, gain_rows[0:1], head_rows, cos_t, sin_t, row_map, places
     )
     down_second = down_ring.advance(q, *gate_seen)
-    gate_ring.advance(q)
+    gate_second = gate_ring.advance(q)
     mixed, lse = attention(tie(q, *gate_seen, out_far, out_near), k, v, base)
     mixed = tie(mixed, *down_second)
     mixed_far, mixed_near = swap(mixed, 2), swap(mixed, 1)
     out_parts = [out_mine, out_near, out_far, swap(tie(out_far, mixed), 1)]
     down_ring.advance(mixed)
     gate_ring.advance(mixed)
-    mixed_parts = [mixed, mixed_near, mixed_far, swap(mixed_far, 1)]
+    mixed_parts = [mixed, mixed_near, mixed_far, swap(tie(mixed_far, *gate_second), 1)]
     proj, pre_low = project(mixed_parts, out_parts, tokens_all, gain_rows, stored_map)
     while gate_ring.hop < ring.hops[0]:
         gate_ring.advance(pre_low)
@@ -1034,14 +1034,14 @@
     resid_grad, proj_low, even, odd, gain_grad_there = residual(
         tie(gate_up_low, far_there, *down_sum.tokens()), half=1, into=(resid_grad, proj_low)
     )
+    near = swap(tie(odd, *gate_sum.came.values(), *down_sum.came.values()), 1)
+    summed = add_low(even[1], near[1])
+    far_here = swap(summed, 2)
     held_gate = gate_sum.absorb(odd)
     held_down = down_sum.absorb(odd)
-    near = swap(tie(odd, *held_gate, *held_down), 1)
-    summed = add_low(even[1], near[1])
-    far_here = swap(summed, 2)
-    gate_sum.send(summed)
-    down_sum.send(summed)
-    proj_low = tie(proj_low, summed)
+    gate_sum.send()
+    down_sum.send()
+    proj_low = tie(proj_low, *held_gate, *held_down)
     grad_out = [mm_tn(m, proj_low).astype(low) for m in mixed_parts]
     far_here = tie(far_here, *grad_out)
     grad_out = reduce_ctx(grad_out).astype(low)
@@ -1057,11 +1057,7 @@
         sin_t,
         base,
     )
-    held_gate = gate_sum.absorb(qkv_low)
-    held_down = down_sum.absorb(qkv_low)
-    gate_sum.send()
-    down_sum.send()
-    grad_in = mm_tn(tie(normed, *held_gate, *held_down), qkv_low).astype(low)
+    grad_in = mm_tn(normed, qkv_low).astype(low)
     grad_out = grad_out.reshape(dp, out_rows, D)
     in_blocks = jnp.concatenate(
         [
@@ -1073,9 +1069,16 @@
         ],
         axis=1,
     )
-    in_sum = Reduce(ring, in_blocks.reshape(-1, qkv_cols)).send()
+    in_sum = Reduce(ring, in_blocks.reshape(-1, qkv_cols))
+    held_gate = gate_sum.absorb(*in_sum.tokens())
+    held_down = down_sum.absorb(*in_sum.tokens())
+    in_sum.send()
+    gate_sum.send()
+    down_sum.send()
+    held_in = in_sum.absorb(*held_gate, *held_down)
+    in_sum.send()
     input_even, input_odd, gain_grad_a = input_back(
-        tie(qkv_low, *in_sum.tokens()),
+        tie(qkv_low, *held_in),
         w_in,
         tokens_all,
         resid_grad,
@@ -1083,19 +1086,25 @@
         pos_map,
         places,
     )
+    held_in = in_sum.absorb(input_odd)
+    in_sum.send()
+    gate_came = list(gate_sum.came.values())
     gate_sum.absorb(input_odd)
-    down_sum.absorb(input_odd)
-    in_sum.absorb(input_odd)
+    down_sum.absorb(*held_in)
     gate_up_own = gate_sum.finish().astype(low)
-    in_sum.send(gate_up_own)
-    down_own = down_sum.finish()[:ff_rows]
     gate_up_own = exchange(gate_up_own.reshape(ctx, in_rows, -1), "ctx")
-    near = swap(input_odd, 1)
+    near = swap(tie(input_odd, *gate_came), 1)
     summed = add_low(input_even[rows:], near[rows:])
     gain_grad_bc = gain_grad_here + gain_grad_there
-    in_sum.absorb()
-
-    in_own = in_sum.finish().astype(low)
+    while in_sum.hop > 1:
+        in_sum.absorb()
+        in_sum.send()
+    held_in = in_sum.tokens()
+
+    in_own = in_sum.absorb()[0].astype(low)
+    down_sum.send(*held_in)
+    down_sum.absorb(in_own)
+    down_own = down_sum.finish()[:ff_rows]
     gate_up_own = unpack_columns(gate_up_own, dp, ctx, ff_rows)
     out_own = in_own[own_rows:]
     out_own = jnp.concatenate(
@@ -1146,7 +1155,7 @@
     seconds = (second_qkv, second_out, second_gate_up, second_down, second_gains, second_head)
     rates = (D ** (-0.5), (H * HD) ** (-0.5), D ** (-0.5), FF ** (-0.5), GAIN_RATE, GAIN_RATE)
     decays = (WEIGHT_DECAY, WEIGHT_DECAY, WEIGHT_DECAY, WEIGHT_DECAY, 0.0, 0.0)
-    reduced = reduced[:2] + (tie(gate_up_own, far, grad_norm),) + reduced[3:]
+    reduced = reduced[:2] + (tie(gate_up_own, far, grad_norm), tie(down_own, far, grad_norm)) + reduced[4:]
     updates = [
         adam_update(
             weights[index],

time: 672 us -> 666 us (level)
  local copies, waits for them, and re-layouts: 32.1 us -> 68.9 us
  Pallas kernels: 223 us -> 192 us
  other arithmetic: 92.5 us -> 79.1 us
    unnamed x154 -> x280, local copies, waits for them, and re-layouts: 16 us -> 53 us
    pallas_call x17, Pallas kernels: 223 us -> 192 us  [call(): pl.pallas_call(kernel, out_shape=out_shape, grid_spec=pltpu.PrefetchScala...]
    ppermute x25, waiting for transfers between devices: 78.4 us -> 53.6 us  [swap(): return lax.ppermute(value, 'ctx', [(i, i ^ bit) for i in range(count)])]
    ppermute x42, waiting for transfers between devices: 80.4 us -> 94.6 us  [send(): return lax.ppermute(value, ('dp', 'ctx'), pairs)]
    all_to_all x4, waiting for transfers between devices: 11.3 us -> 20.5 us  [exchange(): return lax.all_to_all(parts, axis, split_axis=0, concat_axis=0, tiled=True)]
  transfers between devices with their start and end apart: 76 -> 76, of which waited for: 34 -> 33; matrix products, arithmetic and copies ran while one was open for 14% -> 14% of each run, Pallas kernels for 27% -> 24%
where the time goes in v3:
time: 666 us; the launch traced here: 655 us
  Pallas kernels  192 us (29%)
  waiting for transfers between devices  177 us (27%)
  starting transfers between devices  81.2 us (12%)
  other arithmetic  79.1 us (12%)
  local copies, waits for them, and re-layouts  68.9 us (10%)
  matrix products  49.3 us (7%)
  between operations  7.98 us (1%)
    pallas_call x17, Pallas kernels, call(): pl.pallas_call(kernel, out_shape=out_shape, grid_spec=pltpu.PrefetchScala...  192 us
    ppermute x42, waiting for transfers between devices, send(): return lax.ppermute(value, ('dp', 'ctx'), pairs)  94.6 us
    ppermute x25, waiting for transfers between devices, swap(): return lax.ppermute(value, 'ctx', [(i, i ^ bit) for i in range(count)])  53.6 us
    unnamed x280, local copies, waits for them, and re-layouts  53 us
    ppermute x42, starting transfers between devices, send(): return lax.ppermute(value, ('dp', 'ctx'), pairs)  50.4 us
    dot_general x7, matrix products, mm_tn(): lax.dot_general(a, b, (((0,), (0,)), ((), ())), preferred_element_type=F32)  49.3 us
    add x13, other arithmetic, add_low(): return a + b  33.6 us
    all_to_all x4, waiting for transfers between devices, exchange(): return lax.all_to_all(parts, axis, split_axis=0, concat_axis=0, tiled=True)  20.5 us
  transfers between devices with their start and end apart: 76, of which 33 were waited for; matrix products, arithmetic and copies ran while one was open for 14% of the time, Pallas kernels for 24%

profile of v3, /device:TPU:0, one launch (start us, length us, event | category | flops | bytes accessed | tf_op | source)
XLA Modules:
  0.0 655.3 jit_solution(11560586349741389104)
XLA Ops:
  12.0 3.6 all-to-all-done
  17.9 3.9 collective-permute-start.5
  22.5 5.5 multiply_sine_fusion
  32.7 4.2 collective-permute-done.6.refs_4_.refs_11_.refs_10_
  36.9 4.0 collective-permute-done.8.refs_5_.refs_12_.refs_11_
  40.8 3.6 collective-permute-done.1
  45.0 4.3 all-to-all-start.1
  51.8 7.3 %collective-permute-done.10.refs_6_.refs_13_.refs_12_ = bf16[208,768]{1,0:T(8,128)(2,1)S(1)} collective-permute-done((bf16[208,768]{1,0:T(8,128)(2,1)S(1)}, bf16[208,768]{1,0:T(8,128)(2,1)S(1)}, u32[]{:S(2)}, u32[]{:S(2)}) %collective-permute-start.10) | collective-permute-done | bytes 319520 | tf_op jit(solution)/shard_map/ppermute | solution.py:113
  61.6 3.7 all-to-all-done.1
  82.8 5.7 pad_maximum_fusion.refs_2_.refs_3_.refs_9_.refs_8_.refs_4_
  88.6 10.5 %shard_map.402 = (bf16[2048,256]{1,0:T(8,128)(2,1)S(1)}, bf16[2048,256]{1,0:T(8,128)(2,1)S(1)}, bf16[2048,256]{1,0:T(8,128)(2,1)S(1)}, f32[2048,512]{1,0:T(8,128)S(1)}, bf16[2048,1152]{1,0:T(8,128)(2,1)S(1)}) custom-call(s32[8]{0:T(128)S(1)} %fusion.21.refs_0_, s32[8]{0:T(128)S(1)} %fusion.24.refs_0_.refs_1_, ...), custom_call_target="tpu_custom_call" | custom-call | flops 226492416 | bytes 1634720 | tf_op jit(solution)/shard_map/pallas_call | solution.py:223
  112.2 5.6 shard_map.403
  123.8 23.4 %collective-permute-done.22.refs_6_.refs_15_ = bf16[144,3584]{1,0:T(8,128)(2,1)S(1)} collective-permute-done((bf16[144,3584]{1,0:T(8,128)(2,1)S(1)}, bf16[144,3584]{1,0:T(8,128)(2,1)S(1)}, u32[]{:S(2)}, u32[]{:S(2)}) %collective-permute-start.22) | collective-permute-done | bytes 1032224 | tf_op jit(solution)/shard_map/ppermute | solution.py:113
  154.0 11.7 %shard_map.404 = (f32[2048,1152]{1,0:T(8,128)}, bf16[2048,1152]{1,0:T(8,128)(2,1)S(1)}) custom-call(s32[8]{0:T(128)S(1)} %fusion.20.refs_0_, bf16[2048,256]{1,0:T(8,128)(2,1)S(1)} %get-tuple-element.136.refs_1_, bf16[2048,256]{1,0:T(8,128)(2,1)S(1)} %collective-permute-done.19.refs_2_, bf16[2048,256]{1,0:T(8,128)(2,1)S(1)} %collective-permute-done.20.refs_3_, ...), custom_call_target="tpu_custom_call" | custom-call | flops 301989888 | bytes 1590400 | tf_op jit(solution)/shard_map/pallas_call | solution.py:223
  165.7 6.4 collective-permute-done.25.refs_7_.refs_16_
  175.9 21.7 %collective-permute-done.28.refs_7_.refs_8_ = bf16[224,1152]{1,0:T(8,128)(2,1)S(1)} collective-permute-done((bf16[224,1152]{1,0:T(8,128)(2,1)}, bf16[224,1152]{1,0:T(8,128)(2,1)S(1)}, u32[]{:S(2)}, u32[]{:S(2)}) %collective-permute-start.28) | collective-permute-done | bytes 516128 | tf_op jit(solution)/shard_map/ppermute | solution.py:113
  197.9 18.7 %shard_map.405 = (bf16[2048,1792]{1,0:T(8,128)(2,1)}, bf16[2048,3584]{1,0:T(8,128)(2,1)}) custom-call(s32[8]{0:T(128)S(1)} %fusion.24.refs_0_.refs_1_, bf16[2048,1152]{1,0:T(8,128)(2,1)S(1)} %get-tuple-element.151.refs_1_, bf16[144,3584]{1,0:T(8,128)(2,1)S(1)} %reshape.108.refs_2_.refs_11_, bf16[144,3584]{1,0:T(8,128)(2,1)S(1)} %collective-permute-done.13.refs_3_.refs_12_, ...), custom_call_target="tpu_custom_call" | custom-call | flops 528482304 | bytes 2187264 | tf_op jit(solution)/shard_map/pallas_call | solution.py:223
  220.2 7.4 %shard_map.406 = (bf16[512,1152]{1,0:T(8,128)(2,1)S(1)}, bf16[512,1152]{1,0:T(8,128)(2,1)S(1)}) custom-call(s32[8]{0:T(128)S(1)} %fusion.24.refs_0_.refs_1_, bf16[2048,1792]{1,0:T(8,128)(2,1)S(1)} %copy-done.2, bf16[224,1152]{1,0:T(8,128)(2,1)S(1)} %copy-done.28, bf16[224,1152]{1,0:T(8,128)(2,1)} %collective-permute-done.3.refs_3_.refs_4_, ...), custom_call_target="tpu_custom_call" | custom-call | flops 264241152 | bytes 864256 | tf_op jit(solution)/shard_map/pallas_call | solution.py:223
  237.0 19.2 %shard_map.407 = (bf16[2048,1792]{1,0:T(8,128)(2,1)}, bf16[2048,3584]{1,0:T(8,128)(2,1)}) custom-call(s32[8]{0:T(128)S(1)} %fusion.24.refs_0_.refs_1_, bf16[2048,1152]{1,0:T(8,128)(2,1)S(1)} %get-tuple-element.151.refs_1_, bf16[144,3584]{1,0:T(8,128)(2,1)S(1)} %reshape.108.refs_2_.refs_11_, ...), custom_call_target="tpu_custom_call", output_to_operand_aliasing={{0}: (10, {}), {1}: (11, {})} | custom-call | flops 528482304 | bytes 2187264 | tf_op jit(solution)/shard_map/pallas_call | solution.py:223
  265.2 7.4 %shard_map.408 = (bf16[512,1152]{1,0:T(8,128)(2,1)S(1)}, bf16[512,1152]{1,0:T(8,128)(2,1)S(1)}) custom-call(s32[8]{0:T(128)S(1)} %fusion.24.refs_0_.refs_1_, bf16[2048,1792]{1,0:T(8,128)(2,1)S(1)} %copy-done.3, bf16[224,1152]{1,0:T(8,128)(2,1)S(1)} %copy-done.28, bf16[224,1152]{1,0:T(8,128)(2,1)} %collective-permute-done.3.refs_3_.refs_4_, ...), custom_call_target="tpu_custom_call" | custom-call | flops 264241152 | bytes 864256 | tf_op jit(solution)/shard_map/pallas_call | solution.py:223
  275.5 4.4 shard_map.409
  283.1 12.1 %shard_map.410.refs_11_ = bf16[2048,3584]{1,0:T(8,128)(2,1)} custom-call(s32[8]{0:T(128)S(1)} %fusion.24.refs_0_.refs_1_, bf16[1024,1152]{1,0:T(8,128)(2,1)S(1)} %pad_maximum_fusion.2.refs_1_, bf16[2048,3584]{1,0:T(8,128)(2,1)} %get-tuple-element.162.refs_2_, bf16[224,1152]{1,0:T(8,128)(2,1)S(1)} %copy-done.28, ...), custom_call_target="tpu_custom_call" | custom-call | flops 264241152 | bytes 2240512 | tf_op jit(solution)/shard_map/pallas_call | solution.py:223
  295.2 13.2 %collective-permute-done.34 = bf16[512,1152]{1,0:T(8,128)(2,1)S(1)} collective-permute-done((bf16[512,1152]{1,0:T(8,128)(2,1)S(1)}, bf16[512,1152]{1,0:T(8,128)(2,1)S(1)}, u32[]{:S(2)}, u32[]{:S(2)}) %collective-permute-start.34) | collective-permute-done | bytes 1179680 | tf_op jit(solution)/shard_map/ppermute | solution.py:47
  312.4 12.7 %shard_map.411.refs_2_ = bf16[2048,3584]{1,0:T(8,128)(2,1)} custom-call(s32[8]{0:T(128)S(1)} %fusion.24.refs_0_.refs_1_, bf16[1024,1152]{1,0:T(8,128)(2,1)S(1)} %pad_maximum_fusion.3.refs_1_, bf16[2048,3584]{1,0:T(8,128)(2,1)} %get-tuple-element.162.refs_2_, bf16[224,1152]{1,0:T(8,128)(2,1)S(1)} %copy-done.28, ...), custom_call_target="tpu_custom_call", output_to_operand_aliasing={{}: (11, {})} | custom-call | flops 264241152 | bytes 2240512 | tf_op jit(solution)/shard_map/pallas_call | solution.py:223
  325.2 23.2 %convolution_convert_fusion = bf16[1152,3584]{1,0:T(8,128)(2,1)} fusion(bf16[2048,1152]{1,0:T(8,128)(2,1)S(1)} %bitcast.76, bf16[2048,3584]{1,0:T(8,128)(2,1)} %shard_map.411.refs_2_), kind=kOutput, calls=%fused_computation | convolution fusion | flops 16915562496 | bytes 27656192 | tf_op jit(solution)/shard_map/dot_general | solution.py:211
  348.4 3.9 constant_dynamic-slice_fusion.6
  353.8 26.3 %shard_map.412 = (bf16[2048,1152]{1,0:T(8,128)(2,1)S(1)}, bf16[2048,1152]{1,0:T(8,128)(2,1)}, bf16[2,1024,256]{2,1,0:T(8,128)(2,1)S(1)}, bf16[2,1024,256]{2,1,0:T(8,128)(2,1)S(1)}, f32[2,1152]{1,0:T(2,128)S(1)}) custom-call(s32[8]{0:T(128)S(1)} %fusion.20.refs_0_, s32[8]{0:T(128)S(1)} %fusion.24.refs_0_.refs_1_, bf16[2048,3584]{1,0:T(8,128)(2,1)} %shard_map.411.refs_2_, ...), custom_call_target="tpu_custom_call" | custom-call | flops 679477248 | bytes 3262144 | tf_op jit(solution)/shard_map/pallas_call | solution.py:223
  380.1 3.8 dynamic-slice_add_fusion.4
  389.9 14.0 %convolution_convert_fusion.1 = bf16[1792,1152]{1,0:T(8,128)(2,1)} fusion(bf16[2048,1792]{1,0:T(8,128)(2,1)S(1)} %bitcast.74, bf16[2048,1152]{1,0:T(8,128)(2,1)} %pad_maximum_fusion.1), kind=kOutput, calls=%fused_computation.1 | convolution fusion | flops 8457781248 | bytes 16187392 | tf_op jit(solution)/shard_map/dot_general | solution.py:211
  403.9 3.5 constant_dynamic-slice_fusion.4
  408.9 25.6 %shard_map.413 = (bf16[2048,1152]{1,0:T(8,128)(2,1)S(1)}, bf16[2048,1152]{1,0:T(8,128)(2,1)}, bf16[2,1024,256]{2,1,0:T(8,128)(2,1)S(1)}, bf16[2,1024,256]{2,1,0:T(8,128)(2,1)S(1)}, f32[2,1152]{1,0:T(2,128)S(1)}) custom-call(s32[8]{0:T(128)S(1)} %fusion.20.refs_0_, s32[8]{0:T(128)S(1)} %fusion.24.refs_0_.refs_1_, ...), custom_call_target="tpu_custom_call", output_to_operand_aliasing={{0}: (19, {}), {1}: (20, {})} | custom-call | flops 679477248 | bytes 3262144 | tf_op jit(solution)/shard_map/pallas_call | solution.py:223
  437.7 5.4 dynamic-slice_add_fusion.2
  457.8 4.8 collective-permute-done.44.refs_8_
  464.1 12.7 %shard_map.414 = (bf16[2048,768]{1,0:T(8,128)(2,1)S(1)}, f32[2,256]{1,0:T(2,128)S(1)}) custom-call(s32[3]{0:T(128)S(1)} %fusion.17.refs_0_, bf16[2048,256]{1,0:T(8,128)(2,1)S(1)} %copy-done.56, bf16[2048,256]{1,0:T(8,128)(2,1)S(1)} %copy-done.59, bf16[2048,256]{1,0:T(8,128)(2,1)S(1)} %copy-done.62, f32[2048,512]{1,0:T(8,128)} %copy-done.53, ...), custom_call_target="tpu_custom_call" | custom-call | flops 251658240 | bytes 1114880 | tf_op jit(solution)/shard_map/pallas_call | solution.py:223
  476.8 4.2 convolution_convert_fusion.2
  485.9 5.0 dynamic-slice_add_fusion
  491.0 4.2 dynamic-slice_add_fusion.7
  510.2 13.1 %shard_map.415 = (bf16[1024,1152]{1,0:T(8,128)(2,1)S(1)}, bf16[1024,1152]{1,0:T(8,128)(2,1)}, f32[1,1152]{1,0:T(1,128)S(1)}) custom-call(s32[8]{0:T(128)S(1)} %compare_select_fusion.1.refs_0_, s32[8]{0:T(128)S(1)} %fusion.24.refs_0_.refs_1_, bf16[2048,768]{1,0:T(8,128)(2,1)S(1)} %get-tuple-element.189.refs_2_.refs_3_, ...), custom_call_target="tpu_custom_call" | custom-call | flops 226492416 | bytes 1438272 | tf_op jit(solution)/shard_map/pallas_call | solution.py:223
  532.2 4.7 collective-permute-done.56
  536.9 7.5 %collective-permute-done.59 = bf16[192,768]{1,0:T(8,128)(2,1)S(1)} collective-permute-done((bf16[192,768]{1,0:T(8,128)(2,1)S(1)}, bf16[192,768]{1,0:T(8,128)(2,1)S(1)}, u32[]{:S(2)}, u32[]{:S(2)}) %collective-permute-start.59) | collective-permute-done | bytes 294944 | tf_op jit(solution)/shard_map/ppermute | solution.py:113
  553.7 11.9 %collective-permute-done.57 = bf16[192,768]{1,0:T(8,128)(2,1)S(1)} collective-permute-done((bf16[192,768]{1,0:T(8,128)(2,1)S(1)}, bf16[192,768]{1,0:T(8,128)(2,1)S(1)}, u32[]{:S(2)}, u32[]{:S(2)}) %collective-permute-start.57) | collective-permute-done | bytes 294944 | tf_op jit(solution)/shard_map/ppermute | solution.py:113
  572.2 5.1 all-to-all-done.2
  577.4 3.7 all-to-all-start.3
  584.7 3.8 multiply_reduce_fusion.1
  588.5 8.1 %all-to-all-done.3.refs_0_ = bf16[4,36,3584]{2,1,0:T(8,128)(2,1)S(1)} async-done(((bf16[4,36,3584]{2,1,0:T(8,128)(2,1)}), bf16[4,36,3584]{2,1,0:T(8,128)(2,1)S(1)}, u32[]{:S(2)}, u32[]{:S(2)}) %all-to-all-start.3) | async-done | bytes 1032224 | tf_op jit(solution)/shard_map/all_to_all | solution.py:42
  602.7 3.5 collective-permute-done.66
  627.8 14.4 %collective-permute-done.67 = bf16[512,1152]{1,0:T(8,128)(2,1)} collective-permute-done((bf16[512,1152]{1,0:T(8,128)(2,1)}, bf16[512,1152]{1,0:T(8,128)(2,1)}, u32[]{:S(2)}, u32[]{:S(2)}) %collective-permute-start.67) | collective-permute-done | bytes 1179680 | tf_op jit(solution)/shard_map/ppermute | solution.py:47
  646.5 4.0 multiply_subtract_fusion
  (513 shorter events, 210.6 us)
Async XLA Ops:
  2.2 15.2 %collective-permute-start.3 = (bf16[224,1152]{1,0:T(8,128)(2,1)S(1)}, bf16[224,1152]{1,0:T(8,128)(2,1)}, u32[]{:S(2)}, u32[]{:S(2)}) collective-permute-start(bf16[224,1152]{1,0:T(8,128)(2,1)S(1)} %pad.13.refs_2_.refs_3_), channel_id=1, source_target_pairs={{0,8},{1,5},{2,10},{3,7},{8,16},{9,1},{10,18},{11,3},{16,24},{17,9... | collective-permute-start | bytes 1548296 | tf_op jit(solution)/shard_map/ppermute | solution.py:113
  15.7 28.8 %collective-permute-start.1 = (bf16[512,1152]{1,0:T(8,128)(2,1)}, bf16[512,1152]{1,0:T(8,128)(2,1)}, u32[]{:S(2)}, u32[]{:S(2)}) collective-permute-start(bf16[512,1152]{1,0:T(8,128)(2,1)} %bitcast.2.refs_4_), channel_id=1, source_target_pairs={{0,2},{1,3},{2,0},{3,1},{4,6},{5,7},{6,4},{7,5},{8,10},{9,11},{10,... | collective-permute-start | bytes 3538952 | tf_op jit(solution)/shard_map/ppermute | solution.py:47
  44.5 23.7 %collective-permute-start.9 = (bf16[512,1152]{1,0:T(8,128)(2,1)}, bf16[512,1152]{1,0:T(8,128)(2,1)}, u32[]{:S(2)}, u32[]{:S(2)}) collective-permute-start(bf16[512,1152]{1,0:T(8,128)(2,1)} %collective-permute-done.1), channel_id=1, source_target_pairs={{0,1},{1,0},{2,3},{3,2},{4,5},{5,4},{6,7},{7,6},{8,9},{9,8},{10,11... | collective-permute-start | bytes 3538952 | tf_op jit(solution)/shard_map/ppermute | solution.py:47
  44.7 38.2 %collective-permute-start = (bf16[512,1152]{1,0:T(8,128)(2,1)}, bf16[512,1152]{1,0:T(8,128)(2,1)}, u32[]{:S(2)}, u32[]{:S(2)}) collective-permute-start(bf16[512,1152]{1,0:T(8,128)(2,1)} %bitcast.2.refs_4_), channel_id=1, source_target_pairs={{0,1},{1,0},{2,3},{3,2},{4,5},{5,4},{6,7},{7,6},{8,9},{9,8},{10,11... | collective-permute-start | bytes 3538952 | tf_op jit(solution)/shard_map/ppermute | solution.py:47
  45.0 20.3 %all-to-all-start.1 = ((bf16[4,36,3584]{2,1,0:T(8,128)(2,1)}), bf16[4,36,3584]{2,1,0:T(8,128)(2,1)}, u32[]{:S(2)}, u32[]{:S(2)}) async-start(bf16[4,36,3584]{2,1,0:T(8,128)(2,1)} %shard_map.400), calls=%async_computation.1 | async-start | bytes 2293760 | tf_op jit(solution)/shard_map/all_to_all | solution.py:42
  51.3 15.4 %collective-permute-start.11 = (bf16[208,768]{1,0:T(8,128)(2,1)S(1)}, bf16[208,768]{1,0:T(8,128)(2,1)S(1)}, u32[]{:S(2)}, u32[]{:S(2)}) collective-permute-start(bf16[208,768]{1,0:T(8,128)(2,1)S(1)} %collective-permute-done.8.refs_5_.refs_12_.refs_11_), channel_id=1, source_target_pairs={{0,4},{1,9},{2,6},{3,11},{8,0},{9,17},{10,2},{11,19},{16,8},{17,25... | collective-permute-start | bytes 958472 | tf_op jit(solution)/shard_map/ppermute | solution.py:113
  68.1 38.0 %collective-permute-start.13 = (bf16[144,3584]{1,0:T(8,128)(2,1)S(1)}, bf16[144,3584]{1,0:T(8,128)(2,1)S(1)}, u32[]{:S(2)}, u32[]{:S(2)}) collective-permute-start(bf16[144,3584]{1,0:T(8,128)(2,1)S(1)} %reshape.108.refs_2_.refs_11_), channel_id=1, source_target_pairs={{0,8},{1,5},{2,10},{3,7},{8,16},{9,1},{10,18},{11,3},{16,24},{17,9... | collective-permute-start | bytes 3096584 | tf_op jit(solution)/shard_map/ppermute | solution.py:113
  69.6 36.5 %collective-permute-start.14 = (bf16[144,3584]{1,0:T(8,128)(2,1)S(1)}, bf16[144,3584]{1,0:T(8,128)(2,1)S(1)}, u32[]{:S(2)}, u32[]{:S(2)}) collective-permute-start(bf16[144,3584]{1,0:T(8,128)(2,1)S(1)} %reshape.108.refs_2_.refs_11_), channel_id=1, source_target_pairs={{0,4},{1,9},{2,6},{3,11},{8,0},{9,17},{10,2},{11,19},{16,8},{17,25... | collective-permute-start | bytes 3096584 | tf_op jit(solution)/shard_map/ppermute | solution.py:113
  81.5 26.9 %collective-permute-start.15 = (bf16[256,1152]{1,0:T(8,128)(2,1)}, bf16[256,1152]{1,0:T(8,128)(2,1)}, u32[]{:S(2)}, u32[]{:S(2)}) collective-permute-start(bf16[256,1152]{1,0:T(8,128)(2,1)} %get-tuple-element.129.refs_5_.refs_3_), channel_id=1, source_target_pairs={{0,2},{1,3},{2,0},{3,1},{4,6},{5,7},{6,4},{7,5},{8,10},{9,11},{10,... | collective-permute-start | bytes 1769480 | tf_op jit(solution)/shard_map/ppermute | solution.py:47
  82.8 25.7 %collective-permute-start.16 = (bf16[256,1152]{1,0:T(8,128)(2,1)}, bf16[256,1152]{1,0:T(8,128)(2,1)}, u32[]{:S(2)}, u32[]{:S(2)}) collective-permute-start(bf16[256,1152]{1,0:T(8,128)(2,1)} %get-tuple-element.129.refs_5_.refs_3_), channel_id=1, source_target_pairs={{0,1},{1,0},{2,3},{3,2},{4,5},{5,4},{6,7},{7,6},{8,9},{9,8},{10,11... | collective-permute-start | bytes 1769480 | tf_op jit(solution)/shard_map/ppermute | solution.py:47
  106.2 14.1 %collective-permute-start.18 = (bf16[224,1152]{1,0:T(8,128)(2,1)}, bf16[224,1152]{1,0:T(8,128)(2,1)}, u32[]{:S(2)}, u32[]{:S(2)}) collective-permute-start(bf16[224,1152]{1,0:T(8,128)(2,1)} %collective-permute-done.4.refs_4_.refs_5_), channel_id=1, source_target_pairs={{0,4},{1,9},{2,6},{3,11},{8,0},{9,17},{10,2},{11,19},{16,8},{17,25... | collective-permute-start | bytes 1548296 | tf_op jit(solution)/shard_map/ppermute | solution.py:113
  120.8 26.5 %collective-permute-start.20 = (bf16[2048,256]{1,0:T(8,128)(2,1)S(1)}, bf16[2048,256]{1,0:T(8,128)(2,1)S(1)}, u32[]{:S(2)}, u32[]{:S(2)}) collective-permute-start(bf16[2048,256]{1,0:T(8,128)(2,1)S(1)} %get-tuple-element.136.refs_1_), channel_id=1, source_target_pairs={{0,2},{1,3},{2,0},{3,1},{4,6},{5,7},{6,4},{7,5},{8,10},{9,11},{10,... | collective-permute-start | bytes 3145736 | tf_op jit(solution)/shard_map/ppermute | solution.py:47
  121.8 25.4 %collective-permute-start.22 = (bf16[144,3584]{1,0:T(8,128)(2,1)S(1)}, bf16[144,3584]{1,0:T(8,128)(2,1)S(1)}, u32[]{:S(2)}, u32[]{:S(2)}) collective-permute-start(bf16[144,3584]{1,0:T(8,128)(2,1)S(1)} %collective-permute-done.14.refs_4_.refs_13_), channel_id=1, source_target_pairs={{0,4},{1,9},{2,6},{3,11},{8,0},{9,17},{10,2},{11,19},{16,8},{17,25... | collective-permute-start | bytes 3096584 | tf_op jit(solution)/shard_map/ppermute | solution.py:113
  123.6 23.6 %collective-permute-start.21 = (bf16[144,3584]{1,0:T(8,128)(2,1)S(1)}, bf16[144,3584]{1,0:T(8,128)(2,1)S(1)}, u32[]{:S(2)}, u32[]{:S(2)}) collective-permute-start(bf16[144,3584]{1,0:T(8,128)(2,1)S(1)} %collective-permute-done.13.refs_3_.refs_12_), channel_id=1, source_target_pairs={{0,8},{1,5},{2,10},{3,7},{8,16},{9,1},{10,18},{11,3},{16,24},{17,9... | collective-permute-start | bytes 3096584 | tf_op jit(solution)/shard_map/ppermute | solution.py:113
  123.8 27.2 %collective-permute-start.19 = (bf16[2048,256]{1,0:T(8,128)(2,1)S(1)}, bf16[2048,256]{1,0:T(8,128)(2,1)S(1)}, u32[]{:S(2)}, u32[]{:S(2)}) collective-permute-start(bf16[2048,256]{1,0:T(8,128)(2,1)S(1)} %get-tuple-element.136.refs_1_), channel_id=1, source_target_pairs={{0,1},{1,0},{2,3},{3,2},{4,5},{5,4},{6,7},{7,6},{8,9},{9,8},{10,11... | collective-permute-start | bytes 3145736 | tf_op jit(solution)/shard_map/ppermute | solution.py:47
  147.4 24.7 %collective-permute-start.25 = (bf16[144,3584]{1,0:T(8,128)(2,1)S(1)}, bf16[144,3584]{1,0:T(8,128)(2,1)S(1)}, u32[]{:S(2)}, u32[]{:S(2)}) collective-permute-start(bf16[144,3584]{1,0:T(8,128)(2,1)S(1)} %collective-permute-done.21.refs_5_.refs_14_), channel_id=1, source_target_pairs={{0,8},{1,5},{2,10},{3,7},{8,16},{9,1},{10,18},{11,3},{16,24},{17,9... | collective-permute-start | bytes 3096584 | tf_op jit(solution)/shard_map/ppermute | solution.py:113
  148.6 49.3 %collective-permute-start.26 = (bf16[144,3584]{1,0:T(8,128)(2,1)S(1)}, bf16[144,3584]{1,0:T(8,128)(2,1)S(1)}, u32[]{:S(2)}, u32[]{:S(2)}) collective-permute-start(bf16[144,3584]{1,0:T(8,128)(2,1)S(1)} %collective-permute-done.22.refs_6_.refs_15_), channel_id=1, source_target_pairs={{0,4},{1,9},{2,6},{3,11},{8,0},{9,17},{10,2},{11,19},{16,8},{17,25... | collective-permute-start | bytes 3096584 | tf_op jit(solution)/shard_map/ppermute | solution.py:113
  172.2 25.7 %collective-permute-start.27 = (bf16[144,3584]{1,0:T(8,128)(2,1)S(1)}, bf16[144,3584]{1,0:T(8,128)(2,1)S(1)}, u32[]{:S(2)}, u32[]{:S(2)}) collective-permute-start(bf16[144,3584]{1,0:T(8,128)(2,1)S(1)} %collective-permute-done.25.refs_7_.refs_16_), channel_id=1, source_target_pairs={{0,8},{1,5},{2,10},{3,7},{8,16},{9,1},{10,18},{11,3},{16,24},{17,9... | collective-permute-start | bytes 3096584 | tf_op jit(solution)/shard_map/ppermute | solution.py:113
  173.4 24.2 %collective-permute-start.28 = (bf16[224,1152]{1,0:T(8,128)(2,1)}, bf16[224,1152]{1,0:T(8,128)(2,1)S(1)}, u32[]{:S(2)}, u32[]{:S(2)}) collective-permute-start(bf16[224,1152]{1,0:T(8,128)(2,1)} %collective-permute-done.17.refs_5_.refs_6_), channel_id=1, source_target_pairs={{0,8},{1,5},{2,10},{3,7},{8,16},{9,1},{10,18},{11,3},{16,24},{17,9... | collective-permute-start | bytes 1548296 | tf_op jit(solution)/shard_map/ppermute | solution.py:113
  175.9 40.8 %collective-permute-start.29 = (bf16[224,1152]{1,0:T(8,128)(2,1)}, bf16[224,1152]{1,0:T(8,128)(2,1)S(1)}, u32[]{:S(2)}, u32[]{:S(2)}) collective-permute-start(bf16[224,1152]{1,0:T(8,128)(2,1)} %collective-permute-done.18.refs_6_.refs_7_), channel_id=1, source_target_pairs={{0,4},{1,9},{2,6},{3,11},{8,0},{9,17},{10,2},{11,19},{16,8},{17,25... | collective-permute-start | bytes 1548296 | tf_op jit(solution)/shard_map/ppermute | solution.py:113
  197.6 19.1 %collective-permute-start.30 = (bf16[224,1152]{1,0:T(8,128)(2,1)S(1)}, bf16[224,1152]{1,0:T(8,128)(2,1)S(1)}, u32[]{:S(2)}, u32[]{:S(2)}) collective-permute-start(bf16[224,1152]{1,0:T(8,128)(2,1)S(1)} %collective-permute-done.28.refs_7_.refs_8_), channel_id=1, source_target_pairs={{0,8},{1,5},{2,10},{3,7},{8,16},{9,1},{10,18},{11,3},{16,24},{17,9... | collective-permute-start | bytes 1548296 | tf_op jit(solution)/shard_map/ppermute | solution.py:113
  230.9 28.1 %collective-permute-start.32 = (bf16[512,1152]{1,0:T(8,128)(2,1)S(1)}, bf16[512,1152]{1,0:T(8,128)(2,1)S(1)}, u32[]{:S(2)}, u32[]{:S(2)}) collective-permute-start(bf16[512,1152]{1,0:T(8,128)(2,1)S(1)} %add.264), channel_id=1, source_target_pairs={{0,2},{1,3},{2,0},{3,1},{4,6},{5,7},{6,4},{7,5},{8,10},{9,11},{10,... | collective-permute-start | bytes 3538952 | tf_op jit(solution)/shard_map/ppermute | solution.py:47
  280.1 28.3 %collective-permute-start.34 = (bf16[512,1152]{1,0:T(8,128)(2,1)S(1)}, bf16[512,1152]{1,0:T(8,128)(2,1)S(1)}, u32[]{:S(2)}, u32[]{:S(2)}) collective-permute-start(bf16[512,1152]{1,0:T(8,128)(2,1)S(1)} %get-tuple-element.161), channel_id=1, source_target_pairs={{0,2},{1,3},{2,0},{3,1},{4,6},{5,7},{6,4},{7,5},{8,10},{9,11},{10,... | collective-permute-start | bytes 3538952 | tf_op jit(solution)/shard_map/ppermute | solution.py:47
  352.3 27.9 %collective-permute-start.37 = (bf16[144,3584]{1,0:T(8,128)(2,1)S(1)}, bf16[144,3584]{1,0:T(8,128)(2,1)S(1)}, u32[]{:S(2)}, u32[]{:S(2)}) collective-permute-start(bf16[144,3584]{1,0:T(8,128)(2,1)S(1)} %get-tuple-element.238), channel_id=1, source_target_pairs={{0,8},{1,5},{2,10},{3,7},{8,16},{9,1},{10,18},{11,3},{16,24},{17,9... | collective-permute-start | bytes 3096584 | tf_op jit(solution)/shard_map/ppermute | solution.py:113
  384.2 50.4 %collective-permute-start.41 = (bf16[144,3584]{1,0:T(8,128)(2,1)S(1)}, bf16[144,3584]{1,0:T(8,128)(2,1)}, u32[]{:S(2)}, u32[]{:S(2)}) collective-permute-start(bf16[144,3584]{1,0:T(8,128)(2,1)S(1)} %get-tuple-element.237), channel_id=1, source_target_pairs={{0,4},{1,9},{2,6},{3,11},{8,0},{9,17},{10,2},{11,19},{16,8},{17,25... | collective-permute-start | bytes 3096584 | tf_op jit(solution)/shard_map/ppermute | solution.py:113
  387.3 47.2 %collective-permute-start.40 = (bf16[144,3584]{1,0:T(8,128)(2,1)}, bf16[144,3584]{1,0:T(8,128)(2,1)S(1)}, u32[]{:S(2)}, u32[]{:S(2)}) collective-permute-start(bf16[144,3584]{1,0:T(8,128)(2,1)} %dynamic-slice_add_fusion.4), channel_id=1, source_target_pairs={{0,8},{1,5},{2,10},{3,7},{8,16},{9,1},{10,18},{11,3},{16,24},{17,9... | collective-permute-start | bytes 3096584 | tf_op jit(solution)/shard_map/ppermute | solution.py:113
  389.0 19.9 %collective-permute-start.39 = (bf16[1024,256]{1,0:T(8,128)(2,1)S(1)}, bf16[1024,256]{1,0:T(8,128)(2,1)S(1)}, u32[]{:S(2)}, u32[]{:S(2)}) collective-permute-start(bf16[1024,256]{1,0:T(8,128)(2,1)S(1)} %fusion.3), channel_id=1, source_target_pairs={{0,2},{1,3},{2,0},{3,1},{4,6},{5,7},{6,4},{7,5},{8,10},{9,11},{10,... | collective-permute-start | bytes 1572872 | tf_op jit(solution)/shard_map/ppermute | solution.py:47
  407.5 27.1 %collective-permute-start.42 = (bf16[224,1152]{1,0:T(8,128)(2,1)S(1)}, bf16[224,1152]{1,0:T(8,128)(2,1)S(1)}, u32[]{:S(2)}, u32[]{:S(2)}) collective-permute-start(bf16[224,1152]{1,0:T(8,128)(2,1)S(1)} %get-tuple-element.244), channel_id=1, source_target_pairs={{0,8},{1,5},{2,10},{3,7},{8,16},{9,1},{10,18},{11,3},{16,24},{17,9... | collective-permute-start | bytes 1548296 | tf_op jit(solution)/shard_map/ppermute | solution.py:113
  447.6 36.3 %collective-permute-start.51 = (bf16[224,1152]{1,0:T(8,128)(2,1)}, bf16[224,1152]{1,0:T(8,128)(2,1)}, u32[]{:S(2)}, u32[]{:S(2)}) collective-permute-start(bf16[224,1152]{1,0:T(8,128)(2,1)} %get-tuple-element.243), channel_id=1, source_target_pairs={{0,4},{1,9},{2,6},{3,11},{8,0},{9,17},{10,2},{11,19},{16,8},{17,25... | collective-permute-start | bytes 1548296 | tf_op jit(solution)/shard_map/ppermute | solution.py:113
  448.2 14.5 %collective-permute-start.44 = (bf16[1024,256]{1,0:T(8,128)(2,1)S(1)}, bf16[1024,256]{1,0:T(8,128)(2,1)S(1)}, u32[]{:S(2)}, u32[]{:S(2)}) collective-permute-start(bf16[1024,256]{1,0:T(8,128)(2,1)S(1)} %fusion.2), channel_id=1, source_target_pairs={{0,2},{1,3},{2,0},{3,1},{4,6},{5,7},{6,4},{7,5},{8,10},{9,11},{10,... | collective-permute-start | bytes 1572872 | tf_op jit(solution)/shard_map/ppermute | solution.py:47
  451.9 31.9 %collective-permute-start.50 = (bf16[224,1152]{1,0:T(8,128)(2,1)}, bf16[224,1152]{1,0:T(8,128)(2,1)}, u32[]{:S(2)}, u32[]{:S(2)}) collective-permute-start(bf16[224,1152]{1,0:T(8,128)(2,1)} %dynamic-slice_add_fusion.9), channel_id=1, source_target_pairs={{0,8},{1,5},{2,10},{3,7},{8,16},{9,1},{10,18},{11,3},{16,24},{17,9... | collective-permute-start | bytes 1548296 | tf_op jit(solution)/shard_map/ppermute | solution.py:113
  453.4 30.4 %collective-permute-start.48 = (bf16[144,3584]{1,0:T(8,128)(2,1)}, bf16[144,3584]{1,0:T(8,128)(2,1)}, u32[]{:S(2)}, u32[]{:S(2)}) collective-permute-start(bf16[144,3584]{1,0:T(8,128)(2,1)} %get-tuple-element.236), channel_id=1, source_target_pairs={{0,8},{1,5},{2,10},{3,7},{8,16},{9,1},{10,18},{11,3},{16,24},{17,9... | collective-permute-start | bytes 3096584 | tf_op jit(solution)/shard_map/ppermute | solution.py:113
  455.0 28.9 %collective-permute-start.49 = (bf16[144,3584]{1,0:T(8,128)(2,1)S(1)}, bf16[144,3584]{1,0:T(8,128)(2,1)S(1)}, u32[]{:S(2)}, u32[]{:S(2)}) collective-permute-start(bf16[144,3584]{1,0:T(8,128)(2,1)S(1)} %get-tuple-element.235), channel_id=1, source_target_pairs={{0,4},{1,9},{2,6},{3,11},{8,0},{9,17},{10,2},{11,19},{16,8},{17,25... | collective-permute-start | bytes 3096584 | tf_op jit(solution)/shard_map/ppermute | solution.py:113
  462.7 18.4 %collective-permute-start.46 = (bf16[256,1152]{1,0:T(8,128)(2,1)}, bf16[256,1152]{1,0:T(8,128)(2,1)S(1)}, u32[]{:S(2)}, u32[]{:S(2)}) collective-permute-start(bf16[256,1152]{1,0:T(8,128)(2,1)} %slice_add_fusion.1), channel_id=1, source_target_pairs={{0,2},{1,3},{2,0},{3,1},{4,6},{5,7},{6,4},{7,5},{8,10},{9,11},{10,... | collective-permute-start | bytes 1769480 | tf_op jit(solution)/shard_map/ppermute | solution.py:47
  485.1 38.3 %collective-permute-start.58 = (bf16[192,768]{1,0:T(8,128)(2,1)}, bf16[192,768]{1,0:T(8,128)(2,1)}, u32[]{:S(2)}, u32[]{:S(2)}) collective-permute-start(bf16[192,768]{1,0:T(8,128)(2,1)} %get-tuple-element.249), channel_id=1, source_target_pairs={{0,4},{1,9},{2,6},{3,11},{8,0},{9,17},{10,2},{11,19},{16,8},{17,25... | collective-permute-start | bytes 884744 | tf_op jit(solution)/shard_map/ppermute | solution.py:113
  496.7 27.6 %collective-permute-start.55 = (bf16[192,768]{1,0:T(8,128)(2,1)}, bf16[192,768]{1,0:T(8,128)(2,1)}, u32[]{:S(2)}, u32[]{:S(2)}) collective-permute-start(bf16[192,768]{1,0:T(8,128)(2,1)} %dynamic-slice_add_fusion.14), channel_id=1, source_target_pairs={{0,8},{1,5},{2,10},{3,7},{8,16},{9,1},{10,18},{11,3},{16,24},{17,9... | collective-permute-start | bytes 884744 | tf_op jit(solution)/shard_map/ppermute | solution.py:113
  497.8 29.1 %collective-permute-start.64 = (bf16[224,1152]{1,0:T(8,128)(2,1)}, bf16[224,1152]{1,0:T(8,128)(2,1)}, u32[]{:S(2)}, u32[]{:S(2)}) collective-permute-start(bf16[224,1152]{1,0:T(8,128)(2,1)} %get-tuple-element.241), channel_id=1, source_target_pairs={{0,4},{1,9},{2,6},{3,11},{8,0},{9,17},{10,2},{11,19},{16,8},{17,25... | collective-permute-start | bytes 1548296 | tf_op jit(solution)/shard_map/ppermute | solution.py:113
  498.7 28.2 %collective-permute-start.62 = (bf16[224,1152]{1,0:T(8,128)(2,1)}, bf16[224,1152]{1,0:T(8,128)(2,1)}, u32[]{:S(2)}, u32[]{:S(2)}) collective-permute-start(bf16[224,1152]{1,0:T(8,128)(2,1)} %get-tuple-element.242), channel_id=1, source_target_pairs={{0,8},{1,5},{2,10},{3,7},{8,16},{9,1},{10,18},{11,3},{16,24},{17,9... | collective-permute-start | bytes 1548296 | tf_op jit(solution)/shard_map/ppermute | solution.py:113
  499.9 48.9 %collective-permute-start.52 = (bf16[144,3584]{1,0:T(8,128)(2,1)}, bf16[144,3584]{1,0:T(8,128)(2,1)S(1)}, u32[]{:S(2)}, u32[]{:S(2)}) collective-permute-start(bf16[144,3584]{1,0:T(8,128)(2,1)} %get-tuple-element.234), channel_id=1, source_target_pairs={{0,8},{1,5},{2,10},{3,7},{8,16},{9,1},{10,18},{11,3},{16,24},{17,9... | collective-permute-start | bytes 3096584 | tf_op jit(solution)/shard_map/ppermute | solution.py:113
  523.4 26.6 %collective-permute-start.53 = (bf16[144,3584]{1,0:T(8,128)(2,1)S(1)}, bf16[144,3584]{1,0:T(8,128)(2,1)S(1)}, u32[]{:S(2)}, u32[]{:S(2)}) collective-permute-start(bf16[144,3584]{1,0:T(8,128)(2,1)S(1)} %copy-done.108), channel_id=1, source_target_pairs={{0,4},{1,9},{2,6},{3,11},{8,0},{9,17},{10,2},{11,19},{16,8},{17,25... | collective-permute-start | bytes 3096584 | tf_op jit(solution)/shard_map/ppermute | solution.py:113
  528.1 16.3 %collective-permute-start.59 = (bf16[192,768]{1,0:T(8,128)(2,1)S(1)}, bf16[192,768]{1,0:T(8,128)(2,1)S(1)}, u32[]{:S(2)}, u32[]{:S(2)}) collective-permute-start(bf16[192,768]{1,0:T(8,128)(2,1)S(1)} %get-tuple-element.248), channel_id=1, source_target_pairs={{0,4},{1,9},{2,6},{3,11},{8,0},{9,17},{10,2},{11,19},{16,8},{17,25... | collective-permute-start | bytes 884744 | tf_op jit(solution)/shard_map/ppermute | solution.py:113
  545.9 38.7 %collective-permute-start.63 = (bf16[224,1152]{1,0:T(8,128)(2,1)S(1)}, bf16[224,1152]{1,0:T(8,128)(2,1)}, u32[]{:S(2)}, u32[]{:S(2)}) collective-permute-start(bf16[224,1152]{1,0:T(8,128)(2,1)S(1)} %get-tuple-element.204), channel_id=1, source_target_pairs={{0,8},{1,5},{2,10},{3,7},{8,16},{9,1},{10,18},{11,3},{16,24},{17,9... | collective-permute-start | bytes 1548296 | tf_op jit(solution)/shard_map/ppermute | solution.py:113
  546.7 18.9 %collective-permute-start.57 = (bf16[192,768]{1,0:T(8,128)(2,1)S(1)}, bf16[192,768]{1,0:T(8,128)(2,1)S(1)}, u32[]{:S(2)}, u32[]{:S(2)}) collective-permute-start(bf16[192,768]{1,0:T(8,128)(2,1)S(1)} %get-tuple-element.245), channel_id=1, source_target_pairs={{0,8},{1,5},{2,10},{3,7},{8,16},{9,1},{10,18},{11,3},{16,24},{17,9... | collective-permute-start | bytes 884744 | tf_op jit(solution)/shard_map/ppermute | solution.py:113
  547.9 17.7 %collective-permute-start.60 = (bf16[192,768]{1,0:T(8,128)(2,1)S(1)}, bf16[192,768]{1,0:T(8,128)(2,1)S(1)}, u32[]{:S(2)}, u32[]{:S(2)}) collective-permute-start(bf16[192,768]{1,0:T(8,128)(2,1)S(1)} %get-tuple-element.246), channel_id=1, source_target_pairs={{0,4},{1,9},{2,6},{3,11},{8,0},{9,17},{10,2},{11,19},{16,8},{17,25... | collective-permute-start | bytes 884744 | tf_op jit(solution)/shard_map/ppermute | solution.py:113
  548.7 35.9 %collective-permute-start.65 = (bf16[224,1152]{1,0:T(8,128)(2,1)S(1)}, bf16[224,1152]{1,0:T(8,128)(2,1)}, u32[]{:S(2)}, u32[]{:S(2)}) collective-permute-start(bf16[224,1152]{1,0:T(8,128)(2,1)S(1)} %get-tuple-element.207), channel_id=1, source_target_pairs={{0,4},{1,9},{2,6},{3,11},{8,0},{9,17},{10,2},{11,19},{16,8},{17,25... | collective-permute-start | bytes 1548296 | tf_op jit(solution)/shard_map/ppermute | solution.py:113
  550.0 49.4 %collective-permute-start.54 = (bf16[1024,1152]{1,0:T(8,128)(2,1)}, bf16[1024,1152]{1,0:T(8,128)(2,1)}, u32[]{:S(2)}, u32[]{:S(2)}) collective-permute-start(bf16[1024,1152]{1,0:T(8,128)(2,1)} %get-tuple-element.193), channel_id=1, source_target_pairs={{0,1},{1,0},{2,3},{3,2},{4,5},{5,4},{6,7},{7,6},{8,9},{9,8},{10,11... | collective-permute-start | bytes 7077896 | tf_op jit(solution)/shard_map/ppermute | solution.py:47
  577.4 19.2 %all-to-all-start.3 = ((bf16[4,36,3584]{2,1,0:T(8,128)(2,1)}), bf16[4,36,3584]{2,1,0:T(8,128)(2,1)S(1)}, u32[]{:S(2)}, u32[]{:S(2)}) async-start(bf16[4,36,3584]{2,1,0:T(8,128)(2,1)} %reshape.116), calls=%async_computation.3 | async-start | bytes 2293760 | tf_op jit(solution)/shard_map/all_to_all | solution.py:42
  616.4 25.8 %collective-permute-start.67 = (bf16[512,1152]{1,0:T(8,128)(2,1)}, bf16[512,1152]{1,0:T(8,128)(2,1)}, u32[]{:S(2)}, u32[]{:S(2)}) collective-permute-start(bf16[512,1152]{1,0:T(8,128)(2,1)} %slice_add_fusion), channel_id=1, source_target_pairs={{0,2},{1,3},{2,0},{3,1},{4,6},{5,7},{6,4},{7,5},{8,10},{9,11},{10,... | collective-permute-start | bytes 3538952 | tf_op jit(solution)/shard_map/ppermute | solution.py:47
  (167 other events, 1938.0 us)

commit v4 on v3

--- a/solution.py
+++ b/solution.py
@@ -1086,11 +1086,11 @@
         pos_map,
         places,
     )
-    held_in = in_sum.absorb(input_odd)
-    in_sum.send()
     gate_came = list(gate_sum.came.values())
+    in_sum.absorb(input_odd)
+    in_sum.send(*gate_came)
     gate_sum.absorb(input_odd)
-    down_sum.absorb(*held_in)
+    down_sum.absorb(input_odd)
     gate_up_own = gate_sum.finish().astype(low)
     gate_up_own = exchange(gate_up_own.reshape(ctx, in_rows, -1), "ctx")
     near = swap(tie(input_odd, *gate_came), 1)
@@ -1099,11 +1099,10 @@
     while in_sum.hop > 1:
         in_sum.absorb()
         in_sum.send()
-    held_in = in_sum.tokens()
 
     in_own = in_sum.absorb()[0].astype(low)
-    down_sum.send(*held_in)
-    down_sum.absorb(in_own)
+    down_sum.send(in_own)
+    down_sum.absorb()
     down_own = down_sum.finish()[:ff_rows]
     gate_up_own = unpack_columns(gate_up_own, dp, ctx, ff_rows)
     out_own = in_own[own_rows:]

time: 666 us -> 654 us (0.982)
  local copies, waits for them, and re-layouts: 68.9 us -> 61.4 us
  waiting for transfers between devices: 177 us -> 170 us
    unnamed x280 -> x284, local copies, waits for them, and re-layouts: 53 us -> 46.3 us
  transfers between devices with their start and end apart: 76 -> 76, of which waited for: 33 -> 38; matrix products, arithmetic and copies ran while one was open for 14% -> 13% of each run, Pallas kernels for 24% -> 25%
where the time goes in v4:
time: 654 us; the launch traced here: 644 us
  Pallas kernels  192 us (29%)
  waiting for transfers between devices  170 us (26%)
  starting transfers between devices  85.8 us (13%)
  other arithmetic  80.7 us (12%)
  local copies, waits for them, and re-layouts  61.4 us (9%)
  matrix products  46.3 us (7%)
  between operations  8.09 us (1%)
    pallas_call x17, Pallas kernels, call(): pl.pallas_call(kernel, out_shape=out_shape, grid_spec=pltpu.PrefetchScala...  192 us
    ppermute x42, waiting for transfers between devices, send(): return lax.ppermute(value, ('dp', 'ctx'), pairs)  91.9 us
    ppermute x25, waiting for transfers between devices, swap(): return lax.ppermute(value, 'ctx', [(i, i ^ bit) for i in range(count)])  54.5 us
    ppermute x42, starting transfers between devices, send(): return lax.ppermute(value, ('dp', 'ctx'), pairs)  50.7 us
    dot_general x7, matrix products, mm_tn(): lax.dot_general(a, b, (((0,), (0,)), ((), ())), preferred_element_type=F32)  46.3 us
    unnamed x284, local copies, waits for them, and re-layouts  46.3 us
    add x13, other arithmetic, add_low(): return a + b  34.9 us
    all_to_all x4, waiting for transfers between devices, exchange(): return lax.all_to_all(parts, axis, split_axis=0, concat_axis=0, tiled=True)  18.2 us
  transfers between devices with their start and end apart: 76, of which 38 were waited for; matrix products, arithmetic and copies ran while one was open for 13% of the time, Pallas kernels for 25%

profile of v4, /device:TPU:0, one launch (start us, length us, event | category | flops | bytes accessed | tf_op | source)
XLA Modules:
  0.0 644.4 jit_solution(2941576978946852832)
XLA Ops:
  12.0 3.6 all-to-all-done
  17.9 3.9 collective-permute-start.5
  22.5 5.5 multiply_sine_fusion
  32.6 4.2 collective-permute-done.6.refs_4_.refs_11_.refs_10_
  36.9 3.9 collective-permute-done.8.refs_5_.refs_12_.refs_11_
  40.8 3.6 collective-permute-done.1
  45.0 4.3 all-to-all-start.1
  51.8 7.3 %collective-permute-done.10.refs_6_.refs_13_.refs_12_ = bf16[208,768]{1,0:T(8,128)(2,1)S(1)} collective-permute-done((bf16[208,768]{1,0:T(8,128)(2,1)S(1)}, bf16[208,768]{1,0:T(8,128)(2,1)S(1)}, u32[]{:S(2)}, u32[]{:S(2)}) %collective-permute-start.10) | collective-permute-done | bytes 319520 | tf_op jit(solution)/shard_map/ppermute | solution.py:113
  61.6 3.7 all-to-all-done.1
  82.8 5.6 pad_maximum_fusion.refs_2_.refs_3_.refs_9_.refs_8_.refs_4_
  88.5 10.5 %shard_map.402 = (bf16[2048,256]{1,0:T(8,128)(2,1)S(1)}, bf16[2048,256]{1,0:T(8,128)(2,1)S(1)}, bf16[2048,256]{1,0:T(8,128)(2,1)S(1)}, f32[2048,512]{1,0:T(8,128)S(1)}, bf16[2048,1152]{1,0:T(8,128)(2,1)S(1)}) custom-call(s32[8]{0:T(128)S(1)} %fusion.21.refs_0_, s32[8]{0:T(128)S(1)} %fusion.24.refs_0_.refs_1_, ...), custom_call_target="tpu_custom_call" | custom-call | flops 226492416 | bytes 1634720 | tf_op jit(solution)/shard_map/pallas_call | solution.py:223
  112.1 5.6 shard_map.403
  123.7 23.4 %collective-permute-done.22.refs_6_.refs_15_ = bf16[144,3584]{1,0:T(8,128)(2,1)S(1)} collective-permute-done((bf16[144,3584]{1,0:T(8,128)(2,1)S(1)}, bf16[144,3584]{1,0:T(8,128)(2,1)S(1)}, u32[]{:S(2)}, u32[]{:S(2)}) %collective-permute-start.22) | collective-permute-done | bytes 1032224 | tf_op jit(solution)/shard_map/ppermute | solution.py:113
  153.9 11.7 %shard_map.404 = (f32[2048,1152]{1,0:T(8,128)}, bf16[2048,1152]{1,0:T(8,128)(2,1)S(1)}) custom-call(s32[8]{0:T(128)S(1)} %fusion.20.refs_0_, bf16[2048,256]{1,0:T(8,128)(2,1)S(1)} %get-tuple-element.136.refs_1_, bf16[2048,256]{1,0:T(8,128)(2,1)S(1)} %collective-permute-done.19.refs_2_, bf16[2048,256]{1,0:T(8,128)(2,1)S(1)} %collective-permute-done.20.refs_3_, ...), custom_call_target="tpu_custom_call" | custom-call | flops 301989888 | bytes 1590400 | tf_op jit(solution)/shard_map/pallas_call | solution.py:223
  165.6 6.5 %collective-permute-done.25.refs_7_.refs_16_ = bf16[144,3584]{1,0:T(8,128)(2,1)S(1)} collective-permute-done((bf16[144,3584]{1,0:T(8,128)(2,1)S(1)}, bf16[144,3584]{1,0:T(8,128)(2,1)S(1)}, u32[]{:S(2)}, u32[]{:S(2)}) %collective-permute-start.25) | collective-permute-done | bytes 1032224 | tf_op jit(solution)/shard_map/ppermute | solution.py:113
  175.8 21.7 %collective-permute-done.28.refs_7_.refs_8_ = bf16[224,1152]{1,0:T(8,128)(2,1)S(1)} collective-permute-done((bf16[224,1152]{1,0:T(8,128)(2,1)}, bf16[224,1152]{1,0:T(8,128)(2,1)S(1)}, u32[]{:S(2)}, u32[]{:S(2)}) %collective-permute-start.28) | collective-permute-done | bytes 516128 | tf_op jit(solution)/shard_map/ppermute | solution.py:113
  197.8 18.7 %shard_map.405 = (bf16[2048,1792]{1,0:T(8,128)(2,1)}, bf16[2048,3584]{1,0:T(8,128)(2,1)}) custom-call(s32[8]{0:T(128)S(1)} %fusion.24.refs_0_.refs_1_, bf16[2048,1152]{1,0:T(8,128)(2,1)S(1)} %get-tuple-element.151.refs_1_, bf16[144,3584]{1,0:T(8,128)(2,1)S(1)} %reshape.108.refs_2_.refs_11_, bf16[144,3584]{1,0:T(8,128)(2,1)S(1)} %collective-permute-done.13.refs_3_.refs_12_, ...), custom_call_target="tpu_custom_call" | custom-call | flops 528482304 | bytes 2187264 | tf_op jit(solution)/shard_map/pallas_call | solution.py:223
  220.0 7.4 %shard_map.406 = (bf16[512,1152]{1,0:T(8,128)(2,1)S(1)}, bf16[512,1152]{1,0:T(8,128)(2,1)S(1)}) custom-call(s32[8]{0:T(128)S(1)} %fusion.24.refs_0_.refs_1_, bf16[2048,1792]{1,0:T(8,128)(2,1)S(1)} %copy-done.1, bf16[224,1152]{1,0:T(8,128)(2,1)S(1)} %copy-done.27, bf16[224,1152]{1,0:T(8,128)(2,1)} %collective-permute-done.3.refs_3_.refs_4_, ...), custom_call_target="tpu_custom_call" | custom-call | flops 264241152 | bytes 864256 | tf_op jit(solution)/shard_map/pallas_call | solution.py:223
  236.9 19.2 %shard_map.407 = (bf16[2048,1792]{1,0:T(8,128)(2,1)}, bf16[2048,3584]{1,0:T(8,128)(2,1)}) custom-call(s32[8]{0:T(128)S(1)} %fusion.24.refs_0_.refs_1_, bf16[2048,1152]{1,0:T(8,128)(2,1)S(1)} %get-tuple-element.151.refs_1_, bf16[144,3584]{1,0:T(8,128)(2,1)S(1)} %reshape.108.refs_2_.refs_11_, ...), custom_call_target="tpu_custom_call", output_to_operand_aliasing={{0}: (10, {}), {1}: (11, {})} | custom-call | flops 528482304 | bytes 2187264 | tf_op jit(solution)/shard_map/pallas_call | solution.py:223
  265.0 7.4 %shard_map.408 = (bf16[512,1152]{1,0:T(8,128)(2,1)S(1)}, bf16[512,1152]{1,0:T(8,128)(2,1)S(1)}) custom-call(s32[8]{0:T(128)S(1)} %fusion.24.refs_0_.refs_1_, bf16[2048,1792]{1,0:T(8,128)(2,1)S(1)} %copy-done.2, bf16[224,1152]{1,0:T(8,128)(2,1)S(1)} %copy-done.27, bf16[224,1152]{1,0:T(8,128)(2,1)} %collective-permute-done.3.refs_3_.refs_4_, ...), custom_call_target="tpu_custom_call" | custom-call | flops 264241152 | bytes 864256 | tf_op jit(solution)/shard_map/pallas_call | solution.py:223
  275.4 4.4 shard_map.409
  282.9 12.2 %shard_map.410.refs_11_ = bf16[2048,3584]{1,0:T(8,128)(2,1)} custom-call(s32[8]{0:T(128)S(1)} %fusion.24.refs_0_.refs_1_, bf16[1024,1152]{1,0:T(8,128)(2,1)S(1)} %pad_maximum_fusion.2.refs_1_, bf16[2048,3584]{1,0:T(8,128)(2,1)} %get-tuple-element.162.refs_2_, bf16[224,1152]{1,0:T(8,128)(2,1)S(1)} %copy-done.27, ...), custom_call_target="tpu_custom_call" | custom-call | flops 264241152 | bytes 2240512 | tf_op jit(solution)/shard_map/pallas_call | solution.py:223
  295.1 13.1 %collective-permute-done.34 = bf16[512,1152]{1,0:T(8,128)(2,1)S(1)} collective-permute-done((bf16[512,1152]{1,0:T(8,128)(2,1)S(1)}, bf16[512,1152]{1,0:T(8,128)(2,1)S(1)}, u32[]{:S(2)}, u32[]{:S(2)}) %collective-permute-start.34) | collective-permute-done | bytes 1179680 | tf_op jit(solution)/shard_map/ppermute | solution.py:47
  312.3 12.7 %shard_map.411.refs_2_ = bf16[2048,3584]{1,0:T(8,128)(2,1)} custom-call(s32[8]{0:T(128)S(1)} %fusion.24.refs_0_.refs_1_, bf16[1024,1152]{1,0:T(8,128)(2,1)S(1)} %pad_maximum_fusion.3.refs_1_, bf16[2048,3584]{1,0:T(8,128)(2,1)} %get-tuple-element.162.refs_2_, bf16[224,1152]{1,0:T(8,128)(2,1)S(1)} %copy-done.27, ...), custom_call_target="tpu_custom_call", output_to_operand_aliasing={{}: (11, {})} | custom-call | flops 264241152 | bytes 2240512 | tf_op jit(solution)/shard_map/pallas_call | solution.py:223
  325.0 23.2 %convolution_convert_fusion = bf16[1152,3584]{1,0:T(8,128)(2,1)} fusion(bf16[2048,1152]{1,0:T(8,128)(2,1)S(1)} %bitcast.78, bf16[2048,3584]{1,0:T(8,128)(2,1)} %shard_map.411.refs_2_), kind=kOutput, calls=%fused_computation | convolution fusion | flops 16915562496 | bytes 27656192 | tf_op jit(solution)/shard_map/dot_general | solution.py:211
  348.2 4.9 constant_dynamic-slice_fusion.6
  355.7 26.3 %shard_map.412 = (bf16[2048,1152]{1,0:T(8,128)(2,1)S(1)}, bf16[2048,1152]{1,0:T(8,128)(2,1)}, bf16[2,1024,256]{2,1,0:T(8,128)(2,1)S(1)}, bf16[2,1024,256]{2,1,0:T(8,128)(2,1)S(1)}, f32[2,1152]{1,0:T(2,128)S(1)}) custom-call(s32[8]{0:T(128)S(1)} %fusion.20.refs_0_, s32[8]{0:T(128)S(1)} %fusion.24.refs_0_.refs_1_, bf16[2048,3584]{1,0:T(8,128)(2,1)} %shard_map.411.refs_2_, ...), custom_call_target="tpu_custom_call" | custom-call | flops 679477248 | bytes 3262144 | tf_op jit(solution)/shard_map/pallas_call | solution.py:223
  382.0 3.8 dynamic-slice_add_fusion.4
  391.8 12.7 %convolution_convert_fusion.1 = bf16[1792,1152]{1,0:T(8,128)(2,1)S(1)} fusion(bf16[2048,1792]{1,0:T(8,128)(2,1)S(1)} %bitcast.76, bf16[2048,1152]{1,0:T(8,128)(2,1)} %pad_maximum_fusion.1), kind=kOutput, calls=%fused_computation.1 | convolution fusion | flops 8457781248 | bytes 16187392 | tf_op jit(solution)/shard_map/dot_general | solution.py:211
  408.4 25.6 %shard_map.413 = (bf16[2048,1152]{1,0:T(8,128)(2,1)S(1)}, bf16[2048,1152]{1,0:T(8,128)(2,1)}, bf16[2,1024,256]{2,1,0:T(8,128)(2,1)S(1)}, bf16[2,1024,256]{2,1,0:T(8,128)(2,1)S(1)}, f32[2,1152]{1,0:T(2,128)S(1)}) custom-call(s32[8]{0:T(128)S(1)} %fusion.20.refs_0_, s32[8]{0:T(128)S(1)} %fusion.24.refs_0_.refs_1_, ...), custom_call_target="tpu_custom_call", output_to_operand_aliasing={{0}: (19, {}), {1}: (20, {})} | custom-call | flops 679477248 | bytes 3262144 | tf_op jit(solution)/shard_map/pallas_call | solution.py:223
  437.2 5.4 dynamic-slice_add_fusion.2
  455.7 6.5 %collective-permute-done.44.refs_8_ = bf16[1024,256]{1,0:T(8,128)(2,1)S(1)} collective-permute-done((bf16[1024,256]{1,0:T(8,128)(2,1)S(1)}, bf16[1024,256]{1,0:T(8,128)(2,1)S(1)}, u32[]{:S(2)}, u32[]{:S(2)}) %collective-permute-start.44) | collective-permute-done | bytes 524320 | tf_op jit(solution)/shard_map/ppermute | solution.py:47
  463.5 12.7 %shard_map.414 = (bf16[2048,768]{1,0:T(8,128)(2,1)S(1)}, f32[2,256]{1,0:T(2,128)S(1)}) custom-call(s32[3]{0:T(128)S(1)} %fusion.17.refs_0_, bf16[2048,256]{1,0:T(8,128)(2,1)S(1)} %copy-done.56, bf16[2048,256]{1,0:T(8,128)(2,1)S(1)} %copy-done.59, bf16[2048,256]{1,0:T(8,128)(2,1)S(1)} %copy-done.62, f32[2048,512]{1,0:T(8,128)} %copy-done.53, ...), custom_call_target="tpu_custom_call" | custom-call | flops 251658240 | bytes 1114880 | tf_op jit(solution)/shard_map/pallas_call | solution.py:223
  476.2 4.3 convolution_convert_fusion.2
  485.2 4.8 dynamic-slice_add_fusion
  492.1 4.1 dynamic-slice_add_fusion.7
  499.3 13.1 %shard_map.415 = (bf16[1024,1152]{1,0:T(8,128)(2,1)S(1)}, bf16[1024,1152]{1,0:T(8,128)(2,1)}, f32[1,1152]{1,0:T(1,128)S(1)}) custom-call(s32[8]{0:T(128)S(1)} %compare_select_fusion.1.refs_0_, s32[8]{0:T(128)S(1)} %fusion.24.refs_0_.refs_1_, bf16[2048,768]{1,0:T(8,128)(2,1)S(1)} %get-tuple-element.189.refs_2_.refs_3_, ...), custom_call_target="tpu_custom_call" | custom-call | flops 226492416 | bytes 1438272 | tf_op jit(solution)/shard_map/pallas_call | solution.py:223
  515.2 6.9 %collective-permute-done.55 = bf16[192,768]{1,0:T(8,128)(2,1)S(1)} collective-permute-done((bf16[192,768]{1,0:T(8,128)(2,1)S(1)}, bf16[192,768]{1,0:T(8,128)(2,1)S(1)}, u32[]{:S(2)}, u32[]{:S(2)}) %collective-permute-start.55) | collective-permute-done | bytes 294944 | tf_op jit(solution)/shard_map/ppermute | solution.py:113
  528.4 4.2 collective-permute-done.62
  545.2 3.4 collective-permute-done.57
  555.5 5.1 all-to-all-done.2
  560.6 3.5 all-to-all-start.3
  564.1 4.0 dynamic-slice_add_fusion.6
  573.8 5.8 all-to-all-done.3.refs_0_
  582.8 3.8 multiply_reduce_fusion.1
  615.8 15.4 %collective-permute-done.67 = bf16[512,1152]{1,0:T(8,128)(2,1)} collective-permute-done((bf16[512,1152]{1,0:T(8,128)(2,1)}, bf16[512,1152]{1,0:T(8,128)(2,1)}, u32[]{:S(2)}, u32[]{:S(2)}) %collective-permute-start.67) | collective-permute-done | bytes 1179680 | tf_op jit(solution)/shard_map/ppermute | solution.py:47
  631.3 3.5 multiply_subtract_fusion.1
  635.6 4.0 multiply_subtract_fusion
  (518 shorter events, 209.3 us)
Async XLA Ops:
  2.2 15.2 %collective-permute-start.3 = (bf16[224,1152]{1,0:T(8,128)(2,1)S(1)}, bf16[224,1152]{1,0:T(8,128)(2,1)}, u32[]{:S(2)}, u32[]{:S(2)}) collective-permute-start(bf16[224,1152]{1,0:T(8,128)(2,1)S(1)} %pad.13.refs_2_.refs_3_), channel_id=1, source_target_pairs={{0,8},{1,5},{2,10},{3,7},{8,16},{9,1},{10,18},{11,3},{16,24},{17,9... | collective-permute-start | bytes 1548296 | tf_op jit(solution)/shard_map/ppermute | solution.py:113
  15.7 28.8 %collective-permute-start.1 = (bf16[512,1152]{1,0:T(8,128)(2,1)}, bf16[512,1152]{1,0:T(8,128)(2,1)}, u32[]{:S(2)}, u32[]{:S(2)}) collective-permute-start(bf16[512,1152]{1,0:T(8,128)(2,1)} %bitcast.2.refs_4_), channel_id=1, source_target_pairs={{0,2},{1,3},{2,0},{3,1},{4,6},{5,7},{6,4},{7,5},{8,10},{9,11},{10,... | collective-permute-start | bytes 3538952 | tf_op jit(solution)/shard_map/ppermute | solution.py:47
  44.5 23.7 %collective-permute-start.9 = (bf16[512,1152]{1,0:T(8,128)(2,1)}, bf16[512,1152]{1,0:T(8,128)(2,1)}, u32[]{:S(2)}, u32[]{:S(2)}) collective-permute-start(bf16[512,1152]{1,0:T(8,128)(2,1)} %collective-permute-done.1), channel_id=1, source_target_pairs={{0,1},{1,0},{2,3},{3,2},{4,5},{5,4},{6,7},{7,6},{8,9},{9,8},{10,11... | collective-permute-start | bytes 3538952 | tf_op jit(solution)/shard_map/ppermute | solution.py:47
  44.7 38.2 %collective-permute-start = (bf16[512,1152]{1,0:T(8,128)(2,1)}, bf16[512,1152]{1,0:T(8,128)(2,1)}, u32[]{:S(2)}, u32[]{:S(2)}) collective-permute-start(bf16[512,1152]{1,0:T(8,128)(2,1)} %bitcast.2.refs_4_), channel_id=1, source_target_pairs={{0,1},{1,0},{2,3},{3,2},{4,5},{5,4},{6,7},{7,6},{8,9},{9,8},{10,11... | collective-permute-start | bytes 3538952 | tf_op jit(solution)/shard_map/ppermute | solution.py:47
  45.0 20.3 %all-to-all-start.1 = ((bf16[4,36,3584]{2,1,0:T(8,128)(2,1)}), bf16[4,36,3584]{2,1,0:T(8,128)(2,1)}, u32[]{:S(2)}, u32[]{:S(2)}) async-start(bf16[4,36,3584]{2,1,0:T(8,128)(2,1)} %shard_map.400), calls=%async_computation.1 | async-start | bytes 2293760 | tf_op jit(solution)/shard_map/all_to_all | solution.py:42
  51.3 15.4 %collective-permute-start.11 = (bf16[208,768]{1,0:T(8,128)(2,1)S(1)}, bf16[208,768]{1,0:T(8,128)(2,1)S(1)}, u32[]{:S(2)}, u32[]{:S(2)}) collective-permute-start(bf16[208,768]{1,0:T(8,128)(2,1)S(1)} %collective-permute-done.8.refs_5_.refs_12_.refs_11_), channel_id=1, source_target_pairs={{0,4},{1,9},{2,6},{3,11},{8,0},{9,17},{10,2},{11,19},{16,8},{17,25... | collective-permute-start | bytes 958472 | tf_op jit(solution)/shard_map/ppermute | solution.py:113
  68.1 37.9 %collective-permute-start.13 = (bf16[144,3584]{1,0:T(8,128)(2,1)S(1)}, bf16[144,3584]{1,0:T(8,128)(2,1)S(1)}, u32[]{:S(2)}, u32[]{:S(2)}) collective-permute-start(bf16[144,3584]{1,0:T(8,128)(2,1)S(1)} %reshape.108.refs_2_.refs_11_), channel_id=1, source_target_pairs={{0,8},{1,5},{2,10},{3,7},{8,16},{9,1},{10,18},{11,3},{16,24},{17,9... | collective-permute-start | bytes 3096584 | tf_op jit(solution)/shard_map/ppermute | solution.py:113
  69.6 36.4 %collective-permute-start.14 = (bf16[144,3584]{1,0:T(8,128)(2,1)S(1)}, bf16[144,3584]{1,0:T(8,128)(2,1)S(1)}, u32[]{:S(2)}, u32[]{:S(2)}) collective-permute-start(bf16[144,3584]{1,0:T(8,128)(2,1)S(1)} %reshape.108.refs_2_.refs_11_), channel_id=1, source_target_pairs={{0,4},{1,9},{2,6},{3,11},{8,0},{9,17},{10,2},{11,19},{16,8},{17,25... | collective-permute-start | bytes 3096584 | tf_op jit(solution)/shard_map/ppermute | solution.py:113
  81.5 26.8 %collective-permute-start.15 = (bf16[256,1152]{1,0:T(8,128)(2,1)}, bf16[256,1152]{1,0:T(8,128)(2,1)}, u32[]{:S(2)}, u32[]{:S(2)}) collective-permute-start(bf16[256,1152]{1,0:T(8,128)(2,1)} %get-tuple-element.129.refs_5_.refs_3_), channel_id=1, source_target_pairs={{0,2},{1,3},{2,0},{3,1},{4,6},{5,7},{6,4},{7,5},{8,10},{9,11},{10,... | collective-permute-start | bytes 1769480 | tf_op jit(solution)/shard_map/ppermute | solution.py:47
  82.8 25.6 %collective-permute-start.16 = (bf16[256,1152]{1,0:T(8,128)(2,1)}, bf16[256,1152]{1,0:T(8,128)(2,1)}, u32[]{:S(2)}, u32[]{:S(2)}) collective-permute-start(bf16[256,1152]{1,0:T(8,128)(2,1)} %get-tuple-element.129.refs_5_.refs_3_), channel_id=1, source_target_pairs={{0,1},{1,0},{2,3},{3,2},{4,5},{5,4},{6,7},{7,6},{8,9},{9,8},{10,11... | collective-permute-start | bytes 1769480 | tf_op jit(solution)/shard_map/ppermute | solution.py:47
  106.1 14.1 %collective-permute-start.18 = (bf16[224,1152]{1,0:T(8,128)(2,1)}, bf16[224,1152]{1,0:T(8,128)(2,1)}, u32[]{:S(2)}, u32[]{:S(2)}) collective-permute-start(bf16[224,1152]{1,0:T(8,128)(2,1)} %collective-permute-done.4.refs_4_.refs_5_), channel_id=1, source_target_pairs={{0,4},{1,9},{2,6},{3,11},{8,0},{9,17},{10,2},{11,19},{16,8},{17,25... | collective-permute-start | bytes 1548296 | tf_op jit(solution)/shard_map/ppermute | solution.py:113
  107.9 12.7 %collective-permute-start.17 = (bf16[224,1152]{1,0:T(8,128)(2,1)}, bf16[224,1152]{1,0:T(8,128)(2,1)}, u32[]{:S(2)}, u32[]{:S(2)}) collective-permute-start(bf16[224,1152]{1,0:T(8,128)(2,1)} %collective-permute-done.3.refs_3_.refs_4_), channel_id=1, source_target_pairs={{0,8},{1,5},{2,10},{3,7},{8,16},{9,1},{10,18},{11,3},{16,24},{17,9... | collective-permute-start | bytes 1548296 | tf_op jit(solution)/shard_map/ppermute | solution.py:113
  120.7 26.4 %collective-permute-start.20 = (bf16[2048,256]{1,0:T(8,128)(2,1)S(1)}, bf16[2048,256]{1,0:T(8,128)(2,1)S(1)}, u32[]{:S(2)}, u32[]{:S(2)}) collective-permute-start(bf16[2048,256]{1,0:T(8,128)(2,1)S(1)} %get-tuple-element.136.refs_1_), channel_id=1, source_target_pairs={{0,2},{1,3},{2,0},{3,1},{4,6},{5,7},{6,4},{7,5},{8,10},{9,11},{10,... | collective-permute-start | bytes 3145736 | tf_op jit(solution)/shard_map/ppermute | solution.py:47
  121.7 25.4 %collective-permute-start.22 = (bf16[144,3584]{1,0:T(8,128)(2,1)S(1)}, bf16[144,3584]{1,0:T(8,128)(2,1)S(1)}, u32[]{:S(2)}, u32[]{:S(2)}) collective-permute-start(bf16[144,3584]{1,0:T(8,128)(2,1)S(1)} %collective-permute-done.14.refs_4_.refs_13_), channel_id=1, source_target_pairs={{0,4},{1,9},{2,6},{3,11},{8,0},{9,17},{10,2},{11,19},{16,8},{17,25... | collective-permute-start | bytes 3096584 | tf_op jit(solution)/shard_map/ppermute | solution.py:113
  123.5 23.6 %collective-permute-start.21 = (bf16[144,3584]{1,0:T(8,128)(2,1)S(1)}, bf16[144,3584]{1,0:T(8,128)(2,1)S(1)}, u32[]{:S(2)}, u32[]{:S(2)}) collective-permute-start(bf16[144,3584]{1,0:T(8,128)(2,1)S(1)} %collective-permute-done.13.refs_3_.refs_12_), channel_id=1, source_target_pairs={{0,8},{1,5},{2,10},{3,7},{8,16},{9,1},{10,18},{11,3},{16,24},{17,9... | collective-permute-start | bytes 3096584 | tf_op jit(solution)/shard_map/ppermute | solution.py:113
  123.7 27.2 %collective-permute-start.19 = (bf16[2048,256]{1,0:T(8,128)(2,1)S(1)}, bf16[2048,256]{1,0:T(8,128)(2,1)S(1)}, u32[]{:S(2)}, u32[]{:S(2)}) collective-permute-start(bf16[2048,256]{1,0:T(8,128)(2,1)S(1)} %get-tuple-element.136.refs_1_), channel_id=1, source_target_pairs={{0,1},{1,0},{2,3},{3,2},{4,5},{5,4},{6,7},{7,6},{8,9},{9,8},{10,11... | collective-permute-start | bytes 3145736 | tf_op jit(solution)/shard_map/ppermute | solution.py:47
  147.3 24.8 %collective-permute-start.25 = (bf16[144,3584]{1,0:T(8,128)(2,1)S(1)}, bf16[144,3584]{1,0:T(8,128)(2,1)S(1)}, u32[]{:S(2)}, u32[]{:S(2)}) collective-permute-start(bf16[144,3584]{1,0:T(8,128)(2,1)S(1)} %collective-permute-done.21.refs_5_.refs_14_), channel_id=1, source_target_pairs={{0,8},{1,5},{2,10},{3,7},{8,16},{9,1},{10,18},{11,3},{16,24},{17,9... | collective-permute-start | bytes 3096584 | tf_op jit(solution)/shard_map/ppermute | solution.py:113
  148.5 49.2 %collective-permute-start.26 = (bf16[144,3584]{1,0:T(8,128)(2,1)S(1)}, bf16[144,3584]{1,0:T(8,128)(2,1)S(1)}, u32[]{:S(2)}, u32[]{:S(2)}) collective-permute-start(bf16[144,3584]{1,0:T(8,128)(2,1)S(1)} %collective-permute-done.22.refs_6_.refs_15_), channel_id=1, source_target_pairs={{0,4},{1,9},{2,6},{3,11},{8,0},{9,17},{10,2},{11,19},{16,8},{17,25... | collective-permute-start | bytes 3096584 | tf_op jit(solution)/shard_map/ppermute | solution.py:113
  172.1 25.7 %collective-permute-start.27 = (bf16[144,3584]{1,0:T(8,128)(2,1)S(1)}, bf16[144,3584]{1,0:T(8,128)(2,1)S(1)}, u32[]{:S(2)}, u32[]{:S(2)}) collective-permute-start(bf16[144,3584]{1,0:T(8,128)(2,1)S(1)} %collective-permute-done.25.refs_7_.refs_16_), channel_id=1, source_target_pairs={{0,8},{1,5},{2,10},{3,7},{8,16},{9,1},{10,18},{11,3},{16,24},{17,9... | collective-permute-start | bytes 3096584 | tf_op jit(solution)/shard_map/ppermute | solution.py:113
  173.3 24.2 %collective-permute-start.28 = (bf16[224,1152]{1,0:T(8,128)(2,1)}, bf16[224,1152]{1,0:T(8,128)(2,1)S(1)}, u32[]{:S(2)}, u32[]{:S(2)}) collective-permute-start(bf16[224,1152]{1,0:T(8,128)(2,1)} %collective-permute-done.17.refs_5_.refs_6_), channel_id=1, source_target_pairs={{0,8},{1,5},{2,10},{3,7},{8,16},{9,1},{10,18},{11,3},{16,24},{17,9... | collective-permute-start | bytes 1548296 | tf_op jit(solution)/shard_map/ppermute | solution.py:113
  175.8 40.8 %collective-permute-start.29 = (bf16[224,1152]{1,0:T(8,128)(2,1)}, bf16[224,1152]{1,0:T(8,128)(2,1)S(1)}, u32[]{:S(2)}, u32[]{:S(2)}) collective-permute-start(bf16[224,1152]{1,0:T(8,128)(2,1)} %collective-permute-done.18.refs_6_.refs_7_), channel_id=1, source_target_pairs={{0,4},{1,9},{2,6},{3,11},{8,0},{9,17},{10,2},{11,19},{16,8},{17,25... | collective-permute-start | bytes 1548296 | tf_op jit(solution)/shard_map/ppermute | solution.py:113
  197.4 19.1 %collective-permute-start.30 = (bf16[224,1152]{1,0:T(8,128)(2,1)S(1)}, bf16[224,1152]{1,0:T(8,128)(2,1)S(1)}, u32[]{:S(2)}, u32[]{:S(2)}) collective-permute-start(bf16[224,1152]{1,0:T(8,128)(2,1)S(1)} %collective-permute-done.28.refs_7_.refs_8_), channel_id=1, source_target_pairs={{0,8},{1,5},{2,10},{3,7},{8,16},{9,1},{10,18},{11,3},{16,24},{17,9... | collective-permute-start | bytes 1548296 | tf_op jit(solution)/shard_map/ppermute | solution.py:113
  230.7 28.1 %collective-permute-start.32 = (bf16[512,1152]{1,0:T(8,128)(2,1)S(1)}, bf16[512,1152]{1,0:T(8,128)(2,1)S(1)}, u32[]{:S(2)}, u32[]{:S(2)}) collective-permute-start(bf16[512,1152]{1,0:T(8,128)(2,1)S(1)} %add.264), channel_id=1, source_target_pairs={{0,2},{1,3},{2,0},{3,1},{4,6},{5,7},{6,4},{7,5},{8,10},{9,11},{10,... | collective-permute-start | bytes 3538952 | tf_op jit(solution)/shard_map/ppermute | solution.py:47
  280.0 28.3 %collective-permute-start.34 = (bf16[512,1152]{1,0:T(8,128)(2,1)S(1)}, bf16[512,1152]{1,0:T(8,128)(2,1)S(1)}, u32[]{:S(2)}, u32[]{:S(2)}) collective-permute-start(bf16[512,1152]{1,0:T(8,128)(2,1)S(1)} %get-tuple-element.161), channel_id=1, source_target_pairs={{0,2},{1,3},{2,0},{3,1},{4,6},{5,7},{6,4},{7,5},{8,10},{9,11},{10,... | collective-permute-start | bytes 3538952 | tf_op jit(solution)/shard_map/ppermute | solution.py:47
  353.1 28.9 %collective-permute-start.37 = (bf16[144,3584]{1,0:T(8,128)(2,1)S(1)}, bf16[144,3584]{1,0:T(8,128)(2,1)S(1)}, u32[]{:S(2)}, u32[]{:S(2)}) collective-permute-start(bf16[144,3584]{1,0:T(8,128)(2,1)S(1)} %get-tuple-element.238), channel_id=1, source_target_pairs={{0,8},{1,5},{2,10},{3,7},{8,16},{9,1},{10,18},{11,3},{16,24},{17,9... | collective-permute-start | bytes 3096584 | tf_op jit(solution)/shard_map/ppermute | solution.py:113
  386.0 48.1 %collective-permute-start.41 = (bf16[144,3584]{1,0:T(8,128)(2,1)}, bf16[144,3584]{1,0:T(8,128)(2,1)}, u32[]{:S(2)}, u32[]{:S(2)}) collective-permute-start(bf16[144,3584]{1,0:T(8,128)(2,1)} %get-tuple-element.237), channel_id=1, source_target_pairs={{0,4},{1,9},{2,6},{3,11},{8,0},{9,17},{10,2},{11,19},{16,8},{17,25... | collective-permute-start | bytes 3096584 | tf_op jit(solution)/shard_map/ppermute | solution.py:113
  389.1 44.9 %collective-permute-start.40 = (bf16[144,3584]{1,0:T(8,128)(2,1)}, bf16[144,3584]{1,0:T(8,128)(2,1)S(1)}, u32[]{:S(2)}, u32[]{:S(2)}) collective-permute-start(bf16[144,3584]{1,0:T(8,128)(2,1)} %dynamic-slice_add_fusion.4), channel_id=1, source_target_pairs={{0,8},{1,5},{2,10},{3,7},{8,16},{9,1},{10,18},{11,3},{16,24},{17,9... | collective-permute-start | bytes 3096584 | tf_op jit(solution)/shard_map/ppermute | solution.py:113
  390.9 17.6 %collective-permute-start.39 = (bf16[1024,256]{1,0:T(8,128)(2,1)S(1)}, bf16[1024,256]{1,0:T(8,128)(2,1)S(1)}, u32[]{:S(2)}, u32[]{:S(2)}) collective-permute-start(bf16[1024,256]{1,0:T(8,128)(2,1)S(1)} %fusion.3), channel_id=1, source_target_pairs={{0,2},{1,3},{2,0},{3,1},{4,6},{5,7},{6,4},{7,5},{8,10},{9,11},{10,... | collective-permute-start | bytes 1572872 | tf_op jit(solution)/shard_map/ppermute | solution.py:47
  407.0 27.1 %collective-permute-start.42 = (bf16[224,1152]{1,0:T(8,128)(2,1)S(1)}, bf16[224,1152]{1,0:T(8,128)(2,1)S(1)}, u32[]{:S(2)}, u32[]{:S(2)}) collective-permute-start(bf16[224,1152]{1,0:T(8,128)(2,1)S(1)} %get-tuple-element.244), channel_id=1, source_target_pairs={{0,8},{1,5},{2,10},{3,7},{8,16},{9,1},{10,18},{11,3},{16,24},{17,9... | collective-permute-start | bytes 1548296 | tf_op jit(solution)/shard_map/ppermute | solution.py:113
  447.1 35.4 %collective-permute-start.51 = (bf16[224,1152]{1,0:T(8,128)(2,1)}, bf16[224,1152]{1,0:T(8,128)(2,1)}, u32[]{:S(2)}, u32[]{:S(2)}) collective-permute-start(bf16[224,1152]{1,0:T(8,128)(2,1)} %get-tuple-element.243), channel_id=1, source_target_pairs={{0,4},{1,9},{2,6},{3,11},{8,0},{9,17},{10,2},{11,19},{16,8},{17,25... | collective-permute-start | bytes 1548296 | tf_op jit(solution)/shard_map/ppermute | solution.py:113
  447.7 14.5 %collective-permute-start.44 = (bf16[1024,256]{1,0:T(8,128)(2,1)S(1)}, bf16[1024,256]{1,0:T(8,128)(2,1)S(1)}, u32[]{:S(2)}, u32[]{:S(2)}) collective-permute-start(bf16[1024,256]{1,0:T(8,128)(2,1)S(1)} %fusion.2), channel_id=1, source_target_pairs={{0,2},{1,3},{2,0},{3,1},{4,6},{5,7},{6,4},{7,5},{8,10},{9,11},{10,... | collective-permute-start | bytes 1572872 | tf_op jit(solution)/shard_map/ppermute | solution.py:47
  450.6 31.9 %collective-permute-start.50 = (bf16[224,1152]{1,0:T(8,128)(2,1)}, bf16[224,1152]{1,0:T(8,128)(2,1)}, u32[]{:S(2)}, u32[]{:S(2)}) collective-permute-start(bf16[224,1152]{1,0:T(8,128)(2,1)} %dynamic-slice_add_fusion.9), channel_id=1, source_target_pairs={{0,8},{1,5},{2,10},{3,7},{8,16},{9,1},{10,18},{11,3},{16,24},{17,9... | collective-permute-start | bytes 1548296 | tf_op jit(solution)/shard_map/ppermute | solution.py:113
  452.1 31.1 %collective-permute-start.48 = (bf16[144,3584]{1,0:T(8,128)(2,1)}, bf16[144,3584]{1,0:T(8,128)(2,1)}, u32[]{:S(2)}, u32[]{:S(2)}) collective-permute-start(bf16[144,3584]{1,0:T(8,128)(2,1)} %get-tuple-element.236), channel_id=1, source_target_pairs={{0,8},{1,5},{2,10},{3,7},{8,16},{9,1},{10,18},{11,3},{16,24},{17,9... | collective-permute-start | bytes 3096584 | tf_op jit(solution)/shard_map/ppermute | solution.py:113
  453.6 29.5 %collective-permute-start.49 = (bf16[144,3584]{1,0:T(8,128)(2,1)S(1)}, bf16[144,3584]{1,0:T(8,128)(2,1)}, u32[]{:S(2)}, u32[]{:S(2)}) collective-permute-start(bf16[144,3584]{1,0:T(8,128)(2,1)S(1)} %get-tuple-element.235), channel_id=1, source_target_pairs={{0,4},{1,9},{2,6},{3,11},{8,0},{9,17},{10,2},{11,19},{16,8},{17,25... | collective-permute-start | bytes 3096584 | tf_op jit(solution)/shard_map/ppermute | solution.py:113
  462.2 18.3 %collective-permute-start.46 = (bf16[256,1152]{1,0:T(8,128)(2,1)S(1)}, bf16[256,1152]{1,0:T(8,128)(2,1)S(1)}, u32[]{:S(2)}, u32[]{:S(2)}) collective-permute-start(bf16[256,1152]{1,0:T(8,128)(2,1)S(1)} %slice_add_fusion.1), channel_id=1, source_target_pairs={{0,2},{1,3},{2,0},{3,1},{4,6},{5,7},{6,4},{7,5},{8,10},{9,11},{10,... | collective-permute-start | bytes 1769480 | tf_op jit(solution)/shard_map/ppermute | solution.py:47
  483.2 13.1 %collective-permute-start.47 = (bf16[192,768]{1,0:T(8,128)(2,1)S(1)}, bf16[192,768]{1,0:T(8,128)(2,1)S(1)}, u32[]{:S(2)}, u32[]{:S(2)}) collective-permute-start(bf16[192,768]{1,0:T(8,128)(2,1)S(1)} %get-tuple-element.250), channel_id=1, source_target_pairs={{0,8},{1,5},{2,10},{3,7},{8,16},{9,1},{10,18},{11,3},{16,24},{17,9... | collective-permute-start | bytes 884744 | tf_op jit(solution)/shard_map/ppermute | solution.py:113
  484.6 29.2 %collective-permute-start.58 = (bf16[192,768]{1,0:T(8,128)(2,1)S(1)}, bf16[192,768]{1,0:T(8,128)(2,1)S(1)}, u32[]{:S(2)}, u32[]{:S(2)}) collective-permute-start(bf16[192,768]{1,0:T(8,128)(2,1)S(1)} %get-tuple-element.249), channel_id=1, source_target_pairs={{0,4},{1,9},{2,6},{3,11},{8,0},{9,17},{10,2},{11,19},{16,8},{17,25... | collective-permute-start | bytes 884744 | tf_op jit(solution)/shard_map/ppermute | solution.py:113
  490.1 34.2 %collective-permute-start.52 = (bf16[144,3584]{1,0:T(8,128)(2,1)S(1)}, bf16[144,3584]{1,0:T(8,128)(2,1)S(1)}, u32[]{:S(2)}, u32[]{:S(2)}) collective-permute-start(bf16[144,3584]{1,0:T(8,128)(2,1)S(1)} %get-tuple-element.234), channel_id=1, source_target_pairs={{0,8},{1,5},{2,10},{3,7},{8,16},{9,1},{10,18},{11,3},{16,24},{17,9... | collective-permute-start | bytes 3096584 | tf_op jit(solution)/shard_map/ppermute | solution.py:113
  491.5 32.8 %collective-permute-start.53 = (bf16[144,3584]{1,0:T(8,128)(2,1)S(1)}, bf16[144,3584]{1,0:T(8,128)(2,1)S(1)}, u32[]{:S(2)}, u32[]{:S(2)}) collective-permute-start(bf16[144,3584]{1,0:T(8,128)(2,1)S(1)} %get-tuple-element.233), channel_id=1, source_target_pairs={{0,4},{1,9},{2,6},{3,11},{8,0},{9,17},{10,2},{11,19},{16,8},{17,25... | collective-permute-start | bytes 3096584 | tf_op jit(solution)/shard_map/ppermute | solution.py:113
  497.1 25.0 %collective-permute-start.55 = (bf16[192,768]{1,0:T(8,128)(2,1)S(1)}, bf16[192,768]{1,0:T(8,128)(2,1)S(1)}, u32[]{:S(2)}, u32[]{:S(2)}) collective-permute-start(bf16[192,768]{1,0:T(8,128)(2,1)S(1)} %dynamic-slice_add_fusion.14), channel_id=1, source_target_pairs={{0,8},{1,5},{2,10},{3,7},{8,16},{9,1},{10,18},{11,3},{16,24},{17,9... | collective-permute-start | bytes 884744 | tf_op jit(solution)/shard_map/ppermute | solution.py:113
  498.5 29.9 %collective-permute-start.64 = (bf16[224,1152]{1,0:T(8,128)(2,1)}, bf16[224,1152]{1,0:T(8,128)(2,1)}, u32[]{:S(2)}, u32[]{:S(2)}) collective-permute-start(bf16[224,1152]{1,0:T(8,128)(2,1)} %get-tuple-element.241), channel_id=1, source_target_pairs={{0,4},{1,9},{2,6},{3,11},{8,0},{9,17},{10,2},{11,19},{16,8},{17,25... | collective-permute-start | bytes 1548296 | tf_op jit(solution)/shard_map/ppermute | solution.py:113
  513.8 18.9 %collective-permute-start.62 = (bf16[224,1152]{1,0:T(8,128)(2,1)}, bf16[224,1152]{1,0:T(8,128)(2,1)S(1)}, u32[]{:S(2)}, u32[]{:S(2)}) collective-permute-start(bf16[224,1152]{1,0:T(8,128)(2,1)} %get-tuple-element.242), channel_id=1, source_target_pairs={{0,8},{1,5},{2,10},{3,7},{8,16},{9,1},{10,18},{11,3},{16,24},{17,9... | collective-permute-start | bytes 1548296 | tf_op jit(solution)/shard_map/ppermute | solution.py:113
  532.7 54.7 %collective-permute-start.54 = (bf16[1024,1152]{1,0:T(8,128)(2,1)}, bf16[1024,1152]{1,0:T(8,128)(2,1)}, u32[]{:S(2)}, u32[]{:S(2)}) collective-permute-start(bf16[1024,1152]{1,0:T(8,128)(2,1)} %get-tuple-element.193), channel_id=1, source_target_pairs={{0,1},{1,0},{2,3},{3,2},{4,5},{5,4},{6,7},{7,6},{8,9},{9,8},{10,11... | collective-permute-start | bytes 7077896 | tf_op jit(solution)/shard_map/ppermute | solution.py:47
  554.8 15.6 %collective-permute-start.61 = (bf16[32,1152]{1,0:T(8,128)(2,1)S(1)}, bf16[32,1152]{1,0:T(8,128)(2,1)S(1)}, u32[]{:S(2)}, u32[]{:S(2)}) collective-permute-start(bf16[32,1152]{1,0:T(8,128)(2,1)S(1)} %maximum_maximum_fusion.2), channel_id=1, source_target_pairs={{0,0},{1,8},{2,16},{3,24},{4,1},{5,9},{6,17},{7,25},{8,2},{9,10},{... | collective-permute-start | bytes 221192 | tf_op jit(solution)/shard_map/ppermute | solution.py:1118
  560.6 19.0 %all-to-all-start.3 = ((bf16[4,36,3584]{2,1,0:T(8,128)(2,1)}), bf16[4,36,3584]{2,1,0:T(8,128)(2,1)S(1)}, u32[]{:S(2)}, u32[]{:S(2)}) async-start(bf16[4,36,3584]{2,1,0:T(8,128)(2,1)} %reshape.116), calls=%async_computation.3 | async-start | bytes 2293760 | tf_op jit(solution)/shard_map/all_to_all | solution.py:42
  568.1 14.6 %collective-permute-start.63 = (bf16[224,1152]{1,0:T(8,128)(2,1)}, bf16[224,1152]{1,0:T(8,128)(2,1)}, u32[]{:S(2)}, u32[]{:S(2)}) collective-permute-start(bf16[224,1152]{1,0:T(8,128)(2,1)} %get-tuple-element.206), channel_id=1, source_target_pairs={{0,8},{1,5},{2,10},{3,7},{8,16},{9,1},{10,18},{11,3},{16,24},{17,9... | collective-permute-start | bytes 1548296 | tf_op jit(solution)/shard_map/ppermute | solution.py:113
  569.6 13.1 %collective-permute-start.65 = (bf16[224,1152]{1,0:T(8,128)(2,1)}, bf16[224,1152]{1,0:T(8,128)(2,1)}, u32[]{:S(2)}, u32[]{:S(2)}) collective-permute-start(bf16[224,1152]{1,0:T(8,128)(2,1)} %get-tuple-element.208), channel_id=1, source_target_pairs={{0,4},{1,9},{2,6},{3,11},{8,0},{9,17},{10,2},{11,19},{16,8},{17,25... | collective-permute-start | bytes 1548296 | tf_op jit(solution)/shard_map/ppermute | solution.py:113
  605.5 25.8 %collective-permute-start.67 = (bf16[512,1152]{1,0:T(8,128)(2,1)}, bf16[512,1152]{1,0:T(8,128)(2,1)}, u32[]{:S(2)}, u32[]{:S(2)}) collective-permute-start(bf16[512,1152]{1,0:T(8,128)(2,1)} %slice_add_fusion), channel_id=1, source_target_pairs={{0,2},{1,3},{2,0},{3,1},{4,6},{5,7},{6,4},{7,5},{8,10},{9,11},{10,... | collective-permute-start | bytes 3538952 | tf_op jit(solution)/shard_map/ppermute | solution.py:47
  (169 other events, 1986.7 us)

commit v5 on v4

--- a/solution.py
+++ b/solution.py
@@ -75,7 +75,7 @@
     return jnp.concatenate([parts[j ^ bit] for j in range(len(parts))])
 
 
-def sum_rest(value):
+def sum_others(value):
     value = value + swap(value, 1)
     bit = 1
     while bit < lax.axis_size("dp"):
@@ -1104,7 +1104,6 @@
     down_sum.send(in_own)
     down_sum.absorb()
     down_own = down_sum.finish()[:ff_rows]
-    gate_up_own = unpack_columns(gate_up_own, dp, ctx, ff_rows)
     out_own = in_own[own_rows:]
     out_own = jnp.concatenate(
         [
@@ -1116,7 +1115,14 @@
         axis=1,
     )
     out_own = lax.ppermute(out_own, ("dp", "ctx"), to_owner).astype(f32)
-    in_own = exchange(in_own[:own_rows].reshape(ctx, in_rows, qkv_cols), "ctx").astype(f32)
+    in_own = exchange(
+        tie(in_own[:own_rows], gate_up_own, down_own).reshape(ctx, in_rows, qkv_cols), "ctx"
+    ).astype(f32)
+    far = swap(tie(summed, gate_up_own, in_own), 2)
+    input_grad = (
+        input_even[:rows].astype(f32) + near[:rows].astype(f32) + far.astype(f32)
+    )
+    gate_up_own = unpack_columns(gate_up_own, dp, ctx, ff_rows)
     qkv_own = jnp.concatenate(
         [
             in_own[:, :, :HD].transpose(1, 0, 2).reshape(in_rows, H * HD),
@@ -1130,13 +1136,8 @@
         local_squares = local_squares + jnp.sum(piece * piece)
     lines = jnp.concatenate([gain_grads.reshape(-1, 128), head_grads.reshape(-1, 128)])
     squares = jnp.pad(local_squares.reshape(1, 1), ((0, 7), (0, 127)))
-    sums = tie(jnp.concatenate([lines, squares]), summed)
-    sums = sums + swap(sums, 2)
-    far = swap(tie(summed, sums), 2)
-    input_grad = (
-        input_even[:rows].astype(f32) + near[:rows].astype(f32) + far.astype(f32)
-    )
-    sums = sum_rest(sums)
+    sums = sum_others(jnp.concatenate([lines, squares]))
+    sums = sums + swap(tie(sums, far), 2)
     small_grads = sums[: lines.shape[0]]
     index = lax.axis_index("dp") * ctx + place
     gains_own = lax.dynamic_slice_in_dim(
@@ -1154,7 +1155,6 @@
     seconds = (second_qkv, second_out, second_gate_up, second_down, second_gains, second_head)
     rates = (D ** (-0.5), (H * HD) ** (-0.5), D ** (-0.5), FF ** (-0.5), GAIN_RATE, GAIN_RATE)
     decays = (WEIGHT_DECAY, WEIGHT_DECAY, WEIGHT_DECAY, WEIGHT_DECAY, 0.0, 0.0)
-    reduced = reduced[:2] + (tie(gate_up_own, far, grad_norm), tie(down_own, far, grad_norm)) + reduced[4:]
     updates = [
         adam_update(
             weights[index],

time: 654 us -> 645 us (0.986)
  other arithmetic: 80.7 us -> 73.2 us
    ppermute x25, waiting for transfers between devices: 54.5 us -> 44.5 us  [swap(): return lax.ppermute(value, 'ctx', [(i, i ^ bit) for i in range(count)])]
    ppermute x42, waiting for transfers between devices: 91.9 us -> 101 us  [send(): return lax.ppermute(value, ('dp', 'ctx'), pairs)]
    unnamed x284 -> x286, local copies, waits for them, and re-layouts: 46.3 us -> 44.3 us
  transfers between devices with their start and end apart: 76 -> 76, of which waited for: 38 -> 37; matrix products, arithmetic and copies ran while one was open for 13% -> 13% of each run, Pallas kernels for 25% -> 25%
where the time goes in v5:
time: 645 us; the launch traced here: 635 us
  Pallas kernels  191 us (30%)
  waiting for transfers between devices  172 us (27%)
  starting transfers between devices  83.9 us (13%)
  other arithmetic  73.2 us (11%)
  local copies, waits for them, and re-layouts  60.5 us (9%)
  matrix products  46.9 us (7%)
  between operations  8.07 us (1%)
    pallas_call x17, Pallas kernels, call(): pl.pallas_call(kernel, out_shape=out_shape, grid_spec=pltpu.PrefetchScala...  191 us
    ppermute x42, waiting for transfers between devices, send(): return lax.ppermute(value, ('dp', 'ctx'), pairs)  101 us
    ppermute x42, starting transfers between devices, send(): return lax.ppermute(value, ('dp', 'ctx'), pairs)  50.8 us
    dot_general x7, matrix products, mm_tn(): lax.dot_general(a, b, (((0,), (0,)), ((), ())), preferred_element_type=F32)  46.9 us
    ppermute x25, waiting for transfers between devices, swap(): return lax.ppermute(value, 'ctx', [(i, i ^ bit) for i in range(count)])  44.5 us
    unnamed x286, local copies, waits for them, and re-layouts  44.3 us
    add x13, other arithmetic, add_low(): return a + b  28.8 us
    all_to_all x4, waiting for transfers between devices, exchange(): return lax.all_to_all(parts, axis, split_axis=0, concat_axis=0, tiled=True)  19.2 us
  transfers between devices with their start and end apart: 76, of which 37 were waited for; matrix products, arithmetic and copies ran while one was open for 13% of the time, Pallas kernels for 25%

profile of v5, /device:TPU:0, one launch (start us, length us, event | category | flops | bytes accessed | tf_op | source)
XLA Modules:
  0.0 634.8 jit_solution(16850761174672061530)
XLA Ops:
  12.0 3.6 all-to-all-done
  17.9 3.9 collective-permute-start.5
  22.5 5.5 multiply_sine_fusion
  32.6 4.2 collective-permute-done.6.refs_4_.refs_11_.refs_10_
  36.9 4.0 collective-permute-done.8.refs_5_.refs_12_.refs_11_
  40.8 3.6 collective-permute-done.1
  45.0 4.3 all-to-all-start.1
  51.8 7.3 %collective-permute-done.10.refs_6_.refs_13_.refs_12_ = bf16[208,768]{1,0:T(8,128)(2,1)S(1)} collective-permute-done((bf16[208,768]{1,0:T(8,128)(2,1)S(1)}, bf16[208,768]{1,0:T(8,128)(2,1)S(1)}, u32[]{:S(2)}, u32[]{:S(2)}) %collective-permute-start.10) | collective-permute-done | bytes 319520 | tf_op jit(solution)/shard_map/ppermute | solution.py:113
  61.6 3.7 all-to-all-done.1
  82.8 5.7 pad_maximum_fusion.refs_2_.refs_3_.refs_9_.refs_8_.refs_4_
  88.6 10.5 %shard_map.402 = (bf16[2048,256]{1,0:T(8,128)(2,1)S(1)}, bf16[2048,256]{1,0:T(8,128)(2,1)S(1)}, bf16[2048,256]{1,0:T(8,128)(2,1)S(1)}, f32[2048,512]{1,0:T(8,128)S(1)}, bf16[2048,1152]{1,0:T(8,128)(2,1)S(1)}) custom-call(s32[8]{0:T(128)S(1)} %fusion.21.refs_0_, s32[8]{0:T(128)S(1)} %fusion.24.refs_0_.refs_1_, ...), custom_call_target="tpu_custom_call" | custom-call | flops 226492416 | bytes 1634720 | tf_op jit(solution)/shard_map/pallas_call | solution.py:223
  112.1 5.6 shard_map.403
  123.8 23.4 %collective-permute-done.22.refs_6_.refs_15_ = bf16[144,3584]{1,0:T(8,128)(2,1)S(1)} collective-permute-done((bf16[144,3584]{1,0:T(8,128)(2,1)S(1)}, bf16[144,3584]{1,0:T(8,128)(2,1)S(1)}, u32[]{:S(2)}, u32[]{:S(2)}) %collective-permute-start.22) | collective-permute-done | bytes 1032224 | tf_op jit(solution)/shard_map/ppermute | solution.py:113
  154.0 11.7 %shard_map.404 = (f32[2048,1152]{1,0:T(8,128)}, bf16[2048,1152]{1,0:T(8,128)(2,1)S(1)}) custom-call(s32[8]{0:T(128)S(1)} %fusion.20.refs_0_, bf16[2048,256]{1,0:T(8,128)(2,1)S(1)} %get-tuple-element.135.refs_1_, bf16[2048,256]{1,0:T(8,128)(2,1)S(1)} %collective-permute-done.19.refs_2_, bf16[2048,256]{1,0:T(8,128)(2,1)S(1)} %collective-permute-done.20.refs_3_, ...), custom_call_target="tpu_custom_call" | custom-call | flops 301989888 | bytes 1590400 | tf_op jit(solution)/shard_map/pallas_call | solution.py:223
  165.7 6.5 %collective-permute-done.25.refs_7_.refs_16_ = bf16[144,3584]{1,0:T(8,128)(2,1)S(1)} collective-permute-done((bf16[144,3584]{1,0:T(8,128)(2,1)S(1)}, bf16[144,3584]{1,0:T(8,128)(2,1)S(1)}, u32[]{:S(2)}, u32[]{:S(2)}) %collective-permute-start.25) | collective-permute-done | bytes 1032224 | tf_op jit(solution)/shard_map/ppermute | solution.py:113
  175.9 21.7 %collective-permute-done.28.refs_7_.refs_8_ = bf16[224,1152]{1,0:T(8,128)(2,1)S(1)} collective-permute-done((bf16[224,1152]{1,0:T(8,128)(2,1)}, bf16[224,1152]{1,0:T(8,128)(2,1)S(1)}, u32[]{:S(2)}, u32[]{:S(2)}) %collective-permute-start.28) | collective-permute-done | bytes 516128 | tf_op jit(solution)/shard_map/ppermute | solution.py:113
  197.9 18.7 %shard_map.405 = (bf16[2048,1792]{1,0:T(8,128)(2,1)}, bf16[2048,3584]{1,0:T(8,128)(2,1)}) custom-call(s32[8]{0:T(128)S(1)} %fusion.24.refs_0_.refs_1_, bf16[2048,1152]{1,0:T(8,128)(2,1)S(1)} %get-tuple-element.150.refs_1_, bf16[144,3584]{1,0:T(8,128)(2,1)S(1)} %reshape.108.refs_2_.refs_11_, bf16[144,3584]{1,0:T(8,128)(2,1)S(1)} %collective-permute-done.13.refs_3_.refs_12_, ...), custom_call_target="tpu_custom_call" | custom-call | flops 528482304 | bytes 2187264 | tf_op jit(solution)/shard_map/pallas_call | solution.py:223
  220.1 7.4 %shard_map.406 = (bf16[512,1152]{1,0:T(8,128)(2,1)S(1)}, bf16[512,1152]{1,0:T(8,128)(2,1)S(1)}) custom-call(s32[8]{0:T(128)S(1)} %fusion.24.refs_0_.refs_1_, bf16[2048,1792]{1,0:T(8,128)(2,1)S(1)} %copy-done.1, bf16[224,1152]{1,0:T(8,128)(2,1)S(1)} %copy-done.27, bf16[224,1152]{1,0:T(8,128)(2,1)} %collective-permute-done.3.refs_3_.refs_4_, ...), custom_call_target="tpu_custom_call" | custom-call | flops 264241152 | bytes 864256 | tf_op jit(solution)/shard_map/pallas_call | solution.py:223
  237.0 19.2 %shard_map.407 = (bf16[2048,1792]{1,0:T(8,128)(2,1)}, bf16[2048,3584]{1,0:T(8,128)(2,1)}) custom-call(s32[8]{0:T(128)S(1)} %fusion.24.refs_0_.refs_1_, bf16[2048,1152]{1,0:T(8,128)(2,1)S(1)} %get-tuple-element.150.refs_1_, bf16[144,3584]{1,0:T(8,128)(2,1)S(1)} %reshape.108.refs_2_.refs_11_, ...), custom_call_target="tpu_custom_call", output_to_operand_aliasing={{0}: (10, {}), {1}: (11, {})} | custom-call | flops 528482304 | bytes 2187264 | tf_op jit(solution)/shard_map/pallas_call | solution.py:223
  265.1 7.4 %shard_map.408 = (bf16[512,1152]{1,0:T(8,128)(2,1)S(1)}, bf16[512,1152]{1,0:T(8,128)(2,1)S(1)}) custom-call(s32[8]{0:T(128)S(1)} %fusion.24.refs_0_.refs_1_, bf16[2048,1792]{1,0:T(8,128)(2,1)S(1)} %copy-done.2, bf16[224,1152]{1,0:T(8,128)(2,1)S(1)} %copy-done.27, bf16[224,1152]{1,0:T(8,128)(2,1)} %collective-permute-done.3.refs_3_.refs_4_, ...), custom_call_target="tpu_custom_call" | custom-call | flops 264241152 | bytes 864256 | tf_op jit(solution)/shard_map/pallas_call | solution.py:223
  275.5 4.4 shard_map.409
  283.0 12.2 %shard_map.410.refs_11_ = bf16[2048,3584]{1,0:T(8,128)(2,1)} custom-call(s32[8]{0:T(128)S(1)} %fusion.24.refs_0_.refs_1_, bf16[1024,1152]{1,0:T(8,128)(2,1)S(1)} %pad_maximum_fusion.2.refs_1_, bf16[2048,3584]{1,0:T(8,128)(2,1)} %get-tuple-element.161.refs_2_, bf16[224,1152]{1,0:T(8,128)(2,1)S(1)} %copy-done.27, ...), custom_call_target="tpu_custom_call" | custom-call | flops 264241152 | bytes 2240512 | tf_op jit(solution)/shard_map/pallas_call | solution.py:223
  295.2 13.1 %collective-permute-done.34 = bf16[512,1152]{1,0:T(8,128)(2,1)S(1)} collective-permute-done((bf16[512,1152]{1,0:T(8,128)(2,1)S(1)}, bf16[512,1152]{1,0:T(8,128)(2,1)S(1)}, u32[]{:S(2)}, u32[]{:S(2)}) %collective-permute-start.34) | collective-permute-done | bytes 1179680 | tf_op jit(solution)/shard_map/ppermute | solution.py:47
  312.4 12.7 %shard_map.411.refs_2_ = bf16[2048,3584]{1,0:T(8,128)(2,1)} custom-call(s32[8]{0:T(128)S(1)} %fusion.24.refs_0_.refs_1_, bf16[1024,1152]{1,0:T(8,128)(2,1)S(1)} %pad_maximum_fusion.3.refs_1_, bf16[2048,3584]{1,0:T(8,128)(2,1)} %get-tuple-element.161.refs_2_, bf16[224,1152]{1,0:T(8,128)(2,1)S(1)} %copy-done.27, ...), custom_call_target="tpu_custom_call", output_to_operand_aliasing={{}: (11, {})} | custom-call | flops 264241152 | bytes 2240512 | tf_op jit(solution)/shard_map/pallas_call | solution.py:223
  325.1 23.2 %convolution_convert_fusion = bf16[1152,3584]{1,0:T(8,128)(2,1)} fusion(bf16[2048,1152]{1,0:T(8,128)(2,1)S(1)} %bitcast.78, bf16[2048,3584]{1,0:T(8,128)(2,1)} %shard_map.411.refs_2_), kind=kOutput, calls=%fused_computation | convolution fusion | flops 16915562496 | bytes 27656192 | tf_op jit(solution)/shard_map/dot_general | solution.py:211
  348.3 4.9 constant_dynamic-slice_fusion.6
  355.7 26.3 %shard_map.412 = (bf16[2048,1152]{1,0:T(8,128)(2,1)S(1)}, bf16[2048,1152]{1,0:T(8,128)(2,1)}, bf16[2,1024,256]{2,1,0:T(8,128)(2,1)S(1)}, bf16[2,1024,256]{2,1,0:T(8,128)(2,1)S(1)}, f32[2,1152]{1,0:T(2,128)S(1)}) custom-call(s32[8]{0:T(128)S(1)} %fusion.20.refs_0_, s32[8]{0:T(128)S(1)} %fusion.24.refs_0_.refs_1_, bf16[2048,3584]{1,0:T(8,128)(2,1)} %shard_map.411.refs_2_, ...), custom_call_target="tpu_custom_call" | custom-call | flops 679477248 | bytes 3262144 | tf_op jit(solution)/shard_map/pallas_call | solution.py:223
  382.1 3.8 dynamic-slice_add_fusion.4
  392.8 12.5 %convolution_convert_fusion.1 = bf16[1792,1152]{1,0:T(8,128)(2,1)S(1)} fusion(bf16[2048,1792]{1,0:T(8,128)(2,1)S(1)} %bitcast.76, bf16[2048,1152]{1,0:T(8,128)(2,1)} %pad_maximum_fusion.1), kind=kOutput, calls=%fused_computation.1 | convolution fusion | flops 8457781248 | bytes 16187392 | tf_op jit(solution)/shard_map/dot_general | solution.py:211
  409.3 25.6 %shard_map.413 = (bf16[2048,1152]{1,0:T(8,128)(2,1)S(1)}, bf16[2048,1152]{1,0:T(8,128)(2,1)}, bf16[2,1024,256]{2,1,0:T(8,128)(2,1)S(1)}, bf16[2,1024,256]{2,1,0:T(8,128)(2,1)S(1)}, f32[2,1152]{1,0:T(2,128)S(1)}) custom-call(s32[8]{0:T(128)S(1)} %fusion.20.refs_0_, s32[8]{0:T(128)S(1)} %fusion.24.refs_0_.refs_1_, ...), custom_call_target="tpu_custom_call", output_to_operand_aliasing={{0}: (19, {}), {1}: (20, {})} | custom-call | flops 679477248 | bytes 3262144 | tf_op jit(solution)/shard_map/pallas_call | solution.py:223
  438.1 4.7 dynamic-slice_add_fusion.2
  456.1 5.7 collective-permute-done.44.refs_8_
  463.2 12.3 %shard_map.414 = (bf16[2048,768]{1,0:T(8,128)(2,1)S(1)}, f32[2,256]{1,0:T(2,128)S(1)}) custom-call(s32[3]{0:T(128)S(1)} %fusion.17.refs_0_, bf16[2048,256]{1,0:T(8,128)(2,1)S(1)} %copy-done.56, bf16[2048,256]{1,0:T(8,128)(2,1)S(1)} %copy-done.59, bf16[2048,256]{1,0:T(8,128)(2,1)S(1)} %copy-done.62, f32[2048,512]{1,0:T(8,128)} %copy-done.53, ...), custom_call_target="tpu_custom_call" | custom-call | flops 251658240 | bytes 1114880 | tf_op jit(solution)/shard_map/pallas_call | solution.py:223
  475.5 4.2 convolution_convert_fusion.2
  484.9 4.8 dynamic-slice_add_fusion
  497.7 12.5 %shard_map.415 = (bf16[1024,1152]{1,0:T(8,128)(2,1)S(1)}, bf16[1024,1152]{1,0:T(8,128)(2,1)}, f32[1,1152]{1,0:T(1,128)S(1)}) custom-call(s32[8]{0:T(128)S(1)} %compare_select_fusion.1.refs_0_, s32[8]{0:T(128)S(1)} %fusion.24.refs_0_.refs_1_, bf16[2048,768]{1,0:T(8,128)(2,1)S(1)} %get-tuple-element.188.refs_2_.refs_3_, ...), custom_call_target="tpu_custom_call" | custom-call | flops 226492416 | bytes 1438272 | tf_op jit(solution)/shard_map/pallas_call | solution.py:223
  511.6 10.1 %collective-permute-done.55 = bf16[192,768]{1,0:T(8,128)(2,1)S(1)} collective-permute-done((bf16[192,768]{1,0:T(8,128)(2,1)S(1)}, bf16[192,768]{1,0:T(8,128)(2,1)S(1)}, u32[]{:S(2)}, u32[]{:S(2)}) %collective-permute-start.55) | collective-permute-done | bytes 294944 | tf_op jit(solution)/shard_map/ppermute | solution.py:113
  527.9 4.3 collective-permute-done.61
  541.5 4.5 collective-permute-done.57
  552.3 3.5 all-to-all-start.2
  556.0 4.6 collective-permute-done.62
  560.6 3.8 multiply_reduce_fusion.1
  564.4 7.0 %all-to-all-done.2.refs_0_ = bf16[4,36,3584]{2,1,0:T(8,128)(2,1)S(1)} async-done(((bf16[4,36,3584]{2,1,0:T(8,128)(2,1)}), bf16[4,36,3584]{2,1,0:T(8,128)(2,1)S(1)}, u32[]{:S(2)}, u32[]{:S(2)}) %all-to-all-start.2) | async-done | bytes 1032224 | tf_op jit(solution)/shard_map/all_to_all | solution.py:42
  576.4 4.9 all-to-all-done.3
  604.6 8.1 %collective-permute-done.65 = bf16[512,1152]{1,0:T(8,128)(2,1)} collective-permute-done((bf16[512,1152]{1,0:T(8,128)(2,1)}, bf16[512,1152]{1,0:T(8,128)(2,1)}, u32[]{:S(2)}, u32[]{:S(2)}) %collective-permute-start.65) | collective-permute-done | bytes 1179680 | tf_op jit(solution)/shard_map/ppermute | solution.py:47
  613.6 3.8 add_bitcast_fusion
  620.6 4.0 multiply_subtract_fusion.1
  625.6 3.9 multiply_subtract_fusion
  (522 shorter events, 203.5 us)
Async XLA Ops:
  2.2 15.2 %collective-permute-start.3 = (bf16[224,1152]{1,0:T(8,128)(2,1)S(1)}, bf16[224,1152]{1,0:T(8,128)(2,1)}, u32[]{:S(2)}, u32[]{:S(2)}) collective-permute-start(bf16[224,1152]{1,0:T(8,128)(2,1)S(1)} %pad.13.refs_2_.refs_3_), channel_id=1, source_target_pairs={{0,8},{1,5},{2,10},{3,7},{8,16},{9,1},{10,18},{11,3},{16,24},{17,9... | collective-permute-start | bytes 1548296 | tf_op jit(solution)/shard_map/ppermute | solution.py:113
  5.3 12.6 %collective-permute-start.4 = (bf16[224,1152]{1,0:T(8,128)(2,1)S(1)}, bf16[224,1152]{1,0:T(8,128)(2,1)}, u32[]{:S(2)}, u32[]{:S(2)}) collective-permute-start(bf16[224,1152]{1,0:T(8,128)(2,1)S(1)} %pad.13.refs_2_.refs_3_), channel_id=1, source_target_pairs={{0,4},{1,9},{2,6},{3,11},{8,0},{9,17},{10,2},{11,19},{16,8},{17,25... | collective-permute-start | bytes 1548296 | tf_op jit(solution)/shard_map/ppermute | solution.py:113
  15.7 28.8 %collective-permute-start.1 = (bf16[512,1152]{1,0:T(8,128)(2,1)}, bf16[512,1152]{1,0:T(8,128)(2,1)}, u32[]{:S(2)}, u32[]{:S(2)}) collective-permute-start(bf16[512,1152]{1,0:T(8,128)(2,1)} %bitcast.2.refs_4_), channel_id=1, source_target_pairs={{0,2},{1,3},{2,0},{3,1},{4,6},{5,7},{6,4},{7,5},{8,10},{9,11},{10,... | collective-permute-start | bytes 3538952 | tf_op jit(solution)/shard_map/ppermute | solution.py:47
  44.5 23.7 %collective-permute-start.9 = (bf16[512,1152]{1,0:T(8,128)(2,1)}, bf16[512,1152]{1,0:T(8,128)(2,1)}, u32[]{:S(2)}, u32[]{:S(2)}) collective-permute-start(bf16[512,1152]{1,0:T(8,128)(2,1)} %collective-permute-done.1), channel_id=1, source_target_pairs={{0,1},{1,0},{2,3},{3,2},{4,5},{5,4},{6,7},{7,6},{8,9},{9,8},{10,11... | collective-permute-start | bytes 3538952 | tf_op jit(solution)/shard_map/ppermute | solution.py:47
  44.7 38.2 %collective-permute-start = (bf16[512,1152]{1,0:T(8,128)(2,1)}, bf16[512,1152]{1,0:T(8,128)(2,1)}, u32[]{:S(2)}, u32[]{:S(2)}) collective-permute-start(bf16[512,1152]{1,0:T(8,128)(2,1)} %bitcast.2.refs_4_), channel_id=1, source_target_pairs={{0,1},{1,0},{2,3},{3,2},{4,5},{5,4},{6,7},{7,6},{8,9},{9,8},{10,11... | collective-permute-start | bytes 3538952 | tf_op jit(solution)/shard_map/ppermute | solution.py:47
  45.0 20.3 %all-to-all-start.1 = ((bf16[4,36,3584]{2,1,0:T(8,128)(2,1)}), bf16[4,36,3584]{2,1,0:T(8,128)(2,1)}, u32[]{:S(2)}, u32[]{:S(2)}) async-start(bf16[4,36,3584]{2,1,0:T(8,128)(2,1)} %shard_map.400), calls=%async_computation.1 | async-start | bytes 2293760 | tf_op jit(solution)/shard_map/all_to_all | solution.py:42
  51.3 15.4 %collective-permute-start.11 = (bf16[208,768]{1,0:T(8,128)(2,1)S(1)}, bf16[208,768]{1,0:T(8,128)(2,1)S(1)}, u32[]{:S(2)}, u32[]{:S(2)}) collective-permute-start(bf16[208,768]{1,0:T(8,128)(2,1)S(1)} %collective-permute-done.8.refs_5_.refs_12_.refs_11_), channel_id=1, source_target_pairs={{0,4},{1,9},{2,6},{3,11},{8,0},{9,17},{10,2},{11,19},{16,8},{17,25... | collective-permute-start | bytes 958472 | tf_op jit(solution)/shard_map/ppermute | solution.py:113
  68.2 38.0 %collective-permute-start.13 = (bf16[144,3584]{1,0:T(8,128)(2,1)S(1)}, bf16[144,3584]{1,0:T(8,128)(2,1)S(1)}, u32[]{:S(2)}, u32[]{:S(2)}) collective-permute-start(bf16[144,3584]{1,0:T(8,128)(2,1)S(1)} %reshape.108.refs_2_.refs_11_), channel_id=1, source_target_pairs={{0,8},{1,5},{2,10},{3,7},{8,16},{9,1},{10,18},{11,3},{16,24},{17,9... | collective-permute-start | bytes 3096584 | tf_op jit(solution)/shard_map/ppermute | solution.py:113
  69.6 36.5 %collective-permute-start.14 = (bf16[144,3584]{1,0:T(8,128)(2,1)S(1)}, bf16[144,3584]{1,0:T(8,128)(2,1)S(1)}, u32[]{:S(2)}, u32[]{:S(2)}) collective-permute-start(bf16[144,3584]{1,0:T(8,128)(2,1)S(1)} %reshape.108.refs_2_.refs_11_), channel_id=1, source_target_pairs={{0,4},{1,9},{2,6},{3,11},{8,0},{9,17},{10,2},{11,19},{16,8},{17,25... | collective-permute-start | bytes 3096584 | tf_op jit(solution)/shard_map/ppermute | solution.py:113
  81.5 26.9 %collective-permute-start.15 = (bf16[256,1152]{1,0:T(8,128)(2,1)}, bf16[256,1152]{1,0:T(8,128)(2,1)}, u32[]{:S(2)}, u32[]{:S(2)}) collective-permute-start(bf16[256,1152]{1,0:T(8,128)(2,1)} %get-tuple-element.128.refs_5_.refs_3_), channel_id=1, source_target_pairs={{0,2},{1,3},{2,0},{3,1},{4,6},{5,7},{6,4},{7,5},{8,10},{9,11},{10,... | collective-permute-start | bytes 1769480 | tf_op jit(solution)/shard_map/ppermute | solution.py:47
  82.8 25.7 %collective-permute-start.16 = (bf16[256,1152]{1,0:T(8,128)(2,1)}, bf16[256,1152]{1,0:T(8,128)(2,1)}, u32[]{:S(2)}, u32[]{:S(2)}) collective-permute-start(bf16[256,1152]{1,0:T(8,128)(2,1)} %get-tuple-element.128.refs_5_.refs_3_), channel_id=1, source_target_pairs={{0,1},{1,0},{2,3},{3,2},{4,5},{5,4},{6,7},{7,6},{8,9},{9,8},{10,11... | collective-permute-start | bytes 1769480 | tf_op jit(solution)/shard_map/ppermute | solution.py:47
  106.2 14.1 %collective-permute-start.18 = (bf16[224,1152]{1,0:T(8,128)(2,1)}, bf16[224,1152]{1,0:T(8,128)(2,1)}, u32[]{:S(2)}, u32[]{:S(2)}) collective-permute-start(bf16[224,1152]{1,0:T(8,128)(2,1)} %collective-permute-done.4.refs_4_.refs_5_), channel_id=1, source_target_pairs={{0,4},{1,9},{2,6},{3,11},{8,0},{9,17},{10,2},{11,19},{16,8},{17,25... | collective-permute-start | bytes 1548296 | tf_op jit(solution)/shard_map/ppermute | solution.py:113
  108.1 12.7 %collective-permute-start.17 = (bf16[224,1152]{1,0:T(8,128)(2,1)}, bf16[224,1152]{1,0:T(8,128)(2,1)}, u32[]{:S(2)}, u32[]{:S(2)}) collective-permute-start(bf16[224,1152]{1,0:T(8,128)(2,1)} %collective-permute-done.3.refs_3_.refs_4_), channel_id=1, source_target_pairs={{0,8},{1,5},{2,10},{3,7},{8,16},{9,1},{10,18},{11,3},{16,24},{17,9... | collective-permute-start | bytes 1548296 | tf_op jit(solution)/shard_map/ppermute | solution.py:113
  120.8 26.4 %collective-permute-start.20 = (bf16[2048,256]{1,0:T(8,128)(2,1)S(1)}, bf16[2048,256]{1,0:T(8,128)(2,1)S(1)}, u32[]{:S(2)}, u32[]{:S(2)}) collective-permute-start(bf16[2048,256]{1,0:T(8,128)(2,1)S(1)} %get-tuple-element.135.refs_1_), channel_id=1, source_target_pairs={{0,2},{1,3},{2,0},{3,1},{4,6},{5,7},{6,4},{7,5},{8,10},{9,11},{10,... | collective-permute-start | bytes 3145736 | tf_op jit(solution)/shard_map/ppermute | solution.py:47
  121.8 25.4 %collective-permute-start.22 = (bf16[144,3584]{1,0:T(8,128)(2,1)S(1)}, bf16[144,3584]{1,0:T(8,128)(2,1)S(1)}, u32[]{:S(2)}, u32[]{:S(2)}) collective-permute-start(bf16[144,3584]{1,0:T(8,128)(2,1)S(1)} %collective-permute-done.14.refs_4_.refs_13_), channel_id=1, source_target_pairs={{0,4},{1,9},{2,6},{3,11},{8,0},{9,17},{10,2},{11,19},{16,8},{17,25... | collective-permute-start | bytes 3096584 | tf_op jit(solution)/shard_map/ppermute | solution.py:113
  123.6 23.6 %collective-permute-start.21 = (bf16[144,3584]{1,0:T(8,128)(2,1)S(1)}, bf16[144,3584]{1,0:T(8,128)(2,1)S(1)}, u32[]{:S(2)}, u32[]{:S(2)}) collective-permute-start(bf16[144,3584]{1,0:T(8,128)(2,1)S(1)} %collective-permute-done.13.refs_3_.refs_12_), channel_id=1, source_target_pairs={{0,8},{1,5},{2,10},{3,7},{8,16},{9,1},{10,18},{11,3},{16,24},{17,9... | collective-permute-start | bytes 3096584 | tf_op jit(solution)/shard_map/ppermute | solution.py:113
  123.8 27.2 %collective-permute-start.19 = (bf16[2048,256]{1,0:T(8,128)(2,1)S(1)}, bf16[2048,256]{1,0:T(8,128)(2,1)S(1)}, u32[]{:S(2)}, u32[]{:S(2)}) collective-permute-start(bf16[2048,256]{1,0:T(8,128)(2,1)S(1)} %get-tuple-element.135.refs_1_), channel_id=1, source_target_pairs={{0,1},{1,0},{2,3},{3,2},{4,5},{5,4},{6,7},{7,6},{8,9},{9,8},{10,11... | collective-permute-start | bytes 3145736 | tf_op jit(solution)/shard_map/ppermute | solution.py:47
  147.4 24.8 %collective-permute-start.25 = (bf16[144,3584]{1,0:T(8,128)(2,1)S(1)}, bf16[144,3584]{1,0:T(8,128)(2,1)S(1)}, u32[]{:S(2)}, u32[]{:S(2)}) collective-permute-start(bf16[144,3584]{1,0:T(8,128)(2,1)S(1)} %collective-permute-done.21.refs_5_.refs_14_), channel_id=1, source_target_pairs={{0,8},{1,5},{2,10},{3,7},{8,16},{9,1},{10,18},{11,3},{16,24},{17,9... | collective-permute-start | bytes 3096584 | tf_op jit(solution)/shard_map/ppermute | solution.py:113
  148.6 49.2 %collective-permute-start.26 = (bf16[144,3584]{1,0:T(8,128)(2,1)S(1)}, bf16[144,3584]{1,0:T(8,128)(2,1)S(1)}, u32[]{:S(2)}, u32[]{:S(2)}) collective-permute-start(bf16[144,3584]{1,0:T(8,128)(2,1)S(1)} %collective-permute-done.22.refs_6_.refs_15_), channel_id=1, source_target_pairs={{0,4},{1,9},{2,6},{3,11},{8,0},{9,17},{10,2},{11,19},{16,8},{17,25... | collective-permute-start | bytes 3096584 | tf_op jit(solution)/shard_map/ppermute | solution.py:113
  172.2 25.6 %collective-permute-start.27 = (bf16[144,3584]{1,0:T(8,128)(2,1)S(1)}, bf16[144,3584]{1,0:T(8,128)(2,1)S(1)}, u32[]{:S(2)}, u32[]{:S(2)}) collective-permute-start(bf16[144,3584]{1,0:T(8,128)(2,1)S(1)} %collective-permute-done.25.refs_7_.refs_16_), channel_id=1, source_target_pairs={{0,8},{1,5},{2,10},{3,7},{8,16},{9,1},{10,18},{11,3},{16,24},{17,9... | collective-permute-start | bytes 3096584 | tf_op jit(solution)/shard_map/ppermute | solution.py:113
  173.4 24.2 %collective-permute-start.28 = (bf16[224,1152]{1,0:T(8,128)(2,1)}, bf16[224,1152]{1,0:T(8,128)(2,1)S(1)}, u32[]{:S(2)}, u32[]{:S(2)}) collective-permute-start(bf16[224,1152]{1,0:T(8,128)(2,1)} %collective-permute-done.17.refs_5_.refs_6_), channel_id=1, source_target_pairs={{0,8},{1,5},{2,10},{3,7},{8,16},{9,1},{10,18},{11,3},{16,24},{17,9... | collective-permute-start | bytes 1548296 | tf_op jit(solution)/shard_map/ppermute | solution.py:113
  175.9 40.8 %collective-permute-start.29 = (bf16[224,1152]{1,0:T(8,128)(2,1)}, bf16[224,1152]{1,0:T(8,128)(2,1)S(1)}, u32[]{:S(2)}, u32[]{:S(2)}) collective-permute-start(bf16[224,1152]{1,0:T(8,128)(2,1)} %collective-permute-done.18.refs_6_.refs_7_), channel_id=1, source_target_pairs={{0,4},{1,9},{2,6},{3,11},{8,0},{9,17},{10,2},{11,19},{16,8},{17,25... | collective-permute-start | bytes 1548296 | tf_op jit(solution)/shard_map/ppermute | solution.py:113
  197.5 19.1 %collective-permute-start.30 = (bf16[224,1152]{1,0:T(8,128)(2,1)S(1)}, bf16[224,1152]{1,0:T(8,128)(2,1)S(1)}, u32[]{:S(2)}, u32[]{:S(2)}) collective-permute-start(bf16[224,1152]{1,0:T(8,128)(2,1)S(1)} %collective-permute-done.28.refs_7_.refs_8_), channel_id=1, source_target_pairs={{0,8},{1,5},{2,10},{3,7},{8,16},{9,1},{10,18},{11,3},{16,24},{17,9... | collective-permute-start | bytes 1548296 | tf_op jit(solution)/shard_map/ppermute | solution.py:113
  230.8 28.1 %collective-permute-start.32 = (bf16[512,1152]{1,0:T(8,128)(2,1)S(1)}, bf16[512,1152]{1,0:T(8,128)(2,1)S(1)}, u32[]{:S(2)}, u32[]{:S(2)}) collective-permute-start(bf16[512,1152]{1,0:T(8,128)(2,1)S(1)} %add.264), channel_id=1, source_target_pairs={{0,2},{1,3},{2,0},{3,1},{4,6},{5,7},{6,4},{7,5},{8,10},{9,11},{10,... | collective-permute-start | bytes 3538952 | tf_op jit(solution)/shard_map/ppermute | solution.py:47
  280.1 28.3 %collective-permute-start.34 = (bf16[512,1152]{1,0:T(8,128)(2,1)S(1)}, bf16[512,1152]{1,0:T(8,128)(2,1)S(1)}, u32[]{:S(2)}, u32[]{:S(2)}) collective-permute-start(bf16[512,1152]{1,0:T(8,128)(2,1)S(1)} %get-tuple-element.160), channel_id=1, source_target_pairs={{0,2},{1,3},{2,0},{3,1},{4,6},{5,7},{6,4},{7,5},{8,10},{9,11},{10,... | collective-permute-start | bytes 3538952 | tf_op jit(solution)/shard_map/ppermute | solution.py:47
  353.1 28.9 %collective-permute-start.37 = (bf16[144,3584]{1,0:T(8,128)(2,1)S(1)}, bf16[144,3584]{1,0:T(8,128)(2,1)S(1)}, u32[]{:S(2)}, u32[]{:S(2)}) collective-permute-start(bf16[144,3584]{1,0:T(8,128)(2,1)S(1)} %get-tuple-element.236), channel_id=1, source_target_pairs={{0,8},{1,5},{2,10},{3,7},{8,16},{9,1},{10,18},{11,3},{16,24},{17,9... | collective-permute-start | bytes 3096584 | tf_op jit(solution)/shard_map/ppermute | solution.py:113
  386.8 48.2 %collective-permute-start.41 = (bf16[144,3584]{1,0:T(8,128)(2,1)}, bf16[144,3584]{1,0:T(8,128)(2,1)}, u32[]{:S(2)}, u32[]{:S(2)}) collective-permute-start(bf16[144,3584]{1,0:T(8,128)(2,1)} %get-tuple-element.235), channel_id=1, source_target_pairs={{0,4},{1,9},{2,6},{3,11},{8,0},{9,17},{10,2},{11,19},{16,8},{17,25... | collective-permute-start | bytes 3096584 | tf_op jit(solution)/shard_map/ppermute | solution.py:113
  390.0 45.0 %collective-permute-start.40 = (bf16[144,3584]{1,0:T(8,128)(2,1)}, bf16[144,3584]{1,0:T(8,128)(2,1)S(1)}, u32[]{:S(2)}, u32[]{:S(2)}) collective-permute-start(bf16[144,3584]{1,0:T(8,128)(2,1)} %dynamic-slice_add_fusion.4), channel_id=1, source_target_pairs={{0,8},{1,5},{2,10},{3,7},{8,16},{9,1},{10,18},{11,3},{16,24},{17,9... | collective-permute-start | bytes 3096584 | tf_op jit(solution)/shard_map/ppermute | solution.py:113
  391.8 17.4 %collective-permute-start.39 = (bf16[1024,256]{1,0:T(8,128)(2,1)S(1)}, bf16[1024,256]{1,0:T(8,128)(2,1)S(1)}, u32[]{:S(2)}, u32[]{:S(2)}) collective-permute-start(bf16[1024,256]{1,0:T(8,128)(2,1)S(1)} %fusion.3), channel_id=1, source_target_pairs={{0,2},{1,3},{2,0},{3,1},{4,6},{5,7},{6,4},{7,5},{8,10},{9,11},{10,... | collective-permute-start | bytes 1572872 | tf_op jit(solution)/shard_map/ppermute | solution.py:47
  407.8 27.2 %collective-permute-start.42 = (bf16[224,1152]{1,0:T(8,128)(2,1)S(1)}, bf16[224,1152]{1,0:T(8,128)(2,1)S(1)}, u32[]{:S(2)}, u32[]{:S(2)}) collective-permute-start(bf16[224,1152]{1,0:T(8,128)(2,1)S(1)} %get-tuple-element.242), channel_id=1, source_target_pairs={{0,8},{1,5},{2,10},{3,7},{8,16},{9,1},{10,18},{11,3},{16,24},{17,9... | collective-permute-start | bytes 1548296 | tf_op jit(solution)/shard_map/ppermute | solution.py:113
  446.7 35.3 %collective-permute-start.51 = (bf16[224,1152]{1,0:T(8,128)(2,1)}, bf16[224,1152]{1,0:T(8,128)(2,1)}, u32[]{:S(2)}, u32[]{:S(2)}) collective-permute-start(bf16[224,1152]{1,0:T(8,128)(2,1)} %get-tuple-element.241), channel_id=1, source_target_pairs={{0,4},{1,9},{2,6},{3,11},{8,0},{9,17},{10,2},{11,19},{16,8},{17,25... | collective-permute-start | bytes 1548296 | tf_op jit(solution)/shard_map/ppermute | solution.py:113
  447.3 14.5 %collective-permute-start.44 = (bf16[1024,256]{1,0:T(8,128)(2,1)S(1)}, bf16[1024,256]{1,0:T(8,128)(2,1)S(1)}, u32[]{:S(2)}, u32[]{:S(2)}) collective-permute-start(bf16[1024,256]{1,0:T(8,128)(2,1)S(1)} %fusion.2), channel_id=1, source_target_pairs={{0,2},{1,3},{2,0},{3,1},{4,6},{5,7},{6,4},{7,5},{8,10},{9,11},{10,... | collective-permute-start | bytes 1572872 | tf_op jit(solution)/shard_map/ppermute | solution.py:47
  450.1 31.9 %collective-permute-start.50 = (bf16[224,1152]{1,0:T(8,128)(2,1)}, bf16[224,1152]{1,0:T(8,128)(2,1)}, u32[]{:S(2)}, u32[]{:S(2)}) collective-permute-start(bf16[224,1152]{1,0:T(8,128)(2,1)} %dynamic-slice_add_fusion.9), channel_id=1, source_target_pairs={{0,8},{1,5},{2,10},{3,7},{8,16},{9,1},{10,18},{11,3},{16,24},{17,9... | collective-permute-start | bytes 1548296 | tf_op jit(solution)/shard_map/ppermute | solution.py:113
  451.7 31.2 %collective-permute-start.48 = (bf16[144,3584]{1,0:T(8,128)(2,1)S(1)}, bf16[144,3584]{1,0:T(8,128)(2,1)}, u32[]{:S(2)}, u32[]{:S(2)}) collective-permute-start(bf16[144,3584]{1,0:T(8,128)(2,1)S(1)} %get-tuple-element.234), channel_id=1, source_target_pairs={{0,8},{1,5},{2,10},{3,7},{8,16},{9,1},{10,18},{11,3},{16,24},{17,9... | collective-permute-start | bytes 3096584 | tf_op jit(solution)/shard_map/ppermute | solution.py:113
  453.2 29.6 %collective-permute-start.49 = (bf16[144,3584]{1,0:T(8,128)(2,1)S(1)}, bf16[144,3584]{1,0:T(8,128)(2,1)}, u32[]{:S(2)}, u32[]{:S(2)}) collective-permute-start(bf16[144,3584]{1,0:T(8,128)(2,1)S(1)} %get-tuple-element.233), channel_id=1, source_target_pairs={{0,4},{1,9},{2,6},{3,11},{8,0},{9,17},{10,2},{11,19},{16,8},{17,25... | collective-permute-start | bytes 3096584 | tf_op jit(solution)/shard_map/ppermute | solution.py:113
  461.8 17.8 %collective-permute-start.46 = (bf16[256,1152]{1,0:T(8,128)(2,1)}, bf16[256,1152]{1,0:T(8,128)(2,1)S(1)}, u32[]{:S(2)}, u32[]{:S(2)}) collective-permute-start(bf16[256,1152]{1,0:T(8,128)(2,1)} %slice_add_fusion.1), channel_id=1, source_target_pairs={{0,2},{1,3},{2,0},{3,1},{4,6},{5,7},{6,4},{7,5},{8,10},{9,11},{10,... | collective-permute-start | bytes 1769480 | tf_op jit(solution)/shard_map/ppermute | solution.py:47
  482.8 11.9 %collective-permute-start.47 = (bf16[192,768]{1,0:T(8,128)(2,1)S(1)}, bf16[192,768]{1,0:T(8,128)(2,1)S(1)}, u32[]{:S(2)}, u32[]{:S(2)}) collective-permute-start(bf16[192,768]{1,0:T(8,128)(2,1)S(1)} %get-tuple-element.248), channel_id=1, source_target_pairs={{0,8},{1,5},{2,10},{3,7},{8,16},{9,1},{10,18},{11,3},{16,24},{17,9... | collective-permute-start | bytes 884744 | tf_op jit(solution)/shard_map/ppermute | solution.py:113
  484.2 26.1 %collective-permute-start.58 = (bf16[192,768]{1,0:T(8,128)(2,1)S(1)}, bf16[192,768]{1,0:T(8,128)(2,1)S(1)}, u32[]{:S(2)}, u32[]{:S(2)}) collective-permute-start(bf16[192,768]{1,0:T(8,128)(2,1)S(1)} %get-tuple-element.247), channel_id=1, source_target_pairs={{0,4},{1,9},{2,6},{3,11},{8,0},{9,17},{10,2},{11,19},{16,8},{17,25... | collective-permute-start | bytes 884744 | tf_op jit(solution)/shard_map/ppermute | solution.py:113
  489.7 33.5 %collective-permute-start.52 = (bf16[144,3584]{1,0:T(8,128)(2,1)S(1)}, bf16[144,3584]{1,0:T(8,128)(2,1)S(1)}, u32[]{:S(2)}, u32[]{:S(2)}) collective-permute-start(bf16[144,3584]{1,0:T(8,128)(2,1)S(1)} %get-tuple-element.232), channel_id=1, source_target_pairs={{0,8},{1,5},{2,10},{3,7},{8,16},{9,1},{10,18},{11,3},{16,24},{17,9... | collective-permute-start | bytes 3096584 | tf_op jit(solution)/shard_map/ppermute | solution.py:113
  491.1 32.2 %collective-permute-start.53 = (bf16[144,3584]{1,0:T(8,128)(2,1)S(1)}, bf16[144,3584]{1,0:T(8,128)(2,1)S(1)}, u32[]{:S(2)}, u32[]{:S(2)}) collective-permute-start(bf16[144,3584]{1,0:T(8,128)(2,1)S(1)} %get-tuple-element.231), channel_id=1, source_target_pairs={{0,4},{1,9},{2,6},{3,11},{8,0},{9,17},{10,2},{11,19},{16,8},{17,25... | collective-permute-start | bytes 3096584 | tf_op jit(solution)/shard_map/ppermute | solution.py:113
  495.5 26.3 %collective-permute-start.55 = (bf16[192,768]{1,0:T(8,128)(2,1)S(1)}, bf16[192,768]{1,0:T(8,128)(2,1)S(1)}, u32[]{:S(2)}, u32[]{:S(2)}) collective-permute-start(bf16[192,768]{1,0:T(8,128)(2,1)S(1)} %dynamic-slice_add_fusion.14), channel_id=1, source_target_pairs={{0,8},{1,5},{2,10},{3,7},{8,16},{9,1},{10,18},{11,3},{16,24},{17,9... | collective-permute-start | bytes 884744 | tf_op jit(solution)/shard_map/ppermute | solution.py:113
  496.8 31.1 %collective-permute-start.63 = (bf16[224,1152]{1,0:T(8,128)(2,1)S(1)}, bf16[224,1152]{1,0:T(8,128)(2,1)S(1)}, u32[]{:S(2)}, u32[]{:S(2)}) collective-permute-start(bf16[224,1152]{1,0:T(8,128)(2,1)S(1)} %get-tuple-element.239), channel_id=1, source_target_pairs={{0,4},{1,9},{2,6},{3,11},{8,0},{9,17},{10,2},{11,19},{16,8},{17,25... | collective-permute-start | bytes 1548296 | tf_op jit(solution)/shard_map/ppermute | solution.py:113
  510.3 22.0 %collective-permute-start.61 = (bf16[224,1152]{1,0:T(8,128)(2,1)S(1)}, bf16[224,1152]{1,0:T(8,128)(2,1)S(1)}, u32[]{:S(2)}, u32[]{:S(2)}) collective-permute-start(bf16[224,1152]{1,0:T(8,128)(2,1)S(1)} %get-tuple-element.240), channel_id=1, source_target_pairs={{0,8},{1,5},{2,10},{3,7},{8,16},{9,1},{10,18},{11,3},{16,24},{17,9... | collective-permute-start | bytes 1548296 | tf_op jit(solution)/shard_map/ppermute | solution.py:113
  532.2 49.9 %collective-permute-start.54 = (bf16[1024,1152]{1,0:T(8,128)(2,1)}, bf16[1024,1152]{1,0:T(8,128)(2,1)}, u32[]{:S(2)}, u32[]{:S(2)}) collective-permute-start(bf16[1024,1152]{1,0:T(8,128)(2,1)} %get-tuple-element.192), channel_id=1, source_target_pairs={{0,1},{1,0},{2,3},{3,2},{4,5},{5,4},{6,7},{7,6},{8,9},{9,8},{10,11... | collective-permute-start | bytes 7077896 | tf_op jit(solution)/shard_map/ppermute | solution.py:47
  546.8 13.8 %collective-permute-start.62 = (bf16[224,1152]{1,0:T(8,128)(2,1)}, bf16[224,1152]{1,0:T(8,128)(2,1)}, u32[]{:S(2)}, u32[]{:S(2)}) collective-permute-start(bf16[224,1152]{1,0:T(8,128)(2,1)} %get-tuple-element.200), channel_id=1, source_target_pairs={{0,8},{1,5},{2,10},{3,7},{8,16},{9,1},{10,18},{11,3},{16,24},{17,9... | collective-permute-start | bytes 1548296 | tf_op jit(solution)/shard_map/ppermute | solution.py:113
  548.4 12.2 %collective-permute-start.64 = (bf16[224,1152]{1,0:T(8,128)(2,1)S(1)}, bf16[224,1152]{1,0:T(8,128)(2,1)}, u32[]{:S(2)}, u32[]{:S(2)}) collective-permute-start(bf16[224,1152]{1,0:T(8,128)(2,1)S(1)} %get-tuple-element.202), channel_id=1, source_target_pairs={{0,4},{1,9},{2,6},{3,11},{8,0},{9,17},{10,2},{11,19},{16,8},{17,25... | collective-permute-start | bytes 1548296 | tf_op jit(solution)/shard_map/ppermute | solution.py:113
  552.3 19.0 %all-to-all-start.2 = ((bf16[4,36,3584]{2,1,0:T(8,128)(2,1)}), bf16[4,36,3584]{2,1,0:T(8,128)(2,1)S(1)}, u32[]{:S(2)}, u32[]{:S(2)}) async-start(bf16[4,36,3584]{2,1,0:T(8,128)(2,1)} %reshape.112), calls=%async_computation.2 | async-start | bytes 2293760 | tf_op jit(solution)/shard_map/all_to_all | solution.py:42
  584.9 27.8 %collective-permute-start.65 = (bf16[512,1152]{1,0:T(8,128)(2,1)}, bf16[512,1152]{1,0:T(8,128)(2,1)}, u32[]{:S(2)}, u32[]{:S(2)}) collective-permute-start(bf16[512,1152]{1,0:T(8,128)(2,1)} %slice_add_fusion), channel_id=1, source_target_pairs={{0,2},{1,3},{2,0},{3,1},{4,6},{5,7},{6,4},{7,5},{8,10},{9,11},{10,... | collective-permute-start | bytes 3538952 | tf_op jit(solution)/shard_map/ppermute | solution.py:47
  (172 other events, 1846.9 us)

commit v6 on v5

--- a/solution.py
+++ b/solution.py
@@ -1114,9 +1114,13 @@
         ],
         axis=1,
     )
-    out_own = lax.ppermute(out_own, ("dp", "ctx"), to_owner).astype(f32)
+    out_low = lax.ppermute(out_own, ("dp", "ctx"), to_owner)
+    out_own = out_low.astype(f32)
     in_own = exchange(
-        tie(in_own[:own_rows], gate_up_own, down_own).reshape(ctx, in_rows, qkv_cols), "ctx"
+        tie(in_own[:own_rows], gate_up_own, down_own, out_low, summed).reshape(
+            ctx, in_rows, qkv_cols
+        ),
+        "ctx",
     ).astype(f32)
     far = swap(tie(summed, gate_up_own, in_own), 2)
     input_grad = (

time: 645 us -> 642 us (level)
    unnamed x286 -> x288, local copies, waits for them, and re-layouts: 44.3 us -> 44.3 us
where the time goes in v6:
time: 642 us; the launch traced here: 632 us
  Pallas kernels  190 us (30%)
  waiting for transfers between devices  168 us (26%)
  starting transfers between devices  85.1 us (13%)
  other arithmetic  72.9 us (11%)
  local copies, waits for them, and re-layouts  60.4 us (9%)
  matrix products  46.9 us (7%)
  between operations  8.06 us (1%)
    pallas_call x17, Pallas kernels, call(): pl.pallas_call(kernel, out_shape=out_shape, grid_spec=pltpu.PrefetchScala...  190 us
    ppermute x42, waiting for transfers between devices, send(): return lax.ppermute(value, ('dp', 'ctx'), pairs)  99.6 us
    ppermute x42, starting transfers between devices, send(): return lax.ppermute(value, ('dp', 'ctx'), pairs)  50.9 us
    dot_general x7, matrix products, mm_tn(): lax.dot_general(a, b, (((0,), (0,)), ((), ())), preferred_element_type=F32)  46.9 us
    unnamed x288, local copies, waits for them, and re-layouts  44.3 us
    ppermute x25, waiting for transfers between devices, swap(): return lax.ppermute(value, 'ctx', [(i, i ^ bit) for i in range(count)])  43.2 us
    add x13, other arithmetic, add_low(): return a + b  28.4 us
    all_to_all x4, waiting for transfers between devices, exchange(): return lax.all_to_all(parts, axis, split_axis=0, concat_axis=0, tiled=True)  17.7 us
  transfers between devices with their start and end apart: 76, of which 37 were waited for; matrix products, arithmetic and copies ran while one was open for 13% of the time, Pallas kernels for 25%

profile of v6, /device:TPU:0, one launch (start us, length us, event | category | flops | bytes accessed | tf_op | source)
XLA Modules:
  0.0 631.8 jit_solution(16540298301176107342)
XLA Ops:
  12.0 3.6 all-to-all-done
  17.9 3.9 collective-permute-start.5
  22.5 5.5 multiply_sine_fusion
  32.6 4.2 collective-permute-done.6.refs_4_.refs_11_.refs_10_
  36.9 3.9 collective-permute-done.8.refs_5_.refs_12_.refs_11_
  40.8 3.6 collective-permute-done.1
  45.0 4.3 all-to-all-start.1
  51.8 7.3 %collective-permute-done.10.refs_6_.refs_13_.refs_12_ = bf16[208,768]{1,0:T(8,128)(2,1)S(1)} collective-permute-done((bf16[208,768]{1,0:T(8,128)(2,1)S(1)}, bf16[208,768]{1,0:T(8,128)(2,1)S(1)}, u32[]{:S(2)}, u32[]{:S(2)}) %collective-permute-start.10) | collective-permute-done | bytes 319520 | tf_op jit(solution)/shard_map/ppermute | solution.py:113
  61.6 3.7 all-to-all-done.1
  82.9 5.6 pad_maximum_fusion.refs_2_.refs_3_.refs_9_.refs_8_.refs_4_
  88.5 10.4 %shard_map.402 = (bf16[2048,256]{1,0:T(8,128)(2,1)S(1)}, bf16[2048,256]{1,0:T(8,128)(2,1)S(1)}, bf16[2048,256]{1,0:T(8,128)(2,1)S(1)}, f32[2048,512]{1,0:T(8,128)S(1)}, bf16[2048,1152]{1,0:T(8,128)(2,1)S(1)}) custom-call(s32[8]{0:T(128)S(1)} %fusion.21.refs_0_, s32[8]{0:T(128)S(1)} %fusion.24.refs_0_.refs_1_, ...), custom_call_target="tpu_custom_call" | custom-call | flops 226492416 | bytes 1634720 | tf_op jit(solution)/shard_map/pallas_call | solution.py:223
  112.1 5.6 shard_map.403
  123.8 23.4 %collective-permute-done.22.refs_6_.refs_15_ = bf16[144,3584]{1,0:T(8,128)(2,1)S(1)} collective-permute-done((bf16[144,3584]{1,0:T(8,128)(2,1)S(1)}, bf16[144,3584]{1,0:T(8,128)(2,1)S(1)}, u32[]{:S(2)}, u32[]{:S(2)}) %collective-permute-start.22) | collective-permute-done | bytes 1032224 | tf_op jit(solution)/shard_map/ppermute | solution.py:113
  153.9 11.7 %shard_map.404 = (f32[2048,1152]{1,0:T(8,128)}, bf16[2048,1152]{1,0:T(8,128)(2,1)S(1)}) custom-call(s32[8]{0:T(128)S(1)} %fusion.20.refs_0_, bf16[2048,256]{1,0:T(8,128)(2,1)S(1)} %get-tuple-element.135.refs_1_, bf16[2048,256]{1,0:T(8,128)(2,1)S(1)} %collective-permute-done.19.refs_2_, bf16[2048,256]{1,0:T(8,128)(2,1)S(1)} %collective-permute-done.20.refs_3_, ...), custom_call_target="tpu_custom_call" | custom-call | flops 301989888 | bytes 1590400 | tf_op jit(solution)/shard_map/pallas_call | solution.py:223
  165.7 6.6 %collective-permute-done.25.refs_7_.refs_16_ = bf16[144,3584]{1,0:T(8,128)(2,1)S(1)} collective-permute-done((bf16[144,3584]{1,0:T(8,128)(2,1)S(1)}, bf16[144,3584]{1,0:T(8,128)(2,1)S(1)}, u32[]{:S(2)}, u32[]{:S(2)}) %collective-permute-start.25) | collective-permute-done | bytes 1032224 | tf_op jit(solution)/shard_map/ppermute | solution.py:113
  175.8 21.6 %collective-permute-done.28.refs_7_.refs_8_ = bf16[224,1152]{1,0:T(8,128)(2,1)S(1)} collective-permute-done((bf16[224,1152]{1,0:T(8,128)(2,1)}, bf16[224,1152]{1,0:T(8,128)(2,1)S(1)}, u32[]{:S(2)}, u32[]{:S(2)}) %collective-permute-start.28) | collective-permute-done | bytes 516128 | tf_op jit(solution)/shard_map/ppermute | solution.py:113
  197.7 18.7 %shard_map.405 = (bf16[2048,1792]{1,0:T(8,128)(2,1)}, bf16[2048,3584]{1,0:T(8,128)(2,1)}) custom-call(s32[8]{0:T(128)S(1)} %fusion.24.refs_0_.refs_1_, bf16[2048,1152]{1,0:T(8,128)(2,1)S(1)} %get-tuple-element.150.refs_1_, bf16[144,3584]{1,0:T(8,128)(2,1)S(1)} %reshape.108.refs_2_.refs_11_, bf16[144,3584]{1,0:T(8,128)(2,1)S(1)} %collective-permute-done.13.refs_3_.refs_12_, ...), custom_call_target="tpu_custom_call" | custom-call | flops 528482304 | bytes 2187264 | tf_op jit(solution)/shard_map/pallas_call | solution.py:223
  219.9 7.4 %shard_map.406 = (bf16[512,1152]{1,0:T(8,128)(2,1)S(1)}, bf16[512,1152]{1,0:T(8,128)(2,1)S(1)}) custom-call(s32[8]{0:T(128)S(1)} %fusion.24.refs_0_.refs_1_, bf16[2048,1792]{1,0:T(8,128)(2,1)S(1)} %copy-done.1, bf16[224,1152]{1,0:T(8,128)(2,1)S(1)} %copy-done.27, bf16[224,1152]{1,0:T(8,128)(2,1)} %collective-permute-done.3.refs_3_.refs_4_, ...), custom_call_target="tpu_custom_call" | custom-call | flops 264241152 | bytes 864256 | tf_op jit(solution)/shard_map/pallas_call | solution.py:223
  237.0 19.2 %shard_map.407 = (bf16[2048,1792]{1,0:T(8,128)(2,1)}, bf16[2048,3584]{1,0:T(8,128)(2,1)}) custom-call(s32[8]{0:T(128)S(1)} %fusion.24.refs_0_.refs_1_, bf16[2048,1152]{1,0:T(8,128)(2,1)S(1)} %get-tuple-element.150.refs_1_, bf16[144,3584]{1,0:T(8,128)(2,1)S(1)} %reshape.108.refs_2_.refs_11_, ...), custom_call_target="tpu_custom_call", output_to_operand_aliasing={{0}: (10, {}), {1}: (11, {})} | custom-call | flops 528482304 | bytes 2187264 | tf_op jit(solution)/shard_map/pallas_call | solution.py:223
  264.9 7.4 %shard_map.408 = (bf16[512,1152]{1,0:T(8,128)(2,1)S(1)}, bf16[512,1152]{1,0:T(8,128)(2,1)S(1)}) custom-call(s32[8]{0:T(128)S(1)} %fusion.24.refs_0_.refs_1_, bf16[2048,1792]{1,0:T(8,128)(2,1)S(1)} %copy-done.2, bf16[224,1152]{1,0:T(8,128)(2,1)S(1)} %copy-done.27, bf16[224,1152]{1,0:T(8,128)(2,1)} %collective-permute-done.3.refs_3_.refs_4_, ...), custom_call_target="tpu_custom_call" | custom-call | flops 264241152 | bytes 864256 | tf_op jit(solution)/shard_map/pallas_call | solution.py:223
  275.3 4.3 shard_map.409
  282.8 12.2 %shard_map.410.refs_11_ = bf16[2048,3584]{1,0:T(8,128)(2,1)} custom-call(s32[8]{0:T(128)S(1)} %fusion.24.refs_0_.refs_1_, bf16[1024,1152]{1,0:T(8,128)(2,1)S(1)} %pad_maximum_fusion.2.refs_1_, bf16[2048,3584]{1,0:T(8,128)(2,1)} %get-tuple-element.161.refs_2_, bf16[224,1152]{1,0:T(8,128)(2,1)S(1)} %copy-done.27, ...), custom_call_target="tpu_custom_call" | custom-call | flops 264241152 | bytes 2240512 | tf_op jit(solution)/shard_map/pallas_call | solution.py:223
  295.0 13.1 %collective-permute-done.34 = bf16[512,1152]{1,0:T(8,128)(2,1)S(1)} collective-permute-done((bf16[512,1152]{1,0:T(8,128)(2,1)S(1)}, bf16[512,1152]{1,0:T(8,128)(2,1)S(1)}, u32[]{:S(2)}, u32[]{:S(2)}) %collective-permute-start.34) | collective-permute-done | bytes 1179680 | tf_op jit(solution)/shard_map/ppermute | solution.py:47
  312.2 12.7 %shard_map.411.refs_2_ = bf16[2048,3584]{1,0:T(8,128)(2,1)} custom-call(s32[8]{0:T(128)S(1)} %fusion.24.refs_0_.refs_1_, bf16[1024,1152]{1,0:T(8,128)(2,1)S(1)} %pad_maximum_fusion.3.refs_1_, bf16[2048,3584]{1,0:T(8,128)(2,1)} %get-tuple-element.161.refs_2_, bf16[224,1152]{1,0:T(8,128)(2,1)S(1)} %copy-done.27, ...), custom_call_target="tpu_custom_call", output_to_operand_aliasing={{}: (11, {})} | custom-call | flops 264241152 | bytes 2240512 | tf_op jit(solution)/shard_map/pallas_call | solution.py:223
  325.0 23.2 %convolution_convert_fusion = bf16[1152,3584]{1,0:T(8,128)(2,1)} fusion(bf16[2048,1152]{1,0:T(8,128)(2,1)S(1)} %bitcast.78, bf16[2048,3584]{1,0:T(8,128)(2,1)} %shard_map.411.refs_2_), kind=kOutput, calls=%fused_computation | convolution fusion | flops 16915562496 | bytes 27656192 | tf_op jit(solution)/shard_map/dot_general | solution.py:211
  348.1 4.9 constant_dynamic-slice_fusion.6
  355.7 26.2 %shard_map.412 = (bf16[2048,1152]{1,0:T(8,128)(2,1)S(1)}, bf16[2048,1152]{1,0:T(8,128)(2,1)}, bf16[2,1024,256]{2,1,0:T(8,128)(2,1)S(1)}, bf16[2,1024,256]{2,1,0:T(8,128)(2,1)S(1)}, f32[2,1152]{1,0:T(2,128)S(1)}) custom-call(s32[8]{0:T(128)S(1)} %fusion.20.refs_0_, s32[8]{0:T(128)S(1)} %fusion.24.refs_0_.refs_1_, bf16[2048,3584]{1,0:T(8,128)(2,1)} %shard_map.411.refs_2_, ...), custom_call_target="tpu_custom_call" | custom-call | flops 679477248 | bytes 3262144 | tf_op jit(solution)/shard_map/pallas_call | solution.py:223
  381.9 3.8 dynamic-slice_add_fusion.4
  392.7 12.5 %convolution_convert_fusion.1 = bf16[1792,1152]{1,0:T(8,128)(2,1)S(1)} fusion(bf16[2048,1792]{1,0:T(8,128)(2,1)S(1)} %bitcast.76, bf16[2048,1152]{1,0:T(8,128)(2,1)} %pad_maximum_fusion.1), kind=kOutput, calls=%fused_computation.1 | convolution fusion | flops 8457781248 | bytes 16187392 | tf_op jit(solution)/shard_map/dot_general | solution.py:211
  409.1 25.5 %shard_map.413 = (bf16[2048,1152]{1,0:T(8,128)(2,1)S(1)}, bf16[2048,1152]{1,0:T(8,128)(2,1)}, bf16[2,1024,256]{2,1,0:T(8,128)(2,1)S(1)}, bf16[2,1024,256]{2,1,0:T(8,128)(2,1)S(1)}, f32[2,1152]{1,0:T(2,128)S(1)}) custom-call(s32[8]{0:T(128)S(1)} %fusion.20.refs_0_, s32[8]{0:T(128)S(1)} %fusion.24.refs_0_.refs_1_, ...), custom_call_target="tpu_custom_call", output_to_operand_aliasing={{0}: (19, {}), {1}: (20, {})} | custom-call | flops 679477248 | bytes 3262144 | tf_op jit(solution)/shard_map/pallas_call | solution.py:223
  437.8 4.7 dynamic-slice_add_fusion.2
  455.8 5.8 collective-permute-done.44.refs_8_
  462.9 12.3 %shard_map.414 = (bf16[2048,768]{1,0:T(8,128)(2,1)S(1)}, f32[2,256]{1,0:T(2,128)S(1)}) custom-call(s32[3]{0:T(128)S(1)} %fusion.17.refs_0_, bf16[2048,256]{1,0:T(8,128)(2,1)S(1)} %copy-done.56, bf16[2048,256]{1,0:T(8,128)(2,1)S(1)} %copy-done.59, bf16[2048,256]{1,0:T(8,128)(2,1)S(1)} %copy-done.62, f32[2048,512]{1,0:T(8,128)} %copy-done.53, ...), custom_call_target="tpu_custom_call" | custom-call | flops 251658240 | bytes 1114880 | tf_op jit(solution)/shard_map/pallas_call | solution.py:223
  475.2 4.2 convolution_convert_fusion.2
  484.5 4.7 dynamic-slice_add_fusion
  497.2 12.5 %shard_map.415 = (bf16[1024,1152]{1,0:T(8,128)(2,1)S(1)}, bf16[1024,1152]{1,0:T(8,128)(2,1)}, f32[1,1152]{1,0:T(1,128)S(1)}) custom-call(s32[8]{0:T(128)S(1)} %compare_select_fusion.1.refs_0_, s32[8]{0:T(128)S(1)} %fusion.24.refs_0_.refs_1_, bf16[2048,768]{1,0:T(8,128)(2,1)S(1)} %get-tuple-element.188.refs_2_.refs_3_, ...), custom_call_target="tpu_custom_call" | custom-call | flops 226492416 | bytes 1438272 | tf_op jit(solution)/shard_map/pallas_call | solution.py:223
  511.4 9.9 %collective-permute-done.55 = bf16[192,768]{1,0:T(8,128)(2,1)S(1)} collective-permute-done((bf16[192,768]{1,0:T(8,128)(2,1)S(1)}, bf16[192,768]{1,0:T(8,128)(2,1)S(1)}, u32[]{:S(2)}, u32[]{:S(2)}) %collective-permute-start.55) | collective-permute-done | bytes 294944 | tf_op jit(solution)/shard_map/ppermute | solution.py:113
  527.6 4.2 collective-permute-done.61
  541.2 4.5 collective-permute-done.57
  556.7 3.8 collective-permute-done.62
  560.4 3.7 multiply_reduce_fusion.1
  566.7 4.6 all-to-all-done.2.refs_0_
  575.7 5.8 all-to-all-done.3
  597.2 4.0 collective-permute-start.70
  603.3 6.8 %collective-permute-done.66 = bf16[512,1152]{1,0:T(8,128)(2,1)} collective-permute-done((bf16[512,1152]{1,0:T(8,128)(2,1)}, bf16[512,1152]{1,0:T(8,128)(2,1)}, u32[]{:S(2)}, u32[]{:S(2)}) %collective-permute-start.66) | collective-permute-done | bytes 1179680 | tf_op jit(solution)/shard_map/ppermute | solution.py:47
  610.7 3.8 add_bitcast_fusion
  617.6 4.0 multiply_subtract_fusion.1
  622.7 3.9 multiply_subtract_fusion
  (523 shorter events, 204.6 us)
Async XLA Ops:
  2.2 15.2 %collective-permute-start.3 = (bf16[224,1152]{1,0:T(8,128)(2,1)S(1)}, bf16[224,1152]{1,0:T(8,128)(2,1)}, u32[]{:S(2)}, u32[]{:S(2)}) collective-permute-start(bf16[224,1152]{1,0:T(8,128)(2,1)S(1)} %pad.13.refs_2_.refs_3_), channel_id=1, source_target_pairs={{0,8},{1,5},{2,10},{3,7},{8,16},{9,1},{10,18},{11,3},{16,24},{17,9... | collective-permute-start | bytes 1548296 | tf_op jit(solution)/shard_map/ppermute | solution.py:113
  5.3 12.6 %collective-permute-start.4 = (bf16[224,1152]{1,0:T(8,128)(2,1)S(1)}, bf16[224,1152]{1,0:T(8,128)(2,1)}, u32[]{:S(2)}, u32[]{:S(2)}) collective-permute-start(bf16[224,1152]{1,0:T(8,128)(2,1)S(1)} %pad.13.refs_2_.refs_3_), channel_id=1, source_target_pairs={{0,4},{1,9},{2,6},{3,11},{8,0},{9,17},{10,2},{11,19},{16,8},{17,25... | collective-permute-start | bytes 1548296 | tf_op jit(solution)/shard_map/ppermute | solution.py:113
  15.7 28.8 %collective-permute-start.1 = (bf16[512,1152]{1,0:T(8,128)(2,1)}, bf16[512,1152]{1,0:T(8,128)(2,1)}, u32[]{:S(2)}, u32[]{:S(2)}) collective-permute-start(bf16[512,1152]{1,0:T(8,128)(2,1)} %bitcast.2.refs_4_), channel_id=1, source_target_pairs={{0,2},{1,3},{2,0},{3,1},{4,6},{5,7},{6,4},{7,5},{8,10},{9,11},{10,... | collective-permute-start | bytes 3538952 | tf_op jit(solution)/shard_map/ppermute | solution.py:47
  44.5 23.7 %collective-permute-start.9 = (bf16[512,1152]{1,0:T(8,128)(2,1)}, bf16[512,1152]{1,0:T(8,128)(2,1)}, u32[]{:S(2)}, u32[]{:S(2)}) collective-permute-start(bf16[512,1152]{1,0:T(8,128)(2,1)} %collective-permute-done.1), channel_id=1, source_target_pairs={{0,1},{1,0},{2,3},{3,2},{4,5},{5,4},{6,7},{7,6},{8,9},{9,8},{10,11... | collective-permute-start | bytes 3538952 | tf_op jit(solution)/shard_map/ppermute | solution.py:47
  44.7 38.2 %collective-permute-start = (bf16[512,1152]{1,0:T(8,128)(2,1)}, bf16[512,1152]{1,0:T(8,128)(2,1)}, u32[]{:S(2)}, u32[]{:S(2)}) collective-permute-start(bf16[512,1152]{1,0:T(8,128)(2,1)} %bitcast.2.refs_4_), channel_id=1, source_target_pairs={{0,1},{1,0},{2,3},{3,2},{4,5},{5,4},{6,7},{7,6},{8,9},{9,8},{10,11... | collective-permute-start | bytes 3538952 | tf_op jit(solution)/shard_map/ppermute | solution.py:47
  45.0 20.3 %all-to-all-start.1 = ((bf16[4,36,3584]{2,1,0:T(8,128)(2,1)}), bf16[4,36,3584]{2,1,0:T(8,128)(2,1)}, u32[]{:S(2)}, u32[]{:S(2)}) async-start(bf16[4,36,3584]{2,1,0:T(8,128)(2,1)} %shard_map.400), calls=%async_computation.1 | async-start | bytes 2293760 | tf_op jit(solution)/shard_map/all_to_all | solution.py:42
  51.3 15.4 %collective-permute-start.11 = (bf16[208,768]{1,0:T(8,128)(2,1)S(1)}, bf16[208,768]{1,0:T(8,128)(2,1)S(1)}, u32[]{:S(2)}, u32[]{:S(2)}) collective-permute-start(bf16[208,768]{1,0:T(8,128)(2,1)S(1)} %collective-permute-done.8.refs_5_.refs_12_.refs_11_), channel_id=1, source_target_pairs={{0,4},{1,9},{2,6},{3,11},{8,0},{9,17},{10,2},{11,19},{16,8},{17,25... | collective-permute-start | bytes 958472 | tf_op jit(solution)/shard_map/ppermute | solution.py:113
  68.2 37.9 %collective-permute-start.13 = (bf16[144,3584]{1,0:T(8,128)(2,1)S(1)}, bf16[144,3584]{1,0:T(8,128)(2,1)S(1)}, u32[]{:S(2)}, u32[]{:S(2)}) collective-permute-start(bf16[144,3584]{1,0:T(8,128)(2,1)S(1)} %reshape.108.refs_2_.refs_11_), channel_id=1, source_target_pairs={{0,8},{1,5},{2,10},{3,7},{8,16},{9,1},{10,18},{11,3},{16,24},{17,9... | collective-permute-start | bytes 3096584 | tf_op jit(solution)/shard_map/ppermute | solution.py:113
  69.6 36.4 %collective-permute-start.14 = (bf16[144,3584]{1,0:T(8,128)(2,1)S(1)}, bf16[144,3584]{1,0:T(8,128)(2,1)S(1)}, u32[]{:S(2)}, u32[]{:S(2)}) collective-permute-start(bf16[144,3584]{1,0:T(8,128)(2,1)S(1)} %reshape.108.refs_2_.refs_11_), channel_id=1, source_target_pairs={{0,4},{1,9},{2,6},{3,11},{8,0},{9,17},{10,2},{11,19},{16,8},{17,25... | collective-permute-start | bytes 3096584 | tf_op jit(solution)/shard_map/ppermute | solution.py:113
  81.6 26.8 %collective-permute-start.15 = (bf16[256,1152]{1,0:T(8,128)(2,1)}, bf16[256,1152]{1,0:T(8,128)(2,1)}, u32[]{:S(2)}, u32[]{:S(2)}) collective-permute-start(bf16[256,1152]{1,0:T(8,128)(2,1)} %get-tuple-element.128.refs_5_.refs_3_), channel_id=1, source_target_pairs={{0,2},{1,3},{2,0},{3,1},{4,6},{5,7},{6,4},{7,5},{8,10},{9,11},{10,... | collective-permute-start | bytes 1769480 | tf_op jit(solution)/shard_map/ppermute | solution.py:47
  82.8 25.6 %collective-permute-start.16 = (bf16[256,1152]{1,0:T(8,128)(2,1)}, bf16[256,1152]{1,0:T(8,128)(2,1)}, u32[]{:S(2)}, u32[]{:S(2)}) collective-permute-start(bf16[256,1152]{1,0:T(8,128)(2,1)} %get-tuple-element.128.refs_5_.refs_3_), channel_id=1, source_target_pairs={{0,1},{1,0},{2,3},{3,2},{4,5},{5,4},{6,7},{7,6},{8,9},{9,8},{10,11... | collective-permute-start | bytes 1769480 | tf_op jit(solution)/shard_map/ppermute | solution.py:47
  106.1 14.2 %collective-permute-start.18 = (bf16[224,1152]{1,0:T(8,128)(2,1)}, bf16[224,1152]{1,0:T(8,128)(2,1)}, u32[]{:S(2)}, u32[]{:S(2)}) collective-permute-start(bf16[224,1152]{1,0:T(8,128)(2,1)} %collective-permute-done.4.refs_4_.refs_5_), channel_id=1, source_target_pairs={{0,4},{1,9},{2,6},{3,11},{8,0},{9,17},{10,2},{11,19},{16,8},{17,25... | collective-permute-start | bytes 1548296 | tf_op jit(solution)/shard_map/ppermute | solution.py:113
  108.0 12.7 %collective-permute-start.17 = (bf16[224,1152]{1,0:T(8,128)(2,1)}, bf16[224,1152]{1,0:T(8,128)(2,1)}, u32[]{:S(2)}, u32[]{:S(2)}) collective-permute-start(bf16[224,1152]{1,0:T(8,128)(2,1)} %collective-permute-done.3.refs_3_.refs_4_), channel_id=1, source_target_pairs={{0,8},{1,5},{2,10},{3,7},{8,16},{9,1},{10,18},{11,3},{16,24},{17,9... | collective-permute-start | bytes 1548296 | tf_op jit(solution)/shard_map/ppermute | solution.py:113
  120.7 26.5 %collective-permute-start.20 = (bf16[2048,256]{1,0:T(8,128)(2,1)S(1)}, bf16[2048,256]{1,0:T(8,128)(2,1)S(1)}, u32[]{:S(2)}, u32[]{:S(2)}) collective-permute-start(bf16[2048,256]{1,0:T(8,128)(2,1)S(1)} %get-tuple-element.135.refs_1_), channel_id=1, source_target_pairs={{0,2},{1,3},{2,0},{3,1},{4,6},{5,7},{6,4},{7,5},{8,10},{9,11},{10,... | collective-permute-start | bytes 3145736 | tf_op jit(solution)/shard_map/ppermute | solution.py:47
  121.7 25.5 %collective-permute-start.22 = (bf16[144,3584]{1,0:T(8,128)(2,1)S(1)}, bf16[144,3584]{1,0:T(8,128)(2,1)S(1)}, u32[]{:S(2)}, u32[]{:S(2)}) collective-permute-start(bf16[144,3584]{1,0:T(8,128)(2,1)S(1)} %collective-permute-done.14.refs_4_.refs_13_), channel_id=1, source_target_pairs={{0,4},{1,9},{2,6},{3,11},{8,0},{9,17},{10,2},{11,19},{16,8},{17,25... | collective-permute-start | bytes 3096584 | tf_op jit(solution)/shard_map/ppermute | solution.py:113
  123.5 23.7 %collective-permute-start.21 = (bf16[144,3584]{1,0:T(8,128)(2,1)S(1)}, bf16[144,3584]{1,0:T(8,128)(2,1)S(1)}, u32[]{:S(2)}, u32[]{:S(2)}) collective-permute-start(bf16[144,3584]{1,0:T(8,128)(2,1)S(1)} %collective-permute-done.13.refs_3_.refs_12_), channel_id=1, source_target_pairs={{0,8},{1,5},{2,10},{3,7},{8,16},{9,1},{10,18},{11,3},{16,24},{17,9... | collective-permute-start | bytes 3096584 | tf_op jit(solution)/shard_map/ppermute | solution.py:113
  123.8 27.2 %collective-permute-start.19 = (bf16[2048,256]{1,0:T(8,128)(2,1)S(1)}, bf16[2048,256]{1,0:T(8,128)(2,1)S(1)}, u32[]{:S(2)}, u32[]{:S(2)}) collective-permute-start(bf16[2048,256]{1,0:T(8,128)(2,1)S(1)} %get-tuple-element.135.refs_1_), channel_id=1, source_target_pairs={{0,1},{1,0},{2,3},{3,2},{4,5},{5,4},{6,7},{7,6},{8,9},{9,8},{10,11... | collective-permute-start | bytes 3145736 | tf_op jit(solution)/shard_map/ppermute | solution.py:47
  147.4 24.8 %collective-permute-start.25 = (bf16[144,3584]{1,0:T(8,128)(2,1)S(1)}, bf16[144,3584]{1,0:T(8,128)(2,1)S(1)}, u32[]{:S(2)}, u32[]{:S(2)}) collective-permute-start(bf16[144,3584]{1,0:T(8,128)(2,1)S(1)} %collective-permute-done.21.refs_5_.refs_14_), channel_id=1, source_target_pairs={{0,8},{1,5},{2,10},{3,7},{8,16},{9,1},{10,18},{11,3},{16,24},{17,9... | collective-permute-start | bytes 3096584 | tf_op jit(solution)/shard_map/ppermute | solution.py:113
  148.5 49.2 %collective-permute-start.26 = (bf16[144,3584]{1,0:T(8,128)(2,1)S(1)}, bf16[144,3584]{1,0:T(8,128)(2,1)S(1)}, u32[]{:S(2)}, u32[]{:S(2)}) collective-permute-start(bf16[144,3584]{1,0:T(8,128)(2,1)S(1)} %collective-permute-done.22.refs_6_.refs_15_), channel_id=1, source_target_pairs={{0,4},{1,9},{2,6},{3,11},{8,0},{9,17},{10,2},{11,19},{16,8},{17,25... | collective-permute-start | bytes 3096584 | tf_op jit(solution)/shard_map/ppermute | solution.py:113
  172.2 25.4 %collective-permute-start.27 = (bf16[144,3584]{1,0:T(8,128)(2,1)S(1)}, bf16[144,3584]{1,0:T(8,128)(2,1)S(1)}, u32[]{:S(2)}, u32[]{:S(2)}) collective-permute-start(bf16[144,3584]{1,0:T(8,128)(2,1)S(1)} %collective-permute-done.25.refs_7_.refs_16_), channel_id=1, source_target_pairs={{0,8},{1,5},{2,10},{3,7},{8,16},{9,1},{10,18},{11,3},{16,24},{17,9... | collective-permute-start | bytes 3096584 | tf_op jit(solution)/shard_map/ppermute | solution.py:113
  173.3 24.1 %collective-permute-start.28 = (bf16[224,1152]{1,0:T(8,128)(2,1)}, bf16[224,1152]{1,0:T(8,128)(2,1)S(1)}, u32[]{:S(2)}, u32[]{:S(2)}) collective-permute-start(bf16[224,1152]{1,0:T(8,128)(2,1)} %collective-permute-done.17.refs_5_.refs_6_), channel_id=1, source_target_pairs={{0,8},{1,5},{2,10},{3,7},{8,16},{9,1},{10,18},{11,3},{16,24},{17,9... | collective-permute-start | bytes 1548296 | tf_op jit(solution)/shard_map/ppermute | solution.py:113
  175.8 40.7 %collective-permute-start.29 = (bf16[224,1152]{1,0:T(8,128)(2,1)}, bf16[224,1152]{1,0:T(8,128)(2,1)S(1)}, u32[]{:S(2)}, u32[]{:S(2)}) collective-permute-start(bf16[224,1152]{1,0:T(8,128)(2,1)} %collective-permute-done.18.refs_6_.refs_7_), channel_id=1, source_target_pairs={{0,4},{1,9},{2,6},{3,11},{8,0},{9,17},{10,2},{11,19},{16,8},{17,25... | collective-permute-start | bytes 1548296 | tf_op jit(solution)/shard_map/ppermute | solution.py:113
  197.4 19.1 %collective-permute-start.30 = (bf16[224,1152]{1,0:T(8,128)(2,1)S(1)}, bf16[224,1152]{1,0:T(8,128)(2,1)S(1)}, u32[]{:S(2)}, u32[]{:S(2)}) collective-permute-start(bf16[224,1152]{1,0:T(8,128)(2,1)S(1)} %collective-permute-done.28.refs_7_.refs_8_), channel_id=1, source_target_pairs={{0,8},{1,5},{2,10},{3,7},{8,16},{9,1},{10,18},{11,3},{16,24},{17,9... | collective-permute-start | bytes 1548296 | tf_op jit(solution)/shard_map/ppermute | solution.py:113
  230.7 28.1 %collective-permute-start.32 = (bf16[512,1152]{1,0:T(8,128)(2,1)S(1)}, bf16[512,1152]{1,0:T(8,128)(2,1)S(1)}, u32[]{:S(2)}, u32[]{:S(2)}) collective-permute-start(bf16[512,1152]{1,0:T(8,128)(2,1)S(1)} %add.264), channel_id=1, source_target_pairs={{0,2},{1,3},{2,0},{3,1},{4,6},{5,7},{6,4},{7,5},{8,10},{9,11},{10,... | collective-permute-start | bytes 3538952 | tf_op jit(solution)/shard_map/ppermute | solution.py:47
  279.9 28.3 %collective-permute-start.34 = (bf16[512,1152]{1,0:T(8,128)(2,1)S(1)}, bf16[512,1152]{1,0:T(8,128)(2,1)S(1)}, u32[]{:S(2)}, u32[]{:S(2)}) collective-permute-start(bf16[512,1152]{1,0:T(8,128)(2,1)S(1)} %get-tuple-element.160), channel_id=1, source_target_pairs={{0,2},{1,3},{2,0},{3,1},{4,6},{5,7},{6,4},{7,5},{8,10},{9,11},{10,... | collective-permute-start | bytes 3538952 | tf_op jit(solution)/shard_map/ppermute | solution.py:47
  353.0 28.9 %collective-permute-start.37 = (bf16[144,3584]{1,0:T(8,128)(2,1)S(1)}, bf16[144,3584]{1,0:T(8,128)(2,1)S(1)}, u32[]{:S(2)}, u32[]{:S(2)}) collective-permute-start(bf16[144,3584]{1,0:T(8,128)(2,1)S(1)} %get-tuple-element.236), channel_id=1, source_target_pairs={{0,8},{1,5},{2,10},{3,7},{8,16},{9,1},{10,18},{11,3},{16,24},{17,9... | collective-permute-start | bytes 3096584 | tf_op jit(solution)/shard_map/ppermute | solution.py:113
  386.5 48.1 %collective-permute-start.41 = (bf16[144,3584]{1,0:T(8,128)(2,1)}, bf16[144,3584]{1,0:T(8,128)(2,1)}, u32[]{:S(2)}, u32[]{:S(2)}) collective-permute-start(bf16[144,3584]{1,0:T(8,128)(2,1)} %get-tuple-element.235), channel_id=1, source_target_pairs={{0,4},{1,9},{2,6},{3,11},{8,0},{9,17},{10,2},{11,19},{16,8},{17,25... | collective-permute-start | bytes 3096584 | tf_op jit(solution)/shard_map/ppermute | solution.py:113
  389.8 44.8 %collective-permute-start.40 = (bf16[144,3584]{1,0:T(8,128)(2,1)}, bf16[144,3584]{1,0:T(8,128)(2,1)S(1)}, u32[]{:S(2)}, u32[]{:S(2)}) collective-permute-start(bf16[144,3584]{1,0:T(8,128)(2,1)} %dynamic-slice_add_fusion.4), channel_id=1, source_target_pairs={{0,8},{1,5},{2,10},{3,7},{8,16},{9,1},{10,18},{11,3},{16,24},{17,9... | collective-permute-start | bytes 3096584 | tf_op jit(solution)/shard_map/ppermute | solution.py:113
  391.6 17.5 %collective-permute-start.39 = (bf16[1024,256]{1,0:T(8,128)(2,1)S(1)}, bf16[1024,256]{1,0:T(8,128)(2,1)S(1)}, u32[]{:S(2)}, u32[]{:S(2)}) collective-permute-start(bf16[1024,256]{1,0:T(8,128)(2,1)S(1)} %fusion.3), channel_id=1, source_target_pairs={{0,2},{1,3},{2,0},{3,1},{4,6},{5,7},{6,4},{7,5},{8,10},{9,11},{10,... | collective-permute-start | bytes 1572872 | tf_op jit(solution)/shard_map/ppermute | solution.py:47
  407.7 26.9 %collective-permute-start.42 = (bf16[224,1152]{1,0:T(8,128)(2,1)S(1)}, bf16[224,1152]{1,0:T(8,128)(2,1)S(1)}, u32[]{:S(2)}, u32[]{:S(2)}) collective-permute-start(bf16[224,1152]{1,0:T(8,128)(2,1)S(1)} %get-tuple-element.242), channel_id=1, source_target_pairs={{0,8},{1,5},{2,10},{3,7},{8,16},{9,1},{10,18},{11,3},{16,24},{17,9... | collective-permute-start | bytes 1548296 | tf_op jit(solution)/shard_map/ppermute | solution.py:113
  446.3 35.4 %collective-permute-start.51 = (bf16[224,1152]{1,0:T(8,128)(2,1)}, bf16[224,1152]{1,0:T(8,128)(2,1)}, u32[]{:S(2)}, u32[]{:S(2)}) collective-permute-start(bf16[224,1152]{1,0:T(8,128)(2,1)} %get-tuple-element.241), channel_id=1, source_target_pairs={{0,4},{1,9},{2,6},{3,11},{8,0},{9,17},{10,2},{11,19},{16,8},{17,25... | collective-permute-start | bytes 1548296 | tf_op jit(solution)/shard_map/ppermute | solution.py:113
  447.0 14.6 %collective-permute-start.44 = (bf16[1024,256]{1,0:T(8,128)(2,1)S(1)}, bf16[1024,256]{1,0:T(8,128)(2,1)S(1)}, u32[]{:S(2)}, u32[]{:S(2)}) collective-permute-start(bf16[1024,256]{1,0:T(8,128)(2,1)S(1)} %fusion.2), channel_id=1, source_target_pairs={{0,2},{1,3},{2,0},{3,1},{4,6},{5,7},{6,4},{7,5},{8,10},{9,11},{10,... | collective-permute-start | bytes 1572872 | tf_op jit(solution)/shard_map/ppermute | solution.py:47
  449.8 32.0 %collective-permute-start.50 = (bf16[224,1152]{1,0:T(8,128)(2,1)}, bf16[224,1152]{1,0:T(8,128)(2,1)}, u32[]{:S(2)}, u32[]{:S(2)}) collective-permute-start(bf16[224,1152]{1,0:T(8,128)(2,1)} %dynamic-slice_add_fusion.9), channel_id=1, source_target_pairs={{0,8},{1,5},{2,10},{3,7},{8,16},{9,1},{10,18},{11,3},{16,24},{17,9... | collective-permute-start | bytes 1548296 | tf_op jit(solution)/shard_map/ppermute | solution.py:113
  451.4 31.1 %collective-permute-start.48 = (bf16[144,3584]{1,0:T(8,128)(2,1)S(1)}, bf16[144,3584]{1,0:T(8,128)(2,1)}, u32[]{:S(2)}, u32[]{:S(2)}) collective-permute-start(bf16[144,3584]{1,0:T(8,128)(2,1)S(1)} %get-tuple-element.234), channel_id=1, source_target_pairs={{0,8},{1,5},{2,10},{3,7},{8,16},{9,1},{10,18},{11,3},{16,24},{17,9... | collective-permute-start | bytes 3096584 | tf_op jit(solution)/shard_map/ppermute | solution.py:113
  452.9 29.5 %collective-permute-start.49 = (bf16[144,3584]{1,0:T(8,128)(2,1)S(1)}, bf16[144,3584]{1,0:T(8,128)(2,1)}, u32[]{:S(2)}, u32[]{:S(2)}) collective-permute-start(bf16[144,3584]{1,0:T(8,128)(2,1)S(1)} %get-tuple-element.233), channel_id=1, source_target_pairs={{0,4},{1,9},{2,6},{3,11},{8,0},{9,17},{10,2},{11,19},{16,8},{17,25... | collective-permute-start | bytes 3096584 | tf_op jit(solution)/shard_map/ppermute | solution.py:113
  461.6 17.7 %collective-permute-start.46 = (bf16[256,1152]{1,0:T(8,128)(2,1)}, bf16[256,1152]{1,0:T(8,128)(2,1)S(1)}, u32[]{:S(2)}, u32[]{:S(2)}) collective-permute-start(bf16[256,1152]{1,0:T(8,128)(2,1)} %slice_add_fusion.1), channel_id=1, source_target_pairs={{0,2},{1,3},{2,0},{3,1},{4,6},{5,7},{6,4},{7,5},{8,10},{9,11},{10,... | collective-permute-start | bytes 1769480 | tf_op jit(solution)/shard_map/ppermute | solution.py:47
  482.5 11.8 %collective-permute-start.47 = (bf16[192,768]{1,0:T(8,128)(2,1)S(1)}, bf16[192,768]{1,0:T(8,128)(2,1)S(1)}, u32[]{:S(2)}, u32[]{:S(2)}) collective-permute-start(bf16[192,768]{1,0:T(8,128)(2,1)S(1)} %get-tuple-element.248), channel_id=1, source_target_pairs={{0,8},{1,5},{2,10},{3,7},{8,16},{9,1},{10,18},{11,3},{16,24},{17,9... | collective-permute-start | bytes 884744 | tf_op jit(solution)/shard_map/ppermute | solution.py:113
  484.0 25.8 %collective-permute-start.58 = (bf16[192,768]{1,0:T(8,128)(2,1)S(1)}, bf16[192,768]{1,0:T(8,128)(2,1)S(1)}, u32[]{:S(2)}, u32[]{:S(2)}) collective-permute-start(bf16[192,768]{1,0:T(8,128)(2,1)S(1)} %get-tuple-element.247), channel_id=1, source_target_pairs={{0,4},{1,9},{2,6},{3,11},{8,0},{9,17},{10,2},{11,19},{16,8},{17,25... | collective-permute-start | bytes 884744 | tf_op jit(solution)/shard_map/ppermute | solution.py:113
  489.3 33.4 %collective-permute-start.52 = (bf16[144,3584]{1,0:T(8,128)(2,1)S(1)}, bf16[144,3584]{1,0:T(8,128)(2,1)S(1)}, u32[]{:S(2)}, u32[]{:S(2)}) collective-permute-start(bf16[144,3584]{1,0:T(8,128)(2,1)S(1)} %get-tuple-element.232), channel_id=1, source_target_pairs={{0,8},{1,5},{2,10},{3,7},{8,16},{9,1},{10,18},{11,3},{16,24},{17,9... | collective-permute-start | bytes 3096584 | tf_op jit(solution)/shard_map/ppermute | solution.py:113
  490.8 31.9 %collective-permute-start.53 = (bf16[144,3584]{1,0:T(8,128)(2,1)S(1)}, bf16[144,3584]{1,0:T(8,128)(2,1)S(1)}, u32[]{:S(2)}, u32[]{:S(2)}) collective-permute-start(bf16[144,3584]{1,0:T(8,128)(2,1)S(1)} %get-tuple-element.231), channel_id=1, source_target_pairs={{0,4},{1,9},{2,6},{3,11},{8,0},{9,17},{10,2},{11,19},{16,8},{17,25... | collective-permute-start | bytes 3096584 | tf_op jit(solution)/shard_map/ppermute | solution.py:113
  495.0 26.2 %collective-permute-start.55 = (bf16[192,768]{1,0:T(8,128)(2,1)S(1)}, bf16[192,768]{1,0:T(8,128)(2,1)S(1)}, u32[]{:S(2)}, u32[]{:S(2)}) collective-permute-start(bf16[192,768]{1,0:T(8,128)(2,1)S(1)} %dynamic-slice_add_fusion.14), channel_id=1, source_target_pairs={{0,8},{1,5},{2,10},{3,7},{8,16},{9,1},{10,18},{11,3},{16,24},{17,9... | collective-permute-start | bytes 884744 | tf_op jit(solution)/shard_map/ppermute | solution.py:113
  496.6 31.1 %collective-permute-start.63 = (bf16[224,1152]{1,0:T(8,128)(2,1)S(1)}, bf16[224,1152]{1,0:T(8,128)(2,1)S(1)}, u32[]{:S(2)}, u32[]{:S(2)}) collective-permute-start(bf16[224,1152]{1,0:T(8,128)(2,1)S(1)} %get-tuple-element.239), channel_id=1, source_target_pairs={{0,4},{1,9},{2,6},{3,11},{8,0},{9,17},{10,2},{11,19},{16,8},{17,25... | collective-permute-start | bytes 1548296 | tf_op jit(solution)/shard_map/ppermute | solution.py:113
  509.8 22.1 %collective-permute-start.61 = (bf16[224,1152]{1,0:T(8,128)(2,1)S(1)}, bf16[224,1152]{1,0:T(8,128)(2,1)S(1)}, u32[]{:S(2)}, u32[]{:S(2)}) collective-permute-start(bf16[224,1152]{1,0:T(8,128)(2,1)S(1)} %get-tuple-element.240), channel_id=1, source_target_pairs={{0,8},{1,5},{2,10},{3,7},{8,16},{9,1},{10,18},{11,3},{16,24},{17,9... | collective-permute-start | bytes 1548296 | tf_op jit(solution)/shard_map/ppermute | solution.py:113
  531.9 32.2 %collective-permute-start.54 = (bf16[1024,1152]{1,0:T(8,128)(2,1)}, bf16[1024,1152]{1,0:T(8,128)(2,1)}, u32[]{:S(2)}, u32[]{:S(2)}) collective-permute-start(bf16[1024,1152]{1,0:T(8,128)(2,1)} %get-tuple-element.192), channel_id=1, source_target_pairs={{0,1},{1,0},{2,3},{3,2},{4,5},{5,4},{6,7},{7,6},{8,9},{9,8},{10,11... | collective-permute-start | bytes 7077896 | tf_op jit(solution)/shard_map/ppermute | solution.py:47
  546.6 13.9 %collective-permute-start.62 = (bf16[224,1152]{1,0:T(8,128)(2,1)}, bf16[224,1152]{1,0:T(8,128)(2,1)S(1)}, u32[]{:S(2)}, u32[]{:S(2)}) collective-permute-start(bf16[224,1152]{1,0:T(8,128)(2,1)} %get-tuple-element.200), channel_id=1, source_target_pairs={{0,8},{1,5},{2,10},{3,7},{8,16},{9,1},{10,18},{11,3},{16,24},{17,9... | collective-permute-start | bytes 1548296 | tf_op jit(solution)/shard_map/ppermute | solution.py:113
  548.0 12.4 %collective-permute-start.64 = (bf16[224,1152]{1,0:T(8,128)(2,1)}, bf16[224,1152]{1,0:T(8,128)(2,1)}, u32[]{:S(2)}, u32[]{:S(2)}) collective-permute-start(bf16[224,1152]{1,0:T(8,128)(2,1)} %get-tuple-element.202), channel_id=1, source_target_pairs={{0,4},{1,9},{2,6},{3,11},{8,0},{9,17},{10,2},{11,19},{16,8},{17,25... | collective-permute-start | bytes 1548296 | tf_op jit(solution)/shard_map/ppermute | solution.py:113
  552.3 19.0 %all-to-all-start.2 = ((bf16[4,36,3584]{2,1,0:T(8,128)(2,1)}), bf16[4,36,3584]{2,1,0:T(8,128)(2,1)S(1)}, u32[]{:S(2)}, u32[]{:S(2)}) async-start(bf16[4,36,3584]{2,1,0:T(8,128)(2,1)} %reshape.112), calls=%async_computation.2 | async-start | bytes 2293760 | tf_op jit(solution)/shard_map/all_to_all | solution.py:42
  582.3 27.8 %collective-permute-start.66 = (bf16[512,1152]{1,0:T(8,128)(2,1)}, bf16[512,1152]{1,0:T(8,128)(2,1)}, u32[]{:S(2)}, u32[]{:S(2)}) collective-permute-start(bf16[512,1152]{1,0:T(8,128)(2,1)} %slice_add_fusion), channel_id=1, source_target_pairs={{0,2},{1,3},{2,0},{3,1},{4,6},{5,7},{6,4},{7,5},{8,10},{9,11},{10,... | collective-permute-start | bytes 3538952 | tf_op jit(solution)/shard_map/ppermute | solution.py:47
  (172 other events, 1829.1 us)
